TPU v7x, 32 devices: a whole 2x2x4 slice. The times are simulated.
32 devices in a mesh: cplx: 4 (over y, x), smp: 4 (over z), qry: 2 (over core).
Axes of the slice: x: 2, y: 2, z: 4, core: 2. Of those that a mesh axis runs over, the one named last changes fastest.
Arguments:
- single: bfloat16 [4, 16, 640, 768], P('cplx', 'smp', 'qry'), may hold values from -6 to 6
- condition: bfloat16 [4, 640, 384], P('cplx', 'qry'), may hold values from -6 to 6
- pair_features: bfloat16 [4, 640, 640, 128], P('cplx', ('qry', 'smp')), may hold values from -6 to 6
- lengths: int32 [4], P('cplx'), may hold values from 448 to 640, as said below
- cotangent: bfloat16 [4, 16, 640, 768], P('cplx', 'smp', 'qry'), may hold values from -6 to 6
- first_gain: bfloat16 [384], replicated, may hold values from 0.099609375 to 1.8984375
- first_scale: bfloat16 [384, 768], replicated, may hold values from -0.3125 to 0.3125
- first_offset: bfloat16 [768], replicated, may hold values from -4 to 4
- first_shift: bfloat16 [384, 768], replicated, may hold values from -0.3125 to 0.3125
- query_projection_weight: bfloat16 [768, 768], replicated, may hold values from -0.21875 to 0.21875
- query_bias_vector: bfloat16 [768], replicated, may hold values from -3 to 3
- key_projection_weight: bfloat16 [768, 768], replicated, may hold values from -0.21875 to 0.21875
- value_projection_weight: bfloat16 [768, 768], replicated, may hold values from -0.21875 to 0.21875
- attention_gate_weight: bfloat16 [768, 768], replicated, may hold values from -0.21875 to 0.21875
- attention_output_weight: bfloat16 [768, 768], replicated, may hold values from -1.25 to 1.25
- pair_gain: bfloat16 [128], replicated, may hold values from 0.099609375 to 1.8984375
- pair_project: bfloat16 [128, 16], replicated, may hold values from -0.5 to 0.5
- finish_weight: bfloat16 [384, 768], replicated, may hold values from -0.3125 to 0.3125
- finish_offset: bfloat16 [768], replicated, may hold values from -4 to 4
- second_gain: bfloat16 [384], replicated, may hold values from 0.099609375 to 1.8984375
- second_scale: bfloat16 [384, 768], replicated, may hold values from -0.3125 to 0.3125
- second_offset: bfloat16 [768], replicated, may hold values from -4 to 4
- second_shift: bfloat16 [384, 768], replicated, may hold values from -0.3125 to 0.3125
- transition_swish_weight: bfloat16 [768, 1536], replicated, may hold values from -0.21875 to 0.21875
- transition_linear_weight: bfloat16 [768, 1536], replicated, may hold values from -0.21875 to 0.21875
- transition_down_weight: bfloat16 [1536, 768], replicated, may hold values from -0.4375 to 0.4375
- closing_weight: bfloat16 [384, 768], replicated, may hold values from -0.3125 to 0.3125
- closing_offset: bfloat16 [768], replicated, may hold values from -4 to 4
Outputs:
- block_out: bfloat16 [4, 16, 640, 768], P('cplx', 'smp', 'qry')
- single_grad: float32 [4, 16, 640, 768], P('cplx', 'smp', 'qry')
- condition_grad: float32 [4, 640, 384], P('cplx', 'qry')
- pair_grad: float32 [4, 640, 640, 128], P('cplx', ('qry', 'smp'))
- first_gain_grad: float32 [384], P('qry')
- first_scale_grad: float32 [384, 768], P(None, 'qry')
- first_offset_grad: float32 [768], P('qry')
- first_shift_grad: float32 [384, 768], P(None, 'qry')
- query_weight_grad: float32 [768, 768], P(None, 'qry')
- query_bias_grad: float32 [768], P('qry')
- key_weight_grad: float32 [768, 768], P(None, 'qry')
- value_weight_grad: float32 [768, 768], P(None, 'qry')
- gating_weight_grad: float32 [768, 768], P(None, 'qry')
- output_weight_grad: float32 [768, 768], P(None, 'qry')
- pair_gain_grad: float32 [128], P('qry')
- pair_project_grad: float32 [128, 16], P(None, 'qry')
- finish_weight_grad: float32 [384, 768], P(None, 'qry')
- finish_offset_grad: float32 [768], P('qry')
- second_gain_grad: float32 [384], P('qry')
- second_scale_grad: float32 [384, 768], P(None, 'qry')
- second_offset_grad: float32 [768], P('qry')
- second_shift_grad: float32 [384, 768], P(None, 'qry')
- swish_weight_grad: float32 [768, 1536], P(None, 'qry')
- linear_weight_grad: float32 [768, 1536], P(None, 'qry')
- down_weight_grad: float32 [1536, 768], P(None, 'qry')
- closing_weight_grad: float32 [384, 768], P(None, 'qry')
- closing_offset_grad: float32 [768], P('qry')
Inputs may be any that keep to these rules, and one draw needn't show every extreme that they name: `lengths`: the complexes have different token counts; one of them fills all 640 slots.
All inputs are finite; a program needn't handle non-finite values.
Results may differ from a plain program's by a relative error of at most 0.013.
The roundings to bfloat16 on the way count: a program that leaves them out, or rounds other values in their place, can miss the bound.
Values may be sent and summed in bfloat16 or wider, within the bound.
No kernel may reach another device: no remote copies, remote signals or barrier semaphores. Data moves between devices by JAX's collectives and lax.ppermute only.
A program may use at most 448 MiB of HBM per device.

v0:
```python
import jax
import jax.numpy as jnp
from jax import lax
from jax.sharding import PartitionSpec as P

EPSILON = 1e-05
HIGHEST = lax.Precision.HIGHEST


def normalize(values):
    centre = values - jnp.mean(values, axis=-1, keepdims=True)
    factor = lax.rsqrt(jnp.mean(centre * centre, axis=-1, keepdims=True) + EPSILON)
    return (centre * factor, factor)


def normalize_back(incoming, normed, factor):
    return factor * (
        incoming
        - jnp.mean(incoming, axis=-1, keepdims=True)
        - normed * jnp.mean(incoming * normed, axis=-1, keepdims=True)
    )


def matmul(left, right):
    return jnp.dot(left, right, preferred_element_type=jnp.float32)


def contract(form, left, right):
    return jnp.einsum(form, left, right, preferred_element_type=jnp.float32)


def exact_contract(form, left, right):
    return jnp.einsum(form, left.astype(jnp.float32), right.astype(jnp.float32), precision=HIGHEST)


def modulate(condition_norm, normed, gain, scale_weight, offset, shift_weight):
    condition_low = (condition_norm * gain.astype(jnp.float32)).astype(jnp.bfloat16)
    lifting = jax.nn.sigmoid(matmul(condition_low, scale_weight) + offset.astype(jnp.float32))
    shifting = matmul(condition_low, shift_weight)
    blended = (lifting[None] * normed + shifting[None]).astype(jnp.bfloat16)
    return (condition_low, lifting, blended)


def modulate_back(delta_blended, normed, condition_low, lifting, scale_weight, shift_weight):
    delta_lift = jnp.sum(delta_blended * normed, axis=0) * lifting * (1.0 - lifting)
    delta_shift = jnp.sum(delta_blended, axis=0)
    scale_total = exact_contract("qc,qd->cd", condition_low, delta_lift)
    offset_total = jnp.sum(delta_lift, axis=0)
    shift_total = exact_contract("qc,qd->cd", condition_low, delta_shift)
    delta_condition = exact_contract("qd,cd->qc", delta_lift, scale_weight) + exact_contract(
        "qd,cd->qc", delta_shift, shift_weight
    )
    return (delta_blended * lifting[None], delta_condition, scale_total, offset_total, shift_total)


def per_device(
    single,
    condition,
    pair_features,
    lengths,
    cotangent,
    first_gain,
    first_scale,
    first_offset,
    first_shift,
    query_projection_weight,
    query_bias_vector,
    key_projection_weight,
    value_projection_weight,
    attention_gate_weight,
    attention_output_weight,
    pair_gain,
    pair_project,
    finish_weight,
    finish_offset,
    second_gain,
    second_scale,
    second_offset,
    second_shift,
    transition_swish_weight,
    transition_linear_weight,
    transition_down_weight,
    closing_weight,
    closing_offset,
):
    samples = single.shape[1]
    row_count = single.shape[2]
    model_width = single.shape[3]
    head_count = pair_project.shape[1]
    head_width = model_width // head_count
    core_count = lax.axis_size("qry")
    full_length = row_count * core_count
    score_scale = head_width ** (-0.5)
    token_count = lengths[0]
    row_ids = lax.axis_index("qry") * row_count + jnp.arange(row_count, dtype=jnp.int32)
    row_mask = (row_ids < token_count).astype(jnp.float32)[:, None]
    key_valid = jnp.arange(full_length, dtype=jnp.int32) < token_count
    residual = single[0].astype(jnp.float32)
    condition_raw = condition[0]
    normed, factor = normalize(residual)
    condition_norm, condition_factor = normalize(condition_raw.astype(jnp.float32))
    condition_first, lifting_first, mixed_first_result = modulate(
        condition_norm, normed, first_gain, first_scale, first_offset, first_shift
    )
    condition_second, lifting_second, mixed_second_result = modulate(
        condition_norm, normed, second_gain, second_scale, second_offset, second_shift
    )
    query_rows = (
        matmul(mixed_first_result, query_projection_weight) + query_bias_vector.astype(jnp.float32)
    ).astype(jnp.bfloat16)
    keys_local = matmul(mixed_first_result, key_projection_weight).astype(jnp.bfloat16)
    values_local = matmul(mixed_first_result, value_projection_weight).astype(jnp.bfloat16)
    gate_activation = jax.nn.sigmoid(matmul(mixed_first_result, attention_gate_weight))
    keys_full, values_full = (
        lax.all_gather(keys_local, "qry", axis=1, tiled=True),
        lax.all_gather(values_local, "qry", axis=1, tiled=True),
    )
    pair_norm, pair_factor = normalize(pair_features[0].astype(jnp.float32))
    pair_low = (pair_norm * pair_gain.astype(jnp.float32)).astype(jnp.bfloat16)
    bias_piece = contract("rcp,ph->hrc", pair_low, pair_project).astype(jnp.bfloat16)
    bias_rows = lax.all_gather(bias_piece, "smp", axis=1, tiled=True)
    query_heads = query_rows.reshape(samples, row_count, head_count, head_width)
    key_heads = keys_full.reshape(samples, full_length, head_count, head_width)
    value_heads = values_full.reshape(samples, full_length, head_count, head_width)

    def score_block():
        scores = (
            contract("sqhe,skhe->shqk", query_heads, key_heads) * score_scale
            + bias_rows.astype(jnp.float32)[None]
        )
        return jnp.where(key_valid[None, None, None, :], scores, -1e30)

    scores = score_block()
    highest = jnp.max(scores, axis=-1, keepdims=True)
    exponent = jnp.exp(scores - highest)
    denominator = jnp.sum(exponent, axis=-1, keepdims=True)
    log_total = highest + jnp.log(denominator)
    probability = (exponent / denominator).astype(jnp.bfloat16)
    attended = contract("shqk,skhe->sqhe", probability, value_heads).reshape(
        samples, row_count, model_width
    )
    gate_applied = (gate_activation * attended).astype(jnp.bfloat16)
    raised_state = matmul(gate_applied, attention_output_weight)
    finish = jax.nn.sigmoid(
        matmul(condition_raw, finish_weight) + finish_offset.astype(jnp.float32)
    )
    raised_swish_part = matmul(mixed_second_result, transition_swish_weight)
    raised_linear_part = matmul(mixed_second_result, transition_linear_weight)
    swish_sigmoid = jax.nn.sigmoid(raised_swish_part)
    hidden_state = (raised_swish_part * swish_sigmoid * raised_linear_part).astype(jnp.bfloat16)
    shifted_state = matmul(hidden_state, transition_down_weight)
    closing = jax.nn.sigmoid(
        matmul(condition_raw, closing_weight) + closing_offset.astype(jnp.float32)
    )
    block_out = (
        residual + row_mask * (finish[None] * raised_state + closing[None] * shifted_state)
    ).astype(jnp.bfloat16)
    outgoing = cotangent[0].astype(jnp.float32)
    branch_grad = row_mask * outgoing
    delta_moved = (closing[None] * branch_grad).astype(jnp.bfloat16)
    delta_closing = jnp.sum(branch_grad * shifted_state, axis=0) * closing * (1.0 - closing)
    closing_total = exact_contract("qc,qd->cd", condition_raw, delta_closing)
    closingoffset_total = jnp.sum(delta_closing, axis=0)
    delta_condition = exact_contract("qd,cd->qc", delta_closing, closing_weight)
    down_total = contract("sqf,sqd->fd", hidden_state, delta_moved)
    delta_hidden = contract("sqd,fd->sqf", delta_moved, transition_down_weight)
    delta_swish = (
        delta_hidden
        * raised_linear_part
        * swish_sigmoid
        * (1.0 + raised_swish_part * (1.0 - swish_sigmoid))
    ).astype(jnp.bfloat16)
    delta_linear = (delta_hidden * raised_swish_part * swish_sigmoid).astype(jnp.bfloat16)
    swish_total = contract("sqd,sqf->df", mixed_second_result, delta_swish)
    linear_total = contract("sqd,sqf->df", mixed_second_result, delta_linear)
    delta_second = contract("sqf,df->sqd", delta_swish, transition_swish_weight) + contract(
        "sqf,df->sqd", delta_linear, transition_linear_weight
    )
    delta_lifted = (finish[None] * branch_grad).astype(jnp.bfloat16)
    delta_finish = jnp.sum(branch_grad * raised_state, axis=0) * finish * (1.0 - finish)
    finish_total = exact_contract("qc,qd->cd", condition_raw, delta_finish)
    finishoffset_total = jnp.sum(delta_finish, axis=0)
    delta_condition = delta_condition + exact_contract("qd,cd->qc", delta_finish, finish_weight)
    output_total = contract("sqd,sqe->de", gate_applied, delta_lifted)
    delta_gated = contract("sqe,de->sqd", delta_lifted, attention_output_weight)
    delta_gating = (delta_gated * attended * gate_activation * (1.0 - gate_activation)).astype(
        jnp.bfloat16
    )
    delta_attended = (delta_gated * gate_activation).astype(jnp.bfloat16)
    gating_total = contract("sqd,sqe->de", mixed_first_result, delta_gating)
    soft = jnp.exp(score_block() - log_total)
    attended_heads = delta_attended.reshape(samples, row_count, head_count, head_width)
    delta_soft = contract("sqhe,skhe->shqk", attended_heads, value_heads)
    delta_scores = (
        soft * (delta_soft - jnp.sum(soft * delta_soft, axis=-1, keepdims=True))
    ).astype(jnp.bfloat16)
    delta_queries = (contract("shqk,skhe->sqhe", delta_scores, key_heads) * score_scale).astype(
        jnp.bfloat16
    )
    delta_queries = delta_queries.reshape(samples, row_count, model_width)
    keys_part = (contract("shqk,sqhe->skhe", delta_scores, query_heads) * score_scale).reshape(
        samples, full_length, model_width
    )
    values_part = contract("shqk,sqhe->skhe", soft.astype(jnp.bfloat16), attended_heads).reshape(
        samples, full_length, model_width
    )
    bias_part = jnp.sum(delta_scores.astype(jnp.float32), axis=0)
    keys_sum, values_sum = (
        lax.psum_scatter(keys_part, "qry", scatter_dimension=1, tiled=True),
        lax.psum_scatter(values_part, "qry", scatter_dimension=1, tiled=True),
    )
    delta_keys = keys_sum.astype(jnp.bfloat16)
    delta_values = values_sum.astype(jnp.bfloat16)
    delta_bias = lax.psum_scatter(
        bias_part.astype(jnp.bfloat16), "smp", scatter_dimension=1, tiled=True
    )
    query_total = contract("sqd,sqe->de", mixed_first_result, delta_queries)
    querybias_total = jnp.sum(delta_queries.astype(jnp.float32), axis=(0, 1))
    key_total = contract("sqd,sqe->de", mixed_first_result, delta_keys)
    value_total = contract("sqd,sqe->de", mixed_first_result, delta_values)
    delta_first = (
        contract("sqe,de->sqd", delta_queries, query_projection_weight)
        + contract("sqe,de->sqd", delta_keys, key_projection_weight)
        + contract("sqe,de->sqd", delta_values, value_projection_weight)
        + contract("sqe,de->sqd", delta_gating, attention_gate_weight)
    )
    normed_first, cond_delta_first, scale_first, offset_first, shift_first = modulate_back(
        delta_first, normed, condition_first, lifting_first, first_scale, first_shift
    )
    normed_second, cond_delta_second, scale_second, offset_second, shift_second = modulate_back(
        delta_second, normed, condition_second, lifting_second, second_scale, second_shift
    )
    gain_first = jnp.sum(cond_delta_first * condition_norm, axis=0)
    gain_second = jnp.sum(cond_delta_second * condition_norm, axis=0)
    single_grad = outgoing + normalize_back(normed_first + normed_second, normed, factor)
    condition_local = (
        normalize_back(
            cond_delta_first * first_gain.astype(jnp.float32)
            + cond_delta_second * second_gain.astype(jnp.float32),
            condition_norm,
            condition_factor,
        )
        + delta_condition
    )
    condition_grad = lax.psum(condition_local, "smp")
    project_total = contract("rcp,hrc->ph", pair_low, delta_bias)
    delta_pairlow = contract("hrc,ph->rcp", delta_bias, pair_project)
    pairgain_total = jnp.sum(delta_pairlow * pair_norm, axis=(0, 1))
    pair_grad = normalize_back(
        delta_pairlow * pair_gain.astype(jnp.float32), pair_norm, pair_factor
    )
    summed = lax.psum(
        (
            gain_first,
            scale_first,
            offset_first,
            shift_first,
            query_total,
            querybias_total,
            key_total,
            value_total,
            gating_total,
            output_total,
            pairgain_total,
            project_total,
            finish_total,
            finishoffset_total,
            gain_second,
            scale_second,
            offset_second,
            shift_second,
            swish_total,
            linear_total,
            down_total,
            closing_total,
            closingoffset_total,
        ),
        ("cplx", "smp", "qry"),
    )
    core_index = lax.axis_index("qry")

    def own_half(whole):
        portion = whole.shape[-1] // core_count
        return lax.dynamic_slice_in_dim(whole, core_index * portion, portion, whole.ndim - 1)

    totals = tuple((own_half(whole) for whole in summed))
    return (block_out[None], single_grad[None], condition_grad[None], pair_grad[None]) + tuple(
        totals
    )


def solution(mesh):
    placed = (
        P("cplx", "smp", "qry", None),
        P("cplx", "qry", None),
        P("cplx", ("qry", "smp"), None, None),
        P("cplx"),
        P("cplx", "smp", "qry", None),
        P(),
        P(),
        P(),
        P(),
        P(),
        P(),
        P(),
        P(),
        P(),
        P(),
        P(),
        P(),
        P(),
        P(),
        P(),
        P(),
        P(),
        P(),
        P(),
        P(),
        P(),
        P(),
        P(),
    )
    return jax.shard_map(
        per_device,
        mesh=mesh,
        in_specs=placed,
        out_specs=(
            P("cplx", "smp", "qry", None),
            P("cplx", "smp", "qry", None),
            P("cplx", "qry", None),
            P("cplx", ("qry", "smp"), None, None),
            P("qry"),
            P(None, "qry"),
            P("qry"),
            P(None, "qry"),
            P(None, "qry"),
            P("qry"),
            P(None, "qry"),
            P(None, "qry"),
            P(None, "qry"),
            P(None, "qry"),
            P("qry"),
            P(None, "qry"),
            P(None, "qry"),
            P("qry"),
            P("qry"),
            P(None, "qry"),
            P("qry"),
            P(None, "qry"),
            P(None, "qry"),
            P(None, "qry"),
            P(None, "qry"),
            P(None, "qry"),
            P("qry"),
        ),
        check_vma=False,
    )
```

profile of v0, /device:TPU:0, one launch (start us, length us, event | category | flops | bytes accessed | tf_op | source)
XLA Modules:
  0.0 1237.0 jit_solution(9660837364765933502)
XLA Ops:
  23.2 3.0 convolution_convert_fusion
  26.3 4.8 convolution_convert_fusion.1
  31.2 18.4 %copy.95 = bf16[1,80,640,128]{2,3,1,0:T(8,128)(2,1)} copy(bf16[1,80,640,128]{3,2,1,0:T(8,128)(2,1)} %param.30) | data formatting | bytes 26214400 | tf_op args[2]
  49.6 9.7 convert_reduce_fusion
  59.4 10.0 fusion.15
  70.2 20.2 %fusion.73 = bf16[16,80,640]{2,0,1:T(8,128)(2,1)} fusion(bf16[1,80,640,128]{2,3,1,0:T(8,128)(2,1)} %copy.95, f32[128]{0:T(128)S(1)} %convert_element_type.170, f32[80,640]{1,0:T(8,128)S(1)} %add_rsqrt_fusion, f32[80,640]{1,0:T(8,128)S(1)} %broadcast_multiply_fusion.3, bf16[128,16]{0,1:T(8,128)(2,1)S(1)} %copy-done.89), kind=kOutput, calls=%fused_computation.103 | convolution fusion | flops 243302400 | bytes 15159808 | tf_op jit(solution)/shard_map/rcp,ph->hrc/dot_general | solution.py:29
  90.5 4.8 add_convert_fusion
  95.3 4.2 copy.93
  102.8 3.8 fusion.97
  106.6 6.3 copy.94
  112.9 6.4 copy.92
  119.3 93.9 %all-gather.8.cloned.1.call-done = bf16[16,320,640]{2,0,1:T(8,128)(2,1)} async-done(((bf16[16,80,640]{2,0,1:T(8,128)(2,1)}), bf16[16,320,640]{2,0,1:T(8,128)(2,1)}) %all-gather.8.cloned.1.call-update) | async-done | bytes 6553616 | tf_op jit(solution)/shard_map/all_gather | solution.py:121
  213.2 9.4 copy.97
  222.6 30.6 %fusion.174 = (f32[4,16,320]{2,1,0:T(8,128)S(1)}, f32[4,16,320,640]{3,2,1,0:T(8,128)}) fusion(f32[16,320,640]{2,1,0:T(8,128)} %copy.97, bf16[4,320,16,48]{1,3,2,0:T(8,128)(2,1)} %bitcast.288, bf16[4,640,16,48]{1,3,2,0:T(8,128)(2,1)S(1)} %bitcast.285, pred[640]{0:T(1024)(128)(4,1)S(1)} %iota_compare_fusion), kind=kOutput, calls=%fused_computation.232 | convolution fusion | flops 1310699520 | bytes 71516800 | tf_op jit(solution)/shard_map/sqhe,skhe->shqk/dot_general | solution.py:29
  253.2 17.1 %fusion = f32[4,16,320]{2,1,0:T(8,128)S(1)} fusion(f32[4,16,320,640]{3,2,1,0:T(8,128)} %get-tuple-element.166, f32[4,16,320]{2,1,0:T(8,128)S(1)} %get-tuple-element.165), kind=kLoop, calls=%fused_computation.6 | loop fusion | flops 26193920 | bytes 52592640 | tf_op jit(solution)/shard_map/reduce_sum | solution.py:136
  270.3 21.6 %fusion.19 = f32[4,16,48,320]{3,2,1,0:T(8,128)} fusion(bf16[4,640,16,48]{1,3,2,0:T(8,128)(2,1)S(1)} %bitcast.293, f32[4,16,320,640]{3,2,1,0:T(8,128)} %get-tuple-element.166, f32[4,16,320]{2,1,0:T(8,128)S(1)} %fusion, f32[4,16,320]{2,1,0:T(8,128)S(1)} %get-tuple-element.165), kind=kOutput, calls=%fused_computation.26 | convolution fusion | flops 1297612800 | bytes 60456960 | tf_op jit(solution)/shard_map/shqk,skhe->sqhe/dot_general | solution.py:29
  291.9 6.2 copy.98
  298.1 9.4 multiply_convert_fusion.5
  307.5 4.1 copy.99
  311.6 39.7 %multiply_reduce_fusion = (f32[4,16,320]{2,1,0:T(8,128)S(1)}, f32[4,16,320,640]{3,2,1,0:T(8,128)}) fusion(f32[4,16,320,640]{3,2,1,0:T(8,128)} %get-tuple-element.166, f32[4,16,320]{2,1,0:T(8,128)S(1)} %log_add_fusion, bf16[4,320,16,48]{1,3,2,0:T(8,128)(2,1)} %bitcast.290, bf16[4,640,16,48]{1,3,2,0:T(8,128)(2,1)} %bitcast.292), kind=kOutput, calls=%fused_computation.1 | convolution fusion | flops 1297592320 | bytes 110919680 | tf_op jit(solution)/shard_map/sqhe,skhe->shqk/dot_general | solution.py:29
  351.3 46.9 %fusion.173 = (bf16[16,320,640]{2,1,0:T(8,128)(2,1)}, bf16[4,16,320,640]{3,2,1,0:T(8,128)(2,1)}) fusion(f32[4,16,320,640]{3,2,1,0:T(8,128)} %get-tuple-element.168, f32[4,16,320]{2,1,0:T(8,128)S(1)} %get-tuple-element.167, f32[4,16,320,640]{3,2,1,0:T(8,128)} %get-tuple-element.166, f32[4,16,320]{2,1,0:T(8,128)S(1)} %log_add_fusion), kind=kLoop, calls=%fused_computation.231 | loop fusion | flops 62259200 | bytes 137789440 | tf_op jit(solution)/shard_map/reduce_sum | solution.py:207
  398.2 13.2 %broadcast_multiply_fusion = f32[4,16,48,640]{3,2,1,0:T(8,128)} fusion(bf16[4,320,16,48]{1,3,2,0:T(8,128)(2,1)S(1)} %bitcast.289, bf16[4,16,320,640]{3,2,1,0:T(8,128)(2,1)} %get-tuple-element.147), kind=kOutput, calls=%fused_computation.71 | convolution fusion | flops 1260257280 | bytes 36044800 | tf_op jit(solution)/shard_map/shqk,sqhe->skhe/dot_general | solution.py:29
  411.4 9.1 copy.101
  420.5 26.1 %fusion.16 = f32[4,16,48,640]{3,2,1,0:T(8,128)} fusion(bf16[4,320,16,48]{1,3,2,0:T(8,128)(2,1)} %bitcast.291, f32[4,16,320,640]{3,2,1,0:T(8,128)} %get-tuple-element.166, f32[4,16,320]{2,1,0:T(8,128)S(1)} %log_add_fusion), kind=kOutput, calls=%fused_computation.24 | convolution fusion | flops 1284505600 | bytes 62341120 | tf_op jit(solution)/shard_map/shqk,sqhe->skhe/dot_general | solution.py:29
  446.7 9.1 copy.102
  459.1 6.5 fusion.56
  465.7 5.7 fusion.50
  471.4 11.5 multiply_convert_fusion.2
  482.9 8.7 fusion.54
  491.6 5.0 convolution_bitcast_fusion.1
  496.7 5.5 convolution_bitcast_fusion
  502.5 8.2 convolution_bitcast_fusion.2
  510.7 5.2 fusion.67
  516.0 3.7 fusion.99
  519.6 14.9 %convert_reduce_fusion.2 = (f32[16,48]{1,0:T(8,128)S(1)}, bf16[4,16,48,320]{3,2,1,0:T(8,128)(2,1)}) fusion(bf16[4,640,16,48]{1,3,2,0:T(8,128)(2,1)} %bitcast.284, bf16[4,16,320,640]{3,2,1,0:T(8,128)(2,1)} %get-tuple-element.147), kind=kOutput, calls=%fused_computation.42 | convolution fusion | flops 1262222592 | bytes 32115712 | tf_op jit(solution)/shard_map/shqk,skhe->sqhe/dot_general | solution.py:29
  534.5 6.3 fusion.104
  540.8 3.2 convolution_bitcast_fusion.4
  544.0 3.5 convolution_bitcast_fusion.7
  547.5 3.4 convolution_bitcast_fusion.3
  551.0 6.1 fusion.101
  557.2 6.3 fusion.107
  563.5 10.3 fusion.169
  578.6 10.2 fusion.48
  588.8 2.4 convolution_bitcast_fusion.8
  591.2 2.4 convolution_bitcast_fusion.9
  595.9 2.3 fusion.152
  598.2 3.2 convolution_bitcast_fusion.6
  601.4 3.2 convolution_bitcast_fusion.5
  604.8 10.8 reduce-scatter.8.cloned.1.call-done
  615.6 19.1 %fusion.14 = (f32[128]{0:T(128)S(1)}, f32[80,640]{1,0:T(8,128)S(1)}, f32[80,640]{1,0:T(8,128)S(1)}, f32[80,640,128]{1,2,0:T(8,128)}) fusion(bf16[1,80,640,128]{2,3,1,0:T(8,128)(2,1)} %copy.95, f32[80,640]{1,0:T(8,128)S(1)} %copy-done.49, f32[80,640]{1,0:T(8,128)S(1)} %copy-done.45, f32[128]{0:T(128)S(1)} %copy-done.77, bf16[128,16]{0,1:T(8,128)(2,1)S(1)} %copy-done.90, ...), kind=kOutput, calls=%fused_computation.22 | convolution fusion | flops 268595072 | bytes 41784320 | tf_op jit(solution)/shard_map/hrc,ph->rcp/dot_general | solution.py:29
  634.7 25.7 %fusion.13 = f32[1,80,640,128]{2,3,1,0:T(8,128)} fusion(bf16[1,80,640,128]{2,3,1,0:T(8,128)(2,1)} %copy.95, f32[80,640,128]{1,2,0:T(8,128)} %get-tuple-element.169, f32[80,640]{1,0:T(8,128)S(1)} %get-tuple-element.176, f32[80,640]{1,0:T(8,128)S(1)} %get-tuple-element.177, f32[128]{0:T(128)S(1)} %copy-done.77, f32[80,640]{1,0:T(8,128)S(1)} %copy-done.49, ...), kind=kLoop, calls=%fused_computation.21 | loop fusion | flops 52428800 | bytes 66355712 | tf_op jit(solution)/shard_map/broadcast_in_dim | solution.py:287
  660.4 28.0 %copy.108 = f32[1,80,640,128]{3,2,1,0:T(8,128)} copy(f32[1,80,640,128]{2,3,1,0:T(8,128)} %fusion.13) | data formatting | bytes 52428800
  688.5 9.8 fusion.112
  704.9 43.3 %all-reduce = (f32[384]{0:T(512)S(1)}, f32[768]{0:T(1024)S(1)}, f32[768]{0:T(1024)S(1)}, f32[128]{0:T(128)S(1)}, f32[128,16]{0,1:T(8,128)S(1)}, /*index=5*/f32[7...) all-reduce(f32[384]{0:T(512)S(1)} %get-tuple-element.122, ...), channel_id=1, replica_groups=mesh['cplx'=4,'smp'=4,'qry'=2] {'cplx','smp','qry'}, use_global_device_ids=true, to_apply=%region_27.28 | all-reduce | flops 6784 | bytes 54272 | tf_op jit(solution)/shard_map/psum | solution.py:252
  753.9 2.7 fusion.155
  756.6 3.5 fusion.96
  760.1 426.2 %all-reduce.7.cloned.1.call-done = (f32[384,768]{1,0:T(8,128)}, f32[384,768]{1,0:T(8,128)}, f32[768,768]{1,0:T(8,128)}, f32[768,768]{1,0:T(8,128)}, f32[768,768]...) async-done(((f32[384,768]{1,0:T(8,128)}, ...) | async-done | bytes 33030160 | tf_op jit(solution)/shard_map/psum | solution.py:252
  1186.3 2.5 constant_dynamic-slice_fusion.12
  1188.8 2.5 constant_dynamic-slice_fusion.4
  1192.7 3.1 constant_dynamic-slice_fusion.8
  1195.8 2.6 constant_dynamic-slice_fusion.2
  1201.7 3.2 constant_dynamic-slice_fusion.10
  1204.8 3.2 constant_dynamic-slice_fusion.1
  1208.1 20.0 %all-reduce.5.cloned.1.call-done = f32[1,320,384]{2,1,0:T(8,128)} async-done(((f32[1,320,384]{2,1,0:T(8,128)}), f32[1,320,384]{2,1,0:T(8,128)}) %all-reduce.5.cloned.1.call-update) | async-done | bytes 491536 | tf_op jit(solution)/shard_map/psum | solution.py:245
  (273 shorter events, 49.1 us)
Async XLA Ops:
  7.2 464.2 %copy-start = (bf16[768,1536]{1,0:T(8,128)(2,1)S(1)}, bf16[768,1536]{1,0:T(8,128)(2,1)}, u32[]{:S(2)}) copy-start(bf16[768,1536]{1,0:T(8,128)(2,1)} %param.51) | copy-start | bytes 7077892
  7.2 9.5 copy-start.2
  7.2 9.5 copy-start.41
  7.2 99.4 %all-gather.6.cloned.1.call-start = ((), (), s32[]{:S(2)}) async-start(), calls=%async_computation.4 | async-start | bytes 5898240 | tf_op jit(solution)/shard_map/all_gather | solution.py:115
  7.3 9.9 copy-start.53
  8.5 9.8 copy-start.59
  9.7 8.6 copy-start.61
  10.4 7.4 copy-start.67
  11.8 6.5 copy-start.69
  26.2 86.7 %all-gather.4.cloned.1.call-start = ((), (), s32[]{:S(2)}) async-start(), calls=%async_computation.3 | async-start | bytes 5898240 | tf_op jit(solution)/shard_map/all_gather | solution.py:116
  31.1 18.5 %copy-start.91 = (bf16[128]{0:T(256)(128)(2,1)S(1)}, bf16[128]{0:T(256)(128)(2,1)}, u32[]{:S(2)}) copy-start(bf16[128]{0:T(256)(128)(2,1)} %param.43) | copy-start | bytes 772
  31.2 182.0 %all-gather.8.cloned.1.call-start = ((), (), s32[]{:S(2)}) async-start(), calls=%async_computation.5 | async-start | bytes 8192000 | tf_op jit(solution)/shard_map/all_gather | solution.py:121
  49.6 19.8 %copy-start.76 = (f32[128]{0:T(128)}, f32[128]{0:T(128)S(1)}, u32[]{:S(2)}) copy-start(f32[128]{0:T(128)S(1)} %convert_element_type.170) | copy-start | bytes 1540
  59.4 10.1 copy-start.44
  59.4 10.7 copy-start.89
  70.2 20.3 %copy-start.71 = (bf16[768]{0:T(1024)(128)(2,1)S(1)}, bf16[768]{0:T(1024)(128)(2,1)}, u32[]{:S(2)}) copy-start(bf16[768]{0:T(1024)(128)(2,1)} %param.38) | copy-start | bytes 4612
  90.4 460.6 %reduce-scatter.4.cloned.1.call-start = ((), (), s32[]{:S(2)}) async-start(), calls=%async_computation.6 | async-start | bytes 11796480 | tf_op jit(solution)/shard_map/reduce_scatter | solution.py:209
  95.3 4.8 copy-start.72
  95.3 4.9 copy-start.56
  213.2 9.4 copy-start.1
  253.2 17.1 %copy-start.13 = (bf16[4,640,768]{1,2,0:T(8,128)(2,1)S(1)}, bf16[4,640,768]{1,2,0:T(8,128)(2,1)}, u32[]{:S(2)}) copy-start(bf16[4,640,768]{1,2,0:T(8,128)(2,1)} %copy.92) | copy-start | bytes 11796484
  351.3 46.9 %copy-start.12 = (bf16[4,320,768]{1,2,0:T(8,128)(2,1)S(1)}, bf16[4,320,768]{1,2,0:T(8,128)(2,1)}, u32[]{:S(2)}) copy-start(bf16[4,320,768]{1,2,0:T(8,128)(2,1)} %copy.93) | copy-start | bytes 5898244
  420.5 136.6 %reduce-scatter.6.cloned.1.call-start = ((), (), s32[]{:S(2)}) async-start(), calls=%async_computation.7 | async-start | bytes 11796480 | tf_op jit(solution)/shard_map/reduce_scatter | solution.py:210
  455.8 159.8 %reduce-scatter.8.cloned.1.call-start = ((), (), s32[]{:S(2)}) async-start(), calls=%async_computation.9 | async-start | bytes 8192000 | tf_op jit(solution)/shard_map/reduce_scatter | solution.py:214
  457.5 39.2 %copy-start.28 = (f32[320,768]{1,0:T(8,128)}, f32[320,768]{1,0:T(8,128)S(1)}, u32[]{:S(2)}) copy-start(f32[320,768]{1,0:T(8,128)S(1)} %fusion.86) | copy-start | bytes 2949124
  459.1 6.5 copy-start.75
  459.1 6.5 copy-start.81
  459.1 6.5 copy-start.84
  482.9 13.8 %copy-start.92 = (bf16[4,320,1536]{2,1,0:T(8,128)(2,1)}, bf16[4,320,1536]{2,1,0:T(8,128)(2,1)S(1)}, u32[]{:S(2)}) copy-start(bf16[4,320,1536]{2,1,0:T(8,128)(2,1)S(1)} %get-tuple-element.151) | copy-start | bytes 11796484
  482.9 8.7 copy-start.94
  502.2 684.1 %all-reduce.7.cloned.1.call-start = ((), (), s32[]{:S(2)}) async-start(), calls=%async_computation.10 | async-start | bytes 66060288 | tf_op jit(solution)/shard_map/psum | solution.py:252
  502.5 8.3 copy-start.93
  502.5 8.3 copy-start.97
  510.7 5.2 copy-start.87
  510.7 5.2 copy-start.95
  534.5 6.3 copy-start.34
  534.5 6.3 copy-start.36
  557.1 6.3 copy-start.64
  557.1 6.3 copy-start.66
  557.1 6.3 copy-start.5
  557.1 6.3 copy-start.7
  557.1 6.3 copy-start.10
  557.2 6.3 copy-start.37
  563.5 10.5 copy-start.60
  563.5 10.5 copy-start.62
  563.5 10.5 copy-start.68
  563.5 12.8 %copy-start.70 = (f32[384]{0:T(512)S(1)}, f32[384]{0:T(512)}, u32[]{:S(2)}) copy-start(f32[384]{0:T(512)} %copy-done.69) | copy-start | bytes 4612
  573.8 4.7 copy-start.24
  573.9 14.9 %copy-start.26 = (f32[320,768]{1,0:T(8,128)}, f32[320,768]{1,0:T(8,128)S(1)}, u32[]{:S(2)}) copy-start(f32[320,768]{1,0:T(8,128)S(1)} %get-tuple-element.111) | copy-start | bytes 2949124
  573.9 19.7 %copy-start.16 = (f32[320,768]{1,0:T(8,128)}, f32[320,768]{1,0:T(8,128)S(1)}, u32[]{:S(2)}) copy-start(f32[320,768]{1,0:T(8,128)S(1)} %get-tuple-element.112) | copy-start | bytes 2949124
  573.9 22.0 %copy-start.14 = (f32[320,768]{1,0:T(8,128)}, f32[320,768]{1,0:T(8,128)S(1)}, u32[]{:S(2)}) copy-start(f32[320,768]{1,0:T(8,128)S(1)} %get-tuple-element.160) | copy-start | bytes 2949124
  588.8 7.1 copy-start.22
  588.8 7.1 copy-start.31
  604.6 10.9 copy-start.45
  604.6 10.9 copy-start.49
  604.6 10.9 copy-start.77
  604.6 10.9 copy-start.90
  604.7 623.4 %all-reduce.5.cloned.1.call-start = ((), (), s32[]{:S(2)}) async-start(), calls=%async_computation.8 | async-start | bytes 983040 | tf_op jit(solution)/shard_map/psum | solution.py:245
  688.4 9.8 copy-start.21
  688.4 9.8 copy-start.23
  688.4 10.0 copy-start.8
  688.5 10.0 copy-start.15
  1186.3 6.5 copy-start.50
  1188.8 7.0 copy-start.47
  (42 other events, 106.5 us)
Sparse Core Ops, SparseCore 0:
  26.4 15.9 all-gather.5
  44.5 14.4 all-gather.3
  90.5 122.6 all-gather.7
  420.6 14.7 reduce-scatter.3
  455.9 14.5 reduce-scatter.5
  502.3 113.2 reduce-scatter.7
  623.7 562.5 all-reduce.6
  1190.6 37.4 all-reduce.4
where the time goes:
time: 1240 us
  waiting for transfers between devices  551 us (44%)
  matrix products  364 us (29%)
  local copies, waits for them, and re-layouts  140 us (11%)
  other arithmetic  122 us (10%)
  blocking collectives  43.3 us (3%)
  between operations  16.1 us (1%)
    psum x1, waiting for transfers between devices, per_device(): lax.psum((gain_first, scale_first, offset_first, shift_first, query_total...  426 us
    dot_general x25, matrix products, contract(): return jnp.einsum(form, left, right, preferred_element_type=jnp.float32)  283 us
    all_gather x1, waiting for transfers between devices, per_device(): bias_rows = lax.all_gather(bias_piece, 'smp', axis=1, tiled=True)  93.9 us
    unnamed x201, local copies, waits for them, and re-layouts  60.3 us
    dot_general x14, matrix products, matmul(): return jnp.dot(left, right, preferred_element_type=jnp.float32)  56.9 us
    reduce_sum x1, other arithmetic, per_device(): bias_part = jnp.sum(delta_scores.astype(jnp.float32), axis=0)  46.9 us
    psum x1, blocking collectives, per_device(): lax.psum((gain_first, scale_first, offset_first, shift_first, query_total...  43.3 us
    broadcast_in_dim x1, other arithmetic, per_device(): pair_grad[None]  25.7 us
  transfers between devices with their start and end apart: 8, of which 4 were waited for; matrix products, arithmetic and copies ran while one was open for 32% of the time, Pallas kernels for 0%

commit v1 on v0

v1 whole, which is shorter than its diff:
```python
import functools

import jax
import jax.numpy as jnp
from jax import lax
from jax.experimental import pallas as pl
from jax.experimental.pallas import tpu as pltpu
from jax.sharding import PartitionSpec as P

EPSILON = 1e-05
HIGHEST = lax.Precision.HIGHEST
LANES = 128
VMEM_LIMIT = 56 * 2**20
PARTS = 2
f32 = jnp.float32
bf16 = jnp.bfloat16


def dot(left, right, left_dim, right_dim):
    return lax.dot_general(
        left, right, (((left_dim,), (right_dim,)), ((), ())), preferred_element_type=f32
    )


def attention_kernel(
    meta, query, key_mine, key_other, value_mine, value_other, gate, delta_gated, bias,
    gated, delta_gate, delta_query, dk_mine, dk_other, dv_mine, dv_other, delta_bias,
    score, prob, slope, *, step
):
    samples, head_width, rows = query.shape
    total = 2 * rows
    pieces, piece_rows = bias.shape[0], bias.shape[2]
    scale = head_width ** (-0.5)
    second = meta[1] == 1
    column = lax.broadcasted_iota(jnp.int32, (16, total), 1)
    line = lax.broadcasted_iota(jnp.int32, (16, total), 0)
    masking = jnp.where((line == 0) & (column >= meta[0]), -1e30, 0.0).astype(bf16)
    pair_ones = jnp.where(line < 2, 1.0, 0.0).astype(bf16)
    query_line = lax.broadcasted_iota(jnp.int32, (16, rows), 0)
    one_line = jnp.where(query_line == 0, 1.0, 0.0).astype(bf16)
    spots = [
        (piece, start, piece * piece_rows + start)
        for piece in range(pieces)
        for start in range(0, piece_rows, step)
    ]

    def joined(mine, other):
        first = jnp.where(second, other, mine)
        last = jnp.where(second, mine, other)
        return jnp.concatenate([first, last], axis=1)

    def parted(whole, mine, other, sample):
        first, last = whole[:, :rows], whole[:, rows:]
        mine[sample] = jnp.where(second, last, first)
        other[sample] = jnp.where(second, first, last).astype(other.dtype)

    keys, values = [], []
    for s in range(samples):
        keys.append(joined(key_mine[s], key_other[s]))
        values.append(joined(value_mine[s], value_other[s]))
        score[s] = dot(
            jnp.concatenate([query[s], one_line], axis=0),
            jnp.concatenate([keys[s], masking], axis=0),
            0,
            0,
        )
    for piece, start, place in spots:
        bias_here = bias[piece, 0, start : start + step, :].astype(f32)
        here = slice(place, place + step)
        for s in range(samples):
            line_scores = score[s, here, :] * scale + bias_here
            highest = jnp.max(line_scores, axis=1, keepdims=True)
            exponent = jnp.exp(line_scores - highest)
            soft = exponent * (1.0 / jnp.sum(exponent, axis=1, keepdims=True))
            score[s, here, :] = soft
            prob[s, here, :] = soft.astype(bf16)
    for s in range(samples):
        attended = dot(values[s], prob[s], 1, 1)
        gate_here, delta_here = gate[s], delta_gated[s]
        gated[s] = (gate_here * attended).astype(bf16)
        delta_attended = (delta_here * gate_here).astype(bf16)
        delta_gate[s] = (delta_here * attended * gate_here * (1.0 - gate_here)).astype(bf16)
        centre = jnp.sum(delta_attended.astype(f32) * attended, axis=0, keepdims=True)
        coarse = centre.astype(bf16).astype(f32)
        rest = jnp.where(
            query_line == 0, -coarse, jnp.where(query_line == 1, coarse - centre, 0.0)
        ).astype(bf16)
        slope[s] = dot(
            jnp.concatenate([delta_attended, rest], axis=0),
            jnp.concatenate([values[s], pair_ones], axis=0),
            0,
            0,
        )
        parted(dot(delta_attended, prob[s], 1, 0), dv_mine, dv_other, s)
    for piece, start, place in spots:
        here = slice(place, place + step)
        total_here = None
        for s in range(samples):
            delta_scores = score[s, here, :] * slope[s, here, :]
            prob[s, here, :] = delta_scores.astype(bf16)
            total_here = delta_scores if total_here is None else total_here + delta_scores
        delta_bias[piece, 0, start : start + step, :] = total_here.astype(bf16)
    for s in range(samples):
        delta_query[s] = (dot(keys[s], prob[s], 1, 1) * scale).astype(bf16)
        parted(dot(query[s], prob[s], 1, 0) * scale, dk_mine, dk_other, s)


def attention(meta, query, key_pair, value_pair, gate, delta_gated, bias, part, parts):
    samples, width, rows = query.shape
    pieces, heads, piece_rows, total = bias.shape
    head_width = width // (heads * parts)
    step = 16 if piece_rows % 16 == 0 else piece_rows
    first = part * heads
    inner = pl.BlockSpec((samples, head_width, rows), lambda h, meta: (0, first + h, 0))
    outer = pl.BlockSpec((samples, head_width, rows), lambda h, meta: (0, h, 0))
    tile = pl.BlockSpec((pieces, 1, piece_rows, total), lambda h, meta: (0, h, 0, 0))

    def made(dtype):
        return jax.ShapeDtypeStruct((samples, heads * head_width, rows), dtype)

    return pl.pallas_call(
        functools.partial(attention_kernel, step=step),
        grid_spec=pltpu.PrefetchScalarGridSpec(
            num_scalar_prefetch=1,
            grid=(heads,),
            in_specs=[inner] * 7 + [tile],
            out_specs=[outer] * 7 + [tile],
            scratch_shapes=[
                pltpu.VMEM((samples, rows, total), f32),
                pltpu.VMEM((samples, rows, total), bf16),
                pltpu.VMEM((samples, rows, total), f32),
            ],
        ),
        out_shape=[
            made(bf16), made(bf16), made(bf16), made(f32), made(f32), made(f32), made(f32),
            jax.ShapeDtypeStruct(bias.shape, bf16),
        ],
        compiler_params=pltpu.CompilerParams(vmem_limit_bytes=VMEM_LIMIT),
        cost_estimate=pl.CostEstimate(
            flops=samples * heads * rows * total * 6 * 256 * 2,
            bytes_accessed=samples * heads * head_width * rows * 34 + 4 * rows * total * heads,
            transcendentals=samples * heads * rows * total,
        ),
    )(meta, query, *key_pair, *value_pair, gate, delta_gated, bias)


def pair_forward_kernel(pair, gain, project, *refs, block, heads, parts):
    outs, wide = refs[:-1], refs[-1]
    gain_here = gain[...].astype(f32)

    def one(i, carry):
        normed, _ = normalize(pair[i].astype(f32))
        low = (normed * gain_here).astype(bf16)
        line = dot(project[...], low, 0, 1)
        for t in range(wide.shape[0]):
            wide[t, pl.ds(pl.multiple_of(i * heads, heads), heads), :] = line[
                :, t * LANES : (t + 1) * LANES
            ]
        return carry

    lax.fori_loop(0, block, one, 0, unroll=2)
    share = heads // parts
    for h in range(heads):
        for t in range(wide.shape[0]):
            outs[h // share][h % share, :, t * LANES : (t + 1) * LANES] = wide[
                t, pl.ds(h, block, stride=heads), :
            ].astype(bf16)


def pair_forward(pair, gain, project, parts):
    rows, length, width = pair.shape
    heads = project.shape[1]
    block = 16 if rows % 16 == 0 else rows
    share = heads // parts
    return pl.pallas_call(
        functools.partial(pair_forward_kernel, block=block, heads=heads, parts=parts),
        grid=(rows // block,),
        in_specs=[
            pl.BlockSpec((block, length, width), lambda i: (i, 0, 0)),
            pl.BlockSpec((1, width), lambda i: (0, 0)),
            pl.BlockSpec((width, heads), lambda i: (0, 0)),
        ],
        out_specs=[pl.BlockSpec((share, block, length), lambda i: (0, i, 0))] * parts,
        out_shape=[jax.ShapeDtypeStruct((share, rows, length), bf16)] * parts,
        scratch_shapes=[pltpu.VMEM((length // LANES, block * heads, LANES), f32)],
        compiler_params=pltpu.CompilerParams(vmem_limit_bytes=VMEM_LIMIT),
        cost_estimate=pl.CostEstimate(
            flops=2 * rows * length * width * 256,
            bytes_accessed=2 * rows * length * (width + heads),
            transcendentals=0,
        ),
    )(pair, gain.reshape(1, width), project)


def pair_backward_kernel(pair, gain, project, *refs, block, heads, parts):
    deltas = refs[:parts]
    out, gain_out, project_out, wide, gain_sum, project_sum = refs[parts:]
    step = pl.program_id(0)
    gain_here = gain[...].astype(f32)
    share = heads // parts

    @pl.when(step == 0)
    def _():
        gain_sum[...] = jnp.zeros_like(gain_sum)
        project_sum[...] = jnp.zeros_like(project_sum)

    for h in range(heads):
        for t in range(wide.shape[0]):
            wide[t, h * block : (h + 1) * block, :] = deltas[h // share][
                h % share, :, t * LANES : (t + 1) * LANES
            ].astype(f32)

    def one(i, carry):
        normed, factor = normalize(pair[i].astype(f32))
        low = (normed * gain_here).astype(bf16)
        delta = jnp.concatenate(
            [wide[t, pl.ds(i, heads, stride=block), :] for t in range(wide.shape[0])], axis=1
        ).astype(bf16)
        delta_low = dot(delta, project[...], 0, 1)
        project_sum[...] += dot(delta, low, 1, 0)
        product = delta_low * normed
        gain_sum[...] += jnp.sum(product.reshape(-1, 8, product.shape[-1]), axis=0)
        incoming = delta_low * gain_here
        out[i] = factor * (
            incoming
            - jnp.mean(incoming, axis=-1, keepdims=True)
            - normed * jnp.mean(product * gain_here, axis=-1, keepdims=True)
        )
        return carry

    lax.fori_loop(0, block, one, 0, unroll=2)

    @pl.when(step == pl.num_programs(0) - 1)
    def _():
        gain_out[...] = jnp.sum(gain_sum[...], axis=0, keepdims=True)
        project_out[...] = project_sum[...]


def pair_backward(pair, gain, project, deltas):
    rows, length, width = pair.shape
    heads = project.shape[1]
    parts = len(deltas)
    block = 16 if rows % 16 == 0 else rows
    share = heads // parts
    return pl.pallas_call(
        functools.partial(pair_backward_kernel, block=block, heads=heads, parts=parts),
        grid=(rows // block,),
        in_specs=[
            pl.BlockSpec((block, length, width), lambda i: (i, 0, 0)),
            pl.BlockSpec((1, width), lambda i: (0, 0)),
            pl.BlockSpec((width, heads), lambda i: (0, 0)),
        ]
        + [pl.BlockSpec((share, block, length), lambda i: (0, i, 0))] * parts,
        out_specs=[
            pl.BlockSpec((block, length, width), lambda i: (i, 0, 0)),
            pl.BlockSpec((1, width), lambda i: (0, 0)),
            pl.BlockSpec((heads, width), lambda i: (0, 0)),
        ],
        out_shape=[
            jax.ShapeDtypeStruct((rows, length, width), f32),
            jax.ShapeDtypeStruct((1, width), f32),
            jax.ShapeDtypeStruct((heads, width), f32),
        ],
        scratch_shapes=[
            pltpu.VMEM((length // LANES, block * heads, LANES), f32),
            pltpu.VMEM((8, width), f32),
            pltpu.VMEM((heads, width), f32),
        ],
        compiler_params=pltpu.CompilerParams(vmem_limit_bytes=VMEM_LIMIT),
        cost_estimate=pl.CostEstimate(
            flops=2 * rows * length * width * 512,
            bytes_accessed=2 * rows * length * (3 * width + heads),
            transcendentals=0,
        ),
    )(pair, gain.reshape(1, width), project, *deltas)


def swap_cores(array):
    return lax.ppermute(array, "qry", [(0, 1), (1, 0)])


def halves(array):
    portion = array.shape[-1] // 2
    core = lax.axis_index("qry")
    mine = lax.dynamic_slice_in_dim(array, core * portion, portion, array.ndim - 1)
    other = lax.dynamic_slice_in_dim(array, (1 - core) * portion, portion, array.ndim - 1)
    return mine, other


def chip_sums(arrays, after=None):
    kept = []
    for array in arrays:
        mine, other = halves(array)
        arrived = swap_cores(other.astype(bf16))
        kept.append((mine + arrived.astype(f32)).astype(bf16))
    if after is not None:
        kept, _ = lax.optimization_barrier((kept, after))
    return lax.psum(tuple(kept), ("cplx", "smp"))


def widened(arrays):
    return tuple(array.astype(f32) for array in arrays)


def gather_rows(piece):
    if piece.shape[1] % 16 == 0:
        return lax.all_gather(piece, "smp", axis=0)
    return lax.all_gather(piece, "smp", axis=1, tiled=True)[None]


def scatter_rows(whole):
    if whole.shape[0] == lax.axis_size("smp"):
        return lax.psum_scatter(whole, "smp", scatter_dimension=0)
    return lax.psum_scatter(whole[0], "smp", scatter_dimension=1, tiled=True)


def normalize(values):
    centre = values - jnp.mean(values, axis=-1, keepdims=True)
    factor = lax.rsqrt(jnp.mean(centre * centre, axis=-1, keepdims=True) + EPSILON)
    return (centre * factor, factor)


def normalize_back(incoming, normed, factor):
    return factor * (
        incoming
        - jnp.mean(incoming, axis=-1, keepdims=True)
        - normed * jnp.mean(incoming * normed, axis=-1, keepdims=True)
    )


def matmul(left, right):
    return jnp.dot(left, right, preferred_element_type=jnp.float32)


def contract(form, left, right):
    return jnp.einsum(form, left, right, preferred_element_type=jnp.float32)


def exact_contract(form, left, right):
    return jnp.einsum(form, left.astype(jnp.float32), right.astype(jnp.float32), precision=HIGHEST)


def modulate(condition_norm, normed, gain, scale_weight, offset, shift_weight):
    condition_low = (condition_norm * gain.astype(jnp.float32)).astype(jnp.bfloat16)
    lifting = jax.nn.sigmoid(matmul(condition_low, scale_weight) + offset.astype(jnp.float32))
    shifting = matmul(condition_low, shift_weight)
    blended = (lifting[None] * normed + shifting[None]).astype(jnp.bfloat16)
    return (condition_low, lifting, blended)


def modulate_back(delta_blended, normed, condition_low, lifting, scale_weight, shift_weight):
    delta_lift = jnp.sum(delta_blended * normed, axis=0) * lifting * (1.0 - lifting)
    delta_shift = jnp.sum(delta_blended, axis=0)
    scale_total = exact_contract("qc,qd->cd", condition_low, delta_lift)
    offset_total = jnp.sum(delta_lift, axis=0)
    shift_total = exact_contract("qc,qd->cd", condition_low, delta_shift)
    delta_condition = exact_contract("qd,cd->qc", delta_lift, scale_weight) + exact_contract(
        "qd,cd->qc", delta_shift, shift_weight
    )
    return (delta_blended * lifting[None], delta_condition, scale_total, offset_total, shift_total)


def per_device(
    single,
    condition,
    pair_features,
    lengths,
    cotangent,
    first_gain,
    first_scale,
    first_offset,
    first_shift,
    query_projection_weight,
    query_bias_vector,
    key_projection_weight,
    value_projection_weight,
    attention_gate_weight,
    attention_output_weight,
    pair_gain,
    pair_project,
    finish_weight,
    finish_offset,
    second_gain,
    second_scale,
    second_offset,
    second_shift,
    transition_swish_weight,
    transition_linear_weight,
    transition_down_weight,
    closing_weight,
    closing_offset,
):
    row_count = single.shape[2]
    model_width = single.shape[3]
    head_count = pair_project.shape[1]
    token_count = lengths[0]
    row_ids = lax.axis_index("qry") * row_count + jnp.arange(row_count, dtype=jnp.int32)
    row_mask = (row_ids < token_count).astype(jnp.float32)[:, None]
    residual = single[0].astype(jnp.float32)
    condition_raw = condition[0]
    normed, factor = normalize(residual)
    condition_norm, condition_factor = normalize(condition_raw.astype(jnp.float32))
    condition_first, lifting_first, mixed_first_result = modulate(
        condition_norm, normed, first_gain, first_scale, first_offset, first_shift
    )
    condition_second, lifting_second, mixed_second_result = modulate(
        condition_norm, normed, second_gain, second_scale, second_offset, second_shift
    )
    finish = jax.nn.sigmoid(
        matmul(condition_raw, finish_weight) + finish_offset.astype(jnp.float32)
    )
    bias_pieces = pair_forward(pair_features[0], pair_gain, pair_project, PARTS)
    bias_rows = [gather_rows(piece) for piece in bias_pieces]
    query_turned = (
        contract("srd,de->ser", mixed_first_result, query_projection_weight)
        + query_bias_vector.astype(jnp.float32)[:, None]
    ).astype(jnp.bfloat16)
    key_turned = contract("srd,de->ser", mixed_first_result, key_projection_weight).astype(
        jnp.bfloat16
    )
    value_turned = contract("srd,de->ser", mixed_first_result, value_projection_weight).astype(
        jnp.bfloat16
    )
    key_pair = (key_turned, swap_cores(key_turned))
    value_pair = (value_turned, swap_cores(value_turned))
    gate_turned = jax.nn.sigmoid(contract("srd,de->ser", mixed_first_result, attention_gate_weight))
    outgoing = cotangent[0].astype(jnp.float32)
    branch_grad = row_mask * outgoing
    delta_lifted = (finish[None] * branch_grad).astype(jnp.bfloat16)
    delta_gated_turned = contract("sre,de->sdr", delta_lifted, attention_output_weight)
    raised_swish_part = matmul(mixed_second_result, transition_swish_weight)
    raised_linear_part = matmul(mixed_second_result, transition_linear_weight)
    swish_sigmoid = jax.nn.sigmoid(raised_swish_part)
    hidden_state = (raised_swish_part * swish_sigmoid * raised_linear_part).astype(jnp.bfloat16)
    shifted_state = matmul(hidden_state, transition_down_weight)
    closing = jax.nn.sigmoid(
        matmul(condition_raw, closing_weight) + closing_offset.astype(jnp.float32)
    )
    delta_moved = (closing[None] * branch_grad).astype(jnp.bfloat16)
    delta_closing = jnp.sum(branch_grad * shifted_state, axis=0) * closing * (1.0 - closing)
    closing_total = exact_contract("qc,qd->cd", condition_raw, delta_closing)
    closingoffset_total = jnp.sum(delta_closing, axis=0)
    delta_condition = exact_contract("qd,cd->qc", delta_closing, closing_weight)
    down_total = contract("sqf,sqd->fd", hidden_state, delta_moved)
    delta_hidden = contract("sqd,fd->sqf", delta_moved, transition_down_weight)
    delta_swish = (
        delta_hidden
        * raised_linear_part
        * swish_sigmoid
        * (1.0 + raised_swish_part * (1.0 - swish_sigmoid))
    ).astype(jnp.bfloat16)
    delta_linear = (delta_hidden * raised_swish_part * swish_sigmoid).astype(jnp.bfloat16)
    swish_total = contract("sqd,sqf->df", mixed_second_result, delta_swish)
    linear_total = contract("sqd,sqf->df", mixed_second_result, delta_linear)
    delta_second = contract("sqf,df->sqd", delta_swish, transition_swish_weight) + contract(
        "sqf,df->sqd", delta_linear, transition_linear_weight
    )
    early = chip_sums((swish_total, linear_total, down_total, closing_total))
    meta = jnp.stack([token_count, lax.axis_index("qry")]).astype(jnp.int32)
    attended_parts = [
        attention(
            meta,
            query_turned,
            key_pair,
            value_pair,
            gate_turned,
            delta_gated_turned,
            bias_rows[part],
            part,
            PARTS,
        )
        for part in range(PARTS)
    ]
    delta_bias = [scatter_rows(part[7]) for part in attended_parts]
    gate_applied, delta_gating, delta_queries, dk_mine, dk_other, dv_mine, dv_other = [
        jnp.concatenate([part[i] for part in attended_parts], axis=1) for i in range(7)
    ]
    delta_keys = (dk_mine + swap_cores(dk_other)).astype(jnp.bfloat16)
    delta_values = (dv_mine + swap_cores(dv_other)).astype(jnp.bfloat16)
    raised_state = contract("ser,ed->srd", gate_applied, attention_output_weight)
    block_out = (
        residual + row_mask * (finish[None] * raised_state + closing[None] * shifted_state)
    ).astype(jnp.bfloat16)
    delta_finish = jnp.sum(branch_grad * raised_state, axis=0) * finish * (1.0 - finish)
    finish_total = exact_contract("qc,qd->cd", condition_raw, delta_finish)
    finishoffset_total = jnp.sum(delta_finish, axis=0)
    delta_condition = delta_condition + exact_contract("qd,cd->qc", delta_finish, finish_weight)
    output_total = contract("ser,srd->ed", gate_applied, delta_lifted)
    gating_total = contract("srd,ser->de", mixed_first_result, delta_gating)
    query_total = contract("srd,ser->de", mixed_first_result, delta_queries)
    querybias_total = jnp.sum(delta_queries.astype(jnp.float32), axis=(0, 2))
    key_total = contract("srd,ser->de", mixed_first_result, delta_keys)
    value_total = contract("srd,ser->de", mixed_first_result, delta_values)
    middle = chip_sums(
        (output_total, gating_total, finish_total, query_total, key_total, value_total),
        early,
    )
    delta_first = (
        contract("ser,de->srd", delta_queries, query_projection_weight)
        + contract("ser,de->srd", delta_keys, key_projection_weight)
        + contract("ser,de->srd", delta_values, value_projection_weight)
        + contract("ser,de->srd", delta_gating, attention_gate_weight)
    )
    normed_first, cond_delta_first, scale_first, offset_first, shift_first = modulate_back(
        delta_first, normed, condition_first, lifting_first, first_scale, first_shift
    )
    normed_second, cond_delta_second, scale_second, offset_second, shift_second = modulate_back(
        delta_second, normed, condition_second, lifting_second, second_scale, second_shift
    )
    gain_first = jnp.sum(cond_delta_first * condition_norm, axis=0)
    gain_second = jnp.sum(cond_delta_second * condition_norm, axis=0)
    single_grad = outgoing + normalize_back(normed_first + normed_second, normed, factor)
    condition_local = (
        normalize_back(
            cond_delta_first * first_gain.astype(jnp.float32)
            + cond_delta_second * second_gain.astype(jnp.float32),
            condition_norm,
            condition_factor,
        )
        + delta_condition
    )
    condition_grad = lax.psum(condition_local, "smp")
    pair_grad, pairgain_total, project_total = pair_backward(
        pair_features[0], pair_gain, pair_project, delta_bias
    )
    small = jnp.concatenate(
        [
            jnp.stack(halves(whole))
            for whole in (
                gain_first,
                offset_first,
                querybias_total,
                pairgain_total[0],
                finishoffset_total,
                gain_second,
                offset_second,
                closingoffset_total,
            )
        ]
        + [jnp.stack([half.reshape(-1) for half in halves(project_total.T)])],
        axis=1,
    )
    late = chip_sums((scale_first, shift_first, scale_second, shift_second), middle)
    vectors = lax.psum(
        (small[0] + swap_cores(small[1])), ("cplx", "smp")
    )
    ends, place = [], 0
    wide, narrow, pair_width = model_width // 2, condition_raw.shape[1] // 2, pair_gain.shape[0]
    sizes = (narrow, wide, wide, pair_width // 2, wide, narrow, wide, wide)
    for size in sizes + (pair_width * head_count // 2,):
        ends.append(vectors[place : place + size])
        place += size
    swish_total, linear_total, down_total, closing_total = widened(early)
    output_total, gating_total, finish_total, query_total, key_total, value_total = widened(middle)
    scale_first, shift_first, scale_second, shift_second = widened(late)
    return (
        block_out[None],
        single_grad[None],
        condition_grad[None],
        pair_grad[None],
        ends[0],
        scale_first,
        ends[1],
        shift_first,
        query_total,
        ends[2],
        key_total,
        value_total,
        gating_total,
        output_total,
        ends[3],
        ends[8].reshape(-1, head_count // 2),
        finish_total,
        ends[4],
        ends[5],
        scale_second,
        ends[6],
        shift_second,
        swish_total,
        linear_total,
        down_total,
        closing_total,
        ends[7],
    )


def solution(mesh):
    placed = (
        P("cplx", "smp", "qry", None),
        P("cplx", "qry", None),
        P("cplx", ("qry", "smp"), None, None),
        P("cplx"),
        P("cplx", "smp", "qry", None),
        P(),
        P(),
        P(),
        P(),
        P(),
        P(),
        P(),
        P(),
        P(),
        P(),
        P(),
        P(),
        P(),
        P(),
        P(),
        P(),
        P(),
        P(),
        P(),
        P(),
        P(),
        P(),
        P(),
    )
    return jax.shard_map(
        per_device,
        mesh=mesh,
        in_specs=placed,
        out_specs=(
            P("cplx", "smp", "qry", None),
            P("cplx", "smp", "qry", None),
            P("cplx", "qry", None),
            P("cplx", ("qry", "smp"), None, None),
            P("qry"),
            P(None, "qry"),
            P("qry"),
            P(None, "qry"),
            P(None, "qry"),
            P("qry"),
            P(None, "qry"),
            P(None, "qry"),
            P(None, "qry"),
            P(None, "qry"),
            P("qry"),
            P(None, "qry"),
            P(None, "qry"),
            P("qry"),
            P("qry"),
            P(None, "qry"),
            P("qry"),
            P(None, "qry"),
            P(None, "qry"),
            P(None, "qry"),
            P(None, "qry"),
            P(None, "qry"),
            P("qry"),
        ),
        check_vma=False,
    )
```

time: 1240 us -> 977 us (0.79)
  matrix products: 364 us -> 151 us
  Pallas kernels: 0 us -> 143 us
  waiting for transfers between devices: 551 us -> 433 us
  local copies, waits for them, and re-layouts: 140 us -> 77 us
  other arithmetic: 122 us -> 65.9 us
  blocking collectives: 43.3 us -> 76.6 us
    dot_general x25 -> x21, matrix products: 283 us -> 102 us  [contract(): return jnp.einsum(form, left, right, preferred_element_type=jnp.float32)]
    psum x1 -> x3, waiting for transfers between devices: 426 us -> 281 us  [chip_sums(): return lax.psum(tuple(kept), ('cplx', 'smp'))]
    pallas_call x0 -> x4, Pallas kernels: none -> 143 us  [the longest x2 73 us: attention(): pl.pallas_call(functools.partial(attention_kernel, step=step), grid_spec=...]
    reduce_scatter x3 -> x2, waiting for transfers between devices: 10.8 us -> 122 us  [scatter_rows(): return lax.psum_scatter(whole, 'smp', scatter_dimension=0)]
    all_gather x3 -> x2, waiting for transfers between devices: 93.9 us -> 7.7 us  [gather_rows(): return lax.all_gather(piece, 'smp', axis=0)]
    reduce_sum x2, other arithmetic: 64 us -> 2.45 us  [the longest x1 2.23 us: per_device(): querybias_total = jnp.sum(delta_queries.astype(jnp.float32), axis=(0, 2))]
    convert_element_type x2 -> x29, other arithmetic: 0.01 us -> 45.4 us  [the longest x14 20.8 us: chip_sums(): kept.append((mine + arrived.astype(f32)).astype(bf16))]
    unnamed x201 -> x227, local copies, waits for them, and re-layouts: 60.3 us -> 22.9 us
  transfers between devices with their start and end apart: 8 -> 27, of which waited for: 4 -> 7; matrix products, arithmetic and copies ran while one was open for 32% -> 23% of each run, Pallas kernels for 0% -> 15%
where the time goes in v1:
time: 977 us; the launch traced here: 970 us
  waiting for transfers between devices  433 us (44%)
  matrix products  151 us (15%)
  Pallas kernels  143 us (15%)
  local copies, waits for them, and re-layouts  77 us (8%)
  blocking collectives  76.6 us (8%)
  other arithmetic  65.9 us (7%)
  between operations  16.3 us (2%)
    psum x3, waiting for transfers between devices, chip_sums(): return lax.psum(tuple(kept), ('cplx', 'smp'))  281 us
    reduce_scatter x2, waiting for transfers between devices, scatter_rows(): return lax.psum_scatter(whole, 'smp', scatter_dimension=0)  122 us
    dot_general x21, matrix products, contract(): return jnp.einsum(form, left, right, preferred_element_type=jnp.float32)  102 us
    psum x1, blocking collectives, per_device(): vectors = lax.psum(small[0] + swap_cores(small[1]), ('cplx', 'smp'))  76.6 us
    pallas_call x2, Pallas kernels, attention(): pl.pallas_call(functools.partial(attention_kernel, step=step), grid_spec=...  73 us
    pallas_call x1, Pallas kernels, pair_backward(): pl.pallas_call(functools.partial(pair_backward_kernel, block=block, heads...  40.7 us
    dot_general x9, matrix products, matmul(): return jnp.dot(left, right, preferred_element_type=jnp.float32)  31.2 us
    pallas_call x1, Pallas kernels, pair_forward(): pl.pallas_call(functools.partial(pair_forward_kernel, block=block, heads=...  28.8 us
  transfers between devices with their start and end apart: 27, of which 7 were waited for; matrix products, arithmetic and copies ran while one was open for 23% of the time, Pallas kernels for 15%

profile of v1, /device:TPU:0, one launch (start us, length us, event | category | flops | bytes accessed | tf_op | source)
XLA Modules:
  0.0 969.6 jit_solution(386612263318158242)
XLA Ops:
  12.7 1.9 convert_reduce_fusion
  18.1 2.2 fusion.17
  20.3 3.0 convolution_convert_fusion.1
  23.7 3.0 convolution_convert_fusion
  27.5 28.8 %shard_map.475 = (bf16[8,80,640]{2,1,0:T(8,128)(2,1)}, bf16[8,80,640]{2,1,0:T(8,128)(2,1)}) custom-call(bf16[80,640,128]{2,1,0:T(8,128)(2,1)} %bitcast.242, bf16[1,128]{1,0:T(2,128)(2,1)} %bitcast.252, bf16[128,16]{1,0:T(8,128)(2,1)} %copy.138.project), custom_call_target="tpu_custom_call" | custom-call | flops 3355443200 | bytes 14745600 | tf_op jit(solution)/shard_map/pallas_call | solution.py:175
  57.4 8.6 fusion.39
  67.5 9.5 fusion.33
  76.9 11.4 %multiply_convert_fusion.1 = (bf16[4,320,1536]{2,1,0:T(8,128)(2,1)S(1)}, bf16[4,320,1536]{2,1,0:T(8,128)(2,1)}, bf16[4,320,1536]{2,1,0:T(8,128)(2,1)S(1)}) fusion(f32[4,320,1536]{2,1,0:T(8,128)} %fusion.33, f32[4,320,1536]{2,1,0:T(8,128)} %fusion.39, bf16[4,320,768]{2,1,0:T(8,128)(2,1)S(1)} %copy-done.52, bf16[768,1536]{1,0:T(8,128)(2,1)S(1)} %copy-done), kind=kOutput, calls=%fused_computation.1 | convolution fusion | flops 3051356160 | bytes 31850496 | tf_op jit(solution)/shard_map/dot_general | solution.py:332
  88.3 3.3 convolution_bitcast_fusion.1
  94.2 3.3 convolution_bitcast_fusion.2
  97.4 2.2 copy-done.32
  101.2 6.5 convolution_bitcast_fusion
  107.7 2.2 copy-done.34
  111.3 4.3 copy.132
  115.5 4.2 copy.130
  122.2 3.3 fusion.32.query
  125.5 3.8 convolution_bitcast_fusion.3.delta_gated
  129.8 5.1 fusion.37
  135.0 4.1 divide_bitcast_fusion.gate
  139.1 4.1 copy.139.key_other
  143.2 4.2 copy.140.value_other
  147.4 36.3 %shard_map.476 = (bf16[4,384,320]{2,1,0:T(8,128)(2,1)}, bf16[4,384,320]{2,1,0:T(8,128)(2,1)}, bf16[4,384,320]{2,1,0:T(8,128)(2,1)}, f32[4,384,320]{2,1,0:T(8,128...) custom-call(s32[2]{0:T(128)} %pad_add_fusion.meta, ...), custom_call_target="tpu_custom_call" | custom-call | flops 20132659200 | bytes 23265280 | tf_op jit(solution)/shard_map/pallas_call | solution.py:121
  183.7 7.7 all-gather.7.cloned.1.call-done
  191.4 36.7 %shard_map.477 = (bf16[4,384,320]{2,1,0:T(8,128)(2,1)}, bf16[4,384,320]{2,1,0:T(8,128)(2,1)}, bf16[4,384,320]{2,1,0:T(8,128)(2,1)}, f32[4,384,320]{2,1,0:T(8,128...) custom-call(s32[2]{0:T(128)} %pad_add_fusion.meta, ...), custom_call_target="tpu_custom_call" | custom-call | flops 20132659200 | bytes 23265280 | tf_op jit(solution)/shard_map/pallas_call | solution.py:121
  228.1 4.2 pad_maximum_fusion
  232.3 5.8 copy.145
  238.1 8.6 fusion.46
  246.6 2.5 pad_maximum_fusion.1
  249.1 6.4 copy.148
  256.3 7.2 fusion.35
  263.5 3.3 add_convert_fusion.2
  266.8 3.4 add_convert_fusion.3
  270.1 3.4 add_convert_fusion.1
  279.2 4.1 fusion.81
  283.3 3.5 convolution_bitcast_fusion.6
  286.9 5.7 copy.146
  292.6 4.4 fusion.6
  298.4 4.2 fusion.78
  302.6 6.0 copy.149
  308.6 3.7 fusion.7
  313.7 4.2 fusion.75
  319.1 12.0 %fusion.138 = (f32[320,768]{1,0:T(8,128)}, f32[320,768]{1,0:T(8,128)}, f32[4,320]{1,0:T(4,128)S(1)}, f32[4,320]{1,0:T(4,128)S(1)}, f32[4,320,768]{2,1,0:T(8,128)}, /*index=5*/f32[320,768]{1,0:T(8,128)}, f32[320,768]{1,0:T(8,128)}) fusion(f32[4,320]{1,0:T(4,128)S(1)} %copy-done.88, f32[4,320]{1,0:T(4,128)S(1)} %copy-done.86, ...), kind=kOutput, calls=%fused_computation.223 | convolution fusion | flops 1526658560 | bytes 30691328 | tf_op jit(solution)/shard_map/ser,de->srd/dot_general | solution.py:336
  331.2 10.2 %fusion.30 = (f32[320,768]{1,0:T(8,128)}, f32[320,768]{1,0:T(8,128)S(1)}, bf16[1,4,320,768]{3,2,1,0:T(8,128)(2,1)}, f32[1,4,320,768]{3,2,1,0:T(8,128)}) fusion(bf16[1,4,320,768]{3,2,1,0:T(8,128)(2,1)} %param.32, f32[320]{0:T(512)S(1)} %fusion.116, f32[4,320,768]{2,1,0:T(8,128)} %fusion.35, f32[320,768]{1,0:T(8,128)S(1)} %copy-done.13, ...), kind=kOutput, calls=%fused_computation.45 | convolution fusion | flops 1529118720 | bytes 24794368 | tf_op jit(solution)/shard_map/ser,ed->srd/dot_general | solution.py:336
  343.3 2.1 convolution_bitcast_fusion.7
  345.4 3.0 dynamic-slice_convert_fusion.5
  350.9 4.2 convolution_bitcast_fusion.8
  355.6 2.3 add_convert_fusion.6
  358.8 2.1 convolution_bitcast_fusion.4
  363.1 2.1 convolution_bitcast_fusion.5
  369.3 142.6 %all-reduce.14.cloned.1.call-done = (bf16[768,768]{1,0:T(8,128)(2,1)}, bf16[768,768]{1,0:T(8,128)(2,1)}, bf16[1536,384]{1,0:T(8,128)(2,1)}, bf16[384,384]{0,1:T(8,128)(2,1)}) async-done(((bf16[768,768]{1,0:T(8,128)(2,1)}, bf16[768,768]{1,0:T(8,128)(2,1)}, bf16[1536,384]{1,0:T(8,128)(2,1)}, bf16[384,384]{0,1:T(8,128)(2,1)}), (bf16[768,768]{1,0:T(8,128)(2,1)}, bf16[768,768]{1,0:T(8,128)(2,1)}, ...) | async-done | bytes 3833872 | tf_op jit(solution)/shard_map/psum | solution.py:298
  513.6 2.2 convert_reduce_fusion.1
  532.0 138.6 %all-reduce.12.cloned.1.call-done = (bf16[384,384]{0,1:T(8,128)(2,1)}, bf16[768,384]{1,0:T(8,128)(2,1)}, bf16[768,384]{1,0:T(8,128)(2,1)}, bf16[768,384]{1,0:T(8...) async-done(((bf16[384,384]{0,1:T(8,128)(2,1)}, bf16[768,384]{1,0:T(8,128)(2,1)}, bf16[768,384]{1,0:T(8,128)(2,1)}, bf16[768,384]{1,0:T(8,128)(2,1)}, ...) | async-done | bytes 3244048 | tf_op jit(solution)/shard_map/psum | solution.py:298
  670.9 2.3 fusion.124
  673.2 3.1 fusion.66
  676.4 57.8 %reduce-scatter.5.cloned.1.call-done = bf16[1,8,80,640]{3,2,1,0:T(8,128)(2,1)} async-done(((bf16[4,8,80,640]{3,2,1,0:T(8,128)(2,1)}), bf16[1,8,80,640]{3,2,1,0:T(8,128)(2,1)}) %reduce-scatter.5.cloned.1.call-update) | async-done | bytes 819216 | tf_op jit(solution)/shard_map/reduce_scatter | solution.py:313
  734.1 64.7 %reduce-scatter.3.cloned.1.call-done = bf16[1,8,80,640]{3,2,1,0:T(8,128)(2,1)} async-done(((bf16[4,8,80,640]{3,2,1,0:T(8,128)(2,1)}), bf16[1,8,80,640]{3,2,1,0:T(8,128)(2,1)}) %reduce-scatter.3.cloned.1.call-update) | async-done | bytes 819216 | tf_op jit(solution)/shard_map/reduce_scatter | solution.py:313
  798.8 40.7 %shard_map.478 = (f32[80,640,128]{2,1,0:T(8,128)}, f32[1,128]{1,0:T(1,128)}, f32[16,128]{1,0:T(8,128)}) custom-call(bf16[80,640,128]{2,1,0:T(8,128)(2,1)} %bitcast.243, bf16[1,128]{1,0:T(2,128)(2,1)} %bitcast.253, bf16[128,16]{1,0:T(8,128)(2,1)} %copy.138.project, bf16[8,80,640]{2,1,0:T(8,128)(2,1)} %bitcast.257, bf16[8,80,640]{2,1,0:T(8,128)(2,1)} %bitcast.256), custom_call_target="tpu_custom_call" | custom-call | flops 6710886400 | bytes 40960000 | tf_op jit(solution)/shard_map/pallas_call | solution.py:245
  843.0 76.6 %psum.113 = f32[3392]{0:T(1024)S(1)} all-reduce(f32[3392]{0:T(1024)S(1)} %add.353), channel_id=1, replica_groups=mesh['cplx'=4,'smp'=4,'qry'=2] {'cplx','smp'}, use_global_device_ids=true, to_apply=%region_24.0 | all-reduce | flops 3392 | bytes 27136 | tf_op jit(solution)/shard_map/psum | solution.py:544
  922.3 1.6 convert_element_type.371
  934.6 1.9 convert_element_type.361
  936.4 1.8 convert_element_type.362
  938.2 1.8 convert_element_type.369
  940.9 19.8 %all-reduce.8.cloned.1.call-done = f32[1,320,384]{2,1,0:T(8,128)} async-done(((f32[1,320,384]{2,1,0:T(8,128)}), f32[1,320,384]{2,1,0:T(8,128)}) %all-reduce.8.cloned.1.call-update) | async-done | bytes 491536 | tf_op jit(solution)/shard_map/psum | solution.py:522
  960.7 1.8 copy.197
  (394 shorter events, 77.9 us)
Async XLA Ops:
  7.2 69.7 %copy-start = (bf16[768,1536]{1,0:T(8,128)(2,1)S(1)}, bf16[768,1536]{1,0:T(8,128)(2,1)}, u32[]{:S(2)}) copy-start(bf16[768,1536]{1,0:T(8,128)(2,1)} %param.51) | copy-start | bytes 7077892
  7.2 8.1 copy-start.2
  7.2 140.2 %all-gather.5.cloned.1.call-start = ((), (), s32[]{:S(2)}) async-start(), calls=%async_computation.5 | async-start | bytes 4096000 | tf_op jit(solution)/shard_map/all_gather | solution.py:307
  7.3 7.3 copy-start.3
  7.3 8.1 copy-start.37
  8.6 8.8 copy-start.81
  9.9 7.5 copy-start.83
  10.6 5.2 copy-start.89
  12.0 5.5 copy-start.91
  23.3 115.8 %collective-permute-start = (bf16[4,768,320]{1,2,0:T(8,128)(2,1)}, bf16[4,768,320]{1,2,0:T(8,128)(2,1)}, u32[]{:S(2)}, u32[]{:S(2)}) collective-permute-start(bf16[4,768,320]{1,2,0:T(8,128)(2,1)} %bitcast.8), channel_id=1, source_target_pairs={{0,1},{1,0},{2,3},{3,2},{4,5},{5,4},{6,7},{7,6},{8,9},{9,8},{10,11... | collective-permute-start | bytes 5898248 | tf_op jit(solution)/shard_map/ppermute | solution.py:279
  26.8 116.4 %collective-permute-start.1 = (bf16[4,768,320]{1,2,0:T(8,128)(2,1)}, bf16[4,768,320]{1,2,0:T(8,128)(2,1)}, u32[]{:S(2)}, u32[]{:S(2)}) collective-permute-start(bf16[4,768,320]{1,2,0:T(8,128)(2,1)} %bitcast.11), channel_id=1, source_target_pairs={{0,1},{1,0},{2,3},{3,2},{4,5},{5,4},{6,7},{7,6},{8,9},{9,8},{10,11... | collective-permute-start | bytes 5898248 | tf_op jit(solution)/shard_map/ppermute | solution.py:279
  27.5 29.9 %copy-start.94 = (bf16[768]{0:T(1024)(128)(2,1)S(1)}, bf16[768]{0:T(1024)(128)(2,1)}, u32[]{:S(2)}) copy-start(bf16[768]{0:T(1024)(128)(2,1)} %param.55) | copy-start | bytes 4612
  56.4 135.0 %all-gather.7.cloned.1.call-start = ((), (), s32[]{:S(2)}) async-start(), calls=%async_computation.6 | async-start | bytes 4096000 | tf_op jit(solution)/shard_map/all_gather | solution.py:307
  57.4 8.6 copy-start.76
  67.5 9.5 copy-start.52
  88.3 5.8 copy-start.107
  93.0 170.5 %collective-permute-start.16 = (bf16[768,768]{1,0:T(8,128)(2,1)}, bf16[768,768]{1,0:T(8,128)(2,1)}, u32[]{:S(2)}, u32[]{:S(2)}) collective-permute-start(bf16[768,768]{1,0:T(8,128)(2,1)} %dynamic-slice_convert_fusion.1), channel_id=1, source_target_pairs={{0,1},{1,0},{2,3},{3,2},{4,5},{5,4},{6,7},{7,6},{8,9},{9,8},{10,11... | collective-permute-start | bytes 3538952 | tf_op jit(solution)/shard_map/ppermute | solution.py:279
  100.8 166.0 %collective-permute-start.15 = (bf16[768,768]{1,0:T(8,128)(2,1)}, bf16[768,768]{1,0:T(8,128)(2,1)}, u32[]{:S(2)}, u32[]{:S(2)}) collective-permute-start(bf16[768,768]{1,0:T(8,128)(2,1)} %dynamic-slice_convert_fusion.2), channel_id=1, source_target_pairs={{0,1},{1,0},{2,3},{3,2},{4,5},{5,4},{6,7},{7,6},{8,9},{9,8},{10,11... | collective-permute-start | bytes 3538952 | tf_op jit(solution)/shard_map/ppermute | solution.py:279
  111.1 159.1 %collective-permute-start.17 = (bf16[1536,384]{1,0:T(8,128)(2,1)}, bf16[1536,384]{1,0:T(8,128)(2,1)}, u32[]{:S(2)}, u32[]{:S(2)}) collective-permute-start(bf16[1536,384]{1,0:T(8,128)(2,1)} %dynamic-slice_convert_fusion), channel_id=1, source_target_pairs={{0,1},{1,0},{2,3},{3,2},{4,5},{5,4},{6,7},{7,6},{8,9},{9,8},{10,11... | collective-permute-start | bytes 3538952 | tf_op jit(solution)/shard_map/ppermute | solution.py:279
  111.2 400.7 %all-reduce.14.cloned.1.call-start = ((), (), s32[]{:S(2)}) async-start(), calls=%async_computation.9 | async-start | bytes 7667712 | tf_op jit(solution)/shard_map/psum | solution.py:298
  115.5 4.8 copy-start.77
  125.5 4.3 copy-start.109
  129.8 5.1 copy-start.56
  191.4 36.7 %copy-start.45 = (f32[4,384,320]{2,1,0:T(8,128)S(1)}, f32[4,384,320]{2,1,0:T(8,128)}, u32[]{:S(2)}) copy-start(f32[4,384,320]{2,1,0:T(8,128)} %get-tuple-element.66) | copy-start | bytes 5898244
  238.0 8.6 copy-start.44
  238.0 8.6 copy-start.46
  238.1 48.8 %collective-permute-start.2 = (f32[4,768,320]{1,2,0:T(8,128)}, f32[4,768,320]{1,2,0:T(8,128)}, u32[]{:S(2)}, u32[]{:S(2)}) collective-permute-start(f32[4,768,320]{1,2,0:T(8,128)} %copy.145), channel_id=1, source_target_pairs={{0,1},{1,0},{2,3},{3,2},{4,5},{5,4},{6,7},{7,6},{8,9},{9,8},{10,11... | collective-permute-start | bytes 11796488 | tf_op jit(solution)/shard_map/ppermute | solution.py:279
  249.1 7.1 copy-start.98
  255.5 47.1 %collective-permute-start.3 = (f32[4,768,320]{1,2,0:T(8,128)}, f32[4,768,320]{1,2,0:T(8,128)}, u32[]{:S(2)}, u32[]{:S(2)}) collective-permute-start(f32[4,768,320]{1,2,0:T(8,128)} %copy.148), channel_id=1, source_target_pairs={{0,1},{1,0},{2,3},{3,2},{4,5},{5,4},{6,7},{7,6},{8,9},{9,8},{10,11... | collective-permute-start | bytes 11796488 | tf_op jit(solution)/shard_map/ppermute | solution.py:279
  277.1 6.2 copy-start.28
  292.6 5.8 copy-start.103
  302.6 6.0 copy-start.39
  308.6 5.1 copy-start.105
  313.7 4.3 copy-start.9
  313.7 5.4 copy-start.31
  313.7 5.4 copy-start.86
  313.7 5.4 copy-start.88
  319.1 12.0 %copy-start.13 = (f32[320,768]{1,0:T(8,128)S(1)}, f32[320,768]{1,0:T(8,128)}, u32[]{:S(2)}) copy-start(f32[320,768]{1,0:T(8,128)} %fusion.56) | copy-start | bytes 2949124
  319.1 12.0 %copy-start.17 = (f32[320,768]{1,0:T(8,128)S(1)}, f32[320,768]{1,0:T(8,128)}, u32[]{:S(2)}) copy-start(f32[320,768]{1,0:T(8,128)} %copy-done.16) | copy-start | bytes 2949124
  342.8 7.0 collective-permute-start.18
  348.4 7.1 collective-permute-start.12
  349.4 8.5 collective-permute-start.10
  350.6 320.0 %all-reduce.12.cloned.1.call-start = ((), (), s32[]{:S(2)}) async-start(), calls=%async_computation.8 | async-start | bytes 6488064 | tf_op jit(solution)/shard_map/psum | solution.py:298
  350.9 4.7 copy-start.53
  350.9 6.9 copy-start.55
  355.3 10.4 %collective-permute-start.9 = (bf16[768,384]{1,0:T(8,128)(2,1)S(1)}, bf16[768,384]{1,0:T(8,128)(2,1)S(1)}, u32[]{:S(2)}, u32[]{:S(2)}) collective-permute-start(bf16[768,384]{1,0:T(8,128)(2,1)S(1)} %dynamic-slice_convert_fusion.7), channel_id=1, source_target_pairs={{0,1},{1,0},{2,3},{3,2},{4,5},{5,4},{6,7},{7,6},{8,9},{9,8},{10,11... | collective-permute-start | bytes 1769480 | tf_op jit(solution)/shard_map/ppermute | solution.py:279
  361.0 6.4 collective-permute-start.14
  362.9 3.8 collective-permute-start.11
  365.3 3.1 collective-permute-start.13
  511.9 222.2 %reduce-scatter.5.cloned.1.call-start = ((), (), s32[]{:S(2)}) async-start(), calls=%async_computation.4 | async-start | bytes 4096000 | tf_op jit(solution)/shard_map/reduce_scatter | solution.py:313
  512.5 286.3 %reduce-scatter.3.cloned.1.call-start = ((), (), s32[]{:S(2)}) async-start(), calls=%async_computation.3 | async-start | bytes 4096000 | tf_op jit(solution)/shard_map/reduce_scatter | solution.py:313
  513.1 421.5 %all-reduce.10.cloned.1.call-start = ((), (), s32[]{:S(2)}) async-start(), calls=%async_computation.7 | async-start | bytes 2359296 | tf_op jit(solution)/shard_map/psum | solution.py:298
  517.3 11.5 %collective-permute-start.8 = (bf16[384,384]{1,0:T(8,128)(2,1)S(1)}, bf16[384,384]{1,0:T(8,128)(2,1)S(1)}, u32[]{:S(2)}, u32[]{:S(2)}) collective-permute-start(bf16[384,384]{1,0:T(8,128)(2,1)S(1)} %dynamic-slice_convert_fusion.10), channel_id=1, source_target_pairs={{0,1},{1,0},{2,3},{3,2},{4,5},{5,4},{6,7},{7,6},{8,9},{9,8},{10,11... | collective-permute-start | bytes 884744 | tf_op jit(solution)/shard_map/ppermute | solution.py:279
  518.9 10.8 %collective-permute-start.7 = (bf16[384,384]{1,0:T(8,128)(2,1)S(1)}, bf16[384,384]{1,0:T(8,128)(2,1)S(1)}, u32[]{:S(2)}, u32[]{:S(2)}) collective-permute-start(bf16[384,384]{1,0:T(8,128)(2,1)S(1)} %dynamic-slice_convert_fusion.11), channel_id=1, source_target_pairs={{0,1},{1,0},{2,3},{3,2},{4,5},{5,4},{6,7},{7,6},{8,9},{9,8},{10,11... | collective-permute-start | bytes 884744 | tf_op jit(solution)/shard_map/ppermute | solution.py:279
  520.8 9.6 collective-permute-start.6
  522.3 8.9 collective-permute-start.5
  529.7 141.3 %copy-start.15 = (f32[320,768]{1,0:T(8,128)S(1)}, f32[320,768]{1,0:T(8,128)}, u32[]{:S(2)}) copy-start(f32[320,768]{1,0:T(8,128)} %fusion.56) | copy-start | bytes 2949124
  532.0 141.2 %copy-start.20 = (f32[320,768]{1,0:T(8,128)S(1)}, f32[320,768]{1,0:T(8,128)}, u32[]{:S(2)}) copy-start(f32[320,768]{1,0:T(8,128)} %copy-done.16) | copy-start | bytes 2949124
  670.6 290.1 %all-reduce.8.cloned.1.call-start = ((), (), s32[]{:S(2)}) async-start(), calls=%async_computation.2 | async-start | bytes 983040 | tf_op jit(solution)/shard_map/psum | solution.py:522
  798.8 123.4 %copy-start.59 = (bf16[768,768]{1,0:T(8,128)(2,1)S(1)}, bf16[768,768]{1,0:T(8,128)(2,1)}, u32[]{:S(2)}) copy-start(bf16[768,768]{1,0:T(8,128)(2,1)} %get-tuple-element.221) | copy-start | bytes 3538948
  839.5 84.3 %copy-start.58 = (bf16[768,768]{1,0:T(8,128)(2,1)S(1)}, bf16[768,768]{1,0:T(8,128)(2,1)}, u32[]{:S(2)}) copy-start(bf16[768,768]{1,0:T(8,128)(2,1)} %get-tuple-element.222) | copy-start | bytes 3538948
  841.8 1.2 collective-permute-start.4
  933.6 29.0 %copy-start.1 = (bf16[768,1536]{1,0:T(8,128)(2,1)S(1)}, bf16[768,1536]{1,0:T(8,128)(2,1)}, u32[]{:S(2)}) copy-start(bf16[768,1536]{1,0:T(8,128)(2,1)} %param.51) | copy-start | bytes 7077892
  934.6 5.5 copy-start.80
  (73 other events, 190.4 us)
Sparse Core Ops, SparseCore 0:
  56.5 68.3 all-gather.4
  127.0 64.2 all-gather.6
  350.8 161.1 all-reduce.13
  519.9 150.6 all-reduce.11
  672.9 61.2 reduce-scatter.4
  736.4 62.3 reduce-scatter.2
  806.1 114.3 all-reduce.9
  923.6 37.0 all-reduce.7

commit v2 on v1

--- a/solution.py
+++ b/solution.py
@@ -8,12 +8,35 @@
 from jax.sharding import PartitionSpec as P
 
 EPSILON = 1e-05
-HIGHEST = lax.Precision.HIGHEST
 LANES = 128
 VMEM_LIMIT = 56 * 2**20
 PARTS = 2
 f32 = jnp.float32
 bf16 = jnp.bfloat16
+
+
+def normalize(values):
+    centre = values - jnp.mean(values, axis=-1, keepdims=True)
+    factor = lax.rsqrt(jnp.mean(centre * centre, axis=-1, keepdims=True) + EPSILON)
+    return (centre * factor, factor)
+
+
+def normalize_back(incoming, normed, factor):
+    return factor * (
+        incoming
+        - jnp.mean(incoming, axis=-1, keepdims=True)
+        - normed * jnp.mean(incoming * normed, axis=-1, keepdims=True)
+    )
+
+
+def matmul(left, right):
+    return jnp.dot(left, right, preferred_element_type=jnp.float32)
+
+
+def contract(form, left, right):
+    return jnp.einsum(
+        form, left.astype(bf16), right.astype(bf16), preferred_element_type=jnp.float32
+    )
 
 
 def dot(left, right, left_dim, right_dim):
@@ -45,6 +68,7 @@
     ]
 
     def joined(mine, other):
+        mine, other = mine[:, :rows], other[:, :rows]
         first = jnp.where(second, other, mine)
         last = jnp.where(second, mine, other)
         return jnp.concatenate([first, last], axis=1)
@@ -52,7 +76,7 @@
     def parted(whole, mine, other, sample):
         first, last = whole[:, :rows], whole[:, rows:]
         mine[sample] = jnp.where(second, last, first)
-        other[sample] = jnp.where(second, first, last).astype(other.dtype)
+        other[sample, :, :rows] = jnp.where(second, first, last).astype(other.dtype)
 
     keys, values = [], []
     for s in range(samples):
@@ -115,16 +139,20 @@
     outer = pl.BlockSpec((samples, head_width, rows), lambda h, meta: (0, h, 0))
     tile = pl.BlockSpec((pieces, 1, piece_rows, total), lambda h, meta: (0, h, 0, 0))
 
-    def made(dtype):
-        return jax.ShapeDtypeStruct((samples, heads * head_width, rows), dtype)
+    padded = key_pair[0].shape[2]
+    inner_wide = pl.BlockSpec((samples, head_width, padded), lambda h, meta: (0, first + h, 0))
+    outer_wide = pl.BlockSpec((samples, head_width, padded), lambda h, meta: (0, h, 0))
+
+    def made(dtype, columns=rows):
+        return jax.ShapeDtypeStruct((samples, heads * head_width, columns), dtype)
 
     return pl.pallas_call(
         functools.partial(attention_kernel, step=step),
         grid_spec=pltpu.PrefetchScalarGridSpec(
             num_scalar_prefetch=1,
             grid=(heads,),
-            in_specs=[inner] * 7 + [tile],
-            out_specs=[outer] * 7 + [tile],
+            in_specs=[inner] + [inner_wide] * 4 + [inner] * 2 + [tile],
+            out_specs=[outer] * 4 + [outer_wide, outer, outer_wide, tile],
             scratch_shapes=[
                 pltpu.VMEM((samples, rows, total), f32),
                 pltpu.VMEM((samples, rows, total), bf16),
@@ -132,7 +160,8 @@
             ],
         ),
         out_shape=[
-            made(bf16), made(bf16), made(bf16), made(f32), made(f32), made(f32), made(f32),
+            made(bf16), made(bf16), made(bf16), made(f32), made(bf16, padded), made(f32),
+            made(bf16, padded),
             jax.ShapeDtypeStruct(bias.shape, bf16),
         ],
         compiler_params=pltpu.CompilerParams(vmem_limit_bytes=VMEM_LIMIT),
@@ -275,8 +304,420 @@
     )(pair, gain.reshape(1, width), project, *deltas)
 
 
+def fixed(shape):
+    return pl.BlockSpec(shape, lambda s, *_: (0,) * len(shape), pipeline_mode=pl.Buffered(1))
+
+
+def by_sample(shape, buffers=2):
+    return pl.BlockSpec(
+        (1,) + shape,
+        lambda s, *_: (s,) + (0,) * len(shape),
+        pipeline_mode=pl.Buffered(buffers),
+    )
+
+
+def row_valid(meta, rows):
+    place = lax.broadcasted_iota(jnp.int32, (rows, 1), 0) + meta[1] * rows
+    return jnp.where(place < meta[0], 1.0, 0.0)
+
+
+def pack_columns(meta, packs, arrays, start=0):
+    tile = packs[0].shape[1]
+    for array in arrays:
+        depth, share = array.shape[0], array.shape[1] // 2
+        for side in range(2):
+            core = meta[1] if side == 0 else 1 - meta[1]
+            for block in range(share // tile):
+                column = pl.multiple_of(core * share + block * tile, LANES)
+                packs[side][start + block * depth : start + (block + 1) * depth, :] = array[
+                    :, pl.ds(column, tile)
+                ].astype(bf16)
+        start += depth * (share // tile)
+
+
+def project_kernel(
+    meta, single, cotangent, lifting, shifting, finish, query_bias,
+    query_weight, key_weight, value_weight, gate_weight, output_weight,
+    query, key, value, gate, delta_gated, mixed_out,
+):
+    rows = single.shape[1]
+    normed, _ = normalize(single[0].astype(f32))
+    mixed = (lifting[...] * normed + shifting[...]).astype(bf16)
+    mixed_out[0] = mixed
+    query[0] = (dot(mixed, query_weight[...], 1, 0) + query_bias[...]).astype(bf16).T
+    key[0, :, :rows] = dot(mixed, key_weight[...], 1, 0).astype(bf16).T
+    value[0, :, :rows] = dot(mixed, value_weight[...], 1, 0).astype(bf16).T
+    gate[0] = jax.nn.sigmoid(dot(mixed, gate_weight[...], 1, 0)).T
+    branch = row_valid(meta, rows) * cotangent[0].astype(f32)
+    lifted = (finish[...] * branch).astype(bf16)
+    delta_gated[0] = dot(lifted, output_weight[...], 1, 1).T
+
+
+def project(meta, single, cotangent, lifting, shifting, finish, query_bias, weights):
+    samples, rows, width = single.shape
+    natural, turned = by_sample((rows, width)), by_sample((width, rows))
+    flat, square = fixed((rows, width)), fixed((width, width))
+    padded = rows + -rows % LANES
+    wide = by_sample((width, padded))
+    return pl.pallas_call(
+        project_kernel,
+        grid_spec=pltpu.PrefetchScalarGridSpec(
+            num_scalar_prefetch=1,
+            grid=(samples,),
+            in_specs=[natural, natural, flat, flat, flat, fixed((1, width))] + [square] * 5,
+            out_specs=[turned, wide, wide, turned, turned, natural],
+        ),
+        out_shape=[
+            jax.ShapeDtypeStruct((samples, width, columns), dtype)
+            for columns, dtype in (
+                (rows, bf16), (padded, bf16), (padded, bf16), (rows, f32), (rows, f32)
+            )
+        ]
+        + [jax.ShapeDtypeStruct((samples, rows, width), bf16)],
+        compiler_params=pltpu.CompilerParams(vmem_limit_bytes=VMEM_LIMIT),
+        cost_estimate=pl.CostEstimate(
+            flops=16 * samples * rows * width * width,
+            bytes_accessed=samples * rows * width * 20 + 10 * width * width,
+            transcendentals=samples * rows * width,
+        ),
+    )(meta, single, cotangent, lifting, shifting, finish, query_bias, *weights)
+
+
+def transition_kernel(
+    meta, single, cotangent, lifting, shifting, closing,
+    swish_weight, linear_weight, down_weight,
+    closed, delta_second, closing_sum, lift_sum, shift_sum, pack_mine, pack_other,
+    swish_sum, linear_sum, down_sum,
+):
+    rows = single.shape[1]
+    sample = pl.program_id(0)
+    normed, _ = normalize(single[0].astype(f32))
+    mixed = (lifting[...] * normed + shifting[...]).astype(bf16)
+    up_swish = dot(mixed, swish_weight[...], 1, 0)
+    up_linear = dot(mixed, linear_weight[...], 1, 0)
+    squash = jax.nn.sigmoid(up_swish)
+    silu = up_swish * squash
+    hidden = (silu * up_linear).astype(bf16)
+    moved = dot(hidden, down_weight[...], 1, 0)
+    closing_here = closing[...]
+    branch = row_valid(meta, rows) * cotangent[0].astype(f32)
+    closed[0] = closing_here * moved
+    delta_moved = (closing_here * branch).astype(bf16)
+    delta_hidden = dot(delta_moved, down_weight[...], 1, 1)
+    delta_swish = (delta_hidden * up_linear * squash * (1.0 + up_swish * (1.0 - squash))).astype(bf16)
+    delta_linear = (delta_hidden * silu).astype(bf16)
+    second = dot(delta_swish, swish_weight[...], 1, 1) + dot(
+        delta_linear, linear_weight[...], 1, 1
+    )
+    delta_second[0] = second
+
+    def collect(first):
+        def put(ref, value):
+            if first:
+                ref[...] = value
+            else:
+                ref[...] += value
+
+        put(closing_sum, branch * moved)
+        put(lift_sum, second * normed)
+        put(shift_sum, second)
+        put(swish_sum, dot(mixed, delta_swish, 0, 0))
+        put(linear_sum, dot(mixed, delta_linear, 0, 0))
+        put(down_sum, dot(hidden, delta_moved, 0, 0))
+
+    @pl.when(sample == 0)
+    def _():
+        collect(True)
+
+    @pl.when(sample > 0)
+    def _():
+        collect(False)
+
+    @pl.when(sample == pl.num_programs(0) - 1)
+    def _():
+        pack_columns(meta, (pack_mine, pack_other), (swish_sum, linear_sum, down_sum))
+
+
+def transition(meta, single, cotangent, lifting, shifting, closing, weights, pack_rows):
+    samples, rows, width = single.shape
+    inner = weights[0].shape[1]
+    natural, flat = by_sample((rows, width)), fixed((rows, width))
+    up, down = (width, inner), (inner, width)
+    pack = (pack_rows, width // 2)
+    return pl.pallas_call(
+        transition_kernel,
+        grid_spec=pltpu.PrefetchScalarGridSpec(
+            num_scalar_prefetch=1,
+            grid=(samples,),
+            in_specs=[natural, natural, flat, flat, flat, fixed(up), fixed(up), fixed(down)],
+            out_specs=[natural, natural, flat, flat, flat, fixed(pack), fixed(pack)],
+            scratch_shapes=[pltpu.VMEM(up, f32), pltpu.VMEM(up, f32), pltpu.VMEM(down, f32)],
+        ),
+        out_shape=[
+            jax.ShapeDtypeStruct(shape, f32)
+            for shape in ((samples, rows, width),) * 2 + ((rows, width),) * 3
+        ]
+        + [jax.ShapeDtypeStruct(pack, bf16)] * 2,
+        compiler_params=pltpu.CompilerParams(vmem_limit_bytes=VMEM_LIMIT),
+        cost_estimate=pl.CostEstimate(
+            flops=18 * samples * rows * width * inner,
+            bytes_accessed=samples * rows * width * 12 + 18 * width * inner,
+            transcendentals=samples * rows * inner,
+        ),
+    )(meta, single, cotangent, lifting, shifting, closing, *weights)
+
+
+def finish_kernel(
+    meta, single, cotangent, closed, delta_second, mixed,
+    gated_a, gated_b, gate_a, gate_b, query_a, query_b, dk_mine_a, dk_mine_b, dk_other_a,
+    dk_other_b, dv_mine_a, dv_mine_b, dv_other_a, dv_other_b,
+    lifting_first, lifting_second, finish,
+    query_weight, key_weight, value_weight, gate_weight, output_weight,
+    block_out, single_grad, finish_sum, lift_first, shift_first, pack_mine, pack_other, bias_sum,
+    query_sum, key_sum, value_sum, gate_sum, output_sum,
+):
+    rows = single.shape[1]
+
+    def whole(*parts):
+        return jnp.concatenate([part[0] for part in parts], axis=0)
+
+    gated, delta_gate, delta_query = (
+        whole(gated_a, gated_b), whole(gate_a, gate_b), whole(query_a, query_b)
+    )
+    delta_key = (whole(dk_mine_a, dk_mine_b) + whole(dk_other_a, dk_other_b)[:, :rows].astype(f32)).astype(bf16)
+    delta_value = (
+        whole(dv_mine_a, dv_mine_b) + whole(dv_other_a, dv_other_b)[:, :rows].astype(f32)
+    ).astype(bf16)
+    rows = single.shape[1]
+    sample = pl.program_id(0)
+    residual = single[0].astype(f32)
+    normed, factor = normalize(residual)
+    valid = row_valid(meta, rows)
+    outgoing = cotangent[0].astype(f32)
+    branch = valid * outgoing
+    finish_here = finish[...]
+    raised = dot(gated, output_weight[...], 0, 0)
+    block_out[0] = (residual + valid * (finish_here * raised + closed[0])).astype(bf16)
+    lifted = (finish_here * branch).astype(bf16)
+    delta_first = (
+        dot(delta_query, query_weight[...], 0, 1)
+        + dot(delta_key, key_weight[...], 0, 1)
+        + dot(delta_value, value_weight[...], 0, 1)
+        + dot(delta_gate, gate_weight[...], 0, 1)
+    )
+    second = delta_second[0]
+    incoming = delta_first * lifting_first[...] + second * lifting_second[...]
+    single_grad[0] = outgoing + normalize_back(incoming, normed, factor)
+
+    def collect(first):
+        def put(ref, value):
+            if first:
+                ref[...] = value
+            else:
+                ref[...] += value
+
+        put(finish_sum, branch * raised)
+        put(lift_first, delta_first * normed)
+        put(shift_first, delta_first)
+        put(query_sum, dot(delta_query, mixed[0], 1, 0))
+        put(key_sum, dot(delta_key, mixed[0], 1, 0))
+        put(value_sum, dot(delta_value, mixed[0], 1, 0))
+        put(gate_sum, dot(delta_gate, mixed[0], 1, 0))
+        put(output_sum, dot(gated, lifted, 1, 0))
+        put(bias_sum, jnp.sum(delta_query.astype(f32), axis=1, keepdims=True))
+
+    @pl.when(sample == 0)
+    def _():
+        collect(True)
+
+    @pl.when(sample > 0)
+    def _():
+        collect(False)
+
+    @pl.when(sample == pl.num_programs(0) - 1)
+    def _():
+        width = query_sum.shape[0]
+        half = width // 2
+        packs = (pack_mine, pack_other)
+        for i, array in enumerate((query_sum, key_sum, value_sum, gate_sum)):
+            for side in range(2):
+                core = meta[1] if side == 0 else 1 - meta[1]
+                row = pl.multiple_of(core * half, LANES)
+                packs[side][i * width : (i + 1) * width, :] = array[
+                    pl.ds(row, half), :
+                ].T.astype(bf16)
+        pack_columns(meta, packs, (output_sum,), 4 * width)
+
+
+def finish_block(meta, naturals, turned, flats, weights, pack_rows):
+    samples, rows, width = naturals[0].shape
+    natural, flat, square = by_sample((rows, width)), fixed((rows, width)), fixed((width, width))
+    pack = (pack_rows, width // 2)
+    return pl.pallas_call(
+        finish_kernel,
+        grid_spec=pltpu.PrefetchScalarGridSpec(
+            num_scalar_prefetch=1,
+            grid=(samples,),
+            in_specs=[natural] * 2
+            + [by_sample((rows, width), 1)] * 2
+            + [natural]
+            + [
+                by_sample((width // 2, array.shape[2]), 1 if array.dtype == f32 else 2)
+                for array in turned
+            ]
+            + [flat] * 3
+            + [square] * 5,
+            out_specs=[natural] * 2 + [flat] * 3 + [fixed(pack)] * 2 + [fixed((width, 1))],
+            scratch_shapes=[pltpu.VMEM((width, width), f32)] * 5,
+        ),
+        out_shape=[
+            jax.ShapeDtypeStruct((samples, rows, width), bf16),
+            jax.ShapeDtypeStruct((samples, rows, width), f32),
+        ]
+        + [jax.ShapeDtypeStruct((rows, width), f32)] * 3
+        + [jax.ShapeDtypeStruct(pack, bf16)] * 2
+        + [jax.ShapeDtypeStruct((width, 1), f32)],
+        compiler_params=pltpu.CompilerParams(vmem_limit_bytes=VMEM_LIMIT),
+        cost_estimate=pl.CostEstimate(
+            flops=20 * samples * rows * width * width,
+            bytes_accessed=samples * rows * width * 42 + 30 * width * width,
+            transcendentals=0,
+        ),
+    )(meta, *naturals, *turned, *flats, *weights)
+
+
 def swap_cores(array):
     return lax.ppermute(array, "qry", [(0, 1), (1, 0)])
+
+
+def exchange(array, axis, bit):
+    return lax.ppermute(array, axis, [(i, i ^ bit) for i in range(lax.axis_size(axis))])
+
+
+def pick(array, index):
+    return lax.dynamic_index_in_dim(array, index, 0, keepdims=False)
+
+
+def placed_by(pieces, place):
+    ordered = []
+    for j in range(len(pieces)):
+        chosen = pieces[j]
+        for shift in range(1, len(pieces)):
+            chosen = jnp.where(place == shift, pieces[j ^ shift], chosen)
+        ordered.append(chosen)
+    return ordered
+
+
+def filled(packs, start, arrays):
+    packs = list(packs)
+    for array in arrays:
+        for side, half in enumerate(halves(array)):
+            packs[side] = lax.dynamic_update_slice(packs[side], half.astype(bf16), (start, 0))
+        start += array.shape[0]
+    return packs
+
+
+def padded_rows(count):
+    return count + -count % 512
+
+
+def gated_by(values, meta):
+    return lax.optimization_barrier((values, meta))
+
+
+class SliceTotal:
+    def __init__(self, mine, other):
+        self.columns = mine.shape[1]
+        self.shape = (2, 2, 2, mine.shape[0] // 8, self.columns)
+        self.mine = mine.reshape(self.shape)
+        self.arrived = swap_cores(other).reshape(self.shape)
+        self.place, self.level = lax.axis_index("cplx"), lax.axis_index("smp")
+        self.levels = lax.axis_size("smp")
+        self.bits = (self.place % 2, self.place // 2)
+
+    def local(self, side, near_bit, far_bit):
+        at = (far_bit, near_bit) if side == 0 else (near_bit, far_bit)
+        pieces = [
+            pick(pick(array[side], at[0]), at[1]).astype(f32)
+            for array in (self.mine, self.arrived)
+        ]
+        return pieces[0] + pieces[1]
+
+    def first_sends(self):
+        return [
+            [
+                self.local(side, 1 - self.bits[side], far).astype(bf16)
+                for far in (self.bits[1 - side], 1 - self.bits[1 - side])
+            ]
+            for side in range(2)
+        ]
+
+    def first(self, sends):
+        self.kept = [
+            [exchange(piece, "cplx", 1 << side) for piece in sends[side]] for side in range(2)
+        ]
+
+    def second_sends(self):
+        return [
+            (
+                self.local(side, self.bits[side], 1 - self.bits[1 - side])
+                + self.kept[side][1].astype(f32)
+            ).astype(bf16)
+            for side in range(2)
+        ]
+
+    def second(self, sends):
+        passed = [exchange(sends[side], "cplx", 2 >> side) for side in range(2)]
+        sums = [
+            self.local(side, self.bits[side], self.bits[1 - side])
+            + self.kept[side][0].astype(f32)
+            + passed[side].astype(f32)
+            for side in range(2)
+        ]
+        self.quarter = jnp.concatenate(sums, axis=0).reshape(self.levels, -1, self.columns)
+
+    def third_sends(self):
+        return [
+            pick(self.quarter, self.level ^ shift).astype(bf16) for shift in range(1, self.levels)
+        ]
+
+    def third(self, sends):
+        own = pick(self.quarter, self.level)
+        for shift, piece in enumerate(sends):
+            own = own + exchange(piece, "smp", shift + 1).astype(f32)
+        self.own = own.astype(bf16)
+
+    def fourth(self):
+        pieces = [self.own] + [
+            exchange(self.own, "smp", shift) for shift in range(1, self.levels)
+        ]
+        quarter = jnp.concatenate(placed_by(pieces, self.level), axis=0)
+        self.quarter = quarter.reshape(2, -1, self.columns)
+
+    def fifth(self):
+        wholes = []
+        for side in range(2):
+            near, far = 1 << side, 2 >> side
+            piece = self.quarter[side]
+            at = [None] * 4
+            at[0], at[near], at[far] = piece, exchange(piece, "cplx", near), exchange(piece, "cplx", far)
+            at[3] = exchange(at[far], "cplx", near)
+            wholes += placed_by(at, self.place)
+        return jnp.concatenate(wholes, axis=0).astype(f32)
+
+
+def total_small(vector):
+    vector = vector[0] + swap_cores(vector[1])
+    for axis in ("cplx", "smp"):
+        arrived = [exchange(vector, axis, shift) for shift in range(1, lax.axis_size(axis))]
+        vector = sum(arrived, vector)
+    return vector
+
+
+def sum_samples(array):
+    narrow = array.astype(bf16)
+    arrived = [exchange(narrow, "smp", shift) for shift in range(1, lax.axis_size("smp"))]
+    return sum((piece.astype(f32) for piece in arrived), array)
 
 
 def halves(array):
@@ -287,21 +728,6 @@
     return mine, other
 
 
-def chip_sums(arrays, after=None):
-    kept = []
-    for array in arrays:
-        mine, other = halves(array)
-        arrived = swap_cores(other.astype(bf16))
-        kept.append((mine + arrived.astype(f32)).astype(bf16))
-    if after is not None:
-        kept, _ = lax.optimization_barrier((kept, after))
-    return lax.psum(tuple(kept), ("cplx", "smp"))
-
-
-def widened(arrays):
-    return tuple(array.astype(f32) for array in arrays)
-
-
 def gather_rows(piece):
     if piece.shape[1] % 16 == 0:
         return lax.all_gather(piece, "smp", axis=0)
@@ -312,52 +738,6 @@
     if whole.shape[0] == lax.axis_size("smp"):
         return lax.psum_scatter(whole, "smp", scatter_dimension=0)
     return lax.psum_scatter(whole[0], "smp", scatter_dimension=1, tiled=True)
-
-
-def normalize(values):
-    centre = values - jnp.mean(values, axis=-1, keepdims=True)
-    factor = lax.rsqrt(jnp.mean(centre * centre, axis=-1, keepdims=True) + EPSILON)
-    return (centre * factor, factor)
-
-
-def normalize_back(incoming, normed, factor):
-    return factor * (
-        incoming
-        - jnp.mean(incoming, axis=-1, keepdims=True)
-        - normed * jnp.mean(incoming * normed, axis=-1, keepdims=True)
-    )
-
-
-def matmul(left, right):
-    return jnp.dot(left, right, preferred_element_type=jnp.float32)
-
-
-def contract(form, left, right):
-    return jnp.einsum(form, left, right, preferred_element_type=jnp.float32)
-
-
-def exact_contract(form, left, right):
-    return jnp.einsum(form, left.astype(jnp.float32), right.astype(jnp.float32), precision=HIGHEST)
-
-
-def modulate(condition_norm, normed, gain, scale_weight, offset, shift_weight):
-    condition_low = (condition_norm * gain.astype(jnp.float32)).astype(jnp.bfloat16)
-    lifting = jax.nn.sigmoid(matmul(condition_low, scale_weight) + offset.astype(jnp.float32))
-    shifting = matmul(condition_low, shift_weight)
-    blended = (lifting[None] * normed + shifting[None]).astype(jnp.bfloat16)
-    return (condition_low, lifting, blended)
-
-
-def modulate_back(delta_blended, normed, condition_low, lifting, scale_weight, shift_weight):
-    delta_lift = jnp.sum(delta_blended * normed, axis=0) * lifting * (1.0 - lifting)
-    delta_shift = jnp.sum(delta_blended, axis=0)
-    scale_total = exact_contract("qc,qd->cd", condition_low, delta_lift)
-    offset_total = jnp.sum(delta_lift, axis=0)
-    shift_total = exact_contract("qc,qd->cd", condition_low, delta_shift)
-    delta_condition = exact_contract("qd,cd->qc", delta_lift, scale_weight) + exact_contract(
-        "qd,cd->qc", delta_shift, shift_weight
-    )
-    return (delta_blended * lifting[None], delta_condition, scale_total, offset_total, shift_total)
 
 
 def per_device(
@@ -390,169 +770,196 @@
     closing_weight,
     closing_offset,
 ):
-    row_count = single.shape[2]
-    model_width = single.shape[3]
-    head_count = pair_project.shape[1]
-    token_count = lengths[0]
-    row_ids = lax.axis_index("qry") * row_count + jnp.arange(row_count, dtype=jnp.int32)
-    row_mask = (row_ids < token_count).astype(jnp.float32)[:, None]
-    residual = single[0].astype(jnp.float32)
+    width = single.shape[3]
+    narrow = condition.shape[2]
+    half = width // 2
+    inner = transition_swish_weight.shape[1]
+    heads = pair_project.shape[1]
+    meta = jnp.stack([lengths[0], lax.axis_index("qry")]).astype(jnp.int32)
     condition_raw = condition[0]
-    normed, factor = normalize(residual)
-    condition_norm, condition_factor = normalize(condition_raw.astype(jnp.float32))
-    condition_first, lifting_first, mixed_first_result = modulate(
-        condition_norm, normed, first_gain, first_scale, first_offset, first_shift
-    )
-    condition_second, lifting_second, mixed_second_result = modulate(
-        condition_norm, normed, second_gain, second_scale, second_offset, second_shift
-    )
-    finish = jax.nn.sigmoid(
-        matmul(condition_raw, finish_weight) + finish_offset.astype(jnp.float32)
-    )
+    condition_norm, condition_factor = normalize(condition_raw.astype(f32))
     bias_pieces = pair_forward(pair_features[0], pair_gain, pair_project, PARTS)
     bias_rows = [gather_rows(piece) for piece in bias_pieces]
-    query_turned = (
-        contract("srd,de->ser", mixed_first_result, query_projection_weight)
-        + query_bias_vector.astype(jnp.float32)[:, None]
-    ).astype(jnp.bfloat16)
-    key_turned = contract("srd,de->ser", mixed_first_result, key_projection_weight).astype(
-        jnp.bfloat16
-    )
-    value_turned = contract("srd,de->ser", mixed_first_result, value_projection_weight).astype(
-        jnp.bfloat16
-    )
-    key_pair = (key_turned, swap_cores(key_turned))
-    value_pair = (value_turned, swap_cores(value_turned))
-    gate_turned = jax.nn.sigmoid(contract("srd,de->ser", mixed_first_result, attention_gate_weight))
-    outgoing = cotangent[0].astype(jnp.float32)
-    branch_grad = row_mask * outgoing
-    delta_lifted = (finish[None] * branch_grad).astype(jnp.bfloat16)
-    delta_gated_turned = contract("sre,de->sdr", delta_lifted, attention_output_weight)
-    raised_swish_part = matmul(mixed_second_result, transition_swish_weight)
-    raised_linear_part = matmul(mixed_second_result, transition_linear_weight)
-    swish_sigmoid = jax.nn.sigmoid(raised_swish_part)
-    hidden_state = (raised_swish_part * swish_sigmoid * raised_linear_part).astype(jnp.bfloat16)
-    shifted_state = matmul(hidden_state, transition_down_weight)
-    closing = jax.nn.sigmoid(
-        matmul(condition_raw, closing_weight) + closing_offset.astype(jnp.float32)
-    )
-    delta_moved = (closing[None] * branch_grad).astype(jnp.bfloat16)
-    delta_closing = jnp.sum(branch_grad * shifted_state, axis=0) * closing * (1.0 - closing)
-    closing_total = exact_contract("qc,qd->cd", condition_raw, delta_closing)
-    closingoffset_total = jnp.sum(delta_closing, axis=0)
-    delta_condition = exact_contract("qd,cd->qc", delta_closing, closing_weight)
-    down_total = contract("sqf,sqd->fd", hidden_state, delta_moved)
-    delta_hidden = contract("sqd,fd->sqf", delta_moved, transition_down_weight)
-    delta_swish = (
-        delta_hidden
-        * raised_linear_part
-        * swish_sigmoid
-        * (1.0 + raised_swish_part * (1.0 - swish_sigmoid))
-    ).astype(jnp.bfloat16)
-    delta_linear = (delta_hidden * raised_swish_part * swish_sigmoid).astype(jnp.bfloat16)
-    swish_total = contract("sqd,sqf->df", mixed_second_result, delta_swish)
-    linear_total = contract("sqd,sqf->df", mixed_second_result, delta_linear)
-    delta_second = contract("sqf,df->sqd", delta_swish, transition_swish_weight) + contract(
-        "sqf,df->sqd", delta_linear, transition_linear_weight
-    )
-    early = chip_sums((swish_total, linear_total, down_total, closing_total))
-    meta = jnp.stack([token_count, lax.axis_index("qry")]).astype(jnp.int32)
-    attended_parts = [
-        attention(
-            meta,
-            query_turned,
-            key_pair,
-            value_pair,
-            gate_turned,
-            delta_gated_turned,
-            bias_rows[part],
-            part,
-            PARTS,
+
+    def modulation(gain, scale_weight, offset, shift_weight):
+        low = (condition_norm * gain.astype(f32)).astype(bf16)
+        lifting = jax.nn.sigmoid(matmul(low, scale_weight) + offset.astype(f32))
+        return low, lifting, matmul(low, shift_weight)
+
+    condition_first, lifting_first, shifting_first = modulation(
+        first_gain, first_scale, first_offset, first_shift
+    )
+    condition_second, lifting_second, shifting_second = modulation(
+        second_gain, second_scale, second_offset, second_shift
+    )
+    finish = jax.nn.sigmoid(matmul(condition_raw, finish_weight) + finish_offset.astype(f32))
+    closing = jax.nn.sigmoid(matmul(condition_raw, closing_weight) + closing_offset.astype(f32))
+    square_weights = (
+        query_projection_weight,
+        key_projection_weight,
+        value_projection_weight,
+        attention_gate_weight,
+        attention_output_weight,
+    )
+    query, key, value, gate, delta_gated, mixed_first = project(
+        meta,
+        single[0],
+        cotangent[0],
+        lifting_first,
+        shifting_first,
+        finish,
+        query_bias_vector.astype(f32)[None],
+        square_weights,
+    )
+    key_pair = (key, swap_cores(key))
+    value_pair = (value, swap_cores(value))
+    closed, delta_second, closing_sum, lift_second, shift_second, *second_packs = transition(
+        meta,
+        single[0],
+        cotangent[0],
+        lifting_second,
+        shifting_second,
+        closing,
+        (transition_swish_weight, transition_linear_weight, transition_down_weight),
+        padded_rows(3 * inner + 3 * narrow),
+    )
+
+    def modulation_back(lift_sum, shift_sum, low, lifting, scale_weight, shift_weight):
+        delta_lift = lift_sum * lifting * (1.0 - lifting)
+        scale_total = contract("qc,qd->cd", low, delta_lift)
+        shift_total = contract("qc,qd->cd", low, shift_sum)
+        delta_condition = contract("qd,cd->qc", delta_lift, scale_weight) + contract(
+            "qd,cd->qc", shift_sum, shift_weight
         )
-        for part in range(PARTS)
-    ]
-    delta_bias = [scatter_rows(part[7]) for part in attended_parts]
-    gate_applied, delta_gating, delta_queries, dk_mine, dk_other, dv_mine, dv_other = [
-        jnp.concatenate([part[i] for part in attended_parts], axis=1) for i in range(7)
-    ]
-    delta_keys = (dk_mine + swap_cores(dk_other)).astype(jnp.bfloat16)
-    delta_values = (dv_mine + swap_cores(dv_other)).astype(jnp.bfloat16)
-    raised_state = contract("ser,ed->srd", gate_applied, attention_output_weight)
-    block_out = (
-        residual + row_mask * (finish[None] * raised_state + closing[None] * shifted_state)
-    ).astype(jnp.bfloat16)
-    delta_finish = jnp.sum(branch_grad * raised_state, axis=0) * finish * (1.0 - finish)
-    finish_total = exact_contract("qc,qd->cd", condition_raw, delta_finish)
-    finishoffset_total = jnp.sum(delta_finish, axis=0)
-    delta_condition = delta_condition + exact_contract("qd,cd->qc", delta_finish, finish_weight)
-    output_total = contract("ser,srd->ed", gate_applied, delta_lifted)
-    gating_total = contract("srd,ser->de", mixed_first_result, delta_gating)
-    query_total = contract("srd,ser->de", mixed_first_result, delta_queries)
-    querybias_total = jnp.sum(delta_queries.astype(jnp.float32), axis=(0, 2))
-    key_total = contract("srd,ser->de", mixed_first_result, delta_keys)
-    value_total = contract("srd,ser->de", mixed_first_result, delta_values)
-    middle = chip_sums(
-        (output_total, gating_total, finish_total, query_total, key_total, value_total),
-        early,
-    )
-    delta_first = (
-        contract("ser,de->srd", delta_queries, query_projection_weight)
-        + contract("ser,de->srd", delta_keys, key_projection_weight)
-        + contract("ser,de->srd", delta_values, value_projection_weight)
-        + contract("ser,de->srd", delta_gating, attention_gate_weight)
-    )
-    normed_first, cond_delta_first, scale_first, offset_first, shift_first = modulate_back(
-        delta_first, normed, condition_first, lifting_first, first_scale, first_shift
-    )
-    normed_second, cond_delta_second, scale_second, offset_second, shift_second = modulate_back(
-        delta_second, normed, condition_second, lifting_second, second_scale, second_shift
-    )
+        return scale_total, jnp.sum(delta_lift, axis=0), shift_total, delta_condition
+
+    def gate_back(branch_sum, opened, weight):
+        delta = branch_sum * opened * (1.0 - opened)
+        return (
+            contract("qc,qd->cd", condition_raw, delta),
+            jnp.sum(delta, axis=0),
+            contract("qd,cd->qc", delta, weight),
+        )
+
+    scale_second, offset_second, shift_total_second, cond_delta_second = modulation_back(
+        lift_second, shift_second, condition_second, lifting_second, second_scale, second_shift
+    )
+    closing_total, closing_offset_total, condition_closing = gate_back(
+        closing_sum, closing, closing_weight
+    )
+    early = SliceTotal(
+        *filled(second_packs, 3 * inner, (scale_second, shift_total_second, closing_total))
+    )
+
+    def attend(meta, part):
+        return attention(
+            meta, query, key_pair, value_pair, gate, delta_gated, bias_rows[part], part, PARTS
+        )
+
+    attended = [attend(meta, 0)]
+    sends, meta_next = gated_by(early.first_sends(), meta)
+    early.first(sends)
+    attended.append(attend(meta_next, 1))
+    sends, meta_next = gated_by(early.second_sends(), meta)
+    early.second(sends)
+    delta_bias = [scatter_rows(part[7]) for part in attended]
+    arrived_keys = [swap_cores(part[4]) for part in attended]
+    arrived_values = [swap_cores(part[6]) for part in attended]
+    turned = (
+        [part[0] for part in attended]
+        + [part[1] for part in attended]
+        + [part[2] for part in attended]
+        + [part[3] for part in attended]
+        + arrived_keys
+        + [part[5] for part in attended]
+        + arrived_values
+    )
+    block_out, single_grad, finish_sum, lift_first, shift_first, *first_packs, query_bias_total = (
+        finish_block(
+            meta_next,
+            (single[0], cotangent[0], closed, delta_second, mixed_first),
+            turned,
+            (lifting_first, lifting_second, finish),
+            square_weights,
+            padded_rows(5 * width + 3 * narrow),
+        )
+    )
+    scale_first, offset_first, shift_total_first, cond_delta_first = modulation_back(
+        lift_first, shift_first, condition_first, lifting_first, first_scale, first_shift
+    )
+    finish_total, finish_offset_total, condition_finish = gate_back(
+        finish_sum, finish, finish_weight
+    )
+    late = SliceTotal(
+        *filled(first_packs, 5 * width, (scale_first, shift_total_first, finish_total))
+    )
+    early.third(early.third_sends())
+    late.first(late.first_sends())
+    early.fourth()
+    late.second(late.second_sends())
+    early = early.fifth()
+    late.third(late.third_sends())
+    late.fourth()
+    late = late.fifth()
     gain_first = jnp.sum(cond_delta_first * condition_norm, axis=0)
     gain_second = jnp.sum(cond_delta_second * condition_norm, axis=0)
-    single_grad = outgoing + normalize_back(normed_first + normed_second, normed, factor)
-    condition_local = (
+    condition_grad = sum_samples(
         normalize_back(
-            cond_delta_first * first_gain.astype(jnp.float32)
-            + cond_delta_second * second_gain.astype(jnp.float32),
+            cond_delta_first * first_gain.astype(f32) + cond_delta_second * second_gain.astype(f32),
             condition_norm,
             condition_factor,
         )
-        + delta_condition
-    )
-    condition_grad = lax.psum(condition_local, "smp")
-    pair_grad, pairgain_total, project_total = pair_backward(
+        + condition_closing
+        + condition_finish
+    )
+    pair_grad, pair_gain_total, pair_project_total = pair_backward(
         pair_features[0], pair_gain, pair_project, delta_bias
     )
-    small = jnp.concatenate(
-        [
-            jnp.stack(halves(whole))
-            for whole in (
-                gain_first,
-                offset_first,
-                querybias_total,
-                pairgain_total[0],
-                finishoffset_total,
-                gain_second,
-                offset_second,
-                closingoffset_total,
+    vectors = (
+        gain_first,
+        offset_first,
+        query_bias_total[:, 0],
+        finish_offset_total,
+        gain_second,
+        offset_second,
+        closing_offset_total,
+        pair_gain_total[0],
+    )
+    small = total_small(
+        jnp.concatenate(
+            [jnp.stack(halves(vector)) for vector in vectors]
+            + [jnp.stack([half.reshape(-1) for half in halves(pair_project_total.T)])],
+            axis=1,
+        )
+    )
+    ends, place = [], 0
+    for vector in vectors:
+        ends.append(small[place : place + vector.shape[0] // 2])
+        place += vector.shape[0] // 2
+    def unpack(total, sizes):
+        arrays, start = [], 0
+        for depth, columns in sizes:
+            blocks = columns // half
+            arrays.append(
+                jnp.concatenate(
+                    [
+                        total[start + b * depth : start + (b + 1) * depth]
+                        for b in range(blocks)
+                    ],
+                    axis=1,
+                )
             )
-        ]
-        + [jnp.stack([half.reshape(-1) for half in halves(project_total.T)])],
-        axis=1,
-    )
-    late = chip_sums((scale_first, shift_first, scale_second, shift_second), middle)
-    vectors = lax.psum(
-        (small[0] + swap_cores(small[1])), ("cplx", "smp")
-    )
-    ends, place = [], 0
-    wide, narrow, pair_width = model_width // 2, condition_raw.shape[1] // 2, pair_gain.shape[0]
-    sizes = (narrow, wide, wide, pair_width // 2, wide, narrow, wide, wide)
-    for size in sizes + (pair_width * head_count // 2,):
-        ends.append(vectors[place : place + size])
-        place += size
-    swish_total, linear_total, down_total, closing_total = widened(early)
-    output_total, gating_total, finish_total, query_total, key_total, value_total = widened(middle)
-    scale_first, shift_first, scale_second, shift_second = widened(late)
+            start += depth * blocks
+        return arrays
+
+    swish_total, linear_total, down_total, scale_second, shift_second, closing_total = unpack(
+        early,
+        ((width, inner // 2), (width, inner // 2), (inner, half)) + ((narrow, half),) * 3,
+    )
+    query_total, key_total, value_total, gate_total, output_total, *others = unpack(
+        late, ((width, half),) * 5 + ((narrow, half),) * 3
+    )
+    scale_first, shift_first, finish_total = others
     return (
         block_out[None],
         single_grad[None],
@@ -566,21 +973,21 @@
         ends[2],
         key_total,
         value_total,
-        gating_total,
+        gate_total,
         output_total,
+        ends[7],
+        small[place:].reshape(-1, heads // 2),
+        finish_total,
         ends[3],
-        ends[8].reshape(-1, head_count // 2),
-        finish_total,
         ends[4],
+        scale_second,
         ends[5],
-        scale_second,
-        ends[6],
         shift_second,
         swish_total,
         linear_total,
         down_total,
         closing_total,
-        ends[7],
+        ends[6],
     )
 
 

time: 977 us -> 580 us (0.59)
  waiting for transfers between devices: 433 us -> 155 us
  matrix products: 151 us -> 18.3 us
  Pallas kernels: 143 us -> 258 us
  blocking collectives: 76.6 us -> 0 us
  starting transfers between devices: 6.89 us -> 62.3 us
  local copies, waits for them, and re-layouts: 77 us -> 31.6 us
  other arithmetic: 65.9 us -> 32.8 us
    psum x4 -> x0, waiting for transfers between devices: 301 us -> none  [the longest x3 281 us: chip_sums(): return lax.psum(tuple(kept), ('cplx', 'smp'))]
    ppermute x0 -> x45, waiting for transfers between devices: none -> 155 us  [exchange(): lax.ppermute(array, axis, [(i, i ^ bit) for i in range(lax.axis_size(axis...]
    reduce_scatter x2, waiting for transfers between devices: 122 us -> 0.01 us  [scatter_rows(): return lax.psum_scatter(whole, 'smp', scatter_dimension=0)]
    pallas_call x0 -> x3, Pallas kernels: none -> 116 us  [the longest x1 51.5 us: transition(): pl.pallas_call(transition_kernel, grid_spec=pltpu.PrefetchScalarGridSpec(...]
    dot_general x33 -> x12, matrix products: 120 us -> 9.53 us  [contract(): jnp.einsum(form, left.astype(bf16), right.astype(bf16), preferred_element...]
    psum x1 -> x0, blocking collectives: 76.6 us -> none  [per_device(): vectors = lax.psum(small[0] + swap_cores(small[1]), ('cplx', 'smp'))]
    ppermute x0 -> x45, starting transfers between devices: none -> 60.2 us  [exchange(): lax.ppermute(array, axis, [(i, i ^ bit) for i in range(lax.axis_size(axis...]
    convert_element_type x37 -> x16, other arithmetic: 50.3 us -> 8.8 us  [the longest x4 5.13 us: second_sends(): return [(self.local(side, self.bits[side], 1 - self.bits[1 - side]) + sel...]
  transfers between devices with their start and end apart: 27 -> 58, of which waited for: 7 -> 18; matrix products, arithmetic and copies ran while one was open for 23% -> 13% of each run, Pallas kernels for 15% -> 40%
where the time goes in v2:
time: 580 us; the launch traced here: 574 us
  Pallas kernels  258 us (44%)
  waiting for transfers between devices  155 us (27%)
  starting transfers between devices  62.3 us (11%)
  other arithmetic  32.8 us (6%)
  local copies, waits for them, and re-layouts  31.6 us (5%)
  matrix products  18.3 us (3%)
  between operations  15.8 us (3%)
    ppermute x45, waiting for transfers between devices, exchange(): lax.ppermute(array, axis, [(i, i ^ bit) for i in range(lax.axis_size(axis...  155 us
    pallas_call x2, Pallas kernels, attention(): pl.pallas_call(functools.partial(attention_kernel, step=step), grid_spec=...  72.5 us
    ppermute x45, starting transfers between devices, exchange(): lax.ppermute(array, axis, [(i, i ^ bit) for i in range(lax.axis_size(axis...  60.2 us
    pallas_call x1, Pallas kernels, transition(): pl.pallas_call(transition_kernel, grid_spec=pltpu.PrefetchScalarGridSpec(...  51.5 us
    pallas_call x1, Pallas kernels, finish_block(): pl.pallas_call(finish_kernel, grid_spec=pltpu.PrefetchScalarGridSpec(num_...  47.1 us
    pallas_call x1, Pallas kernels, pair_backward(): pl.pallas_call(functools.partial(pair_backward_kernel, block=block, heads...  40.6 us
    pallas_call x1, Pallas kernels, pair_forward(): pl.pallas_call(functools.partial(pair_forward_kernel, block=block, heads=...  29 us
    pallas_call x1, Pallas kernels, project(): pl.pallas_call(project_kernel, grid_spec=pltpu.PrefetchScalarGridSpec(num...  17.3 us
  transfers between devices with their start and end apart: 58, of which 18 were waited for; matrix products, arithmetic and copies ran while one was open for 13% of the time, Pallas kernels for 40%

profile of v2, /device:TPU:0, one launch (start us, length us, event | category | flops | bytes accessed | tf_op | source)
XLA Modules:
  0.0 574.1 jit_solution(9684178016784438598)
XLA Ops:
  7.3 1.5 copy.62.project
  8.7 29.0 %shard_map.477 = (bf16[8,80,640]{2,1,0:T(8,128)(2,1)}, bf16[8,80,640]{2,1,0:T(8,128)(2,1)}) custom-call(bf16[80,640,128]{2,1,0:T(8,128)(2,1)} %bitcast.171, bf16[1,128]{1,0:T(2,128)(2,1)} %bitcast.205, bf16[128,16]{1,0:T(8,128)(2,1)} %copy.62.project), custom_call_target="tpu_custom_call" | custom-call | flops 3355443200 | bytes 14745600 | tf_op jit(solution)/shard_map/pallas_call | solution.py:204
  40.1 1.5 fusion.3.finish
  41.6 1.4 fusion.101.shifting
  43.0 1.5 fusion.7.lifting.lifting_first
  44.6 17.3 %shard_map.476 = (bf16[4,768,320]{2,1,0:T(8,128)(2,1)}, bf16[4,768,384]{2,1,0:T(8,128)(2,1)}, bf16[4,768,384]{2,1,0:T(8,128)(2,1)}, f32[4,768,320]{2,1,0:T(8,128...) custom-call(s32[2]{0:T(128)} %pad_add_fusion.meta, bf16[4,320,768]{2,1,0:T(8,128)(2,1)} %bitcast.209, ...), custom_call_target="tpu_custom_call" | custom-call | flops 12079595520 | bytes 25559040 | tf_op jit(solution)/shard_map/pallas_call | solution.py:362
  62.6 1.4 fusion.107.shifting
  64.0 1.5 fusion.15.lifting.lifting_second
  65.5 1.5 fusion.11.closing
  67.0 51.5 %shard_map.475 = (f32[4,320,768]{2,1,0:T(8,128)}, f32[4,320,768]{2,1,0:T(8,128)}, f32[320,768]{1,0:T(8,128)}, f32[320,768]{1,0:T(8,128)}, f32[320,768]{1,0:T(8,1...) custom-call(s32[2]{0:T(128)} %pad_add_fusion.meta, bf16[4,320,768]{2,1,0:T(8,128)(2,1)} %bitcast.210, ...), custom_call_target="tpu_custom_call" | custom-call | flops 27179089920 | bytes 33030144 | tf_op jit(solution)/shard_map/pallas_call | solution.py:447
  118.5 1.8 fusion.54
  125.4 36.2 %shard_map.478 = (bf16[4,384,320]{2,1,0:T(8,128)(2,1)}, bf16[4,384,320]{2,1,0:T(8,128)(2,1)}, bf16[4,384,320]{2,1,0:T(8,128)(2,1)}, f32[4,384,320]{2,1,0:T(8,128...) custom-call(s32[2]{0:T(128)} %pad_add_fusion.meta, ...), custom_call_target="tpu_custom_call" | custom-call | flops 20132659200 | bytes 23265280 | tf_op jit(solution)/shard_map/pallas_call | solution.py:149
  161.7 2.9 fusion.113
  164.6 3.7 fusion.114
  168.3 1.5 fusion.25
  171.2 2.8 collective-permute-start.1
  175.3 1.5 collective-permute-start.2
  176.9 2.7 convolution_add_fusion.6
  180.8 7.6 %collective-permute-done.1 = bf16[768,384]{1,0:T(8,128)(2,1)} collective-permute-done((bf16[768,384]{1,0:T(8,128)(2,1)}, bf16[768,384]{1,0:T(8,128)(2,1)}, u32[]{:S(2)}, u32[]{:S(2)}) %collective-permute-start.1) | collective-permute-done | bytes 589856 | tf_op jit(solution)/shard_map/ppermute | solution.py:594
  188.4 2.5 fusion.19
  191.8 2.3 fusion.18
  194.0 1.5 collective-permute-start.39
  196.7 36.3 %shard_map.479 = (bf16[4,384,320]{2,1,0:T(8,128)(2,1)}, bf16[4,384,320]{2,1,0:T(8,128)(2,1)}, bf16[4,384,320]{2,1,0:T(8,128)(2,1)}, f32[4,384,320]{2,1,0:T(8,128...) custom-call(s32[2]{0:T(128)} %pad_add_fusion.meta, ...), custom_call_target="tpu_custom_call" | custom-call | flops 20132659200 | bytes 23265280 | tf_op jit(solution)/shard_map/pallas_call | solution.py:149
  233.7 1.9 fusion.17
  235.5 1.7 fusion.16
  237.5 1.6 collective-permute-start.42
  239.1 2.5 collective-permute-start.44
  241.8 47.1 %shard_map.480 = (bf16[4,320,768]{2,1,0:T(8,128)(2,1)}, f32[4,320,768]{2,1,0:T(8,128)}, f32[320,768]{1,0:T(8,128)}, f32[320,768]{1,0:T(8,128)}, f32[320,768]{1,0...) custom-call(s32[2]{0:T(128)} %pad_add_fusion.meta, ...), custom_call_target="tpu_custom_call" | custom-call | flops 15099494400 | bytes 58982400 | tf_op jit(solution)/shard_map/pallas_call | solution.py:556
  288.9 1.5 fusion.58
  297.4 1.9 collective-permute-start.47
  299.3 1.8 collective-permute-start.46
  302.3 3.1 collective-permute-start.11
  305.5 20.7 %collective-permute-done.47 = bf16[384,384]{1,0:T(8,128)(2,1)S(1)} collective-permute-done((bf16[384,384]{1,0:T(8,128)(2,1)S(1)}, bf16[384,384]{1,0:T(8,128)(2,1)S(1)}, u32[]{:S(2)}, u32[]{:S(2)}) %collective-permute-start.47) | collective-permute-done | bytes 294944 | tf_op jit(solution)/shard_map/ppermute | solution.py:594
  326.2 18.1 %collective-permute-done.46 = bf16[384,384]{1,0:T(8,128)(2,1)S(1)} collective-permute-done((bf16[384,384]{1,0:T(8,128)(2,1)S(1)}, bf16[384,384]{1,0:T(8,128)(2,1)S(1)}, u32[]{:S(2)}, u32[]{:S(2)}) %collective-permute-start.46) | collective-permute-done | bytes 294944 | tf_op jit(solution)/shard_map/ppermute | solution.py:594
  347.8 19.2 %collective-permute-done.10 = bf16[320,384]{1,0:T(8,128)(2,1)S(1)} collective-permute-done((bf16[320,384]{1,0:T(8,128)(2,1)S(1)}, bf16[320,384]{1,0:T(8,128)(2,1)S(1)}, u32[]{:S(2)}, u32[]{:S(2)}) %collective-permute-start.10) | collective-permute-done | bytes 245792 | tf_op jit(solution)/shard_map/ppermute | solution.py:594
  370.8 12.4 %collective-permute-done.51 = bf16[768,384]{1,0:T(8,128)(2,1)S(1)} collective-permute-done((bf16[768,384]{1,0:T(8,128)(2,1)S(1)}, bf16[768,384]{1,0:T(8,128)(2,1)S(1)}, u32[]{:S(2)}, u32[]{:S(2)}) %collective-permute-start.51) | collective-permute-done | bytes 589856 | tf_op jit(solution)/shard_map/ppermute | solution.py:594
  383.7 11.2 %collective-permute-done.49 = bf16[768,384]{1,0:T(8,128)(2,1)S(1)} collective-permute-done((bf16[768,384]{1,0:T(8,128)(2,1)S(1)}, bf16[768,384]{1,0:T(8,128)(2,1)S(1)}, u32[]{:S(2)}, u32[]{:S(2)}) %collective-permute-start.49) | collective-permute-done | bytes 589856 | tf_op jit(solution)/shard_map/ppermute | solution.py:594
  401.6 1.7 collective-permute-start.23
  404.3 9.0 %collective-permute-done.24 = bf16[640,384]{1,0:T(8,128)(2,1)S(1)} collective-permute-done((bf16[640,384]{1,0:T(8,128)(2,1)S(1)}, bf16[640,384]{1,0:T(8,128)(2,1)S(1)}, u32[]{:S(2)}, u32[]{:S(2)}) %collective-permute-start.24) | collective-permute-done | bytes 491552 | tf_op jit(solution)/shard_map/ppermute | solution.py:594
  414.7 1.5 collective-permute-start.22
  416.2 1.7 fusion.112
  417.9 5.8 %collective-permute-done.23 = bf16[640,384]{1,0:T(8,128)(2,1)S(1)} collective-permute-done((bf16[640,384]{1,0:T(8,128)(2,1)S(1)}, bf16[640,384]{1,0:T(8,128)(2,1)S(1)}, u32[]{:S(2)}, u32[]{:S(2)}) %collective-permute-start.23) | collective-permute-done | bytes 491552 | tf_op jit(solution)/shard_map/ppermute | solution.py:594
  423.8 8.7 %collective-permute-done.25 = bf16[640,384]{1,0:T(8,128)(2,1)S(1)} collective-permute-done((bf16[640,384]{1,0:T(8,128)(2,1)S(1)}, bf16[640,384]{1,0:T(8,128)(2,1)S(1)}, u32[]{:S(2)}, u32[]{:S(2)}) %collective-permute-start.25) | collective-permute-done | bytes 491552 | tf_op jit(solution)/shard_map/ppermute | solution.py:594
  433.2 7.6 %collective-permute-start.26 = (bf16[320,384]{1,0:T(8,128)(2,1)S(1)}, bf16[320,384]{1,0:T(8,128)(2,1)S(1)}, u32[]{:S(2)}, u32[]{:S(2)}) collective-permute-start(bf16[320,384]{1,0:T(8,128)(2,1)S(1)} %get-tuple-element.224), channel_id=1, source_target_pairs={{0,2},{2,0},{4,6},{6,4},{1,3},{3,1},{5,7},{7,5},{8,10},{10,8},{12,... | collective-permute-start | bytes 737288 | tf_op jit(solution)/shard_map/ppermute | solution.py:594
  440.9 1.9 collective-permute-start.28
  444.3 4.5 collective-permute-done.26
  448.8 5.1 collective-permute-done.28
  454.0 7.9 %collective-permute-done.27 = bf16[320,384]{1,0:T(8,128)(2,1)S(1)} collective-permute-done((bf16[320,384]{1,0:T(8,128)(2,1)S(1)}, bf16[320,384]{1,0:T(8,128)(2,1)S(1)}, u32[]{:S(2)}, u32[]{:S(2)}) %collective-permute-start.27) | collective-permute-done | bytes 245792 | tf_op jit(solution)/shard_map/ppermute | solution.py:594
  462.1 2.7 collective-permute-start.30
  464.8 1.7 collective-permute-start.29
  466.4 40.6 %shard_map.481 = (f32[80,640,128]{2,1,0:T(8,128)}, f32[1,128]{1,0:T(1,128)}, f32[16,128]{1,0:T(8,128)}) custom-call(bf16[80,640,128]{2,1,0:T(8,128)(2,1)} %bitcast.172, bf16[1,128]{1,0:T(2,128)(2,1)} %bitcast.206, bf16[128,16]{1,0:T(8,128)(2,1)} %copy.62.project, bf16[8,80,640]{2,1,0:T(8,128)(2,1)} %bitcast.215, bf16[8,80,640]{2,1,0:T(8,128)(2,1)} %bitcast.216), custom_call_target="tpu_custom_call" | custom-call | flops 6710886400 | bytes 40960000 | tf_op jit(solution)/shard_map/pallas_call | solution.py:274
  509.3 3.0 pad_maximum_fusion.2
  512.3 1.8 collective-permute-start.15
  515.9 1.4 select_select_fusion.5
  519.4 1.6 pad_maximum_fusion.1
  521.0 1.6 slice.227
  522.5 2.3 collective-permute-start.18
  524.9 2.1 collective-permute-start.16
  530.6 1.5 collective-permute-done.32
  533.9 1.4 slice.181
  535.3 1.5 copy.66
  538.1 13.8 %collective-permute-done.35 = bf16[640,384]{1,0:T(8,128)(2,1)S(1)} collective-permute-done((bf16[640,384]{1,0:T(8,128)(2,1)}, bf16[640,384]{1,0:T(8,128)(2,1)S(1)}, u32[]{:S(2)}, u32[]{:S(2)}) %collective-permute-start.35) | collective-permute-done | bytes 491552 | tf_op jit(solution)/shard_map/ppermute | solution.py:594
  552.6 7.4 %collective-permute-done.33 = bf16[640,384]{1,0:T(8,128)(2,1)} collective-permute-done((bf16[640,384]{1,0:T(8,128)(2,1)S(1)}, bf16[640,384]{1,0:T(8,128)(2,1)}, u32[]{:S(2)}, u32[]{:S(2)}) %collective-permute-start.33) | collective-permute-done | bytes 491552 | tf_op jit(solution)/shard_map/ppermute | solution.py:594
  564.7 2.6 fusion.116
  (281 shorter events, 60.1 us)
Async XLA Ops:
  7.2 32.9 %copy-start = (bf16[384,768]{1,0:T(8,128)(2,1)S(1)}, bf16[384,768]{1,0:T(8,128)(2,1)}, u32[]{:S(2)}) copy-start(bf16[384,768]{1,0:T(8,128)(2,1)} %param.45) | copy-start | bytes 1769476
  7.2 118.2 %all-gather.5.cloned.1.call-start = ((), (), s32[]{:S(2)}) async-start(), calls=%async_computation.4 | async-start | bytes 4096000 | tf_op jit(solution)/shard_map/all_gather | solution.py:733
  37.8 158.9 %all-gather.7.cloned.1.call-start = ((), (), s32[]{:S(2)}) async-start(), calls=%async_computation.5 | async-start | bytes 4096000 | tf_op jit(solution)/shard_map/all_gather | solution.py:733
  61.8 63.5 %collective-permute-start.3 = (bf16[4,768,384]{2,1,0:T(8,128)(2,1)}, bf16[4,768,384]{2,1,0:T(8,128)(2,1)}, u32[]{:S(2)}, u32[]{:S(2)}) collective-permute-start(bf16[4,768,384]{2,1,0:T(8,128)(2,1)} %get-tuple-element.89.key_mine), channel_id=1, source_target_pairs={{0,1},{1,0},{2,3},{3,2},{4,5},{5,4},{6,7},{7,6},{8,9},{9,8},{10,11... | collective-permute-start | bytes 7077896 | tf_op jit(solution)/shard_map/ppermute | solution.py:590
  62.4 63.0 %collective-permute-start.4 = (bf16[4,768,384]{2,1,0:T(8,128)(2,1)}, bf16[4,768,384]{2,1,0:T(8,128)(2,1)}, u32[]{:S(2)}, u32[]{:S(2)}) collective-permute-start(bf16[4,768,384]{2,1,0:T(8,128)(2,1)} %get-tuple-element.90.value_mine), channel_id=1, source_target_pairs={{0,1},{1,0},{2,3},{3,2},{4,5},{5,4},{6,7},{7,6},{8,9},{9,8},{10,11... | collective-permute-start | bytes 7077896 | tf_op jit(solution)/shard_map/ppermute | solution.py:590
  62.5 404.0 %reduce-scatter.3.cloned.1.call-start = ((), (), s32[]{:S(2)}) async-start(), calls=%async_computation.2 | async-start | bytes 4096000 | tf_op jit(solution)/shard_map/reduce_scatter | solution.py:739
  67.0 51.5 %copy-start.18 = (f32[320,768]{1,0:T(8,128)S(1)}, f32[320,768]{1,0:T(8,128)}, u32[]{:S(2)}) copy-start(f32[320,768]{1,0:T(8,128)} %fusion.15.lifting.lifting_second) | copy-start | bytes 2949124
  67.0 51.5 %copy-start.19 = (f32[320,768]{1,0:T(8,128)S(1)}, f32[320,768]{1,0:T(8,128)}, u32[]{:S(2)}) copy-start(f32[320,768]{1,0:T(8,128)} %fusion.11.closing) | copy-start | bytes 2949124
  124.9 39.7 %collective-permute-start = (bf16[6144,384]{1,0:T(8,128)(2,1)}, bf16[6144,384]{1,0:T(8,128)(2,1)}, u32[]{:S(2)}, u32[]{:S(2)}) collective-permute-start(bf16[6144,384]{1,0:T(8,128)(2,1)} %get-tuple-element.250), channel_id=1, source_target_pairs={{0,1},{1,0},{2,3},{3,2},{4,5},{5,4},{6,7},{7,6},{8,9},{9,8},{10,11... | collective-permute-start | bytes 14155784 | tf_op jit(solution)/shard_map/ppermute | solution.py:590
  161.6 304.8 %reduce-scatter.5.cloned.1.call-start = ((), (), s32[]{:S(2)}) async-start(), calls=%async_computation.3 | async-start | bytes 4096000 | tf_op jit(solution)/shard_map/reduce_scatter | solution.py:739
  171.2 17.2 %collective-permute-start.1 = (bf16[768,384]{1,0:T(8,128)(2,1)}, bf16[768,384]{1,0:T(8,128)(2,1)}, u32[]{:S(2)}, u32[]{:S(2)}) collective-permute-start(bf16[768,384]{1,0:T(8,128)(2,1)} %get-tuple-element.82), channel_id=1, source_target_pairs={{0,8},{8,0},{16,24},{24,16},{1,9},{9,1},{17,25},{25,17},{2,10},{10... | collective-permute-start | bytes 1769480 | tf_op jit(solution)/shard_map/ppermute | solution.py:594
  175.3 16.5 %collective-permute-start.2 = (bf16[768,384]{1,0:T(8,128)(2,1)}, bf16[768,384]{1,0:T(8,128)(2,1)}, u32[]{:S(2)}, u32[]{:S(2)}) collective-permute-start(bf16[768,384]{1,0:T(8,128)(2,1)} %get-tuple-element.83), channel_id=1, source_target_pairs={{0,16},{8,24},{16,0},{24,8},{1,17},{9,25},{17,1},{25,9},{2,18},{10... | collective-permute-start | bytes 1769480 | tf_op jit(solution)/shard_map/ppermute | solution.py:594
  179.6 53.3 %collective-permute-start.38 = (bf16[768,384]{1,0:T(8,128)(2,1)}, bf16[768,384]{1,0:T(8,128)(2,1)}, u32[]{:S(2)}, u32[]{:S(2)}) collective-permute-start(bf16[768,384]{1,0:T(8,128)(2,1)} %get-tuple-element.123), channel_id=1, source_target_pairs={{0,8},{8,0},{16,24},{24,16},{1,9},{9,1},{17,25},{25,17},{2,10},{10... | collective-permute-start | bytes 1769480 | tf_op jit(solution)/shard_map/ppermute | solution.py:594
  180.3 52.7 %collective-permute-start.40 = (bf16[768,384]{1,0:T(8,128)(2,1)}, bf16[768,384]{1,0:T(8,128)(2,1)}, u32[]{:S(2)}, u32[]{:S(2)}) collective-permute-start(bf16[768,384]{1,0:T(8,128)(2,1)} %get-tuple-element.125), channel_id=1, source_target_pairs={{0,16},{8,24},{16,0},{24,8},{1,17},{9,25},{17,1},{25,9},{2,18},{10... | collective-permute-start | bytes 1769480 | tf_op jit(solution)/shard_map/ppermute | solution.py:594
  180.8 58.3 %collective-permute-start.5 = (bf16[4,384,384]{2,1,0:T(8,128)(2,1)}, bf16[4,384,384]{2,1,0:T(8,128)(2,1)}, u32[]{:S(2)}, u32[]{:S(2)}) collective-permute-start(bf16[4,384,384]{2,1,0:T(8,128)(2,1)} %get-tuple-element.104), channel_id=1, source_target_pairs={{0,1},{1,0},{2,3},{3,2},{4,5},{5,4},{6,7},{7,6},{8,9},{9,8},{10,11... | collective-permute-start | bytes 3538952 | tf_op jit(solution)/shard_map/ppermute | solution.py:590
  194.0 39.5 %collective-permute-start.39 = (bf16[768,384]{1,0:T(8,128)(2,1)}, bf16[768,384]{1,0:T(8,128)(2,1)}, u32[]{:S(2)}, u32[]{:S(2)}) collective-permute-start(bf16[768,384]{1,0:T(8,128)(2,1)} %fusion.19), channel_id=1, source_target_pairs={{0,16},{8,24},{16,0},{24,8},{1,17},{9,25},{17,1},{25,9},{2,18},{10... | collective-permute-start | bytes 1769480 | tf_op jit(solution)/shard_map/ppermute | solution.py:594
  195.5 40.0 %collective-permute-start.41 = (bf16[768,384]{1,0:T(8,128)(2,1)}, bf16[768,384]{1,0:T(8,128)(2,1)}, u32[]{:S(2)}, u32[]{:S(2)}) collective-permute-start(bf16[768,384]{1,0:T(8,128)(2,1)} %fusion.18), channel_id=1, source_target_pairs={{0,8},{8,0},{16,24},{24,16},{1,9},{9,1},{17,25},{25,17},{2,10},{10... | collective-permute-start | bytes 1769480 | tf_op jit(solution)/shard_map/ppermute | solution.py:594
  232.9 8.6 %collective-permute-start.7 = (bf16[4,384,384]{2,1,0:T(8,128)(2,1)}, bf16[4,384,384]{2,1,0:T(8,128)(2,1)}, u32[]{:S(2)}, u32[]{:S(2)}) collective-permute-start(bf16[4,384,384]{2,1,0:T(8,128)(2,1)} %get-tuple-element.108), channel_id=1, source_target_pairs={{0,1},{1,0},{2,3},{3,2},{4,5},{5,4},{6,7},{7,6},{8,9},{9,8},{10,11... | collective-permute-start | bytes 3538952 | tf_op jit(solution)/shard_map/ppermute | solution.py:590
  233.0 8.7 %collective-permute-start.6 = (bf16[4,384,384]{2,1,0:T(8,128)(2,1)}, bf16[4,384,384]{2,1,0:T(8,128)(2,1)}, u32[]{:S(2)}, u32[]{:S(2)}) collective-permute-start(bf16[4,384,384]{2,1,0:T(8,128)(2,1)} %get-tuple-element.105), channel_id=1, source_target_pairs={{0,1},{1,0},{2,3},{3,2},{4,5},{5,4},{6,7},{7,6},{8,9},{9,8},{10,11... | collective-permute-start | bytes 3538952 | tf_op jit(solution)/shard_map/ppermute | solution.py:590
  233.5 8.2 %collective-permute-start.8 = (bf16[4,384,384]{2,1,0:T(8,128)(2,1)}, bf16[4,384,384]{2,1,0:T(8,128)(2,1)}, u32[]{:S(2)}, u32[]{:S(2)}) collective-permute-start(bf16[4,384,384]{2,1,0:T(8,128)(2,1)} %get-tuple-element.109), channel_id=1, source_target_pairs={{0,1},{1,0},{2,3},{3,2},{4,5},{5,4},{6,7},{7,6},{8,9},{9,8},{10,11... | collective-permute-start | bytes 3538952 | tf_op jit(solution)/shard_map/ppermute | solution.py:590
  237.5 59.7 %collective-permute-start.42 = (bf16[384,384]{1,0:T(8,128)(2,1)S(1)}, bf16[384,384]{1,0:T(8,128)(2,1)S(1)}, u32[]{:S(2)}, u32[]{:S(2)}) collective-permute-start(bf16[384,384]{1,0:T(8,128)(2,1)S(1)} %get-tuple-element.221), channel_id=1, source_target_pairs={{0,2},{2,0},{4,6},{6,4},{1,3},{3,1},{5,7},{7,5},{8,10},{10,8},{12,... | collective-permute-start | bytes 884744 | tf_op jit(solution)/shard_map/ppermute | solution.py:594
  239.1 58.1 %collective-permute-start.44 = (bf16[384,384]{1,0:T(8,128)(2,1)S(1)}, bf16[384,384]{1,0:T(8,128)(2,1)S(1)}, u32[]{:S(2)}, u32[]{:S(2)}) collective-permute-start(bf16[384,384]{1,0:T(8,128)(2,1)S(1)} %get-tuple-element.222), channel_id=1, source_target_pairs={{0,6},{2,4},{4,2},{6,0},{1,7},{3,5},{5,3},{7,1},{8,14},{10,12},{12... | collective-permute-start | bytes 884744 | tf_op jit(solution)/shard_map/ppermute | solution.py:594
  241.6 55.7 %collective-permute-start.43 = (bf16[384,384]{1,0:T(8,128)(2,1)S(1)}, bf16[384,384]{1,0:T(8,128)(2,1)S(1)}, u32[]{:S(2)}, u32[]{:S(2)}) collective-permute-start(bf16[384,384]{1,0:T(8,128)(2,1)S(1)} %get-tuple-element.223), channel_id=1, source_target_pairs={{0,4},{2,6},{4,0},{6,2},{1,5},{3,7},{5,1},{7,3},{8,12},{10,14},{12... | collective-permute-start | bytes 884744 | tf_op jit(solution)/shard_map/ppermute | solution.py:594
  241.8 47.1 %copy-start.21 = (f32[320,768]{1,0:T(8,128)S(1)}, f32[320,768]{1,0:T(8,128)}, u32[]{:S(2)}) copy-start(f32[320,768]{1,0:T(8,128)} %fusion.7.lifting.lifting_first) | copy-start | bytes 2949124
  295.9 102.4 %collective-permute-start.19 = (bf16[5120,384]{1,0:T(8,128)(2,1)S(1)}, bf16[5120,384]{1,0:T(8,128)(2,1)S(1)}, u32[]{:S(2)}, u32[]{:S(2)}) collective-permute-start(bf16[5120,384]{1,0:T(8,128)(2,1)S(1)} %get-tuple-element.244), channel_id=1, source_target_pairs={{0,1},{1,0},{2,3},{3,2},{4,5},{5,4},{6,7},{7,6},{8,9},{9,8},{10,11... | collective-permute-start | bytes 11796488 | tf_op jit(solution)/shard_map/ppermute | solution.py:590
  297.4 28.8 %collective-permute-start.47 = (bf16[384,384]{1,0:T(8,128)(2,1)S(1)}, bf16[384,384]{1,0:T(8,128)(2,1)S(1)}, u32[]{:S(2)}, u32[]{:S(2)}) collective-permute-start(bf16[384,384]{1,0:T(8,128)(2,1)S(1)} %fusion.30), channel_id=1, source_target_pairs={{0,2},{2,0},{4,6},{6,4},{1,3},{3,1},{5,7},{7,5},{8,10},{10,8},{12,... | collective-permute-start | bytes 884744 | tf_op jit(solution)/shard_map/ppermute | solution.py:594
  299.3 45.0 %collective-permute-start.46 = (bf16[384,384]{1,0:T(8,128)(2,1)S(1)}, bf16[384,384]{1,0:T(8,128)(2,1)S(1)}, u32[]{:S(2)}, u32[]{:S(2)}) collective-permute-start(bf16[384,384]{1,0:T(8,128)(2,1)S(1)} %fusion.30), channel_id=1, source_target_pairs={{0,4},{2,6},{4,0},{6,2},{1,5},{3,7},{5,1},{7,3},{8,12},{10,14},{12... | collective-permute-start | bytes 884744 | tf_op jit(solution)/shard_map/ppermute | solution.py:594
  301.0 44.6 %collective-permute-start.45 = (bf16[384,384]{1,0:T(8,128)(2,1)S(1)}, bf16[384,384]{1,0:T(8,128)(2,1)S(1)}, u32[]{:S(2)}, u32[]{:S(2)}) collective-permute-start(bf16[384,384]{1,0:T(8,128)(2,1)S(1)} %fusion.30), channel_id=1, source_target_pairs={{0,6},{2,4},{4,2},{6,0},{1,7},{3,5},{5,3},{7,1},{8,14},{10,12},{12... | collective-permute-start | bytes 884744 | tf_op jit(solution)/shard_map/ppermute | solution.py:594
  302.3 44.6 %collective-permute-start.11 = (bf16[320,384]{1,0:T(8,128)(2,1)S(1)}, bf16[320,384]{1,0:T(8,128)(2,1)S(1)}, u32[]{:S(2)}, u32[]{:S(2)}) collective-permute-start(bf16[320,384]{1,0:T(8,128)(2,1)S(1)} %get-tuple-element.278), channel_id=1, source_target_pairs={{0,6},{2,4},{4,2},{6,0},{1,7},{3,5},{5,3},{7,1},{8,14},{10,12},{12... | collective-permute-start | bytes 737288 | tf_op jit(solution)/shard_map/ppermute | solution.py:594
  305.5 63.6 %copy-start.29 = (f32[768,1]{1,0:T(8,128)S(1)}, f32[768,1]{1,0:T(8,128)}, u32[]{:S(2)}) copy-start(f32[768,1]{1,0:T(8,128)} %get-tuple-element.118) | copy-start | bytes 9220
  326.2 40.8 %collective-permute-start.10 = (bf16[320,384]{1,0:T(8,128)(2,1)S(1)}, bf16[320,384]{1,0:T(8,128)(2,1)S(1)}, u32[]{:S(2)}, u32[]{:S(2)}) collective-permute-start(bf16[320,384]{1,0:T(8,128)(2,1)S(1)} %get-tuple-element.278), channel_id=1, source_target_pairs={{0,4},{2,6},{4,0},{6,2},{1,5},{3,7},{5,1},{7,3},{8,12},{10,14},{12... | collective-permute-start | bytes 737288 | tf_op jit(solution)/shard_map/ppermute | solution.py:594
  344.3 25.0 %collective-permute-start.9 = (bf16[320,384]{1,0:T(8,128)(2,1)S(1)}, bf16[320,384]{1,0:T(8,128)(2,1)S(1)}, u32[]{:S(2)}, u32[]{:S(2)}) collective-permute-start(bf16[320,384]{1,0:T(8,128)(2,1)S(1)} %get-tuple-element.278), channel_id=1, source_target_pairs={{0,2},{2,0},{4,6},{6,4},{1,3},{3,1},{5,7},{7,5},{8,10},{10,8},{12,... | collective-permute-start | bytes 737288 | tf_op jit(solution)/shard_map/ppermute | solution.py:594
  345.9 22.1 %collective-permute-start.48 = (bf16[768,384]{1,0:T(8,128)(2,1)S(1)}, bf16[768,384]{1,0:T(8,128)(2,1)S(1)}, u32[]{:S(2)}, u32[]{:S(2)}) collective-permute-start(bf16[768,384]{1,0:T(8,128)(2,1)S(1)} %pad_maximum_fusion.4), channel_id=1, source_target_pairs={{0,16},{8,24},{16,0},{24,8},{1,17},{9,25},{17,1},{25,9},{2,18},{10... | collective-permute-start | bytes 1769480 | tf_op jit(solution)/shard_map/ppermute | solution.py:594
  346.9 36.8 %collective-permute-start.50 = (bf16[768,384]{1,0:T(8,128)(2,1)S(1)}, bf16[768,384]{1,0:T(8,128)(2,1)S(1)}, u32[]{:S(2)}, u32[]{:S(2)}) collective-permute-start(bf16[768,384]{1,0:T(8,128)(2,1)S(1)} %pad_maximum_fusion.4), channel_id=1, source_target_pairs={{0,8},{8,0},{16,24},{24,16},{1,9},{9,1},{17,25},{25,17},{2,10},{10... | collective-permute-start | bytes 1769480 | tf_op jit(solution)/shard_map/ppermute | solution.py:594
  367.0 16.2 %collective-permute-start.51 = (bf16[768,384]{1,0:T(8,128)(2,1)S(1)}, bf16[768,384]{1,0:T(8,128)(2,1)S(1)}, u32[]{:S(2)}, u32[]{:S(2)}) collective-permute-start(bf16[768,384]{1,0:T(8,128)(2,1)S(1)} %pad_maximum_fusion.5), channel_id=1, source_target_pairs={{0,8},{8,0},{16,24},{24,16},{1,9},{9,1},{17,25},{25,17},{2,10},{10... | collective-permute-start | bytes 1769480 | tf_op jit(solution)/shard_map/ppermute | solution.py:594
  367.9 26.9 %collective-permute-start.49 = (bf16[768,384]{1,0:T(8,128)(2,1)S(1)}, bf16[768,384]{1,0:T(8,128)(2,1)S(1)}, u32[]{:S(2)}, u32[]{:S(2)}) collective-permute-start(bf16[768,384]{1,0:T(8,128)(2,1)S(1)} %collective-permute-done.48), channel_id=1, source_target_pairs={{0,8},{8,0},{16,24},{24,16},{1,9},{9,1},{17,25},{25,17},{2,10},{10... | collective-permute-start | bytes 1769480 | tf_op jit(solution)/shard_map/ppermute | solution.py:594
  370.2 26.1 %collective-permute-start.53 = (bf16[768,384]{1,0:T(8,128)(2,1)S(1)}, bf16[768,384]{1,0:T(8,128)(2,1)S(1)}, u32[]{:S(2)}, u32[]{:S(2)}) collective-permute-start(bf16[768,384]{1,0:T(8,128)(2,1)S(1)} %pad_maximum_fusion.5), channel_id=1, source_target_pairs={{0,16},{8,24},{16,0},{24,8},{1,17},{9,25},{17,1},{25,9},{2,18},{10... | collective-permute-start | bytes 1769480 | tf_op jit(solution)/shard_map/ppermute | solution.py:594
  383.2 14.4 %collective-permute-start.52 = (bf16[768,384]{1,0:T(8,128)(2,1)S(1)}, bf16[768,384]{1,0:T(8,128)(2,1)S(1)}, u32[]{:S(2)}, u32[]{:S(2)}) collective-permute-start(bf16[768,384]{1,0:T(8,128)(2,1)S(1)} %collective-permute-done.51), channel_id=1, source_target_pairs={{0,16},{8,24},{16,0},{24,8},{1,17},{9,25},{17,1},{25,9},{2,18},{10... | collective-permute-start | bytes 1769480 | tf_op jit(solution)/shard_map/ppermute | solution.py:594
  399.0 14.2 %collective-permute-start.24 = (bf16[640,384]{1,0:T(8,128)(2,1)S(1)}, bf16[640,384]{1,0:T(8,128)(2,1)S(1)}, u32[]{:S(2)}, u32[]{:S(2)}) collective-permute-start(bf16[640,384]{1,0:T(8,128)(2,1)S(1)} %get-tuple-element.220), channel_id=1, source_target_pairs={{0,16},{8,24},{16,0},{24,8},{1,17},{9,25},{17,1},{25,9},{2,18},{10... | collective-permute-start | bytes 1474568 | tf_op jit(solution)/shard_map/ppermute | solution.py:594
  400.3 14.2 %collective-permute-start.21 = (bf16[640,384]{1,0:T(8,128)(2,1)S(1)}, bf16[640,384]{1,0:T(8,128)(2,1)S(1)}, u32[]{:S(2)}, u32[]{:S(2)}) collective-permute-start(bf16[640,384]{1,0:T(8,128)(2,1)S(1)} %get-tuple-element.214), channel_id=1, source_target_pairs={{0,8},{8,0},{16,24},{24,16},{1,9},{9,1},{17,25},{25,17},{2,10},{10... | collective-permute-start | bytes 1474568 | tf_op jit(solution)/shard_map/ppermute | solution.py:594
  401.5 41.5 %copy-start.2 = (bf16[6144,384]{1,0:T(8,128)(2,1)}, bf16[6144,384]{1,0:T(8,128)(2,1)S(1)}, u32[]{:S(2)}) copy-start(bf16[6144,384]{1,0:T(8,128)(2,1)S(1)} %select_dynamic-update-slice_fusion) | copy-start | bytes 14155780
  401.6 22.2 %collective-permute-start.23 = (bf16[640,384]{1,0:T(8,128)(2,1)S(1)}, bf16[640,384]{1,0:T(8,128)(2,1)S(1)}, u32[]{:S(2)}, u32[]{:S(2)}) collective-permute-start(bf16[640,384]{1,0:T(8,128)(2,1)S(1)} %get-tuple-element.219), channel_id=1, source_target_pairs={{0,16},{8,24},{16,0},{24,8},{1,17},{9,25},{17,1},{25,9},{2,18},{10... | collective-permute-start | bytes 1474568 | tf_op jit(solution)/shard_map/ppermute | solution.py:594
  403.2 29.5 %collective-permute-start.20 = (bf16[640,384]{1,0:T(8,128)(2,1)S(1)}, bf16[640,384]{1,0:T(8,128)(2,1)S(1)}, u32[]{:S(2)}, u32[]{:S(2)}) collective-permute-start(bf16[640,384]{1,0:T(8,128)(2,1)S(1)} %get-tuple-element.213), channel_id=1, source_target_pairs={{0,8},{8,0},{16,24},{24,16},{1,9},{9,1},{17,25},{25,17},{2,10},{10... | collective-permute-start | bytes 1474568 | tf_op jit(solution)/shard_map/ppermute | solution.py:594
  413.4 19.1 %collective-permute-start.25 = (bf16[640,384]{1,0:T(8,128)(2,1)S(1)}, bf16[640,384]{1,0:T(8,128)(2,1)S(1)}, u32[]{:S(2)}, u32[]{:S(2)}) collective-permute-start(bf16[640,384]{1,0:T(8,128)(2,1)S(1)} %fusion.20), channel_id=1, source_target_pairs={{0,8},{8,0},{16,24},{24,16},{1,9},{9,1},{17,25},{25,17},{2,10},{10... | collective-permute-start | bytes 1474568 | tf_op jit(solution)/shard_map/ppermute | solution.py:594
  414.7 18.0 %collective-permute-start.22 = (bf16[640,384]{1,0:T(8,128)(2,1)S(1)}, bf16[640,384]{1,0:T(8,128)(2,1)S(1)}, u32[]{:S(2)}, u32[]{:S(2)}) collective-permute-start(bf16[640,384]{1,0:T(8,128)(2,1)S(1)} %fusion.22), channel_id=1, source_target_pairs={{0,16},{8,24},{16,0},{24,8},{1,17},{9,25},{17,1},{25,9},{2,18},{10... | collective-permute-start | bytes 1474568 | tf_op jit(solution)/shard_map/ppermute | solution.py:594
  433.2 15.6 %collective-permute-start.26 = (bf16[320,384]{1,0:T(8,128)(2,1)S(1)}, bf16[320,384]{1,0:T(8,128)(2,1)S(1)}, u32[]{:S(2)}, u32[]{:S(2)}) collective-permute-start(bf16[320,384]{1,0:T(8,128)(2,1)S(1)} %get-tuple-element.224), channel_id=1, source_target_pairs={{0,2},{2,0},{4,6},{6,4},{1,3},{3,1},{5,7},{7,5},{8,10},{10,8},{12,... | collective-permute-start | bytes 737288 | tf_op jit(solution)/shard_map/ppermute | solution.py:594
  440.9 13.1 %collective-permute-start.28 = (bf16[320,384]{1,0:T(8,128)(2,1)S(1)}, bf16[320,384]{1,0:T(8,128)(2,1)S(1)}, u32[]{:S(2)}, u32[]{:S(2)}) collective-permute-start(bf16[320,384]{1,0:T(8,128)(2,1)S(1)} %get-tuple-element.225), channel_id=1, source_target_pairs={{0,6},{2,4},{4,2},{6,0},{1,7},{3,5},{5,3},{7,1},{8,14},{10,12},{12... | collective-permute-start | bytes 737288 | tf_op jit(solution)/shard_map/ppermute | solution.py:594
  442.8 19.1 %collective-permute-start.27 = (bf16[320,384]{1,0:T(8,128)(2,1)S(1)}, bf16[320,384]{1,0:T(8,128)(2,1)S(1)}, u32[]{:S(2)}, u32[]{:S(2)}) collective-permute-start(bf16[320,384]{1,0:T(8,128)(2,1)S(1)} %get-tuple-element.226), channel_id=1, source_target_pairs={{0,4},{2,6},{4,0},{6,2},{1,5},{3,7},{5,1},{7,3},{8,12},{10,14},{12... | collective-permute-start | bytes 737288 | tf_op jit(solution)/shard_map/ppermute | solution.py:594
  462.0 52.7 %collective-permute-start.31 = (bf16[320,384]{1,0:T(8,128)(2,1)S(1)}, bf16[320,384]{1,0:T(8,128)(2,1)}, u32[]{:S(2)}, u32[]{:S(2)}) collective-permute-start(bf16[320,384]{1,0:T(8,128)(2,1)S(1)} %fusion.53), channel_id=1, source_target_pairs={{0,2},{2,0},{4,6},{6,4},{1,3},{3,1},{5,7},{7,5},{8,10},{10,8},{12,... | collective-permute-start | bytes 737288 | tf_op jit(solution)/shard_map/ppermute | solution.py:594
  462.1 53.8 %collective-permute-start.30 = (bf16[320,384]{1,0:T(8,128)(2,1)S(1)}, bf16[320,384]{1,0:T(8,128)(2,1)}, u32[]{:S(2)}, u32[]{:S(2)}) collective-permute-start(bf16[320,384]{1,0:T(8,128)(2,1)S(1)} %fusion.53), channel_id=1, source_target_pairs={{0,4},{2,6},{4,0},{6,2},{1,5},{3,7},{5,1},{7,3},{8,12},{10,14},{12... | collective-permute-start | bytes 737288 | tf_op jit(solution)/shard_map/ppermute | solution.py:594
  464.8 51.1 %collective-permute-start.29 = (bf16[320,384]{1,0:T(8,128)(2,1)S(1)}, bf16[320,384]{1,0:T(8,128)(2,1)}, u32[]{:S(2)}, u32[]{:S(2)}) collective-permute-start(bf16[320,384]{1,0:T(8,128)(2,1)S(1)} %fusion.53), channel_id=1, source_target_pairs={{0,6},{2,4},{4,2},{6,0},{1,7},{3,5},{5,3},{7,1},{8,14},{10,12},{12... | collective-permute-start | bytes 737288 | tf_op jit(solution)/shard_map/ppermute | solution.py:594
  509.2 3.1 collective-permute-start.12
  512.3 10.2 %collective-permute-start.15 = (f32[3392]{0:T(1024)S(1)}, f32[3392]{0:T(1024)S(1)}, u32[]{:S(2)}, u32[]{:S(2)}) collective-permute-start(f32[3392]{0:T(1024)S(1)} %add.559), channel_id=1, source_target_pairs={{0,24},{8,16},{16,8},{24,0},{1,25},{9,17},{17,9},{25,1},{2,26},{10... | collective-permute-start | bytes 40712 | tf_op jit(solution)/shard_map/ppermute | solution.py:594
  514.2 8.4 %collective-permute-start.14 = (f32[3392]{0:T(1024)S(1)}, f32[3392]{0:T(1024)S(1)}, u32[]{:S(2)}, u32[]{:S(2)}) collective-permute-start(f32[3392]{0:T(1024)S(1)} %add.559), channel_id=1, source_target_pairs={{0,16},{8,24},{16,0},{24,8},{1,17},{9,25},{17,1},{25,9},{2,18},{10... | collective-permute-start | bytes 40712 | tf_op jit(solution)/shard_map/ppermute | solution.py:594
  514.7 7.9 %collective-permute-start.13 = (f32[3392]{0:T(1024)S(1)}, f32[3392]{0:T(1024)S(1)}, u32[]{:S(2)}, u32[]{:S(2)}) collective-permute-start(f32[3392]{0:T(1024)S(1)} %add.559), channel_id=1, source_target_pairs={{0,8},{8,0},{16,24},{24,16},{1,9},{9,1},{17,25},{25,17},{2,10},{10... | collective-permute-start | bytes 40712 | tf_op jit(solution)/shard_map/ppermute | solution.py:594
  518.1 14.0 %collective-permute-start.32 = (bf16[640,384]{1,0:T(8,128)(2,1)}, bf16[640,384]{1,0:T(8,128)(2,1)S(1)}, u32[]{:S(2)}, u32[]{:S(2)}) collective-permute-start(bf16[640,384]{1,0:T(8,128)(2,1)} %pad_maximum_fusion.6), channel_id=1, source_target_pairs={{0,16},{8,24},{16,0},{24,8},{1,17},{9,25},{17,1},{25,9},{2,18},{10... | collective-permute-start | bytes 1474568 | tf_op jit(solution)/shard_map/ppermute | solution.py:594
  522.5 6.3 %collective-permute-start.18 = (f32[3392]{0:T(1024)S(1)}, f32[3392]{0:T(1024)S(1)}, u32[]{:S(2)}, u32[]{:S(2)}) collective-permute-start(f32[3392]{0:T(1024)S(1)} %add_add_fusion.1), channel_id=1, source_target_pairs={{0,6},{2,4},{4,2},{6,0},{1,7},{3,5},{5,3},{7,1},{8,14},{10,12},{12... | collective-permute-start | bytes 40712 | tf_op jit(solution)/shard_map/ppermute | solution.py:594
  524.9 4.6 collective-permute-start.17
  524.9 7.9 %collective-permute-start.16 = (f32[3392]{0:T(1024)S(1)}, f32[3392]{0:T(1024)S(1)}, u32[]{:S(2)}, u32[]{:S(2)}) collective-permute-start(f32[3392]{0:T(1024)S(1)} %add_add_fusion.1), channel_id=1, source_target_pairs={{0,2},{2,0},{4,6},{6,4},{1,3},{3,1},{5,7},{7,5},{8,10},{10,8},{12,... | collective-permute-start | bytes 40712 | tf_op jit(solution)/shard_map/ppermute | solution.py:594
  527.0 25.6 %collective-permute-start.34 = (bf16[640,384]{1,0:T(8,128)(2,1)}, bf16[640,384]{1,0:T(8,128)(2,1)S(1)}, u32[]{:S(2)}, u32[]{:S(2)}) collective-permute-start(bf16[640,384]{1,0:T(8,128)(2,1)} %pad_maximum_fusion.6), channel_id=1, source_target_pairs={{0,8},{8,0},{16,24},{24,16},{1,9},{9,1},{17,25},{25,17},{2,10},{10... | collective-permute-start | bytes 1474568 | tf_op jit(solution)/shard_map/ppermute | solution.py:594
  528.9 33.3 %collective-permute-start.37 = (bf16[640,384]{1,0:T(8,128)(2,1)}, bf16[640,384]{1,0:T(8,128)(2,1)S(1)}, u32[]{:S(2)}, u32[]{:S(2)}) collective-permute-start(bf16[640,384]{1,0:T(8,128)(2,1)} %pad_maximum_fusion.7), channel_id=1, source_target_pairs={{0,16},{8,24},{16,0},{24,8},{1,17},{9,25},{17,1},{25,9},{2,18},{10... | collective-permute-start | bytes 1474568 | tf_op jit(solution)/shard_map/ppermute | solution.py:594
  529.5 22.4 %collective-permute-start.35 = (bf16[640,384]{1,0:T(8,128)(2,1)}, bf16[640,384]{1,0:T(8,128)(2,1)S(1)}, u32[]{:S(2)}, u32[]{:S(2)}) collective-permute-start(bf16[640,384]{1,0:T(8,128)(2,1)} %pad_maximum_fusion.7), channel_id=1, source_target_pairs={{0,8},{8,0},{16,24},{24,16},{1,9},{9,1},{17,25},{25,17},{2,10},{10... | collective-permute-start | bytes 1474568 | tf_op jit(solution)/shard_map/ppermute | solution.py:594
  532.1 27.9 %collective-permute-start.33 = (bf16[640,384]{1,0:T(8,128)(2,1)S(1)}, bf16[640,384]{1,0:T(8,128)(2,1)}, u32[]{:S(2)}, u32[]{:S(2)}) collective-permute-start(bf16[640,384]{1,0:T(8,128)(2,1)S(1)} %collective-permute-done.32), channel_id=1, source_target_pairs={{0,8},{8,0},{16,24},{24,16},{1,9},{9,1},{17,25},{25,17},{2,10},{10... | collective-permute-start | bytes 1474568 | tf_op jit(solution)/shard_map/ppermute | solution.py:594
  551.9 10.3 %collective-permute-start.36 = (bf16[640,384]{1,0:T(8,128)(2,1)S(1)}, bf16[640,384]{1,0:T(8,128)(2,1)S(1)}, u32[]{:S(2)}, u32[]{:S(2)}) collective-permute-start(bf16[640,384]{1,0:T(8,128)(2,1)S(1)} %collective-permute-done.35), channel_id=1, source_target_pairs={{0,16},{8,24},{16,0},{24,8},{1,17},{9,25},{17,1},{25,9},{2,18},{10... | collective-permute-start | bytes 1474568 | tf_op jit(solution)/shard_map/ppermute | solution.py:594
  (34 other events, 303.4 us)
Sparse Core Ops, SparseCore 0:
  37.9 68.3 all-gather.4
  107.8 64.2 all-gather.6
  174.5 60.9 reduce-scatter.2
  237.6 102.7 reduce-scatter.4

commit v3 on v2

v3 whole, which is shorter than its diff:
```python
import functools

import jax
import jax.numpy as jnp
from jax import lax
from jax.experimental import pallas as pl
from jax.experimental.pallas import tpu as pltpu
from jax.sharding import PartitionSpec as P

EPSILON = 1e-05
LANES = 128
VMEM_LIMIT = 56 * 2**20
SHARES = (10, 6)
CALLS = 2
EARLY_APART = ("smp",)
LATE_APART = ("smp",)
f32 = jnp.float32
bf16 = jnp.bfloat16


def normalize(values):
    centre = values - jnp.mean(values, axis=-1, keepdims=True)
    factor = lax.rsqrt(jnp.mean(centre * centre, axis=-1, keepdims=True) + EPSILON)
    return (centre * factor, factor)


def normalize_back(incoming, normed, factor):
    return factor * (
        incoming
        - jnp.mean(incoming, axis=-1, keepdims=True)
        - normed * jnp.mean(incoming * normed, axis=-1, keepdims=True)
    )


def matmul(left, right):
    return jnp.dot(left, right, preferred_element_type=jnp.float32)


def contract(form, left, right):
    return jnp.einsum(
        form, left.astype(bf16), right.astype(bf16), preferred_element_type=jnp.float32
    )


def dot(left, right, left_dim, right_dim):
    return lax.dot_general(
        left, right, (((left_dim,), (right_dim,)), ((), ())), preferred_element_type=f32
    )


def attention_kernel(
    meta, query, mine, other, gate, delta_gated, bias, *refs, step
):
    (
        gated, delta_gate, delta_query, kept, sent, delta_bias, score, prob, slope,
    ) = refs[-9:]
    samples, head_width, rows = query.shape
    total = 2 * rows
    pieces, piece_rows = bias.shape[0], bias.shape[2]
    scale = head_width ** (-0.5)
    second = meta[1] == 1
    column = lax.broadcasted_iota(jnp.int32, (16, total), 1)
    line = lax.broadcasted_iota(jnp.int32, (16, total), 0)
    masking = jnp.where((line == 0) & (column >= meta[0]), -1e30, 0.0).astype(bf16)
    pair_ones = jnp.where(line < 2, 1.0, 0.0).astype(bf16)
    query_line = lax.broadcasted_iota(jnp.int32, (16, rows), 0)
    one_line = jnp.where(query_line == 0, 1.0, 0.0).astype(bf16)
    spots = [
        (piece, start, piece * piece_rows + start)
        for piece in range(pieces)
        for start in range(0, piece_rows, step)
    ]

    def joined(mine, other):
        mine, other = mine[:, :rows], other[:, :rows]
        first = jnp.where(second, other, mine)
        last = jnp.where(second, mine, other)
        return jnp.concatenate([first, last], axis=1)

    def parted(whole, sample, which):
        first, last = whole[:, :rows], whole[:, rows:]
        kept[sample, which] = jnp.where(second, last, first)
        sent[sample, which, :, :rows] = jnp.where(second, first, last).astype(sent.dtype)

    keys, values = [], []
    for s in range(samples):
        keys.append(joined(mine[s, 0], other[s, 0]))
        values.append(joined(mine[s, 1], other[s, 1]))
        score[s] = dot(
            jnp.concatenate([query[s], one_line], axis=0),
            jnp.concatenate([keys[s], masking], axis=0),
            0,
            0,
        )
    for piece, start, place in spots:
        bias_here = bias[piece, 0, start : start + step, :].astype(f32)
        here = slice(place, place + step)
        for s in range(samples):
            line_scores = score[s, here, :] * scale + bias_here
            highest = jnp.max(line_scores, axis=1, keepdims=True)
            exponent = jnp.exp(line_scores - highest)
            soft = exponent * (1.0 / jnp.sum(exponent, axis=1, keepdims=True))
            score[s, here, :] = soft
            prob[s, here, :] = soft.astype(bf16)
    for s in range(samples):
        attended = dot(values[s], prob[s], 1, 1)
        gate_here, delta_here = gate[s], delta_gated[s]
        gated[s] = (gate_here * attended).astype(bf16)
        delta_attended = (delta_here * gate_here).astype(bf16)
        delta_gate[s] = (delta_here * attended * gate_here * (1.0 - gate_here)).astype(bf16)
        centre = jnp.sum(delta_attended.astype(f32) * attended, axis=0, keepdims=True)
        coarse = centre.astype(bf16).astype(f32)
        rest = jnp.where(
            query_line == 0, -coarse, jnp.where(query_line == 1, coarse - centre, 0.0)
        ).astype(bf16)
        slope[s] = dot(
            jnp.concatenate([delta_attended, rest], axis=0),
            jnp.concatenate([values[s], pair_ones], axis=0),
            0,
            0,
        )
        parted(dot(delta_attended, prob[s], 1, 0), s, 1)
    for piece, start, place in spots:
        here = slice(place, place + step)
        total_here = None
        for s in range(samples):
            delta_scores = score[s, here, :] * slope[s, here, :]
            prob[s, here, :] = delta_scores.astype(bf16)
            total_here = delta_scores if total_here is None else total_here + delta_scores
        delta_bias[piece, 0, start : start + step, :] = total_here.astype(bf16)
    for s in range(samples):
        delta_query[s] = (dot(keys[s], prob[s], 1, 1) * scale).astype(bf16)
        parted(dot(query[s], prob[s], 1, 0) * scale, s, 0)


def attention(
    meta, query, pair_of_cores, gate, delta_gated, bias, part, call, calls, earlier
):
    samples, width, rows = query.shape
    pieces, heads, piece_rows, total = bias.shape
    head_width = width // sum(SHARES)
    step = 16 if piece_rows % 16 == 0 else piece_rows
    count = heads // calls
    inside = call * count
    first = sum(SHARES[:part]) + inside
    padded = pair_of_cores[0].shape[3]

    def spec(columns, offset):
        return pl.BlockSpec((samples, head_width, columns), lambda h, meta: (0, offset + h, 0))

    inner, outer = spec(rows, first), spec(rows, inside)

    def double(columns, offset):
        return pl.BlockSpec(
            (samples, 2, head_width, columns), lambda h, meta: (0, 0, offset + h, 0)
        )

    tile = pl.BlockSpec((pieces, 1, piece_rows, total), lambda h, meta: (0, inside + h, 0, 0))

    def made(dtype, columns=rows, lead=(samples,)):
        return jax.ShapeDtypeStruct(lead + (heads * head_width, columns), dtype)

    return pl.pallas_call(
        functools.partial(attention_kernel, step=step),
        grid_spec=pltpu.PrefetchScalarGridSpec(
            num_scalar_prefetch=1,
            grid=(count,),
            in_specs=[inner]
            + [double(padded, first)] * 2
            + [inner] * 2
            + [tile]
            + [pl.BlockSpec(memory_space=pl.ANY)] * len(earlier),
            out_specs=[outer] * 3 + [double(rows, inside), double(padded, inside), tile],
            scratch_shapes=[
                pltpu.VMEM((samples, rows, total), f32),
                pltpu.VMEM((samples, rows, total), bf16),
                pltpu.VMEM((samples, rows, total), f32),
            ],
        ),
        out_shape=[
            made(bf16), made(bf16), made(bf16), made(f32, rows, (samples, 2)),
            made(bf16, padded, (samples, 2)),
            jax.ShapeDtypeStruct(bias.shape, bf16),
        ],
        input_output_aliases={7 + i: i for i in range(len(earlier))},
        compiler_params=pltpu.CompilerParams(vmem_limit_bytes=VMEM_LIMIT),
        cost_estimate=pl.CostEstimate(flops=1, bytes_accessed=1, transcendentals=0),
    )(meta, query, *pair_of_cores, gate, delta_gated, bias, *earlier)


def centred_project(gain, project):
    weight = (project.astype(f32) * gain.astype(f32)[:, None]).T
    weight = weight - jnp.mean(weight, axis=1, keepdims=True)
    high = lax.reduce_precision(weight, 8, 7)
    return jnp.concatenate([high.astype(bf16), (weight - high).astype(bf16)], axis=0)


def turned_norm(rows):
    turned = rows.T.astype(f32)
    centre = turned - jnp.mean(turned, axis=0, keepdims=True)
    return centre, lax.rsqrt(jnp.mean(centre * centre, axis=0, keepdims=True) + EPSILON)


def head_spots():
    return [(part, i) for part, share in enumerate(SHARES) for i in range(share)]


def pair_forward_kernel(pair, weight, *refs, block, heads):
    outs, wide = refs[:-1], refs[-1]

    def one(i, carry):
        _, factor = turned_norm(pair[i])
        both = dot(weight[...], pair[i], 1, 1)
        line = (both[:heads] + both[heads:]) * factor
        for t in range(wide.shape[0]):
            wide[t, pl.ds(pl.multiple_of(i * heads, heads), heads), :] = line[
                :, t * LANES : (t + 1) * LANES
            ]
        return carry

    lax.fori_loop(0, block, one, 0, unroll=8 if block % 8 == 0 else 1)
    for h, (part, i) in enumerate(head_spots()):
        for t in range(wide.shape[0]):
            outs[part][i, :, t * LANES : (t + 1) * LANES] = wide[
                t, pl.ds(h, block, stride=heads), :
            ].astype(bf16)


def pair_forward(pair, weight):
    rows, length, width = pair.shape
    heads = weight.shape[0] // 2
    block = 16 if rows % 16 == 0 else rows
    return pl.pallas_call(
        functools.partial(pair_forward_kernel, block=block, heads=heads),
        grid=(rows // block,),
        in_specs=[
            pl.BlockSpec((block, length, width), lambda i: (i, 0, 0)),
            pl.BlockSpec((2 * heads, width), lambda i: (0, 0)),
        ],
        out_specs=[pl.BlockSpec((share, block, length), lambda i: (0, i, 0)) for share in SHARES],
        out_shape=[jax.ShapeDtypeStruct((share, rows, length), bf16) for share in SHARES],
        scratch_shapes=[pltpu.VMEM((length // LANES, block * heads, LANES), f32)],
        compiler_params=pltpu.CompilerParams(vmem_limit_bytes=VMEM_LIMIT),
        cost_estimate=pl.CostEstimate(flops=1, bytes_accessed=1, transcendentals=0),
    )(pair, weight)


def pair_backward_kernel(pair, weight, *refs, block, heads):
    deltas = refs[: len(SHARES)]
    out, inner_out, wide, inner_sum = refs[-4:]
    step = pl.program_id(0)

    @pl.when(step == 0)
    def _():
        inner_sum[...] = jnp.zeros_like(inner_sum)

    for h, (part, place) in enumerate(head_spots()):
        for t in range(wide.shape[0]):
            wide[t, h * block : (h + 1) * block, :] = deltas[part][
                place, :, t * LANES : (t + 1) * LANES
            ].astype(f32)

    def one(i, carry):
        centre, factor = turned_norm(pair[i])
        normed = centre * factor
        delta = jnp.concatenate(
            [wide[t, pl.ds(i, heads, stride=block), :] for t in range(wide.shape[0])], axis=1
        ).astype(bf16)
        incoming = dot(weight[...], jnp.concatenate([delta, delta], axis=0), 0, 0)
        inner_sum[...] += dot(delta, normed.astype(bf16), 1, 1)
        along = jnp.mean(incoming * normed, axis=0, keepdims=True)
        out[i] = ((incoming - normed * along) * factor).T
        return carry

    lax.fori_loop(0, block, one, 0, unroll=4 if block % 4 == 0 else 1)

    @pl.when(step == pl.num_programs(0) - 1)
    def _():
        inner_out[...] = inner_sum[...]


def pair_backward(pair, weight, deltas, start, count, earlier):
    rows, length, width = pair.shape
    heads = weight.shape[0] // 2
    parts = len(deltas)
    block = 16 if rows % 16 == 0 else rows
    return pl.pallas_call(
        functools.partial(pair_backward_kernel, block=block, heads=heads),
        grid=(count,),
        in_specs=[
            pl.BlockSpec((block, length, width), lambda i: (start + i, 0, 0)),
            pl.BlockSpec((2 * heads, width), lambda i: (0, 0)),
        ]
        + [
            pl.BlockSpec((share, block, length), lambda i: (0, start + i, 0)) for share in SHARES
        ]
        + [pl.BlockSpec(memory_space=pl.ANY)] * len(earlier),
        out_specs=[
            pl.BlockSpec((block, length, width), lambda i: (start + i, 0, 0)),
            pl.BlockSpec((heads, width), lambda i: (0, 0)),
        ],
        out_shape=[
            jax.ShapeDtypeStruct((rows, length, width), f32),
            jax.ShapeDtypeStruct((heads, width), f32),
        ],
        scratch_shapes=[
            pltpu.VMEM((length // LANES, block * heads, LANES), f32),
            pltpu.VMEM((heads, width), f32),
        ],
        input_output_aliases={2 + parts: 0} if earlier else {},
        compiler_params=pltpu.CompilerParams(vmem_limit_bytes=VMEM_LIMIT),
        cost_estimate=pl.CostEstimate(flops=1, bytes_accessed=1, transcendentals=0),
    )(pair, weight, *deltas, *earlier)


def fixed(shape):
    return pl.BlockSpec(shape, lambda s, *_: (0,) * len(shape), pipeline_mode=pl.Buffered(1))


def by_sample(shape, buffers=2):
    return pl.BlockSpec(
        (1,) + shape,
        lambda s, *_: (s,) + (0,) * len(shape),
        pipeline_mode=pl.Buffered(buffers),
    )


def row_valid(meta, rows):
    place = lax.broadcasted_iota(jnp.int32, (rows, 1), 0) + meta[1] * rows
    return jnp.where(place < meta[0], 1.0, 0.0)


def pack_columns(meta, packs, arrays, start=0):
    tile = packs[0].shape[1]
    for array in arrays:
        depth, share = array.shape[0], array.shape[1] // 2
        for side in range(2):
            core = meta[1] if side == 0 else 1 - meta[1]
            for block in range(share // tile):
                column = pl.multiple_of(core * share + block * tile, LANES)
                packs[side][start + block * depth : start + (block + 1) * depth, :] = array[
                    :, pl.ds(column, tile)
                ].astype(bf16)
        start += depth * (share // tile)


def project_kernel(
    meta, single, cotangent, lifting, shifting, finish, query_bias,
    query_weight, key_weight, value_weight, gate_weight, output_weight,
    query, key_value, gate, delta_gated, mixed_out,
):
    rows = single.shape[1]
    normed, _ = normalize(single[0].astype(f32))
    mixed = (lifting[...] * normed + shifting[...]).astype(bf16)
    mixed_out[0] = mixed
    query[0] = (dot(mixed, query_weight[...], 1, 0) + query_bias[...]).astype(bf16).T
    key_value[0, 0, :, :rows] = dot(mixed, key_weight[...], 1, 0).astype(bf16).T
    key_value[0, 1, :, :rows] = dot(mixed, value_weight[...], 1, 0).astype(bf16).T
    gate[0] = jax.nn.sigmoid(dot(mixed, gate_weight[...], 1, 0)).T
    branch = row_valid(meta, rows) * cotangent[0].astype(f32)
    lifted = (finish[...] * branch).astype(bf16)
    delta_gated[0] = dot(lifted, output_weight[...], 1, 1).T


def project(meta, single, cotangent, lifting, shifting, finish, query_bias, weights):
    samples, rows, width = single.shape
    natural, turned = by_sample((rows, width)), by_sample((width, rows))
    flat, square = fixed((rows, width)), fixed((width, width))
    padded = rows + -rows % LANES
    wide = by_sample((2, width, padded))
    return pl.pallas_call(
        project_kernel,
        grid_spec=pltpu.PrefetchScalarGridSpec(
            num_scalar_prefetch=1,
            grid=(samples,),
            in_specs=[natural, natural, flat, flat, flat, fixed((1, width))] + [square] * 5,
            out_specs=[turned, wide, turned, turned, natural],
        ),
        out_shape=[
            jax.ShapeDtypeStruct(shape, dtype)
            for shape, dtype in (
                ((samples, width, rows), bf16),
                ((samples, 2, width, padded), bf16),
                ((samples, width, rows), f32),
                ((samples, width, rows), f32),
            )
        ]
        + [jax.ShapeDtypeStruct((samples, rows, width), bf16)],
        compiler_params=pltpu.CompilerParams(vmem_limit_bytes=VMEM_LIMIT),
        cost_estimate=pl.CostEstimate(flops=1, bytes_accessed=1, transcendentals=0),
    )(meta, single, cotangent, lifting, shifting, finish, query_bias, *weights)


def transition_kernel(
    meta, single, cotangent, lifting, shifting, closing,
    swish_weight, linear_weight, down_weight,
    closed, delta_second, closing_sum, lift_sum, shift_sum, pack_mine, pack_other,
    swish_sum, linear_sum, down_sum,
):
    rows = single.shape[1]
    sample = pl.program_id(0)
    normed, _ = normalize(single[0].astype(f32))
    mixed = (lifting[...] * normed + shifting[...]).astype(bf16)
    up_swish = dot(mixed, swish_weight[...], 1, 0)
    up_linear = dot(mixed, linear_weight[...], 1, 0)
    squash = jax.nn.sigmoid(up_swish)
    silu = up_swish * squash
    hidden = (silu * up_linear).astype(bf16)
    moved = dot(hidden, down_weight[...], 1, 0)
    closing_here = closing[...]
    branch = row_valid(meta, rows) * cotangent[0].astype(f32)
    closed[0] = closing_here * moved
    delta_moved = (closing_here * branch).astype(bf16)
    delta_hidden = dot(delta_moved, down_weight[...], 1, 1)
    delta_swish = (delta_hidden * up_linear * squash * (1.0 + up_swish * (1.0 - squash))).astype(bf16)
    delta_linear = (delta_hidden * silu).astype(bf16)
    second = dot(delta_swish, swish_weight[...], 1, 1) + dot(
        delta_linear, linear_weight[...], 1, 1
    )
    delta_second[0] = second

    def collect(first):
        def put(ref, value):
            if first:
                ref[...] = value
            else:
                ref[...] += value

        put(closing_sum, branch * moved)
        put(lift_sum, second * normed)
        put(shift_sum, second)
        put(swish_sum, dot(mixed, delta_swish, 0, 0))
        put(linear_sum, dot(mixed, delta_linear, 0, 0))
        put(down_sum, dot(hidden, delta_moved, 0, 0))

    @pl.when(sample == 0)
    def _():
        collect(True)

    @pl.when(sample > 0)
    def _():
        collect(False)

    @pl.when(sample == pl.num_programs(0) - 1)
    def _():
        pack_columns(meta, (pack_mine, pack_other), (swish_sum, linear_sum, down_sum))


def transition(meta, single, cotangent, lifting, shifting, closing, weights, pack_rows):
    samples, rows, width = single.shape
    inner = weights[0].shape[1]
    natural, flat = by_sample((rows, width)), fixed((rows, width))
    up, down = (width, inner), (inner, width)
    pack = (pack_rows, width // 2)
    return pl.pallas_call(
        transition_kernel,
        grid_spec=pltpu.PrefetchScalarGridSpec(
            num_scalar_prefetch=1,
            grid=(samples,),
            in_specs=[natural, natural, flat, flat, flat, fixed(up), fixed(up), fixed(down)],
            out_specs=[natural, natural, flat, flat, flat, fixed(pack), fixed(pack)],
            scratch_shapes=[pltpu.VMEM(up, f32), pltpu.VMEM(up, f32), pltpu.VMEM(down, f32)],
        ),
        out_shape=[
            jax.ShapeDtypeStruct(shape, f32)
            for shape in ((samples, rows, width),) * 2 + ((rows, width),) * 3
        ]
        + [jax.ShapeDtypeStruct(pack, bf16)] * 2,
        compiler_params=pltpu.CompilerParams(vmem_limit_bytes=VMEM_LIMIT),
        cost_estimate=pl.CostEstimate(flops=1, bytes_accessed=1, transcendentals=0),
    )(meta, single, cotangent, lifting, shifting, closing, *weights)


def whole(*parts):
    return jnp.concatenate([part[0] for part in parts], axis=0)


def whole_at(*parts):
    return [jnp.concatenate([part[0, i] for part in parts], axis=0) for i in range(2)]


def put(first, ref, value):
    if first:
        ref[...] = value
    else:
        ref[...] += value


def weights_kernel(
    meta, cotangent, mixed, finish,
    key, value, gated_a, gated_b, gate_a, gate_b, query_a, query_b,
    pack_mine, pack_other, bias_sum,
    query_sum, key_sum, value_sum, gate_sum, output_sum,
):
    rows = cotangent.shape[1]
    sample = pl.program_id(0)
    delta_query = whole(query_a, query_b)
    branch = row_valid(meta, rows) * cotangent[0].astype(f32)
    lifted = (finish[...] * branch).astype(bf16)

    def collect(first):
        put(first, query_sum, dot(delta_query, mixed[0], 1, 0))
        put(first, key_sum, dot(key[0], mixed[0], 1, 0))
        put(first, value_sum, dot(value[0], mixed[0], 1, 0))
        put(first, gate_sum, dot(whole(gate_a, gate_b), mixed[0], 1, 0))
        put(first, output_sum, dot(whole(gated_a, gated_b), lifted, 1, 0))
        put(first, bias_sum, jnp.sum(delta_query.astype(f32), axis=1, keepdims=True))

    @pl.when(sample == 0)
    def _():
        collect(True)

    @pl.when(sample > 0)
    def _():
        collect(False)

    @pl.when(sample == pl.num_programs(0) - 1)
    def _():
        width = query_sum.shape[0]
        half = width // 2
        packs = (pack_mine, pack_other)
        for i, array in enumerate((query_sum, key_sum, value_sum, gate_sum)):
            for side in range(2):
                core = meta[1] if side == 0 else 1 - meta[1]
                row = pl.multiple_of(core * half, LANES)
                packs[side][i * width : (i + 1) * width, :] = array[
                    pl.ds(row, half), :
                ].T.astype(bf16)
        pack_columns(meta, packs, (output_sum,), 4 * width)


def weight_sums(meta, cotangent, mixed, finish, turned, pack_rows):
    samples, rows, width = cotangent.shape
    pack = (pack_rows, width // 2)
    natural = by_sample((rows, width))
    return pl.pallas_call(
        weights_kernel,
        grid_spec=pltpu.PrefetchScalarGridSpec(
            num_scalar_prefetch=1,
            grid=(samples,),
            in_specs=[natural, natural, fixed((rows, width))]
            + [by_sample(array.shape[1:]) for array in turned],
            out_specs=[fixed(pack)] * 2 + [fixed((width, 1))],
            scratch_shapes=[pltpu.VMEM((width, width), f32)] * 5,
        ),
        out_shape=[jax.ShapeDtypeStruct(pack, bf16)] * 2
        + [jax.ShapeDtypeStruct((width, 1), f32)],
        compiler_params=pltpu.CompilerParams(vmem_limit_bytes=VMEM_LIMIT),
        cost_estimate=pl.CostEstimate(flops=1, bytes_accessed=1, transcendentals=0),
    )(meta, cotangent, mixed, finish, *turned)


def rows_kernel(
    meta, single, cotangent, closed, delta_second,
    gated_a, gated_b, gate_a, gate_b, query_a, query_b, kept_a, kept_b, came_a, came_b,
    lifting_first, lifting_second, finish,
    query_weight, key_weight, value_weight, gate_weight, output_weight,
    *refs,
):
    block_out, single_grad, key_out, value_out, finish_sum, lift_first, shift_first = refs[-7:]
    rows = single.shape[1]
    kept, came = whole_at(kept_a, kept_b), whole_at(came_a, came_b)
    delta_key, delta_value = [
        (kept[i] + came[i][:, :rows].astype(f32)).astype(bf16) for i in range(2)
    ]
    key_out[0] = delta_key
    value_out[0] = delta_value
    sample = pl.program_id(0)
    residual = single[0].astype(f32)
    normed, factor = normalize(residual)
    valid = row_valid(meta, rows)
    outgoing = cotangent[0].astype(f32)
    branch = valid * outgoing
    raised = dot(whole(gated_a, gated_b), output_weight[...], 0, 0)
    block_out[0] = (residual + valid * (finish[...] * raised + closed[0])).astype(bf16)
    delta_first = (
        dot(whole(query_a, query_b), query_weight[...], 0, 1)
        + dot(delta_key, key_weight[...], 0, 1)
        + dot(delta_value, value_weight[...], 0, 1)
        + dot(whole(gate_a, gate_b), gate_weight[...], 0, 1)
    )
    incoming = delta_first * lifting_first[...] + delta_second[0] * lifting_second[...]
    single_grad[0] = outgoing + normalize_back(incoming, normed, factor)

    def collect(first):
        put(first, finish_sum, branch * raised)
        put(first, lift_first, delta_first * normed)
        put(first, shift_first, delta_first)

    @pl.when(sample == 0)
    def _():
        collect(True)

    @pl.when(sample > 0)
    def _():
        collect(False)


def rows_back(meta, naturals, halved, flats, weights, start, count, earlier):
    samples, rows, width = naturals[0].shape
    flat, square = fixed((rows, width)), fixed((width, width))

    def moved(shape):
        return pl.BlockSpec((1,) + shape, lambda s, *_: (start + s,) + (0,) * len(shape))

    natural = moved((rows, width))
    return pl.pallas_call(
        rows_kernel,
        grid_spec=pltpu.PrefetchScalarGridSpec(
            num_scalar_prefetch=1,
            grid=(count,),
            in_specs=[natural] * 4
            + [moved(array.shape[1:]) for array in halved]
            + [flat] * 3
            + [square] * 5
            + [pl.BlockSpec(memory_space=pl.ANY)] * len(earlier),
            out_specs=[natural] * 2 + [moved((width, rows))] * 2 + [flat] * 3,
        ),
        out_shape=[
            jax.ShapeDtypeStruct((samples, rows, width), bf16),
            jax.ShapeDtypeStruct((samples, rows, width), f32),
        ]
        + [jax.ShapeDtypeStruct((samples, width, rows), bf16)] * 2
        + [jax.ShapeDtypeStruct((rows, width), f32)] * 3,
        input_output_aliases={23 + i: i for i in range(len(earlier))},
        compiler_params=pltpu.CompilerParams(vmem_limit_bytes=VMEM_LIMIT),
        cost_estimate=pl.CostEstimate(flops=1, bytes_accessed=1, transcendentals=0),
    )(meta, *naturals, *halved, *flats, *weights, *earlier)


def swap_cores(array):
    return lax.ppermute(array, "qry", [(0, 1), (1, 0)])


def traded(array, axis):
    return lax.all_to_all(array, axis, 0, 0)


def spread(array, axis):
    return traded(jnp.broadcast_to(array[None], (lax.axis_size(axis),) + array.shape), axis)


def exchange(array, axis, bit):
    return lax.ppermute(array, axis, [(i, i ^ bit) for i in range(lax.axis_size(axis))])


def pick(array, index):
    return lax.dynamic_index_in_dim(array, index, 0, keepdims=False)


def traded_apart(array, axis):
    place = lax.axis_index(axis)
    return [pick(array, place)] + [
        exchange(pick(array, place ^ shift), axis, shift)
        for shift in range(1, lax.axis_size(axis))
    ]


def spread_apart(array, axis):
    return [array] + [exchange(array, axis, shift) for shift in range(1, lax.axis_size(axis))]


def in_order(pieces, axis):
    place, ordered = lax.axis_index(axis), []
    for j in range(len(pieces)):
        chosen = pieces[j]
        for shift in range(1, len(pieces)):
            chosen = jnp.where(place == shift, pieces[j ^ shift], chosen)
        ordered.append(chosen)
    return jnp.stack(ordered)


def summed(pieces):
    total = pieces[0].astype(f32)
    for i in range(1, len(pieces)):
        total = total + pieces[i].astype(f32)
    return total


def filled(packs, start, arrays):
    packs = list(packs)
    for array in arrays:
        for side, half in enumerate(halves(array)):
            packs[side] = lax.dynamic_update_slice(packs[side], half.astype(bf16), (start, 0))
        start += array.shape[0]
    return packs


def padded_rows(count):
    return count + -count % 512


def tied(*values):
    return lax.optimization_barrier(values)


class SliceTotal:
    def __init__(self, mine, other, apart):
        self.mine, self.state, self.apart = mine, swap_cores(other), apart

    def first(self):
        total = (self.mine.astype(f32) + self.state.astype(f32)).astype(bf16)
        places = lax.axis_size("cplx")
        self.sent = total.reshape(places, -1, total.shape[1])

    def second(self, *others):
        levels = lax.axis_size("smp")
        self.depths = [group.sent.shape[1] for group in (self, *others)]
        totals = [
            summed(group.state).astype(bf16).reshape(levels, -1, group.sent.shape[2])
            for group in (self, *others)
        ]
        self.sent = totals[0] if len(totals) == 1 else jnp.concatenate(totals, axis=1)

    def third(self):
        self.sent = summed(self.state).astype(bf16)

    def fourth(self):
        pieces = self.state
        pieces = in_order(pieces, "smp") if "smp" in self.apart else pieces
        self.sent = pieces.reshape(-1, pieces.shape[2])

    def wait(self, value):
        self.state, value = tied(self.state, value)
        return value

    def lead(self, value):
        self.sent, value = tied(self.sent, value)
        return value

    def trade(self, axis):
        self.state = (traded_apart if axis in self.apart else traded)(self.sent, axis)

    def share(self, axis):
        self.state = (spread_apart if axis in self.apart else spread)(self.sent, axis)

    def result(self):
        pieces = in_order(self.state, "cplx") if "cplx" in self.apart else self.state
        levels = lax.axis_size("smp")
        pieces = pieces.reshape(pieces.shape[0] * levels, -1, pieces.shape[2])
        totals, start = [], 0
        for depth in self.depths:
            share = depth // levels
            piece = pieces[:, start : start + share]
            totals.append(piece.reshape(-1, pieces.shape[2]).astype(f32))
            start += share
        return totals


def total_line(vector):
    vector = vector[0] + swap_cores(vector[1])
    return summed(spread_apart(vector, "smp"))


def sum_samples(array):
    return summed(spread_apart(array.astype(bf16), "smp"))


def halves(array):
    portion = array.shape[-1] // 2
    core = lax.axis_index("qry")
    mine = lax.dynamic_slice_in_dim(array, core * portion, portion, array.ndim - 1)
    other = lax.dynamic_slice_in_dim(array, (1 - core) * portion, portion, array.ndim - 1)
    return mine, other


def gather_rows(piece):
    if piece.shape[1] % 16 == 0:
        return lax.all_gather(piece, "smp", axis=0)
    return lax.all_gather(piece, "smp", axis=1, tiled=True)[None]


def scatter_rows(whole):
    if whole.shape[0] == lax.axis_size("smp"):
        return lax.psum_scatter(whole, "smp", scatter_dimension=0)
    return lax.psum_scatter(whole[0], "smp", scatter_dimension=1, tiled=True)


def per_device(
    single,
    condition,
    pair_features,
    lengths,
    cotangent,
    first_gain,
    first_scale,
    first_offset,
    first_shift,
    query_projection_weight,
    query_bias_vector,
    key_projection_weight,
    value_projection_weight,
    attention_gate_weight,
    attention_output_weight,
    pair_gain,
    pair_project,
    finish_weight,
    finish_offset,
    second_gain,
    second_scale,
    second_offset,
    second_shift,
    transition_swish_weight,
    transition_linear_weight,
    transition_down_weight,
    closing_weight,
    closing_offset,
):
    width = single.shape[3]
    narrow = condition.shape[2]
    half = width // 2
    inner = transition_swish_weight.shape[1]
    heads = pair_project.shape[1]
    meta = jnp.stack([lengths[0], lax.axis_index("qry")]).astype(jnp.int32)
    condition_raw = condition[0]
    condition_norm, condition_factor = normalize(condition_raw.astype(f32))
    pair_weight = centred_project(pair_gain, pair_project)
    bias_pieces = pair_forward(pair_features[0], pair_weight)
    meta, *bias_pieces = tied(meta, *bias_pieces)
    bias_rows = [gather_rows(bias_pieces[0])]
    bias_rows[0], bias_pieces[1] = tied(bias_rows[0], bias_pieces[1])
    bias_rows.append(gather_rows(bias_pieces[1]))

    def modulation(gain, scale_weight, offset, shift_weight):
        low = (condition_norm * gain.astype(f32)).astype(bf16)
        lifting = jax.nn.sigmoid(matmul(low, scale_weight) + offset.astype(f32))
        return low, lifting, matmul(low, shift_weight)

    condition_first, lifting_first, shifting_first = modulation(
        first_gain, first_scale, first_offset, first_shift
    )
    condition_second, lifting_second, shifting_second = modulation(
        second_gain, second_scale, second_offset, second_shift
    )
    finish = jax.nn.sigmoid(matmul(condition_raw, finish_weight) + finish_offset.astype(f32))
    closing = jax.nn.sigmoid(matmul(condition_raw, closing_weight) + closing_offset.astype(f32))
    square_weights = (
        query_projection_weight,
        key_projection_weight,
        value_projection_weight,
        attention_gate_weight,
        attention_output_weight,
    )
    closed, delta_second, closing_sum, lift_second, shift_second, *second_packs = transition(
        meta,
        single[0],
        cotangent[0],
        lifting_second,
        shifting_second,
        closing,
        (transition_swish_weight, transition_linear_weight, transition_down_weight),
        padded_rows(3 * inner + 3 * narrow),
    )

    def modulation_back(lift_sum, shift_sum, low, lifting, scale_weight, shift_weight):
        delta_lift = lift_sum * lifting * (1.0 - lifting)
        scale_total = contract("qc,qd->cd", low, delta_lift)
        shift_total = contract("qc,qd->cd", low, shift_sum)
        delta_condition = contract("qd,cd->qc", delta_lift, scale_weight) + contract(
            "qd,cd->qc", shift_sum, shift_weight
        )
        return scale_total, jnp.sum(delta_lift, axis=0), shift_total, delta_condition

    def gate_back(branch_sum, opened, weight):
        delta = branch_sum * opened * (1.0 - opened)
        return (
            contract("qc,qd->cd", condition_raw, delta),
            jnp.sum(delta, axis=0),
            contract("qd,cd->qc", delta, weight),
        )

    scale_second, offset_second, shift_total_second, cond_delta_second = modulation_back(
        lift_second, shift_second, condition_second, lifting_second, second_scale, second_shift
    )
    closing_total, closing_offset_total, condition_closing = gate_back(
        closing_sum, closing, closing_weight
    )
    early = SliceTotal(
        *filled(second_packs, 3 * inner, (scale_second, shift_total_second, closing_total)),
        apart=EARLY_APART,
    )

    early.mine, meta = tied(early.mine, meta)
    query, key_value, gate, delta_gated, mixed_first = project(
        meta,
        single[0],
        cotangent[0],
        lifting_first,
        shifting_first,
        finish,
        query_bias_vector.astype(f32)[None],
        square_weights,
    )
    pair_of_cores = (key_value, swap_cores(key_value))
    def attend(meta, part, call, earlier):
        return list(
            attention(
                meta, query, pair_of_cores, gate, delta_gated, bias_rows[part], part, call, CALLS,
                earlier,
            )
        )

    attended = []
    query = early.wait(query)
    early.first()
    meta = early.lead(meta)
    early.trade("cplx")
    attended = [attend(meta, 0, 1, attend(meta, 0, 0, ()))]
    done = attend(meta, 1, 0, ())
    done[0] = early.wait(done[0])
    early.second()
    meta = early.lead(meta)
    early.trade("smp")
    attended.append(attend(meta, 1, 1, done))
    delta_bias = [scatter_rows(part[5]) for part in attended]

    def both(index):
        return [part[index] for part in attended]

    arrived = [swap_cores(part) for part in both(4)]
    halved = both(0) + both(1) + both(2)
    def back(meta, start, earlier):
        outs = rows_back(
            meta,
            (single[0], cotangent[0], closed, delta_second),
            halved + both(3) + arrived,
            (lifting_first, lifting_second, finish),
            square_weights,
            start,
            single.shape[1] // 2,
            earlier,
        )
        return list(outs)

    done = back(meta, 0, ())
    last = back(meta, single.shape[1] // 2, tuple(done[:4]))
    block_out, single_grad, delta_key, delta_value = last[:4]
    finish_sum, lift_first, shift_first = [done[i] + last[i] for i in (4, 5, 6)]
    scale_first, offset_first, shift_total_first, cond_delta_first = modulation_back(
        lift_first, shift_first, condition_first, lifting_first, first_scale, first_shift
    )
    finish_total, finish_offset_total, condition_finish = gate_back(
        finish_sum, finish, finish_weight
    )
    *first_packs, query_bias_total = weight_sums(
        meta,
        cotangent[0],
        mixed_first,
        finish,
        [delta_key, delta_value] + halved,
        padded_rows(5 * width + 3 * narrow),
    )
    first_packs[1] = early.wait(first_packs[1])
    early.third()
    first_packs[1] = early.lead(first_packs[1])
    early.share("smp")
    late = SliceTotal(
        *filled(first_packs, 5 * width, (scale_first, shift_total_first, finish_total)),
        apart=LATE_APART,
    )
    gain_first = jnp.sum(cond_delta_first * condition_norm, axis=0)
    gain_second = jnp.sum(cond_delta_second * condition_norm, axis=0)
    condition_grad = sum_samples(
        normalize_back(
            cond_delta_first * first_gain.astype(f32) + cond_delta_second * second_gain.astype(f32),
            condition_norm,
            condition_factor,
        )
        + condition_closing
        + condition_finish
    )
    blocks = pair_features.shape[1] // 16 if pair_features.shape[1] % 16 == 0 else 1
    sizes = (blocks - blocks // 2, blocks // 2)
    delta_bias[0] = late.wait(delta_bias[0])
    late.first()
    pair_weight = late.lead(pair_weight)
    late.trade("cplx")
    early.state, late.state, delta_bias[1] = tied(early.state, late.state, delta_bias[1])
    early.fourth()
    pair_weight = early.lead(pair_weight)
    early.share("cplx")
    late.second()
    pair_weight = late.lead(pair_weight)
    late.trade("smp")
    pair_grad, inner_total = pair_backward(
        pair_features[0], pair_weight, delta_bias, 0, sizes[0], ()
    )
    inner_total = late.wait(inner_total)
    late.third()
    pair_weight = late.lead(pair_weight)
    late.share("smp")
    if sizes[1]:
        pair_grad, more = pair_backward(
            pair_features[0], pair_weight, delta_bias, *sizes, (pair_grad,)
        )
        inner_total = inner_total + more
    early.state = late.wait(early.state)
    late.fourth()
    late.share("cplx")
    pair_gain_total = jnp.sum(inner_total * pair_project.astype(f32).T, axis=0)
    pair_project_total = inner_total * pair_gain.astype(f32)[None]
    vectors = (
        gain_first,
        offset_first,
        query_bias_total[:, 0],
        finish_offset_total,
        gain_second,
        offset_second,
        closing_offset_total,
        pair_gain_total,
    )
    small = total_line(
        jnp.concatenate(
            [jnp.stack(halves(vector)) for vector in vectors]
            + [jnp.stack([half.reshape(-1) for half in halves(pair_project_total.T)])],
            axis=1,
        )
    )
    small = summed(spread_apart(small, "cplx"))
    late = late.result()[0]
    early = early.result()[0]
    ends, place = [], 0
    for vector in vectors:
        ends.append(small[place : place + vector.shape[0] // 2])
        place += vector.shape[0] // 2
    def unpack(total, sizes):
        arrays, start = [], 0
        for depth, columns in sizes:
            blocks = columns // half
            arrays.append(
                jnp.concatenate(
                    [
                        total[start + b * depth : start + (b + 1) * depth]
                        for b in range(blocks)
                    ],
                    axis=1,
                )
            )
            start += depth * blocks
        return arrays

    swish_total, linear_total, down_total, scale_second, shift_second, closing_total = unpack(
        early,
        ((width, inner // 2), (width, inner // 2), (inner, half)) + ((narrow, half),) * 3,
    )
    query_total, key_total, value_total, gate_total, output_total, *others = unpack(
        late, ((width, half),) * 5 + ((narrow, half),) * 3
    )
    scale_first, shift_first, finish_total = others
    return (
        block_out[None],
        single_grad[None],
        condition_grad[None],
        pair_grad[None],
        ends[0],
        scale_first,
        ends[1],
        shift_first,
        query_total,
        ends[2],
        key_total,
        value_total,
        gate_total,
        output_total,
        ends[7],
        small[place:].reshape(-1, heads // 2),
        finish_total,
        ends[3],
        ends[4],
        scale_second,
        ends[5],
        shift_second,
        swish_total,
        linear_total,
        down_total,
        closing_total,
        ends[6],
    )


def solution(mesh):
    placed = (
        P("cplx", "smp", "qry", None),
        P("cplx", "qry", None),
        P("cplx", ("qry", "smp"), None, None),
        P("cplx"),
        P("cplx", "smp", "qry", None),
        P(),
        P(),
        P(),
        P(),
        P(),
        P(),
        P(),
        P(),
        P(),
        P(),
        P(),
        P(),
        P(),
        P(),
        P(),
        P(),
        P(),
        P(),
        P(),
        P(),
        P(),
        P(),
        P(),
    )
    return jax.shard_map(
        per_device,
        mesh=mesh,
        in_specs=placed,
        out_specs=(
            P("cplx", "smp", "qry", None),
            P("cplx", "smp", "qry", None),
            P("cplx", "qry", None),
            P("cplx", ("qry", "smp"), None, None),
            P("qry"),
            P(None, "qry"),
            P("qry"),
            P(None, "qry"),
            P(None, "qry"),
            P("qry"),
            P(None, "qry"),
            P(None, "qry"),
            P(None, "qry"),
            P(None, "qry"),
            P("qry"),
            P(None, "qry"),
            P(None, "qry"),
            P("qry"),
            P("qry"),
            P(None, "qry"),
            P("qry"),
            P(None, "qry"),
            P(None, "qry"),
            P(None, "qry"),
            P(None, "qry"),
            P(None, "qry"),
            P("qry"),
        ),
        check_vma=False,
    )
```

time: 580 us -> 499 us (0.86)
  waiting for transfers between devices: 155 us -> 93.6 us
  Pallas kernels: 258 us -> 241 us
  starting transfers between devices: 62.3 us -> 52.2 us
  other arithmetic: 32.8 us -> 42.6 us
    ppermute x45 -> x21, waiting for transfers between devices: 155 us -> 82.6 us  [exchange(): lax.ppermute(array, axis, [(i, i ^ bit) for i in range(lax.axis_size(axis...]
    ppermute x45 -> x21, starting transfers between devices: 60.2 us -> 30 us  [exchange(): lax.ppermute(array, axis, [(i, i ^ bit) for i in range(lax.axis_size(axis...]
    all_to_all x0 -> x4, starting transfers between devices: none -> 20.7 us  [traded(): return lax.all_to_all(array, axis, 0, 0)]
    pallas_call x1, Pallas kernels: 29 us -> 11.3 us  [pair_forward(): pl.pallas_call(functools.partial(pair_forward_kernel, block=block, heads=...]
    convert_element_type x10 -> x9, other arithmetic: 8.78 us -> 22.3 us  [the longest x2 13.8 us: first(): total = (self.mine.astype(f32) + self.state.astype(f32)).astype(bf16)]
    pallas_call x1 -> x2, Pallas kernels: 40.6 us -> 28.4 us  [pair_backward(): pl.pallas_call(functools.partial(pair_backward_kernel, block=block, heads...]
    another operation x0 -> x6, other arithmetic: none -> 9.43 us
    slice x5 -> x1, local copies, waits for them, and re-layouts: 7.41 us -> 0.07 us  [total_line(): vector = vector[0] + swap_cores(vector[1])]
  transfers between devices with their start and end apart: 58 -> 35, of which waited for: 18 -> 7; matrix products, arithmetic and copies ran while one was open for 13% -> 15% of each run, Pallas kernels for 40% -> 46%
where the time goes in v3:
time: 499 us; the launch traced here: 495 us
  Pallas kernels  241 us (48%)
  waiting for transfers between devices  93.6 us (19%)
  starting transfers between devices  52.2 us (10%)
  other arithmetic  42.6 us (9%)
  local copies, waits for them, and re-layouts  27 us (5%)
  matrix products  22.8 us (5%)
  between operations  15.5 us (3%)
    ppermute x21, waiting for transfers between devices, exchange(): lax.ppermute(array, axis, [(i, i ^ bit) for i in range(lax.axis_size(axis...  82.6 us
    pallas_call x4, Pallas kernels, attention(): pl.pallas_call(functools.partial(attention_kernel, step=step), grid_spec=...  78.4 us
    pallas_call x1, Pallas kernels, transition(): pl.pallas_call(transition_kernel, grid_spec=pltpu.PrefetchScalarGridSpec(...  52.1 us
    pallas_call x2, Pallas kernels, rows_back(): pl.pallas_call(rows_kernel, grid_spec=pltpu.PrefetchScalarGridSpec(num_sc...  30.8 us
    ppermute x21, starting transfers between devices, exchange(): lax.ppermute(array, axis, [(i, i ^ bit) for i in range(lax.axis_size(axis...  30 us
    pallas_call x2, Pallas kernels, pair_backward(): pl.pallas_call(functools.partial(pair_backward_kernel, block=block, heads...  28.4 us
    pallas_call x1, Pallas kernels, weight_sums(): pl.pallas_call(weights_kernel, grid_spec=pltpu.PrefetchScalarGridSpec(num...  23.6 us
    all_to_all x4, starting transfers between devices, traded(): return lax.all_to_all(array, axis, 0, 0)  20.7 us
  transfers between devices with their start and end apart: 35, of which 7 were waited for; matrix products, arithmetic and copies ran while one was open for 15% of the time, Pallas kernels for 46%

profile of v3, /device:TPU:0, one launch (start us, length us, event | category | flops | bytes accessed | tf_op | source)
XLA Modules:
  0.0 494.5 jit_solution(16418716039809662170)
XLA Ops:
  11.4 11.3 %shard_map.475 = (bf16[10,80,640]{2,1,0:T(8,128)(2,1)}, bf16[6,80,640]{2,1,0:T(8,128)(2,1)}) custom-call(bf16[80,640,128]{2,1,0:T(8,128)(2,1)} %bitcast.146, bf16[32,128]{1,0:T(8,128)(2,1)} %pad_maximum_fusion.4.weight), custom_call_target="tpu_custom_call" | custom-call | flops 1 | bytes 1 | tf_op jit(solution)/shard_map/pallas_call | solution.py:233
  23.3 1.4 fusion.85.shifting
  24.7 1.5 fusion.15.lifting.lifting_second
  26.2 1.4 fusion.11.closing
  27.7 52.1 %shard_map.476 = (f32[4,320,768]{2,1,0:T(8,128)}, f32[4,320,768]{2,1,0:T(8,128)}, f32[320,768]{1,0:T(8,128)}, f32[320,768]{1,0:T(8,128)}, f32[320,768]{1,0:T(8,1...) custom-call(s32[2]{0:T(128)} %pad_add_fusion.meta, bf16[4,320,768]{2,1,0:T(8,128)(2,1)} %bitcast.156, ...), custom_call_target="tpu_custom_call" | custom-call | flops 1 | bytes 1 | tf_op jit(solution)/shard_map/pallas_call | solution.py:455
  79.7 1.5 fusion.33
  87.1 1.4 fusion.3.finish
  88.6 1.4 fusion.79.shifting
  90.0 1.5 fusion.7.lifting.lifting_first
  91.5 16.4 %shard_map.477 = (bf16[4,768,320]{2,1,0:T(8,128)(2,1)}, bf16[4,2,768,384]{3,2,1,0:T(8,128)(2,1)}, f32[4,768,320]{2,1,0:T(8,128)}, f32[4,768,320]{2,1,0:T(8,128)}, bf16[4,320,768]{2,1,0:T(8,128)(2,1)}) custom-call(s32[2]{0:T(128)} %pad_add_fusion.meta, bf16[4,320,768]{2,1,0:T(8,128)(2,1)} %bitcast.157, bf16[4,320,768]{2,1,0:T(8,128)(2,1)} %bitcast.150, ...), custom_call_target="tpu_custom_call" | custom-call | flops 1 | bytes 1 | tf_op jit(solution)/shard_map/pallas_call | solution.py:371
  108.0 7.1 %add_convert_fusion = bf16[6144,384]{1,0:T(8,128)(2,1)} fusion(bf16[6144,384]{1,0:T(8,128)(2,1)} %collective-permute-done, bf16[6144,384]{1,0:T(8,128)(2,1)} %get-tuple-element.141), kind=kLoop, calls=%fused_computation | loop fusion | flops 9437184 | bytes 14155776 | tf_op jit(solution)/shard_map/convert_element_type | solution.py:702
  115.1 5.4 %all-to-all-start = ((bf16[4,1536,384]{2,1,0:T(8,128)(2,1)}), bf16[4,1536,384]{2,1,0:T(8,128)(2,1)}, u32[]{:S(2)}, u32[]{:S(2)}) async-start(bf16[4,1536,384]{2,1,0:T(8,128)(2,1)} %bitcast.161), calls=%async_computation | async-start | bytes 9437184 | tf_op jit(solution)/shard_map/all_to_all | solution.py:636
  120.5 23.7 %shard_map.479 = (bf16[4,480,320]{2,1,0:T(8,128)(2,1)}, bf16[4,480,320]{2,1,0:T(8,128)(2,1)}, bf16[4,480,320]{2,1,0:T(8,128)(2,1)}, f32[4,2,480,320]{3,2,1,0:T(8...) custom-call(s32[2]{0:T(128)} %pad_add_fusion.meta, ...), custom_call_target="tpu_custom_call" | custom-call | flops 1 | bytes 1 | tf_op jit(solution)/shard_map/pallas_call | solution.py:163
  144.2 23.7 %shard_map.480 = (bf16[4,480,320]{2,1,0:T(8,128)(2,1)}, bf16[4,480,320]{2,1,0:T(8,128)(2,1)}, bf16[4,480,320]{2,1,0:T(8,128)(2,1)}, f32[4,2,480,320]{3,2,1,0:T(8...) custom-call(s32[2]{0:T(128)} %pad_add_fusion.meta, ...), custom_call_target="tpu_custom_call", output_to_operand_aliasing={{0}: (7, {}), {1}: (8, {}), {2}: (9, {}), {3}: (10, {}), {4... | custom-call | flops 1 | bytes 1 | tf_op jit(solution)/shard_map/pallas_call | solution.py:163
  168.1 15.7 %shard_map.478 = (bf16[4,288,320]{2,1,0:T(8,128)(2,1)}, bf16[4,288,320]{2,1,0:T(8,128)(2,1)}, bf16[4,288,320]{2,1,0:T(8,128)(2,1)}, f32[4,2,288,320]{3,2,1,0:T(8...) custom-call(s32[2]{0:T(128)} %pad_add_fusion.meta, ...), custom_call_target="tpu_custom_call" | custom-call | flops 1 | bytes 1 | tf_op jit(solution)/shard_map/pallas_call | solution.py:163
  183.7 3.9 add_convert_fusion.2
  187.7 15.5 %shard_map.481 = (bf16[4,288,320]{2,1,0:T(8,128)(2,1)}, bf16[4,288,320]{2,1,0:T(8,128)(2,1)}, bf16[4,288,320]{2,1,0:T(8,128)(2,1)}, f32[4,2,288,320]{3,2,1,0:T(8...) custom-call(s32[2]{0:T(128)} %pad_add_fusion.meta, ...), custom_call_target="tpu_custom_call", output_to_operand_aliasing={{0}: (7, {}), {1}: (8, {}), {2}: (9, {}), {3}: (10, {}), {4... | custom-call | flops 1 | bytes 1 | tf_op jit(solution)/shard_map/pallas_call | solution.py:163
  203.7 2.2 dynamic-slice_bitcast_fusion
  205.9 4.9 collective-permute-start.9
  212.6 15.2 %shard_map.482 = (bf16[4,320,768]{2,1,0:T(8,128)(2,1)}, f32[4,320,768]{2,1,0:T(8,128)}, bf16[4,768,320]{2,1,0:T(8,128)(2,1)}, bf16[4,768,320]{2,1,0:T(8,128)(2,1...) custom-call(s32[2]{0:T(128)} %pad_add_fusion.meta, bf16[4,320,768]{2,1,0:T(8,128)(2,1)} %bitcast.158, ...), custom_call_target="tpu_custom_call" | custom-call | flops 1 | bytes 1 | tf_op jit(solution)/shard_map/pallas_call | solution.py:607
  227.8 15.5 %shard_map.483 = (bf16[4,320,768]{2,1,0:T(8,128)(2,1)}, f32[4,320,768]{2,1,0:T(8,128)}, bf16[4,768,320]{2,1,0:T(8,128)(2,1)}, bf16[4,768,320]{2,1,0:T(8,128)(2,1...) custom-call(s32[2]{0:T(128)} %pad_add_fusion.meta, ...), custom_call_target="tpu_custom_call", output_to_operand_aliasing={{0}: (23, {}), {1}: (24, {}), {2}: (25, {}), {3}: (26, {})} | custom-call | flops 1 | bytes 1 | tf_op jit(solution)/shard_map/pallas_call | solution.py:607
  243.4 23.6 %shard_map.484 = (bf16[5120,384]{1,0:T(8,128)(2,1)}, bf16[5120,384]{1,0:T(8,128)(2,1)}, f32[768,1]{1,0:T(8,128)}) custom-call(s32[2]{0:T(128)} %pad_add_fusion.meta, bf16[4,320,768]{2,1,0:T(8,128)(2,1)} %bitcast.153, bf16[4,320,768]{2,1,0:T(8,128)(2,1)} %get-tuple-element.196.mixed, f32[320,768]{1,0:T(8,128)} %fusion.3.finish, ...), custom_call_target="tpu_custom_call" | custom-call | flops 1 | bytes 1 | tf_op jit(solution)/shard_map/pallas_call | solution.py:536
  267.7 1.3 add_convert_fusion.5
  269.0 1.9 fusion.89
  275.8 7.1 %collective-permute-done.13 = bf16[5120,384]{1,0:T(8,128)(2,1)} collective-permute-done((bf16[5120,384]{1,0:T(8,128)(2,1)}, bf16[5120,384]{1,0:T(8,128)(2,1)}, u32[]{:S(2)}, u32[]{:S(2)}) %collective-permute-start.13) | collective-permute-done | bytes 3932192 | tf_op jit(solution)/shard_map/ppermute | solution.py:632
  282.9 6.7 %add_convert_fusion.1 = bf16[5120,384]{1,0:T(8,128)(2,1)} fusion(bf16[5120,384]{1,0:T(8,128)(2,1)} %collective-permute-done.13, bf16[5120,384]{1,0:T(8,128)(2,1)} %get-tuple-element.343), kind=kLoop, calls=%fused_computation.1 | loop fusion | flops 7864320 | bytes 11796480 | tf_op jit(solution)/shard_map/convert_element_type | solution.py:702
  289.6 5.0 %all-to-all-start.1 = ((bf16[4,1280,384]{2,1,0:T(8,128)(2,1)}), bf16[4,1280,384]{2,1,0:T(8,128)(2,1)}, u32[]{:S(2)}, u32[]{:S(2)}) async-start(bf16[4,1280,384]{2,1,0:T(8,128)(2,1)} %bitcast.164), calls=%async_computation.2 | async-start | bytes 7864320 | tf_op jit(solution)/shard_map/all_to_all | solution.py:636
  294.7 1.7 fusion.103
  296.4 2.3 convolution_add_fusion.6
  298.7 3.8 collective-permute-start.12
  303.2 2.2 fusion.63
  305.5 11.3 %collective-permute-done.12 = bf16[384,384]{1,0:T(8,128)(2,1)S(1)} collective-permute-done((bf16[384,384]{1,0:T(8,128)(2,1)S(1)}, bf16[384,384]{1,0:T(8,128)(2,1)S(1)}, u32[]{:S(2)}, u32[]{:S(2)}) %collective-permute-start.12) | collective-permute-done | bytes 294944 | tf_op jit(solution)/shard_map/ppermute | solution.py:644
  316.7 34.9 %collective-permute-done.11 = bf16[384,384]{1,0:T(8,128)(2,1)S(1)} collective-permute-done((bf16[384,384]{1,0:T(8,128)(2,1)S(1)}, bf16[384,384]{1,0:T(8,128)(2,1)S(1)}, u32[]{:S(2)}, u32[]{:S(2)}) %collective-permute-start.11) | collective-permute-done | bytes 294944 | tf_op jit(solution)/shard_map/ppermute | solution.py:644
  352.4 1.3 select_bitcast_fusion.3
  353.9 2.5 broadcast_in_dim.24
  356.5 5.1 %all-to-all-start.2 = ((bf16[4,1536,384]{2,1,0:T(8,128)(2,1)}), bf16[4,1536,384]{2,1,0:T(8,128)(2,1)}, u32[]{:S(2)}, u32[]{:S(2)}) async-start(bf16[4,1536,384]{2,1,0:T(8,128)(2,1)} %broadcast_in_dim.24), calls=%async_computation.4 | async-start | bytes 9437184 | tf_op jit(solution)/shard_map/all_to_all | solution.py:636
  361.9 2.3 fusion.88
  364.4 2.6 add_convert_fusion.3
  367.1 1.5 collective-permute-start.16
  368.8 2.8 collective-permute-start.14
  371.6 16.2 %shard_map.485 = (f32[80,640,128]{2,1,0:T(8,128)}, f32[16,128]{1,0:T(8,128)}) custom-call(bf16[80,640,128]{2,1,0:T(8,128)(2,1)} %bitcast.147, bf16[32,128]{1,0:T(8,128)(2,1)} %pad_maximum_fusion.4.weight, bf16[10,80,640]{2,1,0:T(8,128)(2,1)} %bitcast.169, bf16[6,80,640]{2,1,0:T(8,128)(2,1)} %bitcast.174), custom_call_target="tpu_custom_call" | custom-call | flops 1 | bytes 1 | tf_op jit(solution)/shard_map/pallas_call | solution.py:287
  387.8 2.2 collective-permute-done.15
  390.1 1.4 collective-permute-start.26
  391.5 3.1 collective-permute-start.24
  394.6 12.2 %shard_map.486 = (f32[80,640,128]{2,1,0:T(8,128)}, f32[16,128]{1,0:T(8,128)}) custom-call(bf16[80,640,128]{2,1,0:T(8,128)(2,1)} %bitcast.148, bf16[32,128]{1,0:T(8,128)(2,1)} %pad_maximum_fusion.4.weight, bf16[10,80,640]{2,1,0:T(8,128)(2,1)} %bitcast.170, bf16[6,80,640]{2,1,0:T(8,128)(2,1)} %bitcast.175, ...), custom_call_target="tpu_custom_call", output_to_operand_aliasing={{0}: (4, {})} | custom-call | flops 1 | bytes 1 | tf_op jit(solution)/shard_map/pallas_call | solution.py:287
  408.3 1.5 convolution_add_fusion.5
  409.9 1.4 collective-permute-start.20
  411.3 3.8 all-to-all-done.2
  416.4 2.3 broadcast_in_dim.26
  418.7 5.2 %all-to-all-start.3 = ((bf16[4,1280,384]{2,1,0:T(8,128)(2,1)}), bf16[4,1280,384]{2,1,0:T(8,128)(2,1)}, u32[]{:S(2)}, u32[]{:S(2)}) async-start(bf16[4,1280,384]{2,1,0:T(8,128)(2,1)} %broadcast_in_dim.26), calls=%async_computation.5 | async-start | bytes 7864320 | tf_op jit(solution)/shard_map/all_to_all | solution.py:636
  424.4 1.4 collective-permute-start.6
  425.8 3.1 collective-permute-start.4
  428.8 1.9 collective-permute-start.18
  430.7 16.1 %collective-permute-done.19 = f32[3392]{0:T(1024)S(1)} collective-permute-done((f32[3392]{0:T(1024)S(1)}, f32[3392]{0:T(1024)S(1)}, u32[]{:S(2)}, u32[]{:S(2)}) %collective-permute-start.19) | collective-permute-done | bytes 13600 | tf_op jit(solution)/shard_map/ppermute | solution.py:644
  446.9 2.7 collective-permute-start.23
  451.3 18.1 %collective-permute-done.23 = f32[3392]{0:T(1024)S(1)} collective-permute-done((f32[3392]{0:T(1024)S(1)}, f32[3392]{0:T(1024)S(1)}, u32[]{:S(2)}, u32[]{:S(2)}) %collective-permute-start.23) | collective-permute-done | bytes 13600 | tf_op jit(solution)/shard_map/ppermute | solution.py:644
  472.1 2.9 convert_element_type.301
  475.3 1.6 pad_maximum_fusion.1
  476.9 1.6 pad_maximum_fusion
  478.5 1.2 fusion.91
  479.7 1.6 slice_bitcast_fusion
  481.3 2.6 bitcast_convert_fusion
  483.9 1.2 fusion.93
  485.2 2.6 fusion.94
  (218 shorter events, 28.8 us)
Async XLA Ops:
  7.2 81.4 %copy-start = (bf16[384,768]{1,0:T(8,128)(2,1)S(1)}, bf16[384,768]{1,0:T(8,128)(2,1)}, u32[]{:S(2)}) copy-start(bf16[384,768]{1,0:T(8,128)(2,1)} %param.36) | copy-start | bytes 1769476
  7.2 100.7 %all-gather.5.cloned.1.call-start = ((), (), s32[]{:S(2)}) async-start(), calls=%async_computation.8 | async-start | bytes 5120000 | tf_op jit(solution)/shard_map/all_gather | solution.py:769
  11.4 11.4 %copy-start.39 = (bf16[384]{0:T(512)(128)(2,1)S(1)}, bf16[384]{0:T(512)(128)(2,1)}, u32[]{:S(2)}) copy-start(bf16[384]{0:T(512)(128)(2,1)} %param.47) | copy-start | bytes 2308
  11.4 11.4 %copy-start.3 = (bf16[1,320,384]{2,1,0:T(8,128)(2,1)S(1)}, bf16[1,320,384]{2,1,0:T(8,128)(2,1)}, u32[]{:S(2)}) copy-start(bf16[1,320,384]{2,1,0:T(8,128)(2,1)} %param.29) | copy-start | bytes 737284
  11.4 11.8 %copy-start.34 = (bf16[768]{0:T(1024)(128)(2,1)S(1)}, bf16[768]{0:T(1024)(128)(2,1)}, u32[]{:S(2)}) copy-start(bf16[768]{0:T(1024)(128)(2,1)} %param.49) | copy-start | bytes 4612
  11.4 11.9 %copy-start.35 = (bf16[768]{0:T(1024)(128)(2,1)S(1)}, bf16[768]{0:T(1024)(128)(2,1)}, u32[]{:S(2)}) copy-start(bf16[768]{0:T(1024)(128)(2,1)} %param.55) | copy-start | bytes 4612
  11.4 11.9 %copy-start.9 = (bf16[384,768]{1,0:T(8,128)(2,1)S(1)}, bf16[384,768]{1,0:T(8,128)(2,1)}, u32[]{:S(2)}) copy-start(bf16[384,768]{1,0:T(8,128)(2,1)} %param.50) | copy-start | bytes 1769476
  22.7 145.3 %all-gather.7.cloned.1.call-start = ((), (), s32[]{:S(2)}) async-start(), calls=%async_computation.9 | async-start | bytes 3072000 | tf_op jit(solution)/shard_map/all_gather | solution.py:769
  27.7 52.1 %copy-start.4 = (f32[320,768]{1,0:T(8,128)S(1)}, f32[320,768]{1,0:T(8,128)}, u32[]{:S(2)}) copy-start(f32[320,768]{1,0:T(8,128)} %fusion.15.lifting.lifting_second) | copy-start | bytes 2949124
  81.2 3.1 copy-start.10
  81.2 3.1 copy-start.8
  81.2 3.1 copy-start.16
  83.4 3.1 copy-start.40
  83.4 3.1 copy-start.38
  83.4 3.7 copy-start.36
  83.4 3.6 copy-start.37
  83.4 3.6 copy-start.21
  85.9 22.0 %collective-permute-start = (bf16[6144,384]{1,0:T(8,128)(2,1)}, bf16[6144,384]{1,0:T(8,128)(2,1)}, u32[]{:S(2)}, u32[]{:S(2)}) collective-permute-start(bf16[6144,384]{1,0:T(8,128)(2,1)} %get-tuple-element.350), channel_id=1, source_target_pairs={{0,1},{1,0},{2,3},{3,2},{4,5},{5,4},{6,7},{7,6},{8,9},{9,8},{10,11... | collective-permute-start | bytes 14155784 | tf_op jit(solution)/shard_map/ppermute | solution.py:632
  107.9 12.7 %collective-permute-start.1 = (bf16[4,2,768,384]{3,2,1,0:T(8,128)(2,1)}, bf16[4,2,768,384]{3,2,1,0:T(8,128)(2,1)}, u32[]{:S(2)}, u32[]{:S(2)}) collective-permute-start(bf16[4,2,768,384]{3,2,1,0:T(8,128)(2,1)} %get-tuple-element.149.mine), channel_id=1, source_target_pairs={{0,1},{1,0},{2,3},{3,2},{4,5},{5,4},{6,7},{7,6},{8,9},{9,8},{10,11... | collective-permute-start | bytes 14155784 | tf_op jit(solution)/shard_map/ppermute | solution.py:632
  115.1 68.7 %all-to-all-start = ((bf16[4,1536,384]{2,1,0:T(8,128)(2,1)}), bf16[4,1536,384]{2,1,0:T(8,128)(2,1)}, u32[]{:S(2)}, u32[]{:S(2)}) async-start(bf16[4,1536,384]{2,1,0:T(8,128)(2,1)} %bitcast.161), calls=%async_computation | async-start | bytes 9437184 | tf_op jit(solution)/shard_map/all_to_all | solution.py:636
  120.5 155.3 %reduce-scatter.3.cloned.1.call-start = ((), (), s32[]{:S(2)}) async-start(), calls=%async_computation.6 | async-start | bytes 5120000 | tf_op jit(solution)/shard_map/reduce_scatter | solution.py:775
  167.8 43.5 %collective-permute-start.2 = (bf16[4,2,480,384]{3,2,1,0:T(8,128)(2,1)}, bf16[4,2,480,384]{3,2,1,0:T(8,128)(2,1)}, u32[]{:S(2)}, u32[]{:S(2)}) collective-permute-start(bf16[4,2,480,384]{3,2,1,0:T(8,128)(2,1)} %get-tuple-element.181), channel_id=1, source_target_pairs={{0,1},{1,0},{2,3},{3,2},{4,5},{5,4},{6,7},{7,6},{8,9},{9,8},{10,11... | collective-permute-start | bytes 8847368 | tf_op jit(solution)/shard_map/ppermute | solution.py:632
  168.0 183.6 %reduce-scatter.5.cloned.1.call-start = ((), (), s32[]{:S(2)}) async-start(), calls=%async_computation.7 | async-start | bytes 3072000 | tf_op jit(solution)/shard_map/reduce_scatter | solution.py:775
  203.1 8.2 %collective-permute-start.3 = (bf16[4,2,288,384]{3,2,1,0:T(8,128)(2,1)}, bf16[4,2,288,384]{3,2,1,0:T(8,128)(2,1)S(1)}, u32[]{:S(2)}, u32[]{:S(2)}) collective-permute-start(bf16[4,2,288,384]{3,2,1,0:T(8,128)(2,1)} %get-tuple-element.182), channel_id=1, source_target_pairs={{0,1},{1,0},{2,3},{3,2},{4,5},{5,4},{6,7},{7,6},{8,9},{9,8},{10,11... | collective-permute-start | bytes 5308424 | tf_op jit(solution)/shard_map/ppermute | solution.py:632
  205.9 61.1 %collective-permute-start.9 = (bf16[384,384]{1,0:T(8,128)(2,1)}, bf16[384,384]{1,0:T(8,128)(2,1)S(1)}, u32[]{:S(2)}, u32[]{:S(2)}) collective-permute-start(bf16[384,384]{1,0:T(8,128)(2,1)} %get-tuple-element.331), channel_id=1, source_target_pairs={{0,6},{2,4},{4,2},{6,0},{1,7},{3,5},{5,3},{7,1},{8,14},{10,12},{12... | collective-permute-start | bytes 884744 | tf_op jit(solution)/shard_map/ppermute | solution.py:644
  210.8 56.2 %collective-permute-start.8 = (bf16[384,384]{1,0:T(8,128)(2,1)}, bf16[384,384]{1,0:T(8,128)(2,1)}, u32[]{:S(2)}, u32[]{:S(2)}) collective-permute-start(bf16[384,384]{1,0:T(8,128)(2,1)} %get-tuple-element.332), channel_id=1, source_target_pairs={{0,4},{2,6},{4,0},{6,2},{1,5},{3,7},{5,1},{7,3},{8,12},{10,14},{12... | collective-permute-start | bytes 884744 | tf_op jit(solution)/shard_map/ppermute | solution.py:644
  210.8 56.2 %collective-permute-start.7 = (bf16[384,384]{1,0:T(8,128)(2,1)S(1)}, bf16[384,384]{1,0:T(8,128)(2,1)}, u32[]{:S(2)}, u32[]{:S(2)}) collective-permute-start(bf16[384,384]{1,0:T(8,128)(2,1)S(1)} %get-tuple-element.333), channel_id=1, source_target_pairs={{0,2},{2,0},{4,6},{6,4},{1,3},{3,1},{5,7},{7,5},{8,10},{10,8},{12,... | collective-permute-start | bytes 884744 | tf_op jit(solution)/shard_map/ppermute | solution.py:644
  243.3 25.6 %copy-start.1 = (f32[320,768]{1,0:T(8,128)S(1)}, f32[320,768]{1,0:T(8,128)}, u32[]{:S(2)}) copy-start(f32[320,768]{1,0:T(8,128)} %fusion.3.finish) | copy-start | bytes 2949124
  243.4 25.6 %copy-start.2 = (f32[320,768]{1,0:T(8,128)S(1)}, f32[320,768]{1,0:T(8,128)}, u32[]{:S(2)}) copy-start(f32[320,768]{1,0:T(8,128)} %fusion.7.lifting.lifting_first) | copy-start | bytes 2949124
  243.4 25.6 %copy-start.14 = (f32[320,768]{1,0:T(8,128)S(1)}, f32[320,768]{1,0:T(8,128)}, u32[]{:S(2)}) copy-start(f32[320,768]{1,0:T(8,128)} %get-tuple-element.193) | copy-start | bytes 2949124
  243.4 25.6 %copy-start.15 = (f32[320,768]{1,0:T(8,128)S(1)}, f32[320,768]{1,0:T(8,128)}, u32[]{:S(2)}) copy-start(f32[320,768]{1,0:T(8,128)} %get-tuple-element.189) | copy-start | bytes 2949124
  275.8 7.1 %collective-permute-start.13 = (bf16[5120,384]{1,0:T(8,128)(2,1)}, bf16[5120,384]{1,0:T(8,128)(2,1)}, u32[]{:S(2)}, u32[]{:S(2)}) collective-permute-start(bf16[5120,384]{1,0:T(8,128)(2,1)} %get-tuple-element.344), channel_id=1, source_target_pairs={{0,1},{1,0},{2,3},{3,2},{4,5},{5,4},{6,7},{7,6},{8,9},{9,8},{10,11... | collective-permute-start | bytes 11796488 | tf_op jit(solution)/shard_map/ppermute | solution.py:632
  289.6 6.9 %copy-start.7 = (f32[320,768]{1,0:T(8,128)S(1)}, f32[320,768]{1,0:T(8,128)}, u32[]{:S(2)}) copy-start(f32[320,768]{1,0:T(8,128)} %get-tuple-element.139) | copy-start | bytes 2949124
  289.6 62.1 %all-to-all-start.1 = ((bf16[4,1280,384]{2,1,0:T(8,128)(2,1)}), bf16[4,1280,384]{2,1,0:T(8,128)(2,1)}, u32[]{:S(2)}, u32[]{:S(2)}) async-start(bf16[4,1280,384]{2,1,0:T(8,128)(2,1)} %bitcast.164), calls=%async_computation.2 | async-start | bytes 7864320 | tf_op jit(solution)/shard_map/all_to_all | solution.py:636
  294.7 8.5 %copy-start.19 = (bf16[384,768]{1,0:T(8,128)(2,1)S(1)}, bf16[384,768]{1,0:T(8,128)(2,1)}, u32[]{:S(2)}) copy-start(bf16[384,768]{1,0:T(8,128)(2,1)} %param.34) | copy-start | bytes 1769476
  298.7 18.0 %collective-permute-start.12 = (bf16[384,384]{1,0:T(8,128)(2,1)S(1)}, bf16[384,384]{1,0:T(8,128)(2,1)S(1)}, u32[]{:S(2)}, u32[]{:S(2)}) collective-permute-start(bf16[384,384]{1,0:T(8,128)(2,1)S(1)} %add_convert_fusion.5), channel_id=1, source_target_pairs={{0,6},{2,4},{4,2},{6,0},{1,7},{3,5},{5,3},{7,1},{8,14},{10,12},{12... | collective-permute-start | bytes 884744 | tf_op jit(solution)/shard_map/ppermute | solution.py:644
  302.5 49.1 %collective-permute-start.11 = (bf16[384,384]{1,0:T(8,128)(2,1)S(1)}, bf16[384,384]{1,0:T(8,128)(2,1)S(1)}, u32[]{:S(2)}, u32[]{:S(2)}) collective-permute-start(bf16[384,384]{1,0:T(8,128)(2,1)S(1)} %add_convert_fusion.5), channel_id=1, source_target_pairs={{0,4},{2,6},{4,0},{6,2},{1,5},{3,7},{5,1},{7,3},{8,12},{10,14},{12... | collective-permute-start | bytes 884744 | tf_op jit(solution)/shard_map/ppermute | solution.py:644
  302.5 49.1 %collective-permute-start.10 = (bf16[384,384]{1,0:T(8,128)(2,1)S(1)}, bf16[384,384]{1,0:T(8,128)(2,1)S(1)}, u32[]{:S(2)}, u32[]{:S(2)}) collective-permute-start(bf16[384,384]{1,0:T(8,128)(2,1)S(1)} %add_convert_fusion.5), channel_id=1, source_target_pairs={{0,2},{2,0},{4,6},{6,4},{1,3},{3,1},{5,7},{7,5},{8,10},{10,8},{12,... | collective-permute-start | bytes 884744 | tf_op jit(solution)/shard_map/ppermute | solution.py:644
  316.7 34.9 %copy-start.28 = (bf16[384,384]{1,0:T(8,128)(2,1)}, bf16[384,384]{1,0:T(8,128)(2,1)S(1)}, u32[]{:S(2)}) copy-start(bf16[384,384]{1,0:T(8,128)(2,1)S(1)} %collective-permute-done.12) | copy-start | bytes 884740
  356.5 5.2 %copy-start.27 = (f32[768,1]{1,0:T(8,128)S(1)}, f32[768,1]{1,0:T(8,128)}, u32[]{:S(2)}) copy-start(f32[768,1]{1,0:T(8,128)} %get-tuple-element.231) | copy-start | bytes 9220
  356.5 5.4 %copy-start.24 = (bf16[320,768]{1,0:T(8,128)(2,1)S(1)}, bf16[320,768]{1,0:T(8,128)(2,1)}, u32[]{:S(2)}) copy-start(bf16[320,768]{1,0:T(8,128)(2,1)} %copy-done.23) | copy-start | bytes 1474564
  356.5 5.4 %copy-start.25 = (f32[320,384]{1,0:T(8,128)S(1)}, f32[320,384]{1,0:T(8,128)}, u32[]{:S(2)}) copy-start(f32[320,384]{1,0:T(8,128)} %convolution_add_fusion.6) | copy-start | bytes 1474564
  356.5 58.6 %all-to-all-start.2 = ((bf16[4,1536,384]{2,1,0:T(8,128)(2,1)}), bf16[4,1536,384]{2,1,0:T(8,128)(2,1)}, u32[]{:S(2)}, u32[]{:S(2)}) async-start(bf16[4,1536,384]{2,1,0:T(8,128)(2,1)} %broadcast_in_dim.24), calls=%async_computation.4 | async-start | bytes 9437184 | tf_op jit(solution)/shard_map/all_to_all | solution.py:636
  367.1 20.7 %collective-permute-start.16 = (bf16[320,384]{1,0:T(8,128)(2,1)S(1)}, bf16[320,384]{1,0:T(8,128)(2,1)S(1)}, u32[]{:S(2)}, u32[]{:S(2)}) collective-permute-start(bf16[320,384]{1,0:T(8,128)(2,1)S(1)} %get-tuple-element.339), channel_id=1, source_target_pairs={{0,6},{2,4},{4,2},{6,0},{1,7},{3,5},{5,3},{7,1},{8,14},{10,12},{12... | collective-permute-start | bytes 737288 | tf_op jit(solution)/shard_map/ppermute | solution.py:644
  368.6 21.4 %collective-permute-start.15 = (bf16[320,384]{1,0:T(8,128)(2,1)S(1)}, bf16[320,384]{1,0:T(8,128)(2,1)S(1)}, u32[]{:S(2)}, u32[]{:S(2)}) collective-permute-start(bf16[320,384]{1,0:T(8,128)(2,1)S(1)} %get-tuple-element.340), channel_id=1, source_target_pairs={{0,4},{2,6},{4,0},{6,2},{1,5},{3,7},{5,1},{7,3},{8,12},{10,14},{12... | collective-permute-start | bytes 737288 | tf_op jit(solution)/shard_map/ppermute | solution.py:644
  368.8 21.2 %collective-permute-start.14 = (bf16[320,384]{1,0:T(8,128)(2,1)S(1)}, bf16[320,384]{1,0:T(8,128)(2,1)S(1)}, u32[]{:S(2)}, u32[]{:S(2)}) collective-permute-start(bf16[320,384]{1,0:T(8,128)(2,1)S(1)} %get-tuple-element.341), channel_id=1, source_target_pairs={{0,2},{2,0},{4,6},{6,4},{1,3},{3,1},{5,7},{7,5},{8,10},{10,8},{12,... | collective-permute-start | bytes 737288 | tf_op jit(solution)/shard_map/ppermute | solution.py:644
  390.1 21.1 %collective-permute-start.26 = (bf16[320,384]{1,0:T(8,128)(2,1)S(1)}, bf16[320,384]{1,0:T(8,128)(2,1)S(1)}, u32[]{:S(2)}, u32[]{:S(2)}) collective-permute-start(bf16[320,384]{1,0:T(8,128)(2,1)S(1)} %add_convert_fusion.6), channel_id=1, source_target_pairs={{0,6},{2,4},{4,2},{6,0},{1,7},{3,5},{5,3},{7,1},{8,14},{10,12},{12... | collective-permute-start | bytes 737288 | tf_op jit(solution)/shard_map/ppermute | solution.py:644
  391.5 19.8 %collective-permute-start.25 = (bf16[320,384]{1,0:T(8,128)(2,1)S(1)}, bf16[320,384]{1,0:T(8,128)(2,1)}, u32[]{:S(2)}, u32[]{:S(2)}) collective-permute-start(bf16[320,384]{1,0:T(8,128)(2,1)S(1)} %add_convert_fusion.6), channel_id=1, source_target_pairs={{0,4},{2,6},{4,0},{6,2},{1,5},{3,7},{5,1},{7,3},{8,12},{10,14},{12... | collective-permute-start | bytes 737288 | tf_op jit(solution)/shard_map/ppermute | solution.py:644
  391.5 19.8 %collective-permute-start.24 = (bf16[320,384]{1,0:T(8,128)(2,1)S(1)}, bf16[320,384]{1,0:T(8,128)(2,1)}, u32[]{:S(2)}, u32[]{:S(2)}) collective-permute-start(bf16[320,384]{1,0:T(8,128)(2,1)S(1)} %add_convert_fusion.6), channel_id=1, source_target_pairs={{0,2},{2,0},{4,6},{6,4},{1,3},{3,1},{5,7},{7,5},{8,10},{10,8},{12,... | collective-permute-start | bytes 737288 | tf_op jit(solution)/shard_map/ppermute | solution.py:644
  394.6 12.2 %copy-start.32 = (bf16[128,16]{0,1:T(8,128)(2,1)S(1)}, bf16[128,16]{0,1:T(8,128)(2,1)}, u32[]{:S(2)}) copy-start(bf16[128,16]{0,1:T(8,128)(2,1)} %param.44) | copy-start | bytes 12292
  394.6 12.2 %copy-start.33 = (f32[16,128]{1,0:T(8,128)S(1)}, f32[16,128]{1,0:T(8,128)}, u32[]{:S(2)}) copy-start(f32[16,128]{1,0:T(8,128)} %get-tuple-element.232) | copy-start | bytes 24580
  394.6 13.7 %copy-start.26 = (f32[320,384]{1,0:T(8,128)S(1)}, f32[320,384]{1,0:T(8,128)}, u32[]{:S(2)}) copy-start(f32[320,384]{1,0:T(8,128)} %get-tuple-element.307) | copy-start | bytes 1474564
  408.2 1.6 collective-permute-start.17
  409.9 18.9 %collective-permute-start.20 = (f32[3392]{0:T(1024)S(1)}, f32[3392]{0:T(1024)S(1)}, u32[]{:S(2)}, u32[]{:S(2)}) collective-permute-start(f32[3392]{0:T(1024)S(1)} %add.292), channel_id=1, source_target_pairs={{0,6},{2,4},{4,2},{6,0},{1,7},{3,5},{5,3},{7,1},{8,14},{10,12},{12... | collective-permute-start | bytes 40712 | tf_op jit(solution)/shard_map/ppermute | solution.py:644
  418.7 5.2 %copy-start.22 = (bf16[384,768]{1,0:T(8,128)(2,1)S(1)}, bf16[384,768]{1,0:T(8,128)(2,1)}, u32[]{:S(2)}) copy-start(bf16[384,768]{1,0:T(8,128)(2,1)} %param.45) | copy-start | bytes 1769476
  418.7 62.6 %all-to-all-start.3 = ((bf16[4,1280,384]{2,1,0:T(8,128)(2,1)}), bf16[4,1280,384]{2,1,0:T(8,128)(2,1)}, u32[]{:S(2)}, u32[]{:S(2)}) async-start(bf16[4,1280,384]{2,1,0:T(8,128)(2,1)} %broadcast_in_dim.26), calls=%async_computation.5 | async-start | bytes 7864320 | tf_op jit(solution)/shard_map/all_to_all | solution.py:636
  424.4 25.8 %collective-permute-start.6 = (bf16[320,384]{1,0:T(8,128)(2,1)S(1)}, bf16[320,384]{1,0:T(8,128)(2,1)S(1)}, u32[]{:S(2)}, u32[]{:S(2)}) collective-permute-start(bf16[320,384]{1,0:T(8,128)(2,1)S(1)} %fusion.16), channel_id=1, source_target_pairs={{0,6},{2,4},{4,2},{6,0},{1,7},{3,5},{5,3},{7,1},{8,14},{10,12},{12... | collective-permute-start | bytes 737288 | tf_op jit(solution)/shard_map/ppermute | solution.py:644
  425.7 24.7 %collective-permute-start.5 = (bf16[320,384]{1,0:T(8,128)(2,1)S(1)}, bf16[320,384]{1,0:T(8,128)(2,1)S(1)}, u32[]{:S(2)}, u32[]{:S(2)}) collective-permute-start(bf16[320,384]{1,0:T(8,128)(2,1)S(1)} %fusion.16), channel_id=1, source_target_pairs={{0,4},{2,6},{4,0},{6,2},{1,5},{3,7},{5,1},{7,3},{8,12},{10,14},{12... | collective-permute-start | bytes 737288 | tf_op jit(solution)/shard_map/ppermute | solution.py:644
  425.8 24.7 %collective-permute-start.4 = (bf16[320,384]{1,0:T(8,128)(2,1)S(1)}, bf16[320,384]{1,0:T(8,128)(2,1)S(1)}, u32[]{:S(2)}, u32[]{:S(2)}) collective-permute-start(bf16[320,384]{1,0:T(8,128)(2,1)S(1)} %fusion.16), channel_id=1, source_target_pairs={{0,2},{2,0},{4,6},{6,4},{1,3},{3,1},{5,7},{7,5},{8,10},{10,8},{12,... | collective-permute-start | bytes 737288 | tf_op jit(solution)/shard_map/ppermute | solution.py:644
  428.8 18.0 %collective-permute-start.19 = (f32[3392]{0:T(1024)S(1)}, f32[3392]{0:T(1024)S(1)}, u32[]{:S(2)}, u32[]{:S(2)}) collective-permute-start(f32[3392]{0:T(1024)S(1)} %add.292), channel_id=1, source_target_pairs={{0,4},{2,6},{4,0},{6,2},{1,5},{3,7},{5,1},{7,3},{8,12},{10,14},{12... | collective-permute-start | bytes 40712 | tf_op jit(solution)/shard_map/ppermute | solution.py:644
  428.8 18.0 %collective-permute-start.18 = (f32[3392]{0:T(1024)S(1)}, f32[3392]{0:T(1024)S(1)}, u32[]{:S(2)}, u32[]{:S(2)}) collective-permute-start(f32[3392]{0:T(1024)S(1)} %add.292), channel_id=1, source_target_pairs={{0,2},{2,0},{4,6},{6,4},{1,3},{3,1},{5,7},{7,5},{8,10},{10,8},{12,... | collective-permute-start | bytes 40712 | tf_op jit(solution)/shard_map/ppermute | solution.py:644
  446.9 22.5 %collective-permute-start.23 = (f32[3392]{0:T(1024)S(1)}, f32[3392]{0:T(1024)S(1)}, u32[]{:S(2)}, u32[]{:S(2)}) collective-permute-start(f32[3392]{0:T(1024)S(1)} %add_add_fusion.1), channel_id=1, source_target_pairs={{0,24},{8,16},{16,8},{24,0},{1,25},{9,17},{17,9},{25,1},{2,26},{10... | collective-permute-start | bytes 40712 | tf_op jit(solution)/shard_map/ppermute | solution.py:644
  449.6 19.9 %collective-permute-start.22 = (f32[3392]{0:T(1024)S(1)}, f32[3392]{0:T(1024)S(1)}, u32[]{:S(2)}, u32[]{:S(2)}) collective-permute-start(f32[3392]{0:T(1024)S(1)} %add_add_fusion.1), channel_id=1, source_target_pairs={{0,16},{8,24},{16,0},{24,8},{1,17},{9,25},{17,1},{25,9},{2,18},{10... | collective-permute-start | bytes 40712 | tf_op jit(solution)/shard_map/ppermute | solution.py:644
  450.1 19.3 %collective-permute-start.21 = (f32[3392]{0:T(1024)S(1)}, f32[3392]{0:T(1024)S(1)}, u32[]{:S(2)}, u32[]{:S(2)}) collective-permute-start(f32[3392]{0:T(1024)S(1)} %add_add_fusion.1), channel_id=1, source_target_pairs={{0,8},{8,0},{16,24},{24,16},{1,9},{9,1},{17,25},{25,17},{2,10},{10... | collective-permute-start | bytes 40712 | tf_op jit(solution)/shard_map/ppermute | solution.py:644
  (12 other events, 21.7 us)
Sparse Core Ops, SparseCore 0:
  22.8 81.8 all-gather.4
  108.1 55.0 all-gather.6
  168.1 96.8 reduce-scatter.2
  275.9 70.1 reduce-scatter.4

commit v4 on v3

--- a/solution.py
+++ b/solution.py
@@ -492,18 +492,27 @@
     pack_mine, pack_other, bias_sum,
     query_sum, key_sum, value_sum, gate_sum, output_sum,
 ):
-    rows = cotangent.shape[1]
+    count, rows, width = cotangent.shape
     sample = pl.program_id(0)
-    delta_query = whole(query_a, query_b)
-    branch = row_valid(meta, rows) * cotangent[0].astype(f32)
-    lifted = (finish[...] * branch).astype(bf16)
+
+    def turned(*parts):
+        return jnp.concatenate(
+            [jnp.concatenate([part[i] for part in parts], axis=0) for i in range(count)], axis=1
+        )
+
+    delta_query = turned(query_a, query_b)
+    mixed_rows = mixed[...].reshape(count * rows, width)
+    masked = finish[...] * row_valid(meta, rows)
+    lifted = jnp.concatenate(
+        [(masked * cotangent[i].astype(f32)).astype(bf16) for i in range(count)], axis=0
+    )
 
     def collect(first):
-        put(first, query_sum, dot(delta_query, mixed[0], 1, 0))
-        put(first, key_sum, dot(key[0], mixed[0], 1, 0))
-        put(first, value_sum, dot(value[0], mixed[0], 1, 0))
-        put(first, gate_sum, dot(whole(gate_a, gate_b), mixed[0], 1, 0))
-        put(first, output_sum, dot(whole(gated_a, gated_b), lifted, 1, 0))
+        put(first, query_sum, dot(delta_query, mixed_rows, 1, 0))
+        put(first, key_sum, dot(turned(key), mixed_rows, 1, 0))
+        put(first, value_sum, dot(turned(value), mixed_rows, 1, 0))
+        put(first, gate_sum, dot(turned(gate_a, gate_b), mixed_rows, 1, 0))
+        put(first, output_sum, dot(turned(gated_a, gated_b), lifted, 1, 0))
         put(first, bias_sum, jnp.sum(delta_query.astype(f32), axis=1, keepdims=True))
 
     @pl.when(sample == 0)
@@ -532,14 +541,19 @@
 def weight_sums(meta, cotangent, mixed, finish, turned, pack_rows):
     samples, rows, width = cotangent.shape
     pack = (pack_rows, width // 2)
-    natural = by_sample((rows, width))
+    count = 2 if samples % 2 == 0 else 1
+
+    def several(shape):
+        return pl.BlockSpec((count,) + shape, lambda s, *_: (s,) + (0,) * len(shape))
+
+    natural = several((rows, width))
     return pl.pallas_call(
         weights_kernel,
         grid_spec=pltpu.PrefetchScalarGridSpec(
             num_scalar_prefetch=1,
-            grid=(samples,),
+            grid=(samples // count,),
             in_specs=[natural, natural, fixed((rows, width))]
-            + [by_sample(array.shape[1:]) for array in turned],
+            + [several(array.shape[1:]) for array in turned],
             out_specs=[fixed(pack)] * 2 + [fixed((width, 1))],
             scratch_shapes=[pltpu.VMEM((width, width), f32)] * 5,
         ),
@@ -1016,13 +1030,6 @@
             axis=1,
         )
     )
-    small = summed(spread_apart(small, "cplx"))
-    late = late.result()[0]
-    early = early.result()[0]
-    ends, place = [], 0
-    for vector in vectors:
-        ends.append(small[place : place + vector.shape[0] // 2])
-        place += vector.shape[0] // 2
     def unpack(total, sizes):
         arrays, start = [], 0
         for depth, columns in sizes:
@@ -1039,10 +1046,18 @@
             start += depth * blocks
         return arrays
 
-    swish_total, linear_total, down_total, scale_second, shift_second, closing_total = unpack(
-        early,
+    early_totals = unpack(
+        early.result()[0],
         ((width, inner // 2), (width, inner // 2), (inner, half)) + ((narrow, half),) * 3,
     )
+    small, *early_totals = tied(small, *early_totals)
+    swish_total, linear_total, down_total, scale_second, shift_second, closing_total = early_totals
+    small = summed(spread_apart(small, "cplx"))
+    late = late.result()[0]
+    ends, place = [], 0
+    for vector in vectors:
+        ends.append(small[place : place + vector.shape[0] // 2])
+        place += vector.shape[0] // 2
     query_total, key_total, value_total, gate_total, output_total, *others = unpack(
         late, ((width, half),) * 5 + ((narrow, half),) * 3
     )

time: 499 us -> 488 us (0.978)
  waiting for transfers between devices: 93.6 us -> 84 us
    ppermute x21, waiting for transfers between devices: 82.6 us -> 76.1 us  [exchange(): lax.ppermute(array, axis, [(i, i ^ bit) for i in range(lax.axis_size(axis...]
  transfers between devices with their start and end apart: 35 -> 35, of which waited for: 7 -> 8; matrix products, arithmetic and copies ran while one was open for 15% -> 16% of each run, Pallas kernels for 46% -> 47%
where the time goes in v4:
time: 488 us; the launch traced here: 483 us
  Pallas kernels  239 us (49%)
  waiting for transfers between devices  84 us (17%)
  starting transfers between devices  53.2 us (11%)
  other arithmetic  42.5 us (9%)
  local copies, waits for them, and re-layouts  26.3 us (5%)
  matrix products  22.8 us (5%)
  between operations  15.5 us (3%)
    pallas_call x4, Pallas kernels, attention(): pl.pallas_call(functools.partial(attention_kernel, step=step), grid_spec=...  78.4 us
    ppermute x21, waiting for transfers between devices, exchange(): lax.ppermute(array, axis, [(i, i ^ bit) for i in range(lax.axis_size(axis...  76.1 us
    pallas_call x1, Pallas kernels, transition(): pl.pallas_call(transition_kernel, grid_spec=pltpu.PrefetchScalarGridSpec(...  51.7 us
    ppermute x21, starting transfers between devices, exchange(): lax.ppermute(array, axis, [(i, i ^ bit) for i in range(lax.axis_size(axis...  31.2 us
    pallas_call x2, Pallas kernels, rows_back(): pl.pallas_call(rows_kernel, grid_spec=pltpu.PrefetchScalarGridSpec(num_sc...  30.9 us
    pallas_call x2, Pallas kernels, pair_backward(): pl.pallas_call(functools.partial(pair_backward_kernel, block=block, heads...  28.4 us
    pallas_call x1, Pallas kernels, weight_sums(): pl.pallas_call(weights_kernel, grid_spec=pltpu.PrefetchScalarGridSpec(num...  22 us
    all_to_all x4, starting transfers between devices, traded(): return lax.all_to_all(array, axis, 0, 0)  20.5 us
  transfers between devices with their start and end apart: 35, of which 8 were waited for; matrix products, arithmetic and copies ran while one was open for 16% of the time, Pallas kernels for 47%

profile of v4, /device:TPU:0, one launch (start us, length us, event | category | flops | bytes accessed | tf_op | source)
XLA Modules:
  0.0 483.5 jit_solution(7650474927923085296)
XLA Ops:
  11.4 11.3 %shard_map.475 = (bf16[10,80,640]{2,1,0:T(8,128)(2,1)}, bf16[6,80,640]{2,1,0:T(8,128)(2,1)}) custom-call(bf16[80,640,128]{2,1,0:T(8,128)(2,1)} %bitcast.146, bf16[32,128]{1,0:T(8,128)(2,1)} %pad_maximum_fusion.4.weight), custom_call_target="tpu_custom_call" | custom-call | flops 1 | bytes 1 | tf_op jit(solution)/shard_map/pallas_call | solution.py:233
  23.3 1.4 fusion.85.shifting
  24.7 1.5 fusion.15.lifting.lifting_second
  26.2 1.4 fusion.11.closing
  27.7 51.7 %shard_map.476 = (f32[4,320,768]{2,1,0:T(8,128)}, f32[4,320,768]{2,1,0:T(8,128)}, f32[320,768]{1,0:T(8,128)}, f32[320,768]{1,0:T(8,128)}, f32[320,768]{1,0:T(8,1...) custom-call(s32[2]{0:T(128)} %pad_add_fusion.meta, bf16[4,320,768]{2,1,0:T(8,128)(2,1)} %bitcast.156, ...), custom_call_target="tpu_custom_call" | custom-call | flops 1 | bytes 1 | tf_op jit(solution)/shard_map/pallas_call | solution.py:455
  79.4 1.5 fusion.33
  86.8 1.4 fusion.3.finish
  88.2 1.4 fusion.79.shifting
  89.6 1.5 fusion.7.lifting.lifting_first
  91.1 16.4 %shard_map.477 = (bf16[4,768,320]{2,1,0:T(8,128)(2,1)}, bf16[4,2,768,384]{3,2,1,0:T(8,128)(2,1)}, f32[4,768,320]{2,1,0:T(8,128)}, f32[4,768,320]{2,1,0:T(8,128)}, bf16[4,320,768]{2,1,0:T(8,128)(2,1)}) custom-call(s32[2]{0:T(128)} %pad_add_fusion.meta, bf16[4,320,768]{2,1,0:T(8,128)(2,1)} %bitcast.157, bf16[4,320,768]{2,1,0:T(8,128)(2,1)} %bitcast.150, ...), custom_call_target="tpu_custom_call" | custom-call | flops 1 | bytes 1 | tf_op jit(solution)/shard_map/pallas_call | solution.py:371
  107.6 7.1 %add_convert_fusion = bf16[6144,384]{1,0:T(8,128)(2,1)} fusion(bf16[6144,384]{1,0:T(8,128)(2,1)} %collective-permute-done, bf16[6144,384]{1,0:T(8,128)(2,1)} %get-tuple-element.148), kind=kLoop, calls=%fused_computation | loop fusion | flops 9437184 | bytes 14155776 | tf_op jit(solution)/shard_map/convert_element_type | solution.py:716
  114.7 5.4 %all-to-all-start = ((bf16[4,1536,384]{2,1,0:T(8,128)(2,1)}), bf16[4,1536,384]{2,1,0:T(8,128)(2,1)}, u32[]{:S(2)}, u32[]{:S(2)}) async-start(bf16[4,1536,384]{2,1,0:T(8,128)(2,1)} %bitcast.161), calls=%async_computation | async-start | bytes 9437184 | tf_op jit(solution)/shard_map/all_to_all | solution.py:650
  120.2 23.6 %shard_map.479 = (bf16[4,480,320]{2,1,0:T(8,128)(2,1)}, bf16[4,480,320]{2,1,0:T(8,128)(2,1)}, bf16[4,480,320]{2,1,0:T(8,128)(2,1)}, f32[4,2,480,320]{3,2,1,0:T(8...) custom-call(s32[2]{0:T(128)} %pad_add_fusion.meta, ...), custom_call_target="tpu_custom_call" | custom-call | flops 1 | bytes 1 | tf_op jit(solution)/shard_map/pallas_call | solution.py:163
  143.8 23.7 %shard_map.480 = (bf16[4,480,320]{2,1,0:T(8,128)(2,1)}, bf16[4,480,320]{2,1,0:T(8,128)(2,1)}, bf16[4,480,320]{2,1,0:T(8,128)(2,1)}, f32[4,2,480,320]{3,2,1,0:T(8...) custom-call(s32[2]{0:T(128)} %pad_add_fusion.meta, ...), custom_call_target="tpu_custom_call", output_to_operand_aliasing={{0}: (7, {}), {1}: (8, {}), {2}: (9, {}), {3}: (10, {}), {4... | custom-call | flops 1 | bytes 1 | tf_op jit(solution)/shard_map/pallas_call | solution.py:163
  167.7 15.7 %shard_map.478 = (bf16[4,288,320]{2,1,0:T(8,128)(2,1)}, bf16[4,288,320]{2,1,0:T(8,128)(2,1)}, bf16[4,288,320]{2,1,0:T(8,128)(2,1)}, f32[4,2,288,320]{3,2,1,0:T(8...) custom-call(s32[2]{0:T(128)} %pad_add_fusion.meta, ...), custom_call_target="tpu_custom_call" | custom-call | flops 1 | bytes 1 | tf_op jit(solution)/shard_map/pallas_call | solution.py:163
  183.4 3.9 add_convert_fusion.2
  187.3 15.5 %shard_map.481 = (bf16[4,288,320]{2,1,0:T(8,128)(2,1)}, bf16[4,288,320]{2,1,0:T(8,128)(2,1)}, bf16[4,288,320]{2,1,0:T(8,128)(2,1)}, f32[4,2,288,320]{3,2,1,0:T(8...) custom-call(s32[2]{0:T(128)} %pad_add_fusion.meta, ...), custom_call_target="tpu_custom_call", output_to_operand_aliasing={{0}: (7, {}), {1}: (8, {}), {2}: (9, {}), {3}: (10, {}), {4... | custom-call | flops 1 | bytes 1 | tf_op jit(solution)/shard_map/pallas_call | solution.py:163
  203.4 2.2 dynamic-slice_bitcast_fusion
  205.5 4.9 %collective-permute-start.9 = (bf16[384,384]{1,0:T(8,128)(2,1)}, bf16[384,384]{1,0:T(8,128)(2,1)S(1)}, u32[]{:S(2)}, u32[]{:S(2)}) collective-permute-start(bf16[384,384]{1,0:T(8,128)(2,1)} %get-tuple-element.345), channel_id=1, source_target_pairs={{0,6},{2,4},{4,2},{6,0},{1,7},{3,5},{5,3},{7,1},{8,14},{10,12},{12... | collective-permute-start | bytes 884744 | tf_op jit(solution)/shard_map/ppermute | solution.py:658
  212.3 15.2 %shard_map.482 = (bf16[4,320,768]{2,1,0:T(8,128)(2,1)}, f32[4,320,768]{2,1,0:T(8,128)}, bf16[4,768,320]{2,1,0:T(8,128)(2,1)}, bf16[4,768,320]{2,1,0:T(8,128)(2,1...) custom-call(s32[2]{0:T(128)} %pad_add_fusion.meta, bf16[4,320,768]{2,1,0:T(8,128)(2,1)} %bitcast.158, ...), custom_call_target="tpu_custom_call" | custom-call | flops 1 | bytes 1 | tf_op jit(solution)/shard_map/pallas_call | solution.py:621
  227.5 15.7 %shard_map.483 = (bf16[4,320,768]{2,1,0:T(8,128)(2,1)}, f32[4,320,768]{2,1,0:T(8,128)}, bf16[4,768,320]{2,1,0:T(8,128)(2,1)}, bf16[4,768,320]{2,1,0:T(8,128)(2,1...) custom-call(s32[2]{0:T(128)} %pad_add_fusion.meta, ...), custom_call_target="tpu_custom_call", output_to_operand_aliasing={{0}: (23, {}), {1}: (24, {}), {2}: (25, {}), {3}: (26, {})} | custom-call | flops 1 | bytes 1 | tf_op jit(solution)/shard_map/pallas_call | solution.py:621
  243.3 22.0 %shard_map.484 = (bf16[5120,384]{1,0:T(8,128)(2,1)}, bf16[5120,384]{1,0:T(8,128)(2,1)}, f32[768,1]{1,0:T(8,128)}) custom-call(s32[2]{0:T(128)} %pad_add_fusion.meta, bf16[4,320,768]{2,1,0:T(8,128)(2,1)} %bitcast.153, bf16[4,320,768]{2,1,0:T(8,128)(2,1)} %get-tuple-element.203.mixed, f32[320,768]{1,0:T(8,128)} %fusion.3.finish, ...), custom_call_target="tpu_custom_call" | custom-call | flops 1 | bytes 1 | tf_op jit(solution)/shard_map/pallas_call | solution.py:550
  266.1 1.3 add_convert_fusion.5
  267.4 1.9 fusion.89
  274.2 7.1 %collective-permute-done.13 = bf16[5120,384]{1,0:T(8,128)(2,1)} collective-permute-done((bf16[5120,384]{1,0:T(8,128)(2,1)}, bf16[5120,384]{1,0:T(8,128)(2,1)}, u32[]{:S(2)}, u32[]{:S(2)}) %collective-permute-start.13) | collective-permute-done | bytes 3932192 | tf_op jit(solution)/shard_map/ppermute | solution.py:646
  281.3 6.6 %add_convert_fusion.1 = bf16[5120,384]{1,0:T(8,128)(2,1)} fusion(bf16[5120,384]{1,0:T(8,128)(2,1)} %collective-permute-done.13, bf16[5120,384]{1,0:T(8,128)(2,1)} %get-tuple-element.357), kind=kLoop, calls=%fused_computation.1 | loop fusion | flops 7864320 | bytes 11796480 | tf_op jit(solution)/shard_map/convert_element_type | solution.py:716
  287.9 5.0 %all-to-all-start.1 = ((bf16[4,1280,384]{2,1,0:T(8,128)(2,1)}), bf16[4,1280,384]{2,1,0:T(8,128)(2,1)}, u32[]{:S(2)}, u32[]{:S(2)}) async-start(bf16[4,1280,384]{2,1,0:T(8,128)(2,1)} %bitcast.164), calls=%async_computation.2 | async-start | bytes 7864320 | tf_op jit(solution)/shard_map/all_to_all | solution.py:650
  293.1 1.7 fusion.103
  294.8 2.3 convolution_add_fusion.6
  297.1 3.7 collective-permute-start.12
  301.6 2.2 fusion.63
  303.8 11.3 %collective-permute-done.12 = bf16[384,384]{1,0:T(8,128)(2,1)S(1)} collective-permute-done((bf16[384,384]{1,0:T(8,128)(2,1)S(1)}, bf16[384,384]{1,0:T(8,128)(2,1)S(1)}, u32[]{:S(2)}, u32[]{:S(2)}) %collective-permute-start.12) | collective-permute-done | bytes 294944 | tf_op jit(solution)/shard_map/ppermute | solution.py:658
  315.1 34.8 %collective-permute-done.11 = bf16[384,384]{1,0:T(8,128)(2,1)S(1)} collective-permute-done((bf16[384,384]{1,0:T(8,128)(2,1)S(1)}, bf16[384,384]{1,0:T(8,128)(2,1)S(1)}, u32[]{:S(2)}, u32[]{:S(2)}) %collective-permute-start.11) | collective-permute-done | bytes 294944 | tf_op jit(solution)/shard_map/ppermute | solution.py:658
  350.7 1.3 select_bitcast_fusion.3
  352.2 2.5 broadcast_in_dim.24
  354.8 5.1 %all-to-all-start.2 = ((bf16[4,1536,384]{2,1,0:T(8,128)(2,1)}), bf16[4,1536,384]{2,1,0:T(8,128)(2,1)}, u32[]{:S(2)}, u32[]{:S(2)}) async-start(bf16[4,1536,384]{2,1,0:T(8,128)(2,1)} %broadcast_in_dim.24), calls=%async_computation.4 | async-start | bytes 9437184 | tf_op jit(solution)/shard_map/all_to_all | solution.py:650
  360.2 2.3 fusion.88
  362.7 2.6 add_convert_fusion.3
  365.4 1.5 collective-permute-start.16
  367.2 2.7 collective-permute-start.14
  369.9 16.2 %shard_map.485 = (f32[80,640,128]{2,1,0:T(8,128)}, f32[16,128]{1,0:T(8,128)}) custom-call(bf16[80,640,128]{2,1,0:T(8,128)(2,1)} %bitcast.147, bf16[32,128]{1,0:T(8,128)(2,1)} %pad_maximum_fusion.4.weight, bf16[10,80,640]{2,1,0:T(8,128)(2,1)} %bitcast.169, bf16[6,80,640]{2,1,0:T(8,128)(2,1)} %bitcast.174), custom_call_target="tpu_custom_call" | custom-call | flops 1 | bytes 1 | tf_op jit(solution)/shard_map/pallas_call | solution.py:287
  386.1 2.2 collective-permute-done.15
  388.5 1.4 collective-permute-start.23
  389.8 3.1 collective-permute-start.21
  392.9 12.2 %shard_map.486 = (f32[80,640,128]{2,1,0:T(8,128)}, f32[16,128]{1,0:T(8,128)}) custom-call(bf16[80,640,128]{2,1,0:T(8,128)(2,1)} %bitcast.148, bf16[32,128]{1,0:T(8,128)(2,1)} %pad_maximum_fusion.4.weight, bf16[10,80,640]{2,1,0:T(8,128)(2,1)} %bitcast.170, bf16[6,80,640]{2,1,0:T(8,128)(2,1)} %bitcast.175, ...), custom_call_target="tpu_custom_call", output_to_operand_aliasing={{0}: (4, {})} | custom-call | flops 1 | bytes 1 | tf_op jit(solution)/shard_map/pallas_call | solution.py:287
  406.7 1.5 convolution_add_fusion.5
  408.2 1.4 collective-permute-start.20
  409.8 2.9 collective-permute-start.18
  413.4 1.2 select_bitcast_fusion.7
  414.8 2.3 broadcast_in_dim.26
  417.0 5.0 %all-to-all-start.3 = ((bf16[4,1280,384]{2,1,0:T(8,128)(2,1)}), bf16[4,1280,384]{2,1,0:T(8,128)(2,1)}, u32[]{:S(2)}, u32[]{:S(2)}) async-start(bf16[4,1280,384]{2,1,0:T(8,128)(2,1)} %broadcast_in_dim.26), calls=%async_computation.5 | async-start | bytes 7864320 | tf_op jit(solution)/shard_map/all_to_all | solution.py:650
  422.5 1.4 collective-permute-start.6
  423.9 3.1 collective-permute-start.4
  427.0 2.9 convert_element_type.299
  430.3 1.6 pad_maximum_fusion.1
  431.8 1.6 pad_maximum_fusion
  433.4 1.6 slice_bitcast_fusion
  435.0 1.2 fusion.91
  436.2 2.9 collective-permute-start.26
  439.7 5.2 %collective-permute-done.5 = bf16[320,384]{1,0:T(8,128)(2,1)S(1)} collective-permute-done((bf16[320,384]{1,0:T(8,128)(2,1)S(1)}, bf16[320,384]{1,0:T(8,128)(2,1)S(1)}, u32[]{:S(2)}, u32[]{:S(2)}) %collective-permute-start.5) | collective-permute-done | bytes 245792 | tf_op jit(solution)/shard_map/ppermute | solution.py:658
  445.9 21.8 %collective-permute-done.26 = f32[3392]{0:T(1024)S(1)} collective-permute-done((f32[3392]{0:T(1024)S(1)}, f32[3392]{0:T(1024)S(1)}, u32[]{:S(2)}, u32[]{:S(2)}) %collective-permute-start.26) | collective-permute-done | bytes 13600 | tf_op jit(solution)/shard_map/ppermute | solution.py:658
  470.3 2.6 bitcast_convert_fusion
  472.9 1.2 fusion.93
  474.1 2.6 fusion.94
  (218 shorter events, 28.4 us)
Async XLA Ops:
  7.2 81.0 %copy-start = (bf16[384,768]{1,0:T(8,128)(2,1)S(1)}, bf16[384,768]{1,0:T(8,128)(2,1)}, u32[]{:S(2)}) copy-start(bf16[384,768]{1,0:T(8,128)(2,1)} %param.36) | copy-start | bytes 1769476
  7.2 100.4 %all-gather.5.cloned.1.call-start = ((), (), s32[]{:S(2)}) async-start(), calls=%async_computation.8 | async-start | bytes 5120000 | tf_op jit(solution)/shard_map/all_gather | solution.py:783
  11.4 11.4 %copy-start.39 = (bf16[384]{0:T(512)(128)(2,1)S(1)}, bf16[384]{0:T(512)(128)(2,1)}, u32[]{:S(2)}) copy-start(bf16[384]{0:T(512)(128)(2,1)} %param.47) | copy-start | bytes 2308
  11.4 11.4 %copy-start.3 = (bf16[1,320,384]{2,1,0:T(8,128)(2,1)S(1)}, bf16[1,320,384]{2,1,0:T(8,128)(2,1)}, u32[]{:S(2)}) copy-start(bf16[1,320,384]{2,1,0:T(8,128)(2,1)} %param.29) | copy-start | bytes 737284
  11.4 11.8 %copy-start.34 = (bf16[768]{0:T(1024)(128)(2,1)S(1)}, bf16[768]{0:T(1024)(128)(2,1)}, u32[]{:S(2)}) copy-start(bf16[768]{0:T(1024)(128)(2,1)} %param.49) | copy-start | bytes 4612
  11.4 11.9 %copy-start.35 = (bf16[768]{0:T(1024)(128)(2,1)S(1)}, bf16[768]{0:T(1024)(128)(2,1)}, u32[]{:S(2)}) copy-start(bf16[768]{0:T(1024)(128)(2,1)} %param.55) | copy-start | bytes 4612
  11.4 11.9 %copy-start.9 = (bf16[384,768]{1,0:T(8,128)(2,1)S(1)}, bf16[384,768]{1,0:T(8,128)(2,1)}, u32[]{:S(2)}) copy-start(bf16[384,768]{1,0:T(8,128)(2,1)} %param.50) | copy-start | bytes 1769476
  22.7 145.0 %all-gather.7.cloned.1.call-start = ((), (), s32[]{:S(2)}) async-start(), calls=%async_computation.9 | async-start | bytes 3072000 | tf_op jit(solution)/shard_map/all_gather | solution.py:783
  27.7 51.7 %copy-start.4 = (f32[320,768]{1,0:T(8,128)S(1)}, f32[320,768]{1,0:T(8,128)}, u32[]{:S(2)}) copy-start(f32[320,768]{1,0:T(8,128)} %fusion.15.lifting.lifting_second) | copy-start | bytes 2949124
  80.9 3.1 copy-start.10
  80.9 3.1 copy-start.8
  80.9 3.1 copy-start.16
  83.1 3.1 copy-start.40
  83.1 3.1 copy-start.38
  83.1 3.6 copy-start.36
  83.1 3.6 copy-start.37
  83.1 3.6 copy-start.21
  85.6 22.0 %collective-permute-start = (bf16[6144,384]{1,0:T(8,128)(2,1)}, bf16[6144,384]{1,0:T(8,128)(2,1)}, u32[]{:S(2)}, u32[]{:S(2)}) collective-permute-start(bf16[6144,384]{1,0:T(8,128)(2,1)} %get-tuple-element.364), channel_id=1, source_target_pairs={{0,1},{1,0},{2,3},{3,2},{4,5},{5,4},{6,7},{7,6},{8,9},{9,8},{10,11... | collective-permute-start | bytes 14155784 | tf_op jit(solution)/shard_map/ppermute | solution.py:646
  107.5 12.7 %collective-permute-start.1 = (bf16[4,2,768,384]{3,2,1,0:T(8,128)(2,1)}, bf16[4,2,768,384]{3,2,1,0:T(8,128)(2,1)}, u32[]{:S(2)}, u32[]{:S(2)}) collective-permute-start(bf16[4,2,768,384]{3,2,1,0:T(8,128)(2,1)} %get-tuple-element.156.mine), channel_id=1, source_target_pairs={{0,1},{1,0},{2,3},{3,2},{4,5},{5,4},{6,7},{7,6},{8,9},{9,8},{10,11... | collective-permute-start | bytes 14155784 | tf_op jit(solution)/shard_map/ppermute | solution.py:646
  114.7 68.7 %all-to-all-start = ((bf16[4,1536,384]{2,1,0:T(8,128)(2,1)}), bf16[4,1536,384]{2,1,0:T(8,128)(2,1)}, u32[]{:S(2)}, u32[]{:S(2)}) async-start(bf16[4,1536,384]{2,1,0:T(8,128)(2,1)} %bitcast.161), calls=%async_computation | async-start | bytes 9437184 | tf_op jit(solution)/shard_map/all_to_all | solution.py:650
  120.2 154.0 %reduce-scatter.3.cloned.1.call-start = ((), (), s32[]{:S(2)}) async-start(), calls=%async_computation.6 | async-start | bytes 5120000 | tf_op jit(solution)/shard_map/reduce_scatter | solution.py:789
  167.5 43.5 %collective-permute-start.2 = (bf16[4,2,480,384]{3,2,1,0:T(8,128)(2,1)}, bf16[4,2,480,384]{3,2,1,0:T(8,128)(2,1)}, u32[]{:S(2)}, u32[]{:S(2)}) collective-permute-start(bf16[4,2,480,384]{3,2,1,0:T(8,128)(2,1)} %get-tuple-element.188), channel_id=1, source_target_pairs={{0,1},{1,0},{2,3},{3,2},{4,5},{5,4},{6,7},{7,6},{8,9},{9,8},{10,11... | collective-permute-start | bytes 8847368 | tf_op jit(solution)/shard_map/ppermute | solution.py:646
  167.6 182.3 %reduce-scatter.5.cloned.1.call-start = ((), (), s32[]{:S(2)}) async-start(), calls=%async_computation.7 | async-start | bytes 3072000 | tf_op jit(solution)/shard_map/reduce_scatter | solution.py:789
  202.8 8.2 %collective-permute-start.3 = (bf16[4,2,288,384]{3,2,1,0:T(8,128)(2,1)}, bf16[4,2,288,384]{3,2,1,0:T(8,128)(2,1)S(1)}, u32[]{:S(2)}, u32[]{:S(2)}) collective-permute-start(bf16[4,2,288,384]{3,2,1,0:T(8,128)(2,1)} %get-tuple-element.189), channel_id=1, source_target_pairs={{0,1},{1,0},{2,3},{3,2},{4,5},{5,4},{6,7},{7,6},{8,9},{9,8},{10,11... | collective-permute-start | bytes 5308424 | tf_op jit(solution)/shard_map/ppermute | solution.py:646
  205.5 59.7 %collective-permute-start.9 = (bf16[384,384]{1,0:T(8,128)(2,1)}, bf16[384,384]{1,0:T(8,128)(2,1)S(1)}, u32[]{:S(2)}, u32[]{:S(2)}) collective-permute-start(bf16[384,384]{1,0:T(8,128)(2,1)} %get-tuple-element.345), channel_id=1, source_target_pairs={{0,6},{2,4},{4,2},{6,0},{1,7},{3,5},{5,3},{7,1},{8,14},{10,12},{12... | collective-permute-start | bytes 884744 | tf_op jit(solution)/shard_map/ppermute | solution.py:658
  210.5 55.6 %collective-permute-start.8 = (bf16[384,384]{1,0:T(8,128)(2,1)}, bf16[384,384]{1,0:T(8,128)(2,1)}, u32[]{:S(2)}, u32[]{:S(2)}) collective-permute-start(bf16[384,384]{1,0:T(8,128)(2,1)} %get-tuple-element.346), channel_id=1, source_target_pairs={{0,4},{2,6},{4,0},{6,2},{1,5},{3,7},{5,1},{7,3},{8,12},{10,14},{12... | collective-permute-start | bytes 884744 | tf_op jit(solution)/shard_map/ppermute | solution.py:658
  210.5 55.6 %collective-permute-start.7 = (bf16[384,384]{1,0:T(8,128)(2,1)S(1)}, bf16[384,384]{1,0:T(8,128)(2,1)}, u32[]{:S(2)}, u32[]{:S(2)}) collective-permute-start(bf16[384,384]{1,0:T(8,128)(2,1)S(1)} %get-tuple-element.347), channel_id=1, source_target_pairs={{0,2},{2,0},{4,6},{6,4},{1,3},{3,1},{5,7},{7,5},{8,10},{10,8},{12,... | collective-permute-start | bytes 884744 | tf_op jit(solution)/shard_map/ppermute | solution.py:658
  243.2 24.1 %copy-start.1 = (f32[320,768]{1,0:T(8,128)S(1)}, f32[320,768]{1,0:T(8,128)}, u32[]{:S(2)}) copy-start(f32[320,768]{1,0:T(8,128)} %fusion.3.finish) | copy-start | bytes 2949124
  243.2 24.1 %copy-start.2 = (f32[320,768]{1,0:T(8,128)S(1)}, f32[320,768]{1,0:T(8,128)}, u32[]{:S(2)}) copy-start(f32[320,768]{1,0:T(8,128)} %fusion.7.lifting.lifting_first) | copy-start | bytes 2949124
  243.2 24.1 %copy-start.14 = (f32[320,768]{1,0:T(8,128)S(1)}, f32[320,768]{1,0:T(8,128)}, u32[]{:S(2)}) copy-start(f32[320,768]{1,0:T(8,128)} %get-tuple-element.200) | copy-start | bytes 2949124
  243.3 24.1 %copy-start.15 = (f32[320,768]{1,0:T(8,128)S(1)}, f32[320,768]{1,0:T(8,128)}, u32[]{:S(2)}) copy-start(f32[320,768]{1,0:T(8,128)} %get-tuple-element.196) | copy-start | bytes 2949124
  274.2 7.1 %collective-permute-start.13 = (bf16[5120,384]{1,0:T(8,128)(2,1)}, bf16[5120,384]{1,0:T(8,128)(2,1)}, u32[]{:S(2)}, u32[]{:S(2)}) collective-permute-start(bf16[5120,384]{1,0:T(8,128)(2,1)} %get-tuple-element.358), channel_id=1, source_target_pairs={{0,1},{1,0},{2,3},{3,2},{4,5},{5,4},{6,7},{7,6},{8,9},{9,8},{10,11... | collective-permute-start | bytes 11796488 | tf_op jit(solution)/shard_map/ppermute | solution.py:646
  287.9 6.9 %copy-start.7 = (f32[320,768]{1,0:T(8,128)S(1)}, f32[320,768]{1,0:T(8,128)}, u32[]{:S(2)}) copy-start(f32[320,768]{1,0:T(8,128)} %get-tuple-element.146) | copy-start | bytes 2949124
  287.9 62.0 %all-to-all-start.1 = ((bf16[4,1280,384]{2,1,0:T(8,128)(2,1)}), bf16[4,1280,384]{2,1,0:T(8,128)(2,1)}, u32[]{:S(2)}, u32[]{:S(2)}) async-start(bf16[4,1280,384]{2,1,0:T(8,128)(2,1)} %bitcast.164), calls=%async_computation.2 | async-start | bytes 7864320 | tf_op jit(solution)/shard_map/all_to_all | solution.py:650
  293.1 8.5 %copy-start.19 = (bf16[384,768]{1,0:T(8,128)(2,1)S(1)}, bf16[384,768]{1,0:T(8,128)(2,1)}, u32[]{:S(2)}) copy-start(bf16[384,768]{1,0:T(8,128)(2,1)} %param.34) | copy-start | bytes 1769476
  297.1 18.0 %collective-permute-start.12 = (bf16[384,384]{1,0:T(8,128)(2,1)S(1)}, bf16[384,384]{1,0:T(8,128)(2,1)S(1)}, u32[]{:S(2)}, u32[]{:S(2)}) collective-permute-start(bf16[384,384]{1,0:T(8,128)(2,1)S(1)} %add_convert_fusion.5), channel_id=1, source_target_pairs={{0,6},{2,4},{4,2},{6,0},{1,7},{3,5},{5,3},{7,1},{8,14},{10,12},{12... | collective-permute-start | bytes 884744 | tf_op jit(solution)/shard_map/ppermute | solution.py:658
  300.8 49.1 %collective-permute-start.11 = (bf16[384,384]{1,0:T(8,128)(2,1)S(1)}, bf16[384,384]{1,0:T(8,128)(2,1)S(1)}, u32[]{:S(2)}, u32[]{:S(2)}) collective-permute-start(bf16[384,384]{1,0:T(8,128)(2,1)S(1)} %add_convert_fusion.5), channel_id=1, source_target_pairs={{0,4},{2,6},{4,0},{6,2},{1,5},{3,7},{5,1},{7,3},{8,12},{10,14},{12... | collective-permute-start | bytes 884744 | tf_op jit(solution)/shard_map/ppermute | solution.py:658
  300.8 49.1 %collective-permute-start.10 = (bf16[384,384]{1,0:T(8,128)(2,1)S(1)}, bf16[384,384]{1,0:T(8,128)(2,1)S(1)}, u32[]{:S(2)}, u32[]{:S(2)}) collective-permute-start(bf16[384,384]{1,0:T(8,128)(2,1)S(1)} %add_convert_fusion.5), channel_id=1, source_target_pairs={{0,2},{2,0},{4,6},{6,4},{1,3},{3,1},{5,7},{7,5},{8,10},{10,8},{12,... | collective-permute-start | bytes 884744 | tf_op jit(solution)/shard_map/ppermute | solution.py:658
  315.1 34.8 %copy-start.28 = (bf16[384,384]{1,0:T(8,128)(2,1)}, bf16[384,384]{1,0:T(8,128)(2,1)S(1)}, u32[]{:S(2)}) copy-start(bf16[384,384]{1,0:T(8,128)(2,1)S(1)} %collective-permute-done.12) | copy-start | bytes 884740
  354.8 5.2 %copy-start.27 = (f32[768,1]{1,0:T(8,128)S(1)}, f32[768,1]{1,0:T(8,128)}, u32[]{:S(2)}) copy-start(f32[768,1]{1,0:T(8,128)} %get-tuple-element.238) | copy-start | bytes 9220
  354.8 5.4 %copy-start.24 = (bf16[320,768]{1,0:T(8,128)(2,1)S(1)}, bf16[320,768]{1,0:T(8,128)(2,1)}, u32[]{:S(2)}) copy-start(bf16[320,768]{1,0:T(8,128)(2,1)} %copy-done.23) | copy-start | bytes 1474564
  354.8 5.4 %copy-start.25 = (f32[320,384]{1,0:T(8,128)S(1)}, f32[320,384]{1,0:T(8,128)}, u32[]{:S(2)}) copy-start(f32[320,384]{1,0:T(8,128)} %convolution_add_fusion.6) | copy-start | bytes 1474564
  354.8 58.6 %all-to-all-start.2 = ((bf16[4,1536,384]{2,1,0:T(8,128)(2,1)}), bf16[4,1536,384]{2,1,0:T(8,128)(2,1)}, u32[]{:S(2)}, u32[]{:S(2)}) async-start(bf16[4,1536,384]{2,1,0:T(8,128)(2,1)} %broadcast_in_dim.24), calls=%async_computation.4 | async-start | bytes 9437184 | tf_op jit(solution)/shard_map/all_to_all | solution.py:650
  365.4 20.6 %collective-permute-start.16 = (bf16[320,384]{1,0:T(8,128)(2,1)S(1)}, bf16[320,384]{1,0:T(8,128)(2,1)S(1)}, u32[]{:S(2)}, u32[]{:S(2)}) collective-permute-start(bf16[320,384]{1,0:T(8,128)(2,1)S(1)} %get-tuple-element.353), channel_id=1, source_target_pairs={{0,6},{2,4},{4,2},{6,0},{1,7},{3,5},{5,3},{7,1},{8,14},{10,12},{12... | collective-permute-start | bytes 737288 | tf_op jit(solution)/shard_map/ppermute | solution.py:658
  366.9 21.4 %collective-permute-start.15 = (bf16[320,384]{1,0:T(8,128)(2,1)S(1)}, bf16[320,384]{1,0:T(8,128)(2,1)S(1)}, u32[]{:S(2)}, u32[]{:S(2)}) collective-permute-start(bf16[320,384]{1,0:T(8,128)(2,1)S(1)} %get-tuple-element.354), channel_id=1, source_target_pairs={{0,4},{2,6},{4,0},{6,2},{1,5},{3,7},{5,1},{7,3},{8,12},{10,14},{12... | collective-permute-start | bytes 737288 | tf_op jit(solution)/shard_map/ppermute | solution.py:658
  367.2 21.2 %collective-permute-start.14 = (bf16[320,384]{1,0:T(8,128)(2,1)S(1)}, bf16[320,384]{1,0:T(8,128)(2,1)S(1)}, u32[]{:S(2)}, u32[]{:S(2)}) collective-permute-start(bf16[320,384]{1,0:T(8,128)(2,1)S(1)} %get-tuple-element.355), channel_id=1, source_target_pairs={{0,2},{2,0},{4,6},{6,4},{1,3},{3,1},{5,7},{7,5},{8,10},{10,8},{12,... | collective-permute-start | bytes 737288 | tf_op jit(solution)/shard_map/ppermute | solution.py:658
  388.5 21.3 %collective-permute-start.23 = (bf16[320,384]{1,0:T(8,128)(2,1)S(1)}, bf16[320,384]{1,0:T(8,128)(2,1)S(1)}, u32[]{:S(2)}, u32[]{:S(2)}) collective-permute-start(bf16[320,384]{1,0:T(8,128)(2,1)S(1)} %add_convert_fusion.6), channel_id=1, source_target_pairs={{0,6},{2,4},{4,2},{6,0},{1,7},{3,5},{5,3},{7,1},{8,14},{10,12},{12... | collective-permute-start | bytes 737288 | tf_op jit(solution)/shard_map/ppermute | solution.py:658
  389.8 22.8 %collective-permute-start.22 = (bf16[320,384]{1,0:T(8,128)(2,1)S(1)}, bf16[320,384]{1,0:T(8,128)(2,1)}, u32[]{:S(2)}, u32[]{:S(2)}) collective-permute-start(bf16[320,384]{1,0:T(8,128)(2,1)S(1)} %add_convert_fusion.6), channel_id=1, source_target_pairs={{0,4},{2,6},{4,0},{6,2},{1,5},{3,7},{5,1},{7,3},{8,12},{10,14},{12... | collective-permute-start | bytes 737288 | tf_op jit(solution)/shard_map/ppermute | solution.py:658
  389.8 22.8 %collective-permute-start.21 = (bf16[320,384]{1,0:T(8,128)(2,1)S(1)}, bf16[320,384]{1,0:T(8,128)(2,1)}, u32[]{:S(2)}, u32[]{:S(2)}) collective-permute-start(bf16[320,384]{1,0:T(8,128)(2,1)S(1)} %add_convert_fusion.6), channel_id=1, source_target_pairs={{0,2},{2,0},{4,6},{6,4},{1,3},{3,1},{5,7},{7,5},{8,10},{10,8},{12,... | collective-permute-start | bytes 737288 | tf_op jit(solution)/shard_map/ppermute | solution.py:658
  392.9 12.2 %copy-start.32 = (bf16[128,16]{0,1:T(8,128)(2,1)S(1)}, bf16[128,16]{0,1:T(8,128)(2,1)}, u32[]{:S(2)}) copy-start(bf16[128,16]{0,1:T(8,128)(2,1)} %param.44) | copy-start | bytes 12292
  392.9 12.2 %copy-start.33 = (f32[16,128]{1,0:T(8,128)S(1)}, f32[16,128]{1,0:T(8,128)}, u32[]{:S(2)}) copy-start(f32[16,128]{1,0:T(8,128)} %get-tuple-element.239) | copy-start | bytes 24580
  392.9 13.7 %copy-start.26 = (f32[320,384]{1,0:T(8,128)S(1)}, f32[320,384]{1,0:T(8,128)}, u32[]{:S(2)}) copy-start(f32[320,384]{1,0:T(8,128)} %get-tuple-element.321) | copy-start | bytes 1474564
  406.6 1.6 collective-permute-start.17
  408.2 15.7 %collective-permute-start.20 = (f32[3392]{0:T(1024)S(1)}, f32[3392]{0:T(1024)S(1)}, u32[]{:S(2)}, u32[]{:S(2)}) collective-permute-start(f32[3392]{0:T(1024)S(1)} %add.292), channel_id=1, source_target_pairs={{0,6},{2,4},{4,2},{6,0},{1,7},{3,5},{5,3},{7,1},{8,14},{10,12},{12... | collective-permute-start | bytes 40712 | tf_op jit(solution)/shard_map/ppermute | solution.py:658
  409.6 17.4 %collective-permute-start.19 = (f32[3392]{0:T(1024)S(1)}, f32[3392]{0:T(1024)S(1)}, u32[]{:S(2)}, u32[]{:S(2)}) collective-permute-start(f32[3392]{0:T(1024)S(1)} %add.292), channel_id=1, source_target_pairs={{0,4},{2,6},{4,0},{6,2},{1,5},{3,7},{5,1},{7,3},{8,12},{10,14},{12... | collective-permute-start | bytes 40712 | tf_op jit(solution)/shard_map/ppermute | solution.py:658
  409.8 17.2 %collective-permute-start.18 = (f32[3392]{0:T(1024)S(1)}, f32[3392]{0:T(1024)S(1)}, u32[]{:S(2)}, u32[]{:S(2)}) collective-permute-start(f32[3392]{0:T(1024)S(1)} %add.292), channel_id=1, source_target_pairs={{0,2},{2,0},{4,6},{6,4},{1,3},{3,1},{5,7},{7,5},{8,10},{10,8},{12,... | collective-permute-start | bytes 40712 | tf_op jit(solution)/shard_map/ppermute | solution.py:658
  417.0 5.0 %copy-start.22 = (bf16[384,768]{1,0:T(8,128)(2,1)S(1)}, bf16[384,768]{1,0:T(8,128)(2,1)}, u32[]{:S(2)}) copy-start(bf16[384,768]{1,0:T(8,128)(2,1)} %param.45) | copy-start | bytes 1769476
  417.0 53.2 %all-to-all-start.3 = ((bf16[4,1280,384]{2,1,0:T(8,128)(2,1)}), bf16[4,1280,384]{2,1,0:T(8,128)(2,1)}, u32[]{:S(2)}, u32[]{:S(2)}) async-start(bf16[4,1280,384]{2,1,0:T(8,128)(2,1)} %broadcast_in_dim.26), calls=%async_computation.5 | async-start | bytes 7864320 | tf_op jit(solution)/shard_map/all_to_all | solution.py:650
  422.5 17.1 %collective-permute-start.6 = (bf16[320,384]{1,0:T(8,128)(2,1)S(1)}, bf16[320,384]{1,0:T(8,128)(2,1)S(1)}, u32[]{:S(2)}, u32[]{:S(2)}) collective-permute-start(bf16[320,384]{1,0:T(8,128)(2,1)S(1)} %fusion.16), channel_id=1, source_target_pairs={{0,6},{2,4},{4,2},{6,0},{1,7},{3,5},{5,3},{7,1},{8,14},{10,12},{12... | collective-permute-start | bytes 737288 | tf_op jit(solution)/shard_map/ppermute | solution.py:658
  423.9 21.1 %collective-permute-start.5 = (bf16[320,384]{1,0:T(8,128)(2,1)S(1)}, bf16[320,384]{1,0:T(8,128)(2,1)S(1)}, u32[]{:S(2)}, u32[]{:S(2)}) collective-permute-start(bf16[320,384]{1,0:T(8,128)(2,1)S(1)} %fusion.16), channel_id=1, source_target_pairs={{0,4},{2,6},{4,0},{6,2},{1,5},{3,7},{5,1},{7,3},{8,12},{10,14},{12... | collective-permute-start | bytes 737288 | tf_op jit(solution)/shard_map/ppermute | solution.py:658
  423.9 21.1 %collective-permute-start.4 = (bf16[320,384]{1,0:T(8,128)(2,1)S(1)}, bf16[320,384]{1,0:T(8,128)(2,1)S(1)}, u32[]{:S(2)}, u32[]{:S(2)}) collective-permute-start(bf16[320,384]{1,0:T(8,128)(2,1)S(1)} %fusion.16), channel_id=1, source_target_pairs={{0,2},{2,0},{4,6},{6,4},{1,3},{3,1},{5,7},{7,5},{8,10},{10,8},{12,... | collective-permute-start | bytes 737288 | tf_op jit(solution)/shard_map/ppermute | solution.py:658
  436.2 31.4 %collective-permute-start.26 = (f32[3392]{0:T(1024)S(1)}, f32[3392]{0:T(1024)S(1)}, u32[]{:S(2)}, u32[]{:S(2)}) collective-permute-start(f32[3392]{0:T(1024)S(1)} %add_add_fusion.1), channel_id=1, source_target_pairs={{0,24},{8,16},{16,8},{24,0},{1,25},{9,17},{17,9},{25,1},{2,26},{10... | collective-permute-start | bytes 40712 | tf_op jit(solution)/shard_map/ppermute | solution.py:658
  439.1 28.5 %collective-permute-start.25 = (f32[3392]{0:T(1024)S(1)}, f32[3392]{0:T(1024)S(1)}, u32[]{:S(2)}, u32[]{:S(2)}) collective-permute-start(f32[3392]{0:T(1024)S(1)} %add_add_fusion.1), channel_id=1, source_target_pairs={{0,16},{8,24},{16,0},{24,8},{1,17},{9,25},{17,1},{25,9},{2,18},{10... | collective-permute-start | bytes 40712 | tf_op jit(solution)/shard_map/ppermute | solution.py:658
  439.7 28.0 %collective-permute-start.24 = (f32[3392]{0:T(1024)S(1)}, f32[3392]{0:T(1024)S(1)}, u32[]{:S(2)}, u32[]{:S(2)}) collective-permute-start(f32[3392]{0:T(1024)S(1)} %add_add_fusion.1), channel_id=1, source_target_pairs={{0,8},{8,0},{16,24},{24,16},{1,9},{9,1},{17,25},{25,17},{2,10},{10... | collective-permute-start | bytes 40712 | tf_op jit(solution)/shard_map/ppermute | solution.py:658
  (12 other events, 21.8 us)
Sparse Core Ops, SparseCore 0:
  22.8 81.8 all-gather.4
  107.7 55.1 all-gather.6
  167.8 96.8 reduce-scatter.2
  274.3 70.1 reduce-scatter.4

commit v5 on v4

--- a/solution.py
+++ b/solution.py
@@ -209,8 +209,8 @@
     outs, wide = refs[:-1], refs[-1]
 
     def one(i, carry):
-        _, factor = turned_norm(pair[i])
-        both = dot(weight[...], pair[i], 1, 1)
+        centre, factor = turned_norm(pair[i])
+        both = dot(weight[...], centre.astype(bf16), 1, 0)
         line = (both[:heads] + both[heads:]) * factor
         for t in range(wide.shape[0]):
             wide[t, pl.ds(pl.multiple_of(i * heads, heads), heads), :] = line[

time: 488 us -> 488 us (level)
  no operation moved by 1% of the time
where the time goes in v5:
time: 488 us; the launch traced here: 484 us
  Pallas kernels  240 us (49%)
  waiting for transfers between devices  84 us (17%)
  starting transfers between devices  53.2 us (11%)
  other arithmetic  42.5 us (9%)
  local copies, waits for them, and re-layouts  26.3 us (5%)
  matrix products  22.8 us (5%)
  between operations  15.5 us (3%)
    pallas_call x4, Pallas kernels, attention(): pl.pallas_call(functools.partial(attention_kernel, step=step), grid_spec=...  78.5 us
    ppermute x21, waiting for transfers between devices, exchange(): lax.ppermute(array, axis, [(i, i ^ bit) for i in range(lax.axis_size(axis...  76.1 us
    pallas_call x1, Pallas kernels, transition(): pl.pallas_call(transition_kernel, grid_spec=pltpu.PrefetchScalarGridSpec(...  51.7 us
    ppermute x21, starting transfers between devices, exchange(): lax.ppermute(array, axis, [(i, i ^ bit) for i in range(lax.axis_size(axis...  31.2 us
    pallas_call x2, Pallas kernels, rows_back(): pl.pallas_call(rows_kernel, grid_spec=pltpu.PrefetchScalarGridSpec(num_sc...  30.9 us
    pallas_call x2, Pallas kernels, pair_backward(): pl.pallas_call(functools.partial(pair_backward_kernel, block=block, heads...  28.4 us
    pallas_call x1, Pallas kernels, weight_sums(): pl.pallas_call(weights_kernel, grid_spec=pltpu.PrefetchScalarGridSpec(num...  22 us
    all_to_all x4, starting transfers between devices, traded(): return lax.all_to_all(array, axis, 0, 0)  20.5 us
  transfers between devices with their start and end apart: 35, of which 8 were waited for; matrix products, arithmetic and copies ran while one was open for 16% of the time, Pallas kernels for 47%

profile of v5, /device:TPU:0, one launch (start us, length us, event | category | flops | bytes accessed | tf_op | source)
XLA Modules:
  0.0 484.4 jit_solution(6122576417689402318)
XLA Ops:
  11.4 12.2 %shard_map.475 = (bf16[10,80,640]{2,1,0:T(8,128)(2,1)}, bf16[6,80,640]{2,1,0:T(8,128)(2,1)}) custom-call(bf16[80,640,128]{2,1,0:T(8,128)(2,1)} %bitcast.146, bf16[32,128]{1,0:T(8,128)(2,1)} %pad_maximum_fusion.4.weight), custom_call_target="tpu_custom_call" | custom-call | flops 1 | bytes 1 | tf_op jit(solution)/shard_map/pallas_call | solution.py:233
  24.2 1.4 fusion.85.shifting
  25.6 1.5 fusion.15.lifting.lifting_second
  27.1 1.4 fusion.11.closing
  28.6 51.7 %shard_map.476 = (f32[4,320,768]{2,1,0:T(8,128)}, f32[4,320,768]{2,1,0:T(8,128)}, f32[320,768]{1,0:T(8,128)}, f32[320,768]{1,0:T(8,128)}, f32[320,768]{1,0:T(8,1...) custom-call(s32[2]{0:T(128)} %pad_add_fusion.meta, bf16[4,320,768]{2,1,0:T(8,128)(2,1)} %bitcast.156, ...), custom_call_target="tpu_custom_call" | custom-call | flops 1 | bytes 1 | tf_op jit(solution)/shard_map/pallas_call | solution.py:455
  80.3 1.5 fusion.33
  87.7 1.4 fusion.3.finish
  89.2 1.4 fusion.79.shifting
  90.6 1.5 fusion.7.lifting.lifting_first
  92.1 16.4 %shard_map.477 = (bf16[4,768,320]{2,1,0:T(8,128)(2,1)}, bf16[4,2,768,384]{3,2,1,0:T(8,128)(2,1)}, f32[4,768,320]{2,1,0:T(8,128)}, f32[4,768,320]{2,1,0:T(8,128)}, bf16[4,320,768]{2,1,0:T(8,128)(2,1)}) custom-call(s32[2]{0:T(128)} %pad_add_fusion.meta, bf16[4,320,768]{2,1,0:T(8,128)(2,1)} %bitcast.157, bf16[4,320,768]{2,1,0:T(8,128)(2,1)} %bitcast.150, ...), custom_call_target="tpu_custom_call" | custom-call | flops 1 | bytes 1 | tf_op jit(solution)/shard_map/pallas_call | solution.py:371
  108.6 7.1 %add_convert_fusion = bf16[6144,384]{1,0:T(8,128)(2,1)} fusion(bf16[6144,384]{1,0:T(8,128)(2,1)} %collective-permute-done, bf16[6144,384]{1,0:T(8,128)(2,1)} %get-tuple-element.148), kind=kLoop, calls=%fused_computation | loop fusion | flops 9437184 | bytes 14155776 | tf_op jit(solution)/shard_map/convert_element_type | solution.py:716
  115.7 5.4 %all-to-all-start = ((bf16[4,1536,384]{2,1,0:T(8,128)(2,1)}), bf16[4,1536,384]{2,1,0:T(8,128)(2,1)}, u32[]{:S(2)}, u32[]{:S(2)}) async-start(bf16[4,1536,384]{2,1,0:T(8,128)(2,1)} %bitcast.161), calls=%async_computation | async-start | bytes 9437184 | tf_op jit(solution)/shard_map/all_to_all | solution.py:650
  121.1 23.6 %shard_map.479 = (bf16[4,480,320]{2,1,0:T(8,128)(2,1)}, bf16[4,480,320]{2,1,0:T(8,128)(2,1)}, bf16[4,480,320]{2,1,0:T(8,128)(2,1)}, f32[4,2,480,320]{3,2,1,0:T(8...) custom-call(s32[2]{0:T(128)} %pad_add_fusion.meta, ...), custom_call_target="tpu_custom_call" | custom-call | flops 1 | bytes 1 | tf_op jit(solution)/shard_map/pallas_call | solution.py:163
  144.8 23.7 %shard_map.480 = (bf16[4,480,320]{2,1,0:T(8,128)(2,1)}, bf16[4,480,320]{2,1,0:T(8,128)(2,1)}, bf16[4,480,320]{2,1,0:T(8,128)(2,1)}, f32[4,2,480,320]{3,2,1,0:T(8...) custom-call(s32[2]{0:T(128)} %pad_add_fusion.meta, ...), custom_call_target="tpu_custom_call", output_to_operand_aliasing={{0}: (7, {}), {1}: (8, {}), {2}: (9, {}), {3}: (10, {}), {4... | custom-call | flops 1 | bytes 1 | tf_op jit(solution)/shard_map/pallas_call | solution.py:163
  168.7 15.7 %shard_map.478 = (bf16[4,288,320]{2,1,0:T(8,128)(2,1)}, bf16[4,288,320]{2,1,0:T(8,128)(2,1)}, bf16[4,288,320]{2,1,0:T(8,128)(2,1)}, f32[4,2,288,320]{3,2,1,0:T(8...) custom-call(s32[2]{0:T(128)} %pad_add_fusion.meta, ...), custom_call_target="tpu_custom_call" | custom-call | flops 1 | bytes 1 | tf_op jit(solution)/shard_map/pallas_call | solution.py:163
  184.3 3.9 add_convert_fusion.2
  188.3 15.5 %shard_map.481 = (bf16[4,288,320]{2,1,0:T(8,128)(2,1)}, bf16[4,288,320]{2,1,0:T(8,128)(2,1)}, bf16[4,288,320]{2,1,0:T(8,128)(2,1)}, f32[4,2,288,320]{3,2,1,0:T(8...) custom-call(s32[2]{0:T(128)} %pad_add_fusion.meta, ...), custom_call_target="tpu_custom_call", output_to_operand_aliasing={{0}: (7, {}), {1}: (8, {}), {2}: (9, {}), {3}: (10, {}), {4... | custom-call | flops 1 | bytes 1 | tf_op jit(solution)/shard_map/pallas_call | solution.py:163
  204.3 2.2 dynamic-slice_bitcast_fusion
  206.5 4.9 %collective-permute-start.9 = (bf16[384,384]{1,0:T(8,128)(2,1)}, bf16[384,384]{1,0:T(8,128)(2,1)S(1)}, u32[]{:S(2)}, u32[]{:S(2)}) collective-permute-start(bf16[384,384]{1,0:T(8,128)(2,1)} %get-tuple-element.345), channel_id=1, source_target_pairs={{0,6},{2,4},{4,2},{6,0},{1,7},{3,5},{5,3},{7,1},{8,14},{10,12},{12... | collective-permute-start | bytes 884744 | tf_op jit(solution)/shard_map/ppermute | solution.py:658
  213.2 15.2 %shard_map.482 = (bf16[4,320,768]{2,1,0:T(8,128)(2,1)}, f32[4,320,768]{2,1,0:T(8,128)}, bf16[4,768,320]{2,1,0:T(8,128)(2,1)}, bf16[4,768,320]{2,1,0:T(8,128)(2,1...) custom-call(s32[2]{0:T(128)} %pad_add_fusion.meta, bf16[4,320,768]{2,1,0:T(8,128)(2,1)} %bitcast.158, ...), custom_call_target="tpu_custom_call" | custom-call | flops 1 | bytes 1 | tf_op jit(solution)/shard_map/pallas_call | solution.py:621
  228.4 15.7 %shard_map.483 = (bf16[4,320,768]{2,1,0:T(8,128)(2,1)}, f32[4,320,768]{2,1,0:T(8,128)}, bf16[4,768,320]{2,1,0:T(8,128)(2,1)}, bf16[4,768,320]{2,1,0:T(8,128)(2,1...) custom-call(s32[2]{0:T(128)} %pad_add_fusion.meta, ...), custom_call_target="tpu_custom_call", output_to_operand_aliasing={{0}: (23, {}), {1}: (24, {}), {2}: (25, {}), {3}: (26, {})} | custom-call | flops 1 | bytes 1 | tf_op jit(solution)/shard_map/pallas_call | solution.py:621
  244.2 22.0 %shard_map.484 = (bf16[5120,384]{1,0:T(8,128)(2,1)}, bf16[5120,384]{1,0:T(8,128)(2,1)}, f32[768,1]{1,0:T(8,128)}) custom-call(s32[2]{0:T(128)} %pad_add_fusion.meta, bf16[4,320,768]{2,1,0:T(8,128)(2,1)} %bitcast.153, bf16[4,320,768]{2,1,0:T(8,128)(2,1)} %get-tuple-element.203.mixed, f32[320,768]{1,0:T(8,128)} %fusion.3.finish, ...), custom_call_target="tpu_custom_call" | custom-call | flops 1 | bytes 1 | tf_op jit(solution)/shard_map/pallas_call | solution.py:550
  267.0 1.3 add_convert_fusion.5
  268.3 1.9 fusion.89
  275.1 7.1 %collective-permute-done.13 = bf16[5120,384]{1,0:T(8,128)(2,1)} collective-permute-done((bf16[5120,384]{1,0:T(8,128)(2,1)}, bf16[5120,384]{1,0:T(8,128)(2,1)}, u32[]{:S(2)}, u32[]{:S(2)}) %collective-permute-start.13) | collective-permute-done | bytes 3932192 | tf_op jit(solution)/shard_map/ppermute | solution.py:646
  282.2 6.6 %add_convert_fusion.1 = bf16[5120,384]{1,0:T(8,128)(2,1)} fusion(bf16[5120,384]{1,0:T(8,128)(2,1)} %collective-permute-done.13, bf16[5120,384]{1,0:T(8,128)(2,1)} %get-tuple-element.357), kind=kLoop, calls=%fused_computation.1 | loop fusion | flops 7864320 | bytes 11796480 | tf_op jit(solution)/shard_map/convert_element_type | solution.py:716
  288.9 5.0 %all-to-all-start.1 = ((bf16[4,1280,384]{2,1,0:T(8,128)(2,1)}), bf16[4,1280,384]{2,1,0:T(8,128)(2,1)}, u32[]{:S(2)}, u32[]{:S(2)}) async-start(bf16[4,1280,384]{2,1,0:T(8,128)(2,1)} %bitcast.164), calls=%async_computation.2 | async-start | bytes 7864320 | tf_op jit(solution)/shard_map/all_to_all | solution.py:650
  294.0 1.7 fusion.103
  295.7 2.3 convolution_add_fusion.6
  298.0 3.7 collective-permute-start.12
  302.5 2.2 fusion.63
  304.7 11.3 %collective-permute-done.12 = bf16[384,384]{1,0:T(8,128)(2,1)S(1)} collective-permute-done((bf16[384,384]{1,0:T(8,128)(2,1)S(1)}, bf16[384,384]{1,0:T(8,128)(2,1)S(1)}, u32[]{:S(2)}, u32[]{:S(2)}) %collective-permute-start.12) | collective-permute-done | bytes 294944 | tf_op jit(solution)/shard_map/ppermute | solution.py:658
  316.0 34.8 %collective-permute-done.11 = bf16[384,384]{1,0:T(8,128)(2,1)S(1)} collective-permute-done((bf16[384,384]{1,0:T(8,128)(2,1)S(1)}, bf16[384,384]{1,0:T(8,128)(2,1)S(1)}, u32[]{:S(2)}, u32[]{:S(2)}) %collective-permute-start.11) | collective-permute-done | bytes 294944 | tf_op jit(solution)/shard_map/ppermute | solution.py:658
  351.6 1.3 select_bitcast_fusion.3
  353.2 2.5 broadcast_in_dim.24
  355.7 5.1 %all-to-all-start.2 = ((bf16[4,1536,384]{2,1,0:T(8,128)(2,1)}), bf16[4,1536,384]{2,1,0:T(8,128)(2,1)}, u32[]{:S(2)}, u32[]{:S(2)}) async-start(bf16[4,1536,384]{2,1,0:T(8,128)(2,1)} %broadcast_in_dim.24), calls=%async_computation.4 | async-start | bytes 9437184 | tf_op jit(solution)/shard_map/all_to_all | solution.py:650
  361.1 2.3 fusion.88
  363.7 2.6 add_convert_fusion.3
  366.4 1.5 collective-permute-start.16
  368.1 2.7 collective-permute-start.14
  370.8 16.2 %shard_map.485 = (f32[80,640,128]{2,1,0:T(8,128)}, f32[16,128]{1,0:T(8,128)}) custom-call(bf16[80,640,128]{2,1,0:T(8,128)(2,1)} %bitcast.147, bf16[32,128]{1,0:T(8,128)(2,1)} %pad_maximum_fusion.4.weight, bf16[10,80,640]{2,1,0:T(8,128)(2,1)} %bitcast.169, bf16[6,80,640]{2,1,0:T(8,128)(2,1)} %bitcast.174), custom_call_target="tpu_custom_call" | custom-call | flops 1 | bytes 1 | tf_op jit(solution)/shard_map/pallas_call | solution.py:287
  387.0 2.2 collective-permute-done.15
  389.3 1.4 collective-permute-start.23
  390.8 3.0 collective-permute-start.21
  393.8 12.2 %shard_map.486 = (f32[80,640,128]{2,1,0:T(8,128)}, f32[16,128]{1,0:T(8,128)}) custom-call(bf16[80,640,128]{2,1,0:T(8,128)(2,1)} %bitcast.148, bf16[32,128]{1,0:T(8,128)(2,1)} %pad_maximum_fusion.4.weight, bf16[10,80,640]{2,1,0:T(8,128)(2,1)} %bitcast.170, bf16[6,80,640]{2,1,0:T(8,128)(2,1)} %bitcast.175, ...), custom_call_target="tpu_custom_call", output_to_operand_aliasing={{0}: (4, {})} | custom-call | flops 1 | bytes 1 | tf_op jit(solution)/shard_map/pallas_call | solution.py:287
  407.6 1.5 convolution_add_fusion.5
  409.1 1.4 collective-permute-start.20
  410.6 2.9 collective-permute-start.18
  414.3 1.2 select_bitcast_fusion.7
  415.7 2.3 broadcast_in_dim.26
  418.0 5.0 %all-to-all-start.3 = ((bf16[4,1280,384]{2,1,0:T(8,128)(2,1)}), bf16[4,1280,384]{2,1,0:T(8,128)(2,1)}, u32[]{:S(2)}, u32[]{:S(2)}) async-start(bf16[4,1280,384]{2,1,0:T(8,128)(2,1)} %broadcast_in_dim.26), calls=%async_computation.5 | async-start | bytes 7864320 | tf_op jit(solution)/shard_map/all_to_all | solution.py:650
  423.4 1.4 collective-permute-start.6
  424.8 3.1 collective-permute-start.4
  427.9 2.9 convert_element_type.299
  431.2 1.6 pad_maximum_fusion.1
  432.8 1.6 pad_maximum_fusion
  434.4 1.6 slice_bitcast_fusion
  435.9 1.2 fusion.91
  437.2 2.9 collective-permute-start.26
  440.6 5.2 %collective-permute-done.5 = bf16[320,384]{1,0:T(8,128)(2,1)S(1)} collective-permute-done((bf16[320,384]{1,0:T(8,128)(2,1)S(1)}, bf16[320,384]{1,0:T(8,128)(2,1)S(1)}, u32[]{:S(2)}, u32[]{:S(2)}) %collective-permute-start.5) | collective-permute-done | bytes 245792 | tf_op jit(solution)/shard_map/ppermute | solution.py:658
  446.7 21.8 %collective-permute-done.26 = f32[3392]{0:T(1024)S(1)} collective-permute-done((f32[3392]{0:T(1024)S(1)}, f32[3392]{0:T(1024)S(1)}, u32[]{:S(2)}, u32[]{:S(2)}) %collective-permute-start.26) | collective-permute-done | bytes 13600 | tf_op jit(solution)/shard_map/ppermute | solution.py:658
  471.2 2.6 bitcast_convert_fusion
  473.8 1.2 fusion.93
  475.1 2.6 fusion.94
  (218 shorter events, 28.4 us)
Async XLA Ops:
  7.2 82.0 %copy-start = (bf16[384,768]{1,0:T(8,128)(2,1)S(1)}, bf16[384,768]{1,0:T(8,128)(2,1)}, u32[]{:S(2)}) copy-start(bf16[384,768]{1,0:T(8,128)(2,1)} %param.36) | copy-start | bytes 1769476
  7.2 101.3 %all-gather.5.cloned.1.call-start = ((), (), s32[]{:S(2)}) async-start(), calls=%async_computation.8 | async-start | bytes 5120000 | tf_op jit(solution)/shard_map/all_gather | solution.py:783
  11.4 12.3 %copy-start.39 = (bf16[384]{0:T(512)(128)(2,1)S(1)}, bf16[384]{0:T(512)(128)(2,1)}, u32[]{:S(2)}) copy-start(bf16[384]{0:T(512)(128)(2,1)} %param.47) | copy-start | bytes 2308
  11.4 12.4 %copy-start.3 = (bf16[1,320,384]{2,1,0:T(8,128)(2,1)S(1)}, bf16[1,320,384]{2,1,0:T(8,128)(2,1)}, u32[]{:S(2)}) copy-start(bf16[1,320,384]{2,1,0:T(8,128)(2,1)} %param.29) | copy-start | bytes 737284
  11.4 12.8 %copy-start.34 = (bf16[768]{0:T(1024)(128)(2,1)S(1)}, bf16[768]{0:T(1024)(128)(2,1)}, u32[]{:S(2)}) copy-start(bf16[768]{0:T(1024)(128)(2,1)} %param.49) | copy-start | bytes 4612
  11.4 12.8 %copy-start.35 = (bf16[768]{0:T(1024)(128)(2,1)S(1)}, bf16[768]{0:T(1024)(128)(2,1)}, u32[]{:S(2)}) copy-start(bf16[768]{0:T(1024)(128)(2,1)} %param.55) | copy-start | bytes 4612
  11.4 12.8 %copy-start.9 = (bf16[384,768]{1,0:T(8,128)(2,1)S(1)}, bf16[384,768]{1,0:T(8,128)(2,1)}, u32[]{:S(2)}) copy-start(bf16[384,768]{1,0:T(8,128)(2,1)} %param.50) | copy-start | bytes 1769476
  23.7 145.0 %all-gather.7.cloned.1.call-start = ((), (), s32[]{:S(2)}) async-start(), calls=%async_computation.9 | async-start | bytes 3072000 | tf_op jit(solution)/shard_map/all_gather | solution.py:783
  28.6 51.7 %copy-start.4 = (f32[320,768]{1,0:T(8,128)S(1)}, f32[320,768]{1,0:T(8,128)}, u32[]{:S(2)}) copy-start(f32[320,768]{1,0:T(8,128)} %fusion.15.lifting.lifting_second) | copy-start | bytes 2949124
  81.8 3.1 copy-start.10
  81.8 3.1 copy-start.8
  81.8 3.1 copy-start.16
  84.0 3.1 copy-start.40
  84.0 3.1 copy-start.38
  84.0 3.7 copy-start.36
  84.0 3.7 copy-start.37
  84.0 3.7 copy-start.21
  86.5 22.0 %collective-permute-start = (bf16[6144,384]{1,0:T(8,128)(2,1)}, bf16[6144,384]{1,0:T(8,128)(2,1)}, u32[]{:S(2)}, u32[]{:S(2)}) collective-permute-start(bf16[6144,384]{1,0:T(8,128)(2,1)} %get-tuple-element.364), channel_id=1, source_target_pairs={{0,1},{1,0},{2,3},{3,2},{4,5},{5,4},{6,7},{7,6},{8,9},{9,8},{10,11... | collective-permute-start | bytes 14155784 | tf_op jit(solution)/shard_map/ppermute | solution.py:646
  108.5 12.7 %collective-permute-start.1 = (bf16[4,2,768,384]{3,2,1,0:T(8,128)(2,1)}, bf16[4,2,768,384]{3,2,1,0:T(8,128)(2,1)}, u32[]{:S(2)}, u32[]{:S(2)}) collective-permute-start(bf16[4,2,768,384]{3,2,1,0:T(8,128)(2,1)} %get-tuple-element.156.mine), channel_id=1, source_target_pairs={{0,1},{1,0},{2,3},{3,2},{4,5},{5,4},{6,7},{7,6},{8,9},{9,8},{10,11... | collective-permute-start | bytes 14155784 | tf_op jit(solution)/shard_map/ppermute | solution.py:646
  115.7 68.7 %all-to-all-start = ((bf16[4,1536,384]{2,1,0:T(8,128)(2,1)}), bf16[4,1536,384]{2,1,0:T(8,128)(2,1)}, u32[]{:S(2)}, u32[]{:S(2)}) async-start(bf16[4,1536,384]{2,1,0:T(8,128)(2,1)} %bitcast.161), calls=%async_computation | async-start | bytes 9437184 | tf_op jit(solution)/shard_map/all_to_all | solution.py:650
  121.1 154.0 %reduce-scatter.3.cloned.1.call-start = ((), (), s32[]{:S(2)}) async-start(), calls=%async_computation.6 | async-start | bytes 5120000 | tf_op jit(solution)/shard_map/reduce_scatter | solution.py:789
  168.4 43.5 %collective-permute-start.2 = (bf16[4,2,480,384]{3,2,1,0:T(8,128)(2,1)}, bf16[4,2,480,384]{3,2,1,0:T(8,128)(2,1)}, u32[]{:S(2)}, u32[]{:S(2)}) collective-permute-start(bf16[4,2,480,384]{3,2,1,0:T(8,128)(2,1)} %get-tuple-element.188), channel_id=1, source_target_pairs={{0,1},{1,0},{2,3},{3,2},{4,5},{5,4},{6,7},{7,6},{8,9},{9,8},{10,11... | collective-permute-start | bytes 8847368 | tf_op jit(solution)/shard_map/ppermute | solution.py:646
  168.6 182.2 %reduce-scatter.5.cloned.1.call-start = ((), (), s32[]{:S(2)}) async-start(), calls=%async_computation.7 | async-start | bytes 3072000 | tf_op jit(solution)/shard_map/reduce_scatter | solution.py:789
  203.8 8.2 %collective-permute-start.3 = (bf16[4,2,288,384]{3,2,1,0:T(8,128)(2,1)}, bf16[4,2,288,384]{3,2,1,0:T(8,128)(2,1)S(1)}, u32[]{:S(2)}, u32[]{:S(2)}) collective-permute-start(bf16[4,2,288,384]{3,2,1,0:T(8,128)(2,1)} %get-tuple-element.189), channel_id=1, source_target_pairs={{0,1},{1,0},{2,3},{3,2},{4,5},{5,4},{6,7},{7,6},{8,9},{9,8},{10,11... | collective-permute-start | bytes 5308424 | tf_op jit(solution)/shard_map/ppermute | solution.py:646
  206.5 59.7 %collective-permute-start.9 = (bf16[384,384]{1,0:T(8,128)(2,1)}, bf16[384,384]{1,0:T(8,128)(2,1)S(1)}, u32[]{:S(2)}, u32[]{:S(2)}) collective-permute-start(bf16[384,384]{1,0:T(8,128)(2,1)} %get-tuple-element.345), channel_id=1, source_target_pairs={{0,6},{2,4},{4,2},{6,0},{1,7},{3,5},{5,3},{7,1},{8,14},{10,12},{12... | collective-permute-start | bytes 884744 | tf_op jit(solution)/shard_map/ppermute | solution.py:658
  211.4 55.6 %collective-permute-start.8 = (bf16[384,384]{1,0:T(8,128)(2,1)}, bf16[384,384]{1,0:T(8,128)(2,1)}, u32[]{:S(2)}, u32[]{:S(2)}) collective-permute-start(bf16[384,384]{1,0:T(8,128)(2,1)} %get-tuple-element.346), channel_id=1, source_target_pairs={{0,4},{2,6},{4,0},{6,2},{1,5},{3,7},{5,1},{7,3},{8,12},{10,14},{12... | collective-permute-start | bytes 884744 | tf_op jit(solution)/shard_map/ppermute | solution.py:658
  211.4 55.6 %collective-permute-start.7 = (bf16[384,384]{1,0:T(8,128)(2,1)S(1)}, bf16[384,384]{1,0:T(8,128)(2,1)}, u32[]{:S(2)}, u32[]{:S(2)}) collective-permute-start(bf16[384,384]{1,0:T(8,128)(2,1)S(1)} %get-tuple-element.347), channel_id=1, source_target_pairs={{0,2},{2,0},{4,6},{6,4},{1,3},{3,1},{5,7},{7,5},{8,10},{10,8},{12,... | collective-permute-start | bytes 884744 | tf_op jit(solution)/shard_map/ppermute | solution.py:658
  244.2 24.1 %copy-start.1 = (f32[320,768]{1,0:T(8,128)S(1)}, f32[320,768]{1,0:T(8,128)}, u32[]{:S(2)}) copy-start(f32[320,768]{1,0:T(8,128)} %fusion.3.finish) | copy-start | bytes 2949124
  244.2 24.1 %copy-start.2 = (f32[320,768]{1,0:T(8,128)S(1)}, f32[320,768]{1,0:T(8,128)}, u32[]{:S(2)}) copy-start(f32[320,768]{1,0:T(8,128)} %fusion.7.lifting.lifting_first) | copy-start | bytes 2949124
  244.2 24.1 %copy-start.14 = (f32[320,768]{1,0:T(8,128)S(1)}, f32[320,768]{1,0:T(8,128)}, u32[]{:S(2)}) copy-start(f32[320,768]{1,0:T(8,128)} %get-tuple-element.200) | copy-start | bytes 2949124
  244.2 24.1 %copy-start.15 = (f32[320,768]{1,0:T(8,128)S(1)}, f32[320,768]{1,0:T(8,128)}, u32[]{:S(2)}) copy-start(f32[320,768]{1,0:T(8,128)} %get-tuple-element.196) | copy-start | bytes 2949124
  275.1 7.1 %collective-permute-start.13 = (bf16[5120,384]{1,0:T(8,128)(2,1)}, bf16[5120,384]{1,0:T(8,128)(2,1)}, u32[]{:S(2)}, u32[]{:S(2)}) collective-permute-start(bf16[5120,384]{1,0:T(8,128)(2,1)} %get-tuple-element.358), channel_id=1, source_target_pairs={{0,1},{1,0},{2,3},{3,2},{4,5},{5,4},{6,7},{7,6},{8,9},{9,8},{10,11... | collective-permute-start | bytes 11796488 | tf_op jit(solution)/shard_map/ppermute | solution.py:646
  288.9 6.9 %copy-start.7 = (f32[320,768]{1,0:T(8,128)S(1)}, f32[320,768]{1,0:T(8,128)}, u32[]{:S(2)}) copy-start(f32[320,768]{1,0:T(8,128)} %get-tuple-element.146) | copy-start | bytes 2949124
  288.9 62.0 %all-to-all-start.1 = ((bf16[4,1280,384]{2,1,0:T(8,128)(2,1)}), bf16[4,1280,384]{2,1,0:T(8,128)(2,1)}, u32[]{:S(2)}, u32[]{:S(2)}) async-start(bf16[4,1280,384]{2,1,0:T(8,128)(2,1)} %bitcast.164), calls=%async_computation.2 | async-start | bytes 7864320 | tf_op jit(solution)/shard_map/all_to_all | solution.py:650
  294.0 8.5 %copy-start.19 = (bf16[384,768]{1,0:T(8,128)(2,1)S(1)}, bf16[384,768]{1,0:T(8,128)(2,1)}, u32[]{:S(2)}) copy-start(bf16[384,768]{1,0:T(8,128)(2,1)} %param.34) | copy-start | bytes 1769476
  298.0 18.0 %collective-permute-start.12 = (bf16[384,384]{1,0:T(8,128)(2,1)S(1)}, bf16[384,384]{1,0:T(8,128)(2,1)S(1)}, u32[]{:S(2)}, u32[]{:S(2)}) collective-permute-start(bf16[384,384]{1,0:T(8,128)(2,1)S(1)} %add_convert_fusion.5), channel_id=1, source_target_pairs={{0,6},{2,4},{4,2},{6,0},{1,7},{3,5},{5,3},{7,1},{8,14},{10,12},{12... | collective-permute-start | bytes 884744 | tf_op jit(solution)/shard_map/ppermute | solution.py:658
  301.8 49.1 %collective-permute-start.11 = (bf16[384,384]{1,0:T(8,128)(2,1)S(1)}, bf16[384,384]{1,0:T(8,128)(2,1)S(1)}, u32[]{:S(2)}, u32[]{:S(2)}) collective-permute-start(bf16[384,384]{1,0:T(8,128)(2,1)S(1)} %add_convert_fusion.5), channel_id=1, source_target_pairs={{0,4},{2,6},{4,0},{6,2},{1,5},{3,7},{5,1},{7,3},{8,12},{10,14},{12... | collective-permute-start | bytes 884744 | tf_op jit(solution)/shard_map/ppermute | solution.py:658
  301.8 49.1 %collective-permute-start.10 = (bf16[384,384]{1,0:T(8,128)(2,1)S(1)}, bf16[384,384]{1,0:T(8,128)(2,1)S(1)}, u32[]{:S(2)}, u32[]{:S(2)}) collective-permute-start(bf16[384,384]{1,0:T(8,128)(2,1)S(1)} %add_convert_fusion.5), channel_id=1, source_target_pairs={{0,2},{2,0},{4,6},{6,4},{1,3},{3,1},{5,7},{7,5},{8,10},{10,8},{12,... | collective-permute-start | bytes 884744 | tf_op jit(solution)/shard_map/ppermute | solution.py:658
  316.0 34.8 %copy-start.28 = (bf16[384,384]{1,0:T(8,128)(2,1)}, bf16[384,384]{1,0:T(8,128)(2,1)S(1)}, u32[]{:S(2)}) copy-start(bf16[384,384]{1,0:T(8,128)(2,1)S(1)} %collective-permute-done.12) | copy-start | bytes 884740
  355.7 5.2 %copy-start.27 = (f32[768,1]{1,0:T(8,128)S(1)}, f32[768,1]{1,0:T(8,128)}, u32[]{:S(2)}) copy-start(f32[768,1]{1,0:T(8,128)} %get-tuple-element.238) | copy-start | bytes 9220
  355.7 5.4 %copy-start.24 = (bf16[320,768]{1,0:T(8,128)(2,1)S(1)}, bf16[320,768]{1,0:T(8,128)(2,1)}, u32[]{:S(2)}) copy-start(bf16[320,768]{1,0:T(8,128)(2,1)} %copy-done.23) | copy-start | bytes 1474564
  355.7 5.4 %copy-start.25 = (f32[320,384]{1,0:T(8,128)S(1)}, f32[320,384]{1,0:T(8,128)}, u32[]{:S(2)}) copy-start(f32[320,384]{1,0:T(8,128)} %convolution_add_fusion.6) | copy-start | bytes 1474564
  355.7 58.6 %all-to-all-start.2 = ((bf16[4,1536,384]{2,1,0:T(8,128)(2,1)}), bf16[4,1536,384]{2,1,0:T(8,128)(2,1)}, u32[]{:S(2)}, u32[]{:S(2)}) async-start(bf16[4,1536,384]{2,1,0:T(8,128)(2,1)} %broadcast_in_dim.24), calls=%async_computation.4 | async-start | bytes 9437184 | tf_op jit(solution)/shard_map/all_to_all | solution.py:650
  366.4 20.7 %collective-permute-start.16 = (bf16[320,384]{1,0:T(8,128)(2,1)S(1)}, bf16[320,384]{1,0:T(8,128)(2,1)S(1)}, u32[]{:S(2)}, u32[]{:S(2)}) collective-permute-start(bf16[320,384]{1,0:T(8,128)(2,1)S(1)} %get-tuple-element.353), channel_id=1, source_target_pairs={{0,6},{2,4},{4,2},{6,0},{1,7},{3,5},{5,3},{7,1},{8,14},{10,12},{12... | collective-permute-start | bytes 737288 | tf_op jit(solution)/shard_map/ppermute | solution.py:658
  367.9 21.3 %collective-permute-start.15 = (bf16[320,384]{1,0:T(8,128)(2,1)S(1)}, bf16[320,384]{1,0:T(8,128)(2,1)S(1)}, u32[]{:S(2)}, u32[]{:S(2)}) collective-permute-start(bf16[320,384]{1,0:T(8,128)(2,1)S(1)} %get-tuple-element.354), channel_id=1, source_target_pairs={{0,4},{2,6},{4,0},{6,2},{1,5},{3,7},{5,1},{7,3},{8,12},{10,14},{12... | collective-permute-start | bytes 737288 | tf_op jit(solution)/shard_map/ppermute | solution.py:658
  368.1 21.1 %collective-permute-start.14 = (bf16[320,384]{1,0:T(8,128)(2,1)S(1)}, bf16[320,384]{1,0:T(8,128)(2,1)S(1)}, u32[]{:S(2)}, u32[]{:S(2)}) collective-permute-start(bf16[320,384]{1,0:T(8,128)(2,1)S(1)} %get-tuple-element.355), channel_id=1, source_target_pairs={{0,2},{2,0},{4,6},{6,4},{1,3},{3,1},{5,7},{7,5},{8,10},{10,8},{12,... | collective-permute-start | bytes 737288 | tf_op jit(solution)/shard_map/ppermute | solution.py:658
  389.3 21.3 %collective-permute-start.23 = (bf16[320,384]{1,0:T(8,128)(2,1)S(1)}, bf16[320,384]{1,0:T(8,128)(2,1)S(1)}, u32[]{:S(2)}, u32[]{:S(2)}) collective-permute-start(bf16[320,384]{1,0:T(8,128)(2,1)S(1)} %add_convert_fusion.6), channel_id=1, source_target_pairs={{0,6},{2,4},{4,2},{6,0},{1,7},{3,5},{5,3},{7,1},{8,14},{10,12},{12... | collective-permute-start | bytes 737288 | tf_op jit(solution)/shard_map/ppermute | solution.py:658
  390.8 22.8 %collective-permute-start.22 = (bf16[320,384]{1,0:T(8,128)(2,1)S(1)}, bf16[320,384]{1,0:T(8,128)(2,1)}, u32[]{:S(2)}, u32[]{:S(2)}) collective-permute-start(bf16[320,384]{1,0:T(8,128)(2,1)S(1)} %add_convert_fusion.6), channel_id=1, source_target_pairs={{0,4},{2,6},{4,0},{6,2},{1,5},{3,7},{5,1},{7,3},{8,12},{10,14},{12... | collective-permute-start | bytes 737288 | tf_op jit(solution)/shard_map/ppermute | solution.py:658
  390.8 22.8 %collective-permute-start.21 = (bf16[320,384]{1,0:T(8,128)(2,1)S(1)}, bf16[320,384]{1,0:T(8,128)(2,1)}, u32[]{:S(2)}, u32[]{:S(2)}) collective-permute-start(bf16[320,384]{1,0:T(8,128)(2,1)S(1)} %add_convert_fusion.6), channel_id=1, source_target_pairs={{0,2},{2,0},{4,6},{6,4},{1,3},{3,1},{5,7},{7,5},{8,10},{10,8},{12,... | collective-permute-start | bytes 737288 | tf_op jit(solution)/shard_map/ppermute | solution.py:658
  393.8 12.2 %copy-start.32 = (bf16[128,16]{0,1:T(8,128)(2,1)S(1)}, bf16[128,16]{0,1:T(8,128)(2,1)}, u32[]{:S(2)}) copy-start(bf16[128,16]{0,1:T(8,128)(2,1)} %param.44) | copy-start | bytes 12292
  393.8 12.2 %copy-start.33 = (f32[16,128]{1,0:T(8,128)S(1)}, f32[16,128]{1,0:T(8,128)}, u32[]{:S(2)}) copy-start(f32[16,128]{1,0:T(8,128)} %get-tuple-element.239) | copy-start | bytes 24580
  393.8 13.7 %copy-start.26 = (f32[320,384]{1,0:T(8,128)S(1)}, f32[320,384]{1,0:T(8,128)}, u32[]{:S(2)}) copy-start(f32[320,384]{1,0:T(8,128)} %get-tuple-element.321) | copy-start | bytes 1474564
  407.5 1.6 collective-permute-start.17
  409.1 15.7 %collective-permute-start.20 = (f32[3392]{0:T(1024)S(1)}, f32[3392]{0:T(1024)S(1)}, u32[]{:S(2)}, u32[]{:S(2)}) collective-permute-start(f32[3392]{0:T(1024)S(1)} %add.292), channel_id=1, source_target_pairs={{0,6},{2,4},{4,2},{6,0},{1,7},{3,5},{5,3},{7,1},{8,14},{10,12},{12... | collective-permute-start | bytes 40712 | tf_op jit(solution)/shard_map/ppermute | solution.py:658
  410.5 17.4 %collective-permute-start.19 = (f32[3392]{0:T(1024)S(1)}, f32[3392]{0:T(1024)S(1)}, u32[]{:S(2)}, u32[]{:S(2)}) collective-permute-start(f32[3392]{0:T(1024)S(1)} %add.292), channel_id=1, source_target_pairs={{0,4},{2,6},{4,0},{6,2},{1,5},{3,7},{5,1},{7,3},{8,12},{10,14},{12... | collective-permute-start | bytes 40712 | tf_op jit(solution)/shard_map/ppermute | solution.py:658
  410.6 17.3 %collective-permute-start.18 = (f32[3392]{0:T(1024)S(1)}, f32[3392]{0:T(1024)S(1)}, u32[]{:S(2)}, u32[]{:S(2)}) collective-permute-start(f32[3392]{0:T(1024)S(1)} %add.292), channel_id=1, source_target_pairs={{0,2},{2,0},{4,6},{6,4},{1,3},{3,1},{5,7},{7,5},{8,10},{10,8},{12,... | collective-permute-start | bytes 40712 | tf_op jit(solution)/shard_map/ppermute | solution.py:658
  418.0 5.0 %copy-start.22 = (bf16[384,768]{1,0:T(8,128)(2,1)S(1)}, bf16[384,768]{1,0:T(8,128)(2,1)}, u32[]{:S(2)}) copy-start(bf16[384,768]{1,0:T(8,128)(2,1)} %param.45) | copy-start | bytes 1769476
  418.0 53.2 %all-to-all-start.3 = ((bf16[4,1280,384]{2,1,0:T(8,128)(2,1)}), bf16[4,1280,384]{2,1,0:T(8,128)(2,1)}, u32[]{:S(2)}, u32[]{:S(2)}) async-start(bf16[4,1280,384]{2,1,0:T(8,128)(2,1)} %broadcast_in_dim.26), calls=%async_computation.5 | async-start | bytes 7864320 | tf_op jit(solution)/shard_map/all_to_all | solution.py:650
  423.4 17.1 %collective-permute-start.6 = (bf16[320,384]{1,0:T(8,128)(2,1)S(1)}, bf16[320,384]{1,0:T(8,128)(2,1)S(1)}, u32[]{:S(2)}, u32[]{:S(2)}) collective-permute-start(bf16[320,384]{1,0:T(8,128)(2,1)S(1)} %fusion.16), channel_id=1, source_target_pairs={{0,6},{2,4},{4,2},{6,0},{1,7},{3,5},{5,3},{7,1},{8,14},{10,12},{12... | collective-permute-start | bytes 737288 | tf_op jit(solution)/shard_map/ppermute | solution.py:658
  424.8 21.0 %collective-permute-start.5 = (bf16[320,384]{1,0:T(8,128)(2,1)S(1)}, bf16[320,384]{1,0:T(8,128)(2,1)S(1)}, u32[]{:S(2)}, u32[]{:S(2)}) collective-permute-start(bf16[320,384]{1,0:T(8,128)(2,1)S(1)} %fusion.16), channel_id=1, source_target_pairs={{0,4},{2,6},{4,0},{6,2},{1,5},{3,7},{5,1},{7,3},{8,12},{10,14},{12... | collective-permute-start | bytes 737288 | tf_op jit(solution)/shard_map/ppermute | solution.py:658
  424.8 21.0 %collective-permute-start.4 = (bf16[320,384]{1,0:T(8,128)(2,1)S(1)}, bf16[320,384]{1,0:T(8,128)(2,1)S(1)}, u32[]{:S(2)}, u32[]{:S(2)}) collective-permute-start(bf16[320,384]{1,0:T(8,128)(2,1)S(1)} %fusion.16), channel_id=1, source_target_pairs={{0,2},{2,0},{4,6},{6,4},{1,3},{3,1},{5,7},{7,5},{8,10},{10,8},{12,... | collective-permute-start | bytes 737288 | tf_op jit(solution)/shard_map/ppermute | solution.py:658
  437.2 31.4 %collective-permute-start.26 = (f32[3392]{0:T(1024)S(1)}, f32[3392]{0:T(1024)S(1)}, u32[]{:S(2)}, u32[]{:S(2)}) collective-permute-start(f32[3392]{0:T(1024)S(1)} %add_add_fusion.1), channel_id=1, source_target_pairs={{0,24},{8,16},{16,8},{24,0},{1,25},{9,17},{17,9},{25,1},{2,26},{10... | collective-permute-start | bytes 40712 | tf_op jit(solution)/shard_map/ppermute | solution.py:658
  440.0 28.5 %collective-permute-start.25 = (f32[3392]{0:T(1024)S(1)}, f32[3392]{0:T(1024)S(1)}, u32[]{:S(2)}, u32[]{:S(2)}) collective-permute-start(f32[3392]{0:T(1024)S(1)} %add_add_fusion.1), channel_id=1, source_target_pairs={{0,16},{8,24},{16,0},{24,8},{1,17},{9,25},{17,1},{25,9},{2,18},{10... | collective-permute-start | bytes 40712 | tf_op jit(solution)/shard_map/ppermute | solution.py:658
  440.6 28.0 %collective-permute-start.24 = (f32[3392]{0:T(1024)S(1)}, f32[3392]{0:T(1024)S(1)}, u32[]{:S(2)}, u32[]{:S(2)}) collective-permute-start(f32[3392]{0:T(1024)S(1)} %add_add_fusion.1), channel_id=1, source_target_pairs={{0,8},{8,0},{16,24},{24,16},{1,9},{9,1},{17,25},{25,17},{2,10},{10... | collective-permute-start | bytes 40712 | tf_op jit(solution)/shard_map/ppermute | solution.py:658
  (12 other events, 21.8 us)
Sparse Core Ops, SparseCore 0:
  23.8 81.8 all-gather.4
  108.7 55.1 all-gather.6
  168.7 96.8 reduce-scatter.2
  275.2 70.1 reduce-scatter.4

commit v6 on v5

--- a/solution.py
+++ b/solution.py
@@ -11,7 +11,7 @@
 LANES = 128
 VMEM_LIMIT = 56 * 2**20
 SHARES = (10, 6)
-CALLS = 2
+CALLS = (1, 2)
 EARLY_APART = ("smp",)
 LATE_APART = ("smp",)
 f32 = jnp.float32
@@ -909,7 +909,7 @@
     def attend(meta, part, call, earlier):
         return list(
             attention(
-                meta, query, pair_of_cores, gate, delta_gated, bias_rows[part], part, call, CALLS,
+                meta, query, pair_of_cores, gate, delta_gated, bias_rows[part], part, call, CALLS[part],
                 earlier,
             )
         )
@@ -919,7 +919,7 @@
     early.first()
     meta = early.lead(meta)
     early.trade("cplx")
-    attended = [attend(meta, 0, 1, attend(meta, 0, 0, ()))]
+    attended = [attend(meta, 0, 0, ())]
     done = attend(meta, 1, 0, ())
     done[0] = early.wait(done[0])
     early.second()

time: 488 us -> 486 us (level)
    pallas_call x4 -> x3, Pallas kernels: 78.5 us -> 75.4 us  [attention(): pl.pallas_call(functools.partial(attention_kernel, step=step), grid_spec=...]
where the time goes in v6:
time: 486 us; the launch traced here: 482 us
  Pallas kernels  237 us (49%)
  waiting for transfers between devices  84.1 us (17%)
  starting transfers between devices  53.1 us (11%)
  other arithmetic  42.5 us (9%)
  local copies, waits for them, and re-layouts  26.4 us (5%)
  matrix products  22.8 us (5%)
  between operations  15.5 us (3%)
    ppermute x21, waiting for transfers between devices, exchange(): lax.ppermute(array, axis, [(i, i ^ bit) for i in range(lax.axis_size(axis...  76.2 us
    pallas_call x3, Pallas kernels, attention(): pl.pallas_call(functools.partial(attention_kernel, step=step), grid_spec=...  75.4 us
    pallas_call x1, Pallas kernels, transition(): pl.pallas_call(transition_kernel, grid_spec=pltpu.PrefetchScalarGridSpec(...  51.9 us
    ppermute x21, starting transfers between devices, exchange(): lax.ppermute(array, axis, [(i, i ^ bit) for i in range(lax.axis_size(axis...  31.1 us
    pallas_call x2, Pallas kernels, rows_back(): pl.pallas_call(rows_kernel, grid_spec=pltpu.PrefetchScalarGridSpec(num_sc...  31 us
    pallas_call x2, Pallas kernels, pair_backward(): pl.pallas_call(functools.partial(pair_backward_kernel, block=block, heads...  28.4 us
    pallas_call x1, Pallas kernels, weight_sums(): pl.pallas_call(weights_kernel, grid_spec=pltpu.PrefetchScalarGridSpec(num...  22 us
    all_to_all x4, starting transfers between devices, traded(): return lax.all_to_all(array, axis, 0, 0)  20.4 us
  transfers between devices with their start and end apart: 35, of which 8 were waited for; matrix products, arithmetic and copies ran while one was open for 16% of the time, Pallas kernels for 47%

profile of v6, /device:TPU:0, one launch (start us, length us, event | category | flops | bytes accessed | tf_op | source)
XLA Modules:
  0.0 481.6 jit_solution(10816456027159235326)
XLA Ops:
  11.4 12.2 %shard_map.475 = (bf16[10,80,640]{2,1,0:T(8,128)(2,1)}, bf16[6,80,640]{2,1,0:T(8,128)(2,1)}) custom-call(bf16[80,640,128]{2,1,0:T(8,128)(2,1)} %bitcast.146, bf16[32,128]{1,0:T(8,128)(2,1)} %pad_maximum_fusion.4.weight), custom_call_target="tpu_custom_call" | custom-call | flops 1 | bytes 1 | tf_op jit(solution)/shard_map/pallas_call | solution.py:233
  24.2 1.4 fusion.85.shifting
  25.6 1.5 fusion.15.lifting.lifting_second
  27.1 1.4 fusion.11.closing
  28.6 51.9 %shard_map.476 = (f32[4,320,768]{2,1,0:T(8,128)}, f32[4,320,768]{2,1,0:T(8,128)}, f32[320,768]{1,0:T(8,128)}, f32[320,768]{1,0:T(8,128)}, f32[320,768]{1,0:T(8,1...) custom-call(s32[2]{0:T(128)} %pad_add_fusion.meta, bf16[4,320,768]{2,1,0:T(8,128)(2,1)} %bitcast.156, ...), custom_call_target="tpu_custom_call" | custom-call | flops 1 | bytes 1 | tf_op jit(solution)/shard_map/pallas_call | solution.py:455
  80.5 1.5 fusion.33
  87.9 1.4 fusion.3.finish
  89.3 1.4 fusion.79.shifting
  90.8 1.5 fusion.7.lifting.lifting_first
  92.3 16.4 %shard_map.477 = (bf16[4,768,320]{2,1,0:T(8,128)(2,1)}, bf16[4,2,768,384]{3,2,1,0:T(8,128)(2,1)}, f32[4,768,320]{2,1,0:T(8,128)}, f32[4,768,320]{2,1,0:T(8,128)}, bf16[4,320,768]{2,1,0:T(8,128)(2,1)}) custom-call(s32[2]{0:T(128)} %pad_add_fusion.meta, bf16[4,320,768]{2,1,0:T(8,128)(2,1)} %bitcast.157, bf16[4,320,768]{2,1,0:T(8,128)(2,1)} %bitcast.150, ...), custom_call_target="tpu_custom_call" | custom-call | flops 1 | bytes 1 | tf_op jit(solution)/shard_map/pallas_call | solution.py:371
  108.7 7.1 %add_convert_fusion = bf16[6144,384]{1,0:T(8,128)(2,1)} fusion(bf16[6144,384]{1,0:T(8,128)(2,1)} %collective-permute-done, bf16[6144,384]{1,0:T(8,128)(2,1)} %get-tuple-element.142), kind=kLoop, calls=%fused_computation | loop fusion | flops 9437184 | bytes 14155776 | tf_op jit(solution)/shard_map/convert_element_type | solution.py:716
  115.9 5.4 %all-to-all-start = ((bf16[4,1536,384]{2,1,0:T(8,128)(2,1)}), bf16[4,1536,384]{2,1,0:T(8,128)(2,1)}, u32[]{:S(2)}, u32[]{:S(2)}) async-start(bf16[4,1536,384]{2,1,0:T(8,128)(2,1)} %bitcast.161), calls=%async_computation | async-start | bytes 9437184 | tf_op jit(solution)/shard_map/all_to_all | solution.py:650
  121.3 44.2 %shard_map.479 = (bf16[4,480,320]{2,1,0:T(8,128)(2,1)}, bf16[4,480,320]{2,1,0:T(8,128)(2,1)}, bf16[4,480,320]{2,1,0:T(8,128)(2,1)}, f32[4,2,480,320]{3,2,1,0:T(8...) custom-call(s32[2]{0:T(128)} %pad_add_fusion.meta, ...), custom_call_target="tpu_custom_call" | custom-call | flops 1 | bytes 1 | tf_op jit(solution)/shard_map/pallas_call | solution.py:163
  165.7 15.7 %shard_map.478 = (bf16[4,288,320]{2,1,0:T(8,128)(2,1)}, bf16[4,288,320]{2,1,0:T(8,128)(2,1)}, bf16[4,288,320]{2,1,0:T(8,128)(2,1)}, f32[4,2,288,320]{3,2,1,0:T(8...) custom-call(s32[2]{0:T(128)} %pad_add_fusion.meta, ...), custom_call_target="tpu_custom_call" | custom-call | flops 1 | bytes 1 | tf_op jit(solution)/shard_map/pallas_call | solution.py:163
  181.4 3.9 add_convert_fusion.2
  185.4 15.5 %shard_map.480 = (bf16[4,288,320]{2,1,0:T(8,128)(2,1)}, bf16[4,288,320]{2,1,0:T(8,128)(2,1)}, bf16[4,288,320]{2,1,0:T(8,128)(2,1)}, f32[4,2,288,320]{3,2,1,0:T(8...) custom-call(s32[2]{0:T(128)} %pad_add_fusion.meta, ...), custom_call_target="tpu_custom_call", output_to_operand_aliasing={{0}: (7, {}), {1}: (8, {}), {2}: (9, {}), {3}: (10, {}), {4... | custom-call | flops 1 | bytes 1 | tf_op jit(solution)/shard_map/pallas_call | solution.py:163
  201.4 2.2 dynamic-slice_bitcast_fusion
  203.6 4.9 %collective-permute-start.9 = (bf16[384,384]{1,0:T(8,128)(2,1)}, bf16[384,384]{1,0:T(8,128)(2,1)S(1)}, u32[]{:S(2)}, u32[]{:S(2)}) collective-permute-start(bf16[384,384]{1,0:T(8,128)(2,1)} %get-tuple-element.333), channel_id=1, source_target_pairs={{0,6},{2,4},{4,2},{6,0},{1,7},{3,5},{5,3},{7,1},{8,14},{10,12},{12... | collective-permute-start | bytes 884744 | tf_op jit(solution)/shard_map/ppermute | solution.py:658
  209.0 1.2 copy-done.5
  210.3 15.2 %shard_map.481 = (bf16[4,320,768]{2,1,0:T(8,128)(2,1)}, f32[4,320,768]{2,1,0:T(8,128)}, bf16[4,768,320]{2,1,0:T(8,128)(2,1)}, bf16[4,768,320]{2,1,0:T(8,128)(2,1...) custom-call(s32[2]{0:T(128)} %pad_add_fusion.meta, bf16[4,320,768]{2,1,0:T(8,128)(2,1)} %bitcast.158, ...), custom_call_target="tpu_custom_call" | custom-call | flops 1 | bytes 1 | tf_op jit(solution)/shard_map/pallas_call | solution.py:621
  225.5 15.8 %shard_map.482 = (bf16[4,320,768]{2,1,0:T(8,128)(2,1)}, f32[4,320,768]{2,1,0:T(8,128)}, bf16[4,768,320]{2,1,0:T(8,128)(2,1)}, bf16[4,768,320]{2,1,0:T(8,128)(2,1...) custom-call(s32[2]{0:T(128)} %pad_add_fusion.meta, ...), custom_call_target="tpu_custom_call", output_to_operand_aliasing={{0}: (23, {}), {1}: (24, {}), {2}: (25, {}), {3}: (26, {})} | custom-call | flops 1 | bytes 1 | tf_op jit(solution)/shard_map/pallas_call | solution.py:621
  241.3 22.0 %shard_map.483 = (bf16[5120,384]{1,0:T(8,128)(2,1)}, bf16[5120,384]{1,0:T(8,128)(2,1)}, f32[768,1]{1,0:T(8,128)}) custom-call(s32[2]{0:T(128)} %pad_add_fusion.meta, bf16[4,320,768]{2,1,0:T(8,128)(2,1)} %bitcast.153, bf16[4,320,768]{2,1,0:T(8,128)(2,1)} %get-tuple-element.191.mixed, f32[320,768]{1,0:T(8,128)} %fusion.3.finish, ...), custom_call_target="tpu_custom_call" | custom-call | flops 1 | bytes 1 | tf_op jit(solution)/shard_map/pallas_call | solution.py:550
  264.0 1.3 add_convert_fusion.5
  265.4 1.9 fusion.89
  272.2 7.1 %collective-permute-done.13 = bf16[5120,384]{1,0:T(8,128)(2,1)} collective-permute-done((bf16[5120,384]{1,0:T(8,128)(2,1)}, bf16[5120,384]{1,0:T(8,128)(2,1)}, u32[]{:S(2)}, u32[]{:S(2)}) %collective-permute-start.13) | collective-permute-done | bytes 3932192 | tf_op jit(solution)/shard_map/ppermute | solution.py:646
  279.3 6.7 %add_convert_fusion.1 = bf16[5120,384]{1,0:T(8,128)(2,1)} fusion(bf16[5120,384]{1,0:T(8,128)(2,1)} %collective-permute-done.13, bf16[5120,384]{1,0:T(8,128)(2,1)} %get-tuple-element.345), kind=kLoop, calls=%fused_computation.1 | loop fusion | flops 7864320 | bytes 11796480 | tf_op jit(solution)/shard_map/convert_element_type | solution.py:716
  285.9 4.9 %all-to-all-start.1 = ((bf16[4,1280,384]{2,1,0:T(8,128)(2,1)}), bf16[4,1280,384]{2,1,0:T(8,128)(2,1)}, u32[]{:S(2)}, u32[]{:S(2)}) async-start(bf16[4,1280,384]{2,1,0:T(8,128)(2,1)} %bitcast.162), calls=%async_computation.2 | async-start | bytes 7864320 | tf_op jit(solution)/shard_map/all_to_all | solution.py:650
  291.1 1.7 fusion.103
  292.8 2.3 convolution_add_fusion.6
  295.1 3.7 collective-permute-start.12
  299.5 2.2 fusion.63
  301.8 11.3 %collective-permute-done.12 = bf16[384,384]{1,0:T(8,128)(2,1)S(1)} collective-permute-done((bf16[384,384]{1,0:T(8,128)(2,1)S(1)}, bf16[384,384]{1,0:T(8,128)(2,1)S(1)}, u32[]{:S(2)}, u32[]{:S(2)}) %collective-permute-start.12) | collective-permute-done | bytes 294944 | tf_op jit(solution)/shard_map/ppermute | solution.py:658
  313.1 34.9 %collective-permute-done.11 = bf16[384,384]{1,0:T(8,128)(2,1)S(1)} collective-permute-done((bf16[384,384]{1,0:T(8,128)(2,1)S(1)}, bf16[384,384]{1,0:T(8,128)(2,1)S(1)}, u32[]{:S(2)}, u32[]{:S(2)}) %collective-permute-start.11) | collective-permute-done | bytes 294944 | tf_op jit(solution)/shard_map/ppermute | solution.py:658
  348.8 1.3 select_bitcast_fusion.3
  350.3 2.5 broadcast_in_dim.24
  352.8 5.1 %all-to-all-start.2 = ((bf16[4,1536,384]{2,1,0:T(8,128)(2,1)}), bf16[4,1536,384]{2,1,0:T(8,128)(2,1)}, u32[]{:S(2)}, u32[]{:S(2)}) async-start(bf16[4,1536,384]{2,1,0:T(8,128)(2,1)} %broadcast_in_dim.24), calls=%async_computation.4 | async-start | bytes 9437184 | tf_op jit(solution)/shard_map/all_to_all | solution.py:650
  358.3 2.3 fusion.88
  360.8 2.6 add_convert_fusion.3
  363.5 1.5 collective-permute-start.16
  365.3 2.7 collective-permute-start.14
  368.0 16.2 %shard_map.484 = (f32[80,640,128]{2,1,0:T(8,128)}, f32[16,128]{1,0:T(8,128)}) custom-call(bf16[80,640,128]{2,1,0:T(8,128)(2,1)} %bitcast.147, bf16[32,128]{1,0:T(8,128)(2,1)} %pad_maximum_fusion.4.weight, bf16[10,80,640]{2,1,0:T(8,128)(2,1)} %bitcast.167, bf16[6,80,640]{2,1,0:T(8,128)(2,1)} %bitcast.173), custom_call_target="tpu_custom_call" | custom-call | flops 1 | bytes 1 | tf_op jit(solution)/shard_map/pallas_call | solution.py:287
  384.2 2.3 collective-permute-done.15
  386.6 1.4 collective-permute-start.23
  388.0 3.1 collective-permute-start.21
  391.0 12.2 %shard_map.485 = (f32[80,640,128]{2,1,0:T(8,128)}, f32[16,128]{1,0:T(8,128)}) custom-call(bf16[80,640,128]{2,1,0:T(8,128)(2,1)} %bitcast.148, bf16[32,128]{1,0:T(8,128)(2,1)} %pad_maximum_fusion.4.weight, bf16[10,80,640]{2,1,0:T(8,128)(2,1)} %bitcast.168, bf16[6,80,640]{2,1,0:T(8,128)(2,1)} %bitcast.174, ...), custom_call_target="tpu_custom_call", output_to_operand_aliasing={{0}: (4, {})} | custom-call | flops 1 | bytes 1 | tf_op jit(solution)/shard_map/pallas_call | solution.py:287
  404.8 1.5 convolution_add_fusion.5
  406.3 1.4 collective-permute-start.20
  407.8 2.9 collective-permute-start.18
  411.5 1.2 select_bitcast_fusion.7
  412.9 2.3 broadcast_in_dim.26
  415.1 5.0 %all-to-all-start.3 = ((bf16[4,1280,384]{2,1,0:T(8,128)(2,1)}), bf16[4,1280,384]{2,1,0:T(8,128)(2,1)}, u32[]{:S(2)}, u32[]{:S(2)}) async-start(bf16[4,1280,384]{2,1,0:T(8,128)(2,1)} %broadcast_in_dim.26), calls=%async_computation.5 | async-start | bytes 7864320 | tf_op jit(solution)/shard_map/all_to_all | solution.py:650
  420.6 1.3 collective-permute-start.6
  422.0 3.1 collective-permute-start.4
  425.1 2.9 convert_element_type.299
  428.4 1.6 pad_maximum_fusion.1
  430.0 1.6 pad_maximum_fusion
  431.5 1.6 slice_bitcast_fusion
  433.1 1.2 fusion.91
  434.3 2.9 collective-permute-start.26
  437.8 5.2 %collective-permute-done.5 = bf16[320,384]{1,0:T(8,128)(2,1)S(1)} collective-permute-done((bf16[320,384]{1,0:T(8,128)(2,1)S(1)}, bf16[320,384]{1,0:T(8,128)(2,1)S(1)}, u32[]{:S(2)}, u32[]{:S(2)}) %collective-permute-start.5) | collective-permute-done | bytes 245792 | tf_op jit(solution)/shard_map/ppermute | solution.py:658
  443.9 21.8 %collective-permute-done.26 = f32[3392]{0:T(1024)S(1)} collective-permute-done((f32[3392]{0:T(1024)S(1)}, f32[3392]{0:T(1024)S(1)}, u32[]{:S(2)}, u32[]{:S(2)}) %collective-permute-start.26) | collective-permute-done | bytes 13600 | tf_op jit(solution)/shard_map/ppermute | solution.py:658
  468.4 2.6 bitcast_convert_fusion
  471.0 1.2 fusion.93
  472.3 2.6 fusion.94
  (217 shorter events, 27.2 us)
Async XLA Ops:
  7.2 82.1 %copy-start = (bf16[384,768]{1,0:T(8,128)(2,1)S(1)}, bf16[384,768]{1,0:T(8,128)(2,1)}, u32[]{:S(2)}) copy-start(bf16[384,768]{1,0:T(8,128)(2,1)} %param.36) | copy-start | bytes 1769476
  7.2 101.5 %all-gather.5.cloned.1.call-start = ((), (), s32[]{:S(2)}) async-start(), calls=%async_computation.8 | async-start | bytes 5120000 | tf_op jit(solution)/shard_map/all_gather | solution.py:783
  11.4 12.3 %copy-start.39 = (bf16[384]{0:T(512)(128)(2,1)S(1)}, bf16[384]{0:T(512)(128)(2,1)}, u32[]{:S(2)}) copy-start(bf16[384]{0:T(512)(128)(2,1)} %param.47) | copy-start | bytes 2308
  11.4 12.4 %copy-start.3 = (bf16[1,320,384]{2,1,0:T(8,128)(2,1)S(1)}, bf16[1,320,384]{2,1,0:T(8,128)(2,1)}, u32[]{:S(2)}) copy-start(bf16[1,320,384]{2,1,0:T(8,128)(2,1)} %param.29) | copy-start | bytes 737284
  11.4 12.8 %copy-start.34 = (bf16[768]{0:T(1024)(128)(2,1)S(1)}, bf16[768]{0:T(1024)(128)(2,1)}, u32[]{:S(2)}) copy-start(bf16[768]{0:T(1024)(128)(2,1)} %param.49) | copy-start | bytes 4612
  11.4 12.8 %copy-start.35 = (bf16[768]{0:T(1024)(128)(2,1)S(1)}, bf16[768]{0:T(1024)(128)(2,1)}, u32[]{:S(2)}) copy-start(bf16[768]{0:T(1024)(128)(2,1)} %param.55) | copy-start | bytes 4612
  11.4 12.8 %copy-start.9 = (bf16[384,768]{1,0:T(8,128)(2,1)S(1)}, bf16[384,768]{1,0:T(8,128)(2,1)}, u32[]{:S(2)}) copy-start(bf16[384,768]{1,0:T(8,128)(2,1)} %param.50) | copy-start | bytes 1769476
  23.7 142.0 %all-gather.7.cloned.1.call-start = ((), (), s32[]{:S(2)}) async-start(), calls=%async_computation.9 | async-start | bytes 3072000 | tf_op jit(solution)/shard_map/all_gather | solution.py:783
  28.6 51.9 %copy-start.4 = (f32[320,768]{1,0:T(8,128)S(1)}, f32[320,768]{1,0:T(8,128)}, u32[]{:S(2)}) copy-start(f32[320,768]{1,0:T(8,128)} %fusion.15.lifting.lifting_second) | copy-start | bytes 2949124
  81.9 3.2 copy-start.10
  82.0 3.2 copy-start.8
  82.0 3.2 copy-start.16
  84.2 3.1 copy-start.40
  84.2 3.1 copy-start.38
  84.2 3.7 copy-start.36
  84.2 3.7 copy-start.37
  84.2 3.7 copy-start.21
  86.7 22.0 %collective-permute-start = (bf16[6144,384]{1,0:T(8,128)(2,1)}, bf16[6144,384]{1,0:T(8,128)(2,1)}, u32[]{:S(2)}, u32[]{:S(2)}) collective-permute-start(bf16[6144,384]{1,0:T(8,128)(2,1)} %get-tuple-element.352), channel_id=1, source_target_pairs={{0,1},{1,0},{2,3},{3,2},{4,5},{5,4},{6,7},{7,6},{8,9},{9,8},{10,11... | collective-permute-start | bytes 14155784 | tf_op jit(solution)/shard_map/ppermute | solution.py:646
  108.6 12.6 %collective-permute-start.1 = (bf16[4,2,768,384]{3,2,1,0:T(8,128)(2,1)}, bf16[4,2,768,384]{3,2,1,0:T(8,128)(2,1)}, u32[]{:S(2)}, u32[]{:S(2)}) collective-permute-start(bf16[4,2,768,384]{3,2,1,0:T(8,128)(2,1)} %get-tuple-element.150.mine), channel_id=1, source_target_pairs={{0,1},{1,0},{2,3},{3,2},{4,5},{5,4},{6,7},{7,6},{8,9},{9,8},{10,11... | collective-permute-start | bytes 14155784 | tf_op jit(solution)/shard_map/ppermute | solution.py:646
  115.9 65.6 %all-to-all-start = ((bf16[4,1536,384]{2,1,0:T(8,128)(2,1)}), bf16[4,1536,384]{2,1,0:T(8,128)(2,1)}, u32[]{:S(2)}, u32[]{:S(2)}) async-start(bf16[4,1536,384]{2,1,0:T(8,128)(2,1)} %bitcast.161), calls=%async_computation | async-start | bytes 9437184 | tf_op jit(solution)/shard_map/all_to_all | solution.py:650
  121.3 150.9 %reduce-scatter.3.cloned.1.call-start = ((), (), s32[]{:S(2)}) async-start(), calls=%async_computation.6 | async-start | bytes 5120000 | tf_op jit(solution)/shard_map/reduce_scatter | solution.py:789
  165.4 43.6 %collective-permute-start.2 = (bf16[4,2,480,384]{3,2,1,0:T(8,128)(2,1)}, bf16[4,2,480,384]{3,2,1,0:T(8,128)(2,1)}, u32[]{:S(2)}, u32[]{:S(2)}) collective-permute-start(bf16[4,2,480,384]{3,2,1,0:T(8,128)(2,1)} %get-tuple-element.176), channel_id=1, source_target_pairs={{0,1},{1,0},{2,3},{3,2},{4,5},{5,4},{6,7},{7,6},{8,9},{9,8},{10,11... | collective-permute-start | bytes 8847368 | tf_op jit(solution)/shard_map/ppermute | solution.py:646
  165.6 182.3 %reduce-scatter.5.cloned.1.call-start = ((), (), s32[]{:S(2)}) async-start(), calls=%async_computation.7 | async-start | bytes 3072000 | tf_op jit(solution)/shard_map/reduce_scatter | solution.py:789
  200.9 8.1 %collective-permute-start.3 = (bf16[4,2,288,384]{3,2,1,0:T(8,128)(2,1)}, bf16[4,2,288,384]{3,2,1,0:T(8,128)(2,1)S(1)}, u32[]{:S(2)}, u32[]{:S(2)}) collective-permute-start(bf16[4,2,288,384]{3,2,1,0:T(8,128)(2,1)} %get-tuple-element.177), channel_id=1, source_target_pairs={{0,1},{1,0},{2,3},{3,2},{4,5},{5,4},{6,7},{7,6},{8,9},{9,8},{10,11... | collective-permute-start | bytes 5308424 | tf_op jit(solution)/shard_map/ppermute | solution.py:646
  203.6 59.7 %collective-permute-start.9 = (bf16[384,384]{1,0:T(8,128)(2,1)}, bf16[384,384]{1,0:T(8,128)(2,1)S(1)}, u32[]{:S(2)}, u32[]{:S(2)}) collective-permute-start(bf16[384,384]{1,0:T(8,128)(2,1)} %get-tuple-element.333), channel_id=1, source_target_pairs={{0,6},{2,4},{4,2},{6,0},{1,7},{3,5},{5,3},{7,1},{8,14},{10,12},{12... | collective-permute-start | bytes 884744 | tf_op jit(solution)/shard_map/ppermute | solution.py:658
  208.4 55.6 %collective-permute-start.8 = (bf16[384,384]{1,0:T(8,128)(2,1)}, bf16[384,384]{1,0:T(8,128)(2,1)}, u32[]{:S(2)}, u32[]{:S(2)}) collective-permute-start(bf16[384,384]{1,0:T(8,128)(2,1)} %get-tuple-element.334), channel_id=1, source_target_pairs={{0,4},{2,6},{4,0},{6,2},{1,5},{3,7},{5,1},{7,3},{8,12},{10,14},{12... | collective-permute-start | bytes 884744 | tf_op jit(solution)/shard_map/ppermute | solution.py:658
  208.4 55.6 %collective-permute-start.7 = (bf16[384,384]{1,0:T(8,128)(2,1)S(1)}, bf16[384,384]{1,0:T(8,128)(2,1)}, u32[]{:S(2)}, u32[]{:S(2)}) collective-permute-start(bf16[384,384]{1,0:T(8,128)(2,1)S(1)} %get-tuple-element.335), channel_id=1, source_target_pairs={{0,2},{2,0},{4,6},{6,4},{1,3},{3,1},{5,7},{7,5},{8,10},{10,8},{12,... | collective-permute-start | bytes 884744 | tf_op jit(solution)/shard_map/ppermute | solution.py:658
  241.3 24.1 %copy-start.1 = (f32[320,768]{1,0:T(8,128)S(1)}, f32[320,768]{1,0:T(8,128)}, u32[]{:S(2)}) copy-start(f32[320,768]{1,0:T(8,128)} %fusion.3.finish) | copy-start | bytes 2949124
  241.3 24.1 %copy-start.2 = (f32[320,768]{1,0:T(8,128)S(1)}, f32[320,768]{1,0:T(8,128)}, u32[]{:S(2)}) copy-start(f32[320,768]{1,0:T(8,128)} %fusion.7.lifting.lifting_first) | copy-start | bytes 2949124
  241.3 24.1 %copy-start.14 = (f32[320,768]{1,0:T(8,128)S(1)}, f32[320,768]{1,0:T(8,128)}, u32[]{:S(2)}) copy-start(f32[320,768]{1,0:T(8,128)} %get-tuple-element.188) | copy-start | bytes 2949124
  241.3 24.1 %copy-start.15 = (f32[320,768]{1,0:T(8,128)S(1)}, f32[320,768]{1,0:T(8,128)}, u32[]{:S(2)}) copy-start(f32[320,768]{1,0:T(8,128)} %get-tuple-element.184) | copy-start | bytes 2949124
  272.2 7.1 %collective-permute-start.13 = (bf16[5120,384]{1,0:T(8,128)(2,1)}, bf16[5120,384]{1,0:T(8,128)(2,1)}, u32[]{:S(2)}, u32[]{:S(2)}) collective-permute-start(bf16[5120,384]{1,0:T(8,128)(2,1)} %get-tuple-element.346), channel_id=1, source_target_pairs={{0,1},{1,0},{2,3},{3,2},{4,5},{5,4},{6,7},{7,6},{8,9},{9,8},{10,11... | collective-permute-start | bytes 11796488 | tf_op jit(solution)/shard_map/ppermute | solution.py:646
  285.9 6.8 %copy-start.7 = (f32[320,768]{1,0:T(8,128)S(1)}, f32[320,768]{1,0:T(8,128)}, u32[]{:S(2)}) copy-start(f32[320,768]{1,0:T(8,128)} %get-tuple-element.140) | copy-start | bytes 2949124
  285.9 62.0 %all-to-all-start.1 = ((bf16[4,1280,384]{2,1,0:T(8,128)(2,1)}), bf16[4,1280,384]{2,1,0:T(8,128)(2,1)}, u32[]{:S(2)}, u32[]{:S(2)}) async-start(bf16[4,1280,384]{2,1,0:T(8,128)(2,1)} %bitcast.162), calls=%async_computation.2 | async-start | bytes 7864320 | tf_op jit(solution)/shard_map/all_to_all | solution.py:650
  291.0 8.5 %copy-start.19 = (bf16[384,768]{1,0:T(8,128)(2,1)S(1)}, bf16[384,768]{1,0:T(8,128)(2,1)}, u32[]{:S(2)}) copy-start(bf16[384,768]{1,0:T(8,128)(2,1)} %param.34) | copy-start | bytes 1769476
  295.1 18.0 %collective-permute-start.12 = (bf16[384,384]{1,0:T(8,128)(2,1)S(1)}, bf16[384,384]{1,0:T(8,128)(2,1)S(1)}, u32[]{:S(2)}, u32[]{:S(2)}) collective-permute-start(bf16[384,384]{1,0:T(8,128)(2,1)S(1)} %add_convert_fusion.5), channel_id=1, source_target_pairs={{0,6},{2,4},{4,2},{6,0},{1,7},{3,5},{5,3},{7,1},{8,14},{10,12},{12... | collective-permute-start | bytes 884744 | tf_op jit(solution)/shard_map/ppermute | solution.py:658
  298.8 49.2 %collective-permute-start.11 = (bf16[384,384]{1,0:T(8,128)(2,1)S(1)}, bf16[384,384]{1,0:T(8,128)(2,1)S(1)}, u32[]{:S(2)}, u32[]{:S(2)}) collective-permute-start(bf16[384,384]{1,0:T(8,128)(2,1)S(1)} %add_convert_fusion.5), channel_id=1, source_target_pairs={{0,4},{2,6},{4,0},{6,2},{1,5},{3,7},{5,1},{7,3},{8,12},{10,14},{12... | collective-permute-start | bytes 884744 | tf_op jit(solution)/shard_map/ppermute | solution.py:658
  298.8 49.2 %collective-permute-start.10 = (bf16[384,384]{1,0:T(8,128)(2,1)S(1)}, bf16[384,384]{1,0:T(8,128)(2,1)S(1)}, u32[]{:S(2)}, u32[]{:S(2)}) collective-permute-start(bf16[384,384]{1,0:T(8,128)(2,1)S(1)} %add_convert_fusion.5), channel_id=1, source_target_pairs={{0,2},{2,0},{4,6},{6,4},{1,3},{3,1},{5,7},{7,5},{8,10},{10,8},{12,... | collective-permute-start | bytes 884744 | tf_op jit(solution)/shard_map/ppermute | solution.py:658
  313.1 34.9 %copy-start.28 = (bf16[384,384]{1,0:T(8,128)(2,1)}, bf16[384,384]{1,0:T(8,128)(2,1)S(1)}, u32[]{:S(2)}) copy-start(bf16[384,384]{1,0:T(8,128)(2,1)S(1)} %collective-permute-done.12) | copy-start | bytes 884740
  352.8 5.2 %copy-start.27 = (f32[768,1]{1,0:T(8,128)S(1)}, f32[768,1]{1,0:T(8,128)}, u32[]{:S(2)}) copy-start(f32[768,1]{1,0:T(8,128)} %get-tuple-element.226) | copy-start | bytes 9220
  352.8 5.4 %copy-start.24 = (bf16[320,768]{1,0:T(8,128)(2,1)S(1)}, bf16[320,768]{1,0:T(8,128)(2,1)}, u32[]{:S(2)}) copy-start(bf16[320,768]{1,0:T(8,128)(2,1)} %copy-done.23) | copy-start | bytes 1474564
  352.8 5.4 %copy-start.25 = (f32[320,384]{1,0:T(8,128)S(1)}, f32[320,384]{1,0:T(8,128)}, u32[]{:S(2)}) copy-start(f32[320,384]{1,0:T(8,128)} %convolution_add_fusion.6) | copy-start | bytes 1474564
  352.8 58.6 %all-to-all-start.2 = ((bf16[4,1536,384]{2,1,0:T(8,128)(2,1)}), bf16[4,1536,384]{2,1,0:T(8,128)(2,1)}, u32[]{:S(2)}, u32[]{:S(2)}) async-start(bf16[4,1536,384]{2,1,0:T(8,128)(2,1)} %broadcast_in_dim.24), calls=%async_computation.4 | async-start | bytes 9437184 | tf_op jit(solution)/shard_map/all_to_all | solution.py:650
  363.5 20.7 %collective-permute-start.16 = (bf16[320,384]{1,0:T(8,128)(2,1)S(1)}, bf16[320,384]{1,0:T(8,128)(2,1)S(1)}, u32[]{:S(2)}, u32[]{:S(2)}) collective-permute-start(bf16[320,384]{1,0:T(8,128)(2,1)S(1)} %get-tuple-element.341), channel_id=1, source_target_pairs={{0,6},{2,4},{4,2},{6,0},{1,7},{3,5},{5,3},{7,1},{8,14},{10,12},{12... | collective-permute-start | bytes 737288 | tf_op jit(solution)/shard_map/ppermute | solution.py:658
  365.0 21.4 %collective-permute-start.15 = (bf16[320,384]{1,0:T(8,128)(2,1)S(1)}, bf16[320,384]{1,0:T(8,128)(2,1)S(1)}, u32[]{:S(2)}, u32[]{:S(2)}) collective-permute-start(bf16[320,384]{1,0:T(8,128)(2,1)S(1)} %get-tuple-element.342), channel_id=1, source_target_pairs={{0,4},{2,6},{4,0},{6,2},{1,5},{3,7},{5,1},{7,3},{8,12},{10,14},{12... | collective-permute-start | bytes 737288 | tf_op jit(solution)/shard_map/ppermute | solution.py:658
  365.3 21.1 %collective-permute-start.14 = (bf16[320,384]{1,0:T(8,128)(2,1)S(1)}, bf16[320,384]{1,0:T(8,128)(2,1)S(1)}, u32[]{:S(2)}, u32[]{:S(2)}) collective-permute-start(bf16[320,384]{1,0:T(8,128)(2,1)S(1)} %get-tuple-element.343), channel_id=1, source_target_pairs={{0,2},{2,0},{4,6},{6,4},{1,3},{3,1},{5,7},{7,5},{8,10},{10,8},{12,... | collective-permute-start | bytes 737288 | tf_op jit(solution)/shard_map/ppermute | solution.py:658
  386.6 21.3 %collective-permute-start.23 = (bf16[320,384]{1,0:T(8,128)(2,1)S(1)}, bf16[320,384]{1,0:T(8,128)(2,1)S(1)}, u32[]{:S(2)}, u32[]{:S(2)}) collective-permute-start(bf16[320,384]{1,0:T(8,128)(2,1)S(1)} %add_convert_fusion.6), channel_id=1, source_target_pairs={{0,6},{2,4},{4,2},{6,0},{1,7},{3,5},{5,3},{7,1},{8,14},{10,12},{12... | collective-permute-start | bytes 737288 | tf_op jit(solution)/shard_map/ppermute | solution.py:658
  387.9 22.8 %collective-permute-start.22 = (bf16[320,384]{1,0:T(8,128)(2,1)S(1)}, bf16[320,384]{1,0:T(8,128)(2,1)}, u32[]{:S(2)}, u32[]{:S(2)}) collective-permute-start(bf16[320,384]{1,0:T(8,128)(2,1)S(1)} %add_convert_fusion.6), channel_id=1, source_target_pairs={{0,4},{2,6},{4,0},{6,2},{1,5},{3,7},{5,1},{7,3},{8,12},{10,14},{12... | collective-permute-start | bytes 737288 | tf_op jit(solution)/shard_map/ppermute | solution.py:658
  388.0 22.8 %collective-permute-start.21 = (bf16[320,384]{1,0:T(8,128)(2,1)S(1)}, bf16[320,384]{1,0:T(8,128)(2,1)}, u32[]{:S(2)}, u32[]{:S(2)}) collective-permute-start(bf16[320,384]{1,0:T(8,128)(2,1)S(1)} %add_convert_fusion.6), channel_id=1, source_target_pairs={{0,2},{2,0},{4,6},{6,4},{1,3},{3,1},{5,7},{7,5},{8,10},{10,8},{12,... | collective-permute-start | bytes 737288 | tf_op jit(solution)/shard_map/ppermute | solution.py:658
  391.0 12.2 %copy-start.32 = (bf16[128,16]{0,1:T(8,128)(2,1)S(1)}, bf16[128,16]{0,1:T(8,128)(2,1)}, u32[]{:S(2)}) copy-start(bf16[128,16]{0,1:T(8,128)(2,1)} %param.44) | copy-start | bytes 12292
  391.0 12.2 %copy-start.33 = (f32[16,128]{1,0:T(8,128)S(1)}, f32[16,128]{1,0:T(8,128)}, u32[]{:S(2)}) copy-start(f32[16,128]{1,0:T(8,128)} %get-tuple-element.227) | copy-start | bytes 24580
  391.0 13.7 %copy-start.26 = (f32[320,384]{1,0:T(8,128)S(1)}, f32[320,384]{1,0:T(8,128)}, u32[]{:S(2)}) copy-start(f32[320,384]{1,0:T(8,128)} %get-tuple-element.309) | copy-start | bytes 1474564
  404.7 1.6 collective-permute-start.17
  406.3 15.7 %collective-permute-start.20 = (f32[3392]{0:T(1024)S(1)}, f32[3392]{0:T(1024)S(1)}, u32[]{:S(2)}, u32[]{:S(2)}) collective-permute-start(f32[3392]{0:T(1024)S(1)} %add.292), channel_id=1, source_target_pairs={{0,6},{2,4},{4,2},{6,0},{1,7},{3,5},{5,3},{7,1},{8,14},{10,12},{12... | collective-permute-start | bytes 40712 | tf_op jit(solution)/shard_map/ppermute | solution.py:658
  407.7 17.4 %collective-permute-start.19 = (f32[3392]{0:T(1024)S(1)}, f32[3392]{0:T(1024)S(1)}, u32[]{:S(2)}, u32[]{:S(2)}) collective-permute-start(f32[3392]{0:T(1024)S(1)} %add.292), channel_id=1, source_target_pairs={{0,4},{2,6},{4,0},{6,2},{1,5},{3,7},{5,1},{7,3},{8,12},{10,14},{12... | collective-permute-start | bytes 40712 | tf_op jit(solution)/shard_map/ppermute | solution.py:658
  407.8 17.2 %collective-permute-start.18 = (f32[3392]{0:T(1024)S(1)}, f32[3392]{0:T(1024)S(1)}, u32[]{:S(2)}, u32[]{:S(2)}) collective-permute-start(f32[3392]{0:T(1024)S(1)} %add.292), channel_id=1, source_target_pairs={{0,2},{2,0},{4,6},{6,4},{1,3},{3,1},{5,7},{7,5},{8,10},{10,8},{12,... | collective-permute-start | bytes 40712 | tf_op jit(solution)/shard_map/ppermute | solution.py:658
  415.1 5.0 %copy-start.22 = (bf16[384,768]{1,0:T(8,128)(2,1)S(1)}, bf16[384,768]{1,0:T(8,128)(2,1)}, u32[]{:S(2)}) copy-start(bf16[384,768]{1,0:T(8,128)(2,1)} %param.45) | copy-start | bytes 1769476
  415.1 53.3 %all-to-all-start.3 = ((bf16[4,1280,384]{2,1,0:T(8,128)(2,1)}), bf16[4,1280,384]{2,1,0:T(8,128)(2,1)}, u32[]{:S(2)}, u32[]{:S(2)}) async-start(bf16[4,1280,384]{2,1,0:T(8,128)(2,1)} %broadcast_in_dim.26), calls=%async_computation.5 | async-start | bytes 7864320 | tf_op jit(solution)/shard_map/all_to_all | solution.py:650
  420.6 17.1 %collective-permute-start.6 = (bf16[320,384]{1,0:T(8,128)(2,1)S(1)}, bf16[320,384]{1,0:T(8,128)(2,1)S(1)}, u32[]{:S(2)}, u32[]{:S(2)}) collective-permute-start(bf16[320,384]{1,0:T(8,128)(2,1)S(1)} %fusion.16), channel_id=1, source_target_pairs={{0,6},{2,4},{4,2},{6,0},{1,7},{3,5},{5,3},{7,1},{8,14},{10,12},{12... | collective-permute-start | bytes 737288 | tf_op jit(solution)/shard_map/ppermute | solution.py:658
  422.0 21.1 %collective-permute-start.5 = (bf16[320,384]{1,0:T(8,128)(2,1)S(1)}, bf16[320,384]{1,0:T(8,128)(2,1)S(1)}, u32[]{:S(2)}, u32[]{:S(2)}) collective-permute-start(bf16[320,384]{1,0:T(8,128)(2,1)S(1)} %fusion.16), channel_id=1, source_target_pairs={{0,4},{2,6},{4,0},{6,2},{1,5},{3,7},{5,1},{7,3},{8,12},{10,14},{12... | collective-permute-start | bytes 737288 | tf_op jit(solution)/shard_map/ppermute | solution.py:658
  422.0 21.1 %collective-permute-start.4 = (bf16[320,384]{1,0:T(8,128)(2,1)S(1)}, bf16[320,384]{1,0:T(8,128)(2,1)S(1)}, u32[]{:S(2)}, u32[]{:S(2)}) collective-permute-start(bf16[320,384]{1,0:T(8,128)(2,1)S(1)} %fusion.16), channel_id=1, source_target_pairs={{0,2},{2,0},{4,6},{6,4},{1,3},{3,1},{5,7},{7,5},{8,10},{10,8},{12,... | collective-permute-start | bytes 737288 | tf_op jit(solution)/shard_map/ppermute | solution.py:658
  434.3 31.4 %collective-permute-start.26 = (f32[3392]{0:T(1024)S(1)}, f32[3392]{0:T(1024)S(1)}, u32[]{:S(2)}, u32[]{:S(2)}) collective-permute-start(f32[3392]{0:T(1024)S(1)} %add_add_fusion.1), channel_id=1, source_target_pairs={{0,24},{8,16},{16,8},{24,0},{1,25},{9,17},{17,9},{25,1},{2,26},{10... | collective-permute-start | bytes 40712 | tf_op jit(solution)/shard_map/ppermute | solution.py:658
  437.2 28.6 %collective-permute-start.25 = (f32[3392]{0:T(1024)S(1)}, f32[3392]{0:T(1024)S(1)}, u32[]{:S(2)}, u32[]{:S(2)}) collective-permute-start(f32[3392]{0:T(1024)S(1)} %add_add_fusion.1), channel_id=1, source_target_pairs={{0,16},{8,24},{16,0},{24,8},{1,17},{9,25},{17,1},{25,9},{2,18},{10... | collective-permute-start | bytes 40712 | tf_op jit(solution)/shard_map/ppermute | solution.py:658
  437.8 28.0 %collective-permute-start.24 = (f32[3392]{0:T(1024)S(1)}, f32[3392]{0:T(1024)S(1)}, u32[]{:S(2)}, u32[]{:S(2)}) collective-permute-start(f32[3392]{0:T(1024)S(1)} %add_add_fusion.1), channel_id=1, source_target_pairs={{0,8},{8,0},{16,24},{24,16},{1,9},{9,1},{17,25},{25,17},{2,10},{10... | collective-permute-start | bytes 40712 | tf_op jit(solution)/shard_map/ppermute | solution.py:658
  (12 other events, 21.8 us)
Sparse Core Ops, SparseCore 0:
  23.8 81.8 all-gather.4
  108.9 55.0 all-gather.6
  166.3 96.2 reduce-scatter.2
  272.3 70.1 reduce-scatter.4
